TPU v7x, 256 devices: a whole 4x4x8 slice. The times are simulated.
256 devices in a mesh: prow: 16 (over y, x), pcol: 16 (over z, core).
Axes of the slice: x: 4, y: 4, z: 8, core: 2. Of those that a mesh axis runs over, the one named last changes fastest.
Arguments:
- ginv_anc: float32 [8192, 8192], P('prow', 'pcol'), as said below
- factor_one: float32 [8192, 2048], P('prow', 'pcol'), may hold values from -0.0625 to 0.0625
- pattern_one: int32 [64, 16], replicated, may hold values from 0 to 1
- dinv_one: float32 [2048, 128], replicated
- factor_two: float32 [8192, 2048], P('prow', 'pcol'), may hold values from -0.0625 to 0.0625
- factor_parent: float32 [128, 2048], P(None, 'pcol'), may hold values from -0.5 to 0.5
- pattern_two: int32 [64, 16], replicated, may hold values from 0 to 1, as said below
- parent: int32 [16], replicated, may hold values from 0 to 15, as said below
- dinv_two: float32 [2048, 128], P('prow')
Outputs:
- anc_one: float32 [2048, 8192], P('prow', 'pcol')
- diag_one: float32 [2048, 128], P('prow')
- anc_two: float32 [2048, 8192], P('prow', 'pcol')
- cross: float32 [2048, 128], P('prow')
- diag_two: float32 [2048, 128], P('prow')
Inputs may be any that keep to these rules, and one draw needn't show every extreme that they name: ginv_anc is symmetric. Each upper supernode is the parent of exactly one lower supernode. pattern_two[i, m] <= pattern_one[i, parent[m]].
All inputs are finite; a program needn't handle non-finite values.
Results may differ from a plain program's by a relative error of at most 0.000086.
Values sent between devices are 32-bit elements; how exact they have to be, the bound alone decides.
No kernel may reach another device: no remote copies, remote signals or barrier semaphores. Data moves between devices by JAX's collectives and lax.ppermute only.
A program may use at most 128 MiB of HBM per device.

v0:
```python
import jax
import jax.numpy as jnp
from jax import lax
from jax.sharding import PartitionSpec as P

precise = lax.Precision.HIGHEST


def block_mask(pattern, rows, cols, row_start, col_start, width):
    blocks = lax.dynamic_slice_in_dim(pattern, row_start // width, rows // width, 0).astype(
        jnp.float32
    )
    column_ids = (col_start + jnp.arange(cols, dtype=jnp.int32)) // width
    select = (column_ids[None, :] == jnp.arange(pattern.shape[1], dtype=jnp.int32)[:, None]).astype(
        jnp.float32
    )
    coarse = jnp.dot(blocks, select, precision=precise, preferred_element_type=jnp.float32)
    return jnp.repeat(coarse, width, axis=0)


def gather_cols(values):
    return lax.all_gather(values, "pcol", axis=1, tiled=True)


def reduce_rows(left, block):
    return lax.psum_scatter(
        -lax.dot_general(
            left,
            block,
            (((0,), (0,)), ((), ())),
            precision=precise,
            preferred_element_type=jnp.float32,
        ),
        "prow",
        scatter_dimension=0,
        tiled=True,
    )


def root_piece(left):
    ratio = lax.axis_size("pcol") // lax.axis_size("prow")
    column = lax.axis_index("pcol")
    root = column // ratio
    return (left, root)


def deliver(piece, root):
    kept = jnp.where(lax.axis_index("prow") == root, piece, jnp.zeros_like(piece))
    return lax.psum_scatter(kept, "prow", scatter_dimension=1, tiled=True)


def diag_sum(values):
    return lax.psum(values, "pcol")


def local(
    ginv_anc,
    factor_one,
    pattern_one,
    dinv_one,
    factor_two,
    factor_parent,
    pattern_two,
    parent,
    dinv_two,
):
    row_index = lax.axis_index("prow")
    col_index = lax.axis_index("pcol")
    anc_rows, anc_cols = ginv_anc.shape
    width = dinv_one.shape[1]
    count_k = dinv_one.shape[0] // width
    one_cols = factor_one.shape[1]
    lower_one = factor_one * block_mask(
        pattern_one, anc_rows, one_cols, row_index * anc_rows, col_index * one_cols, width
    )
    rows_one = gather_cols(lower_one)
    anc_one = reduce_rows(rows_one, ginv_anc)
    piece_one, root = root_piece(rows_one)
    own_cols = deliver(piece_one, root)
    local_k = anc_one.shape[0]
    blocks_k = local_k // width
    part_one = jnp.einsum(
        "kba,akc->kbc",
        anc_one.reshape(blocks_k, width, anc_cols),
        own_cols.reshape(anc_cols, blocks_k, width),
        precision=precise,
    )
    sum_one = diag_sum(part_one)
    own_dinv = lax.dynamic_slice_in_dim(dinv_one, row_index * local_k, local_k, 0)
    diag_one = own_dinv - sum_one.reshape(local_k, width)
    two_cols = factor_two.shape[1]
    lower_two = factor_two * block_mask(
        pattern_two, anc_rows, two_cols, row_index * anc_rows, col_index * two_cols, width
    )
    joined = gather_cols(jnp.concatenate([lower_two, factor_parent], axis=0))
    rows_two = joined[:anc_rows]
    par_all = joined[anc_rows:]
    local_m = dinv_two.shape[0]
    blocks_m = local_m // width
    own_parent = lax.dynamic_slice_in_dim(parent, row_index * blocks_m, blocks_m, 0)
    par_local = lax.dynamic_slice_in_dim(par_all, row_index * local_m, local_m, 1).reshape(
        width, blocks_m, width
    )
    piece_two, root_two = root_piece(rows_two)
    own_two = deliver(piece_two, root_two).reshape(anc_cols, blocks_m, width)
    anc_two = reduce_rows(rows_two, ginv_anc)
    anc_all, diag_all = (
        lax.all_gather(anc_one, "prow", axis=0, tiled=True),
        lax.all_gather(diag_one, "prow", axis=0, tiled=True),
    )
    anc_sel = jnp.take(anc_all.reshape(count_k, width, anc_cols), own_parent, axis=0)
    diag_sel = jnp.take(diag_all.reshape(count_k, width, width), own_parent, axis=0)
    anc_two = anc_two - jnp.einsum("kmj,mka->mja", par_local, anc_sel, precision=precise).reshape(
        local_m, anc_cols
    )
    part_cross = jnp.einsum("amj,mka->mjk", own_two, anc_sel, precision=precise)
    part_diag = jnp.einsum(
        "mja,amc->mjc", anc_two.reshape(blocks_m, width, anc_cols), own_two, precision=precise
    )
    sums = diag_sum(jnp.stack([part_cross, part_diag]))
    cross = -(sums[0] + jnp.einsum("kmj,mkc->mjc", par_local, diag_sel, precision=precise))
    diag_two = dinv_two - (
        sums[1] + jnp.einsum("mjk,kmc->mjc", cross, par_local, precision=precise)
    ).reshape(local_m, width)
    return (anc_one, diag_one, anc_two, cross.reshape(local_m, width), diag_two)


def solution(mesh):
    return jax.shard_map(
        local,
        mesh=mesh,
        in_specs=(
            P("prow", "pcol"),
            P("prow", "pcol"),
            P(),
            P(),
            P("prow", "pcol"),
            P(None, "pcol"),
            P(),
            P(),
            P("prow", None),
        ),
        out_specs=(
            P("prow", "pcol"),
            P("prow", None),
            P("prow", "pcol"),
            P("prow", None),
            P("prow", None),
        ),
        check_vma=False,
    )
```

profile of v0, /device:TPU:7, one launch (start us, length us, event | category | flops | bytes accessed | tf_op | source)
XLA Modules:
  0.0 685.0 jit_solution(12191034714136957755)
XLA Ops:
  7.3 1.0 fusion.22
  8.3 1.7 bitcast_multiply_fusion.1
  12.0 1.6 pad_maximum_fusion
  13.7 48.6 %all-gather.5.cloned.1.call-done = f32[512,2048]{1,0:T(8,128)} async-done(((f32[512,128]{1,0:T(8,128)}), f32[512,2048]{1,0:T(8,128)}) %all-gather.5.cloned.1.call-update) | async-done | bytes 4194320 | tf_op jit(solution)/shard_map/all_gather | solution.py:22
  62.3 9.8 %convolution_negate_fusion = f32[2048,512]{1,0:T(8,128)} fusion(f32[512,2048]{1,0:T(8,128)} %all-gather.5.cloned.1.call-done, f32[512,512]{1,0:T(8,128)S(1)} %copy-done), kind=kOutput, calls=%fused_computation.4 | convolution fusion | flops 6443499520 | bytes 9437184 | tf_op jit(solution)/shard_map/dot_general | solution.py:27
  72.2 2.6 broadcast_select_fusion
  74.9 41.1 %all-gather.7.cloned.1.call-done = f32[640,2048]{1,0:T(8,128)} async-done(((f32[640,128]{1,0:T(8,128)}), f32[640,2048]{1,0:T(8,128)}) %all-gather.7.cloned.1.call-update) | async-done | bytes 5242896 | tf_op jit(solution)/shard_map/all_gather | solution.py:22
  116.0 4.8 slice_select_fusion
  120.9 78.3 %reduce-scatter.5.cloned.1.call-done = f32[128,512]{1,0:T(8,128)} async-done(((f32[2048,512]{1,0:T(8,128)}), f32[128,512]{1,0:T(8,128)}) %reduce-scatter.5.cloned.1.call-update) | async-done | bytes 262160 | tf_op jit(solution)/shard_map/reduce_scatter | solution.py:26
  199.2 9.9 %fusion.2 = f32[2048,512]{1,0:T(8,128)} fusion(f32[512,512]{1,0:T(8,128)S(1)} %copy-done, f32[640,2048]{1,0:T(8,128)} %all-gather.7.cloned.1.call-done), kind=kOutput, calls=%fused_computation.3 | convolution fusion | flops 6443499520 | bytes 9437184 | tf_op jit(solution)/shard_map/dot_general | solution.py:27
  212.3 1.3 slice.35
  213.6 71.5 %reduce-scatter.7.cloned.1.call-done = f32[512,128]{1,0:T(8,128)} async-done(((f32[512,2048]{1,0:T(8,128)}), f32[512,128]{1,0:T(8,128)}) %reduce-scatter.7.cloned.1.call-update) | async-done | bytes 262160 | tf_op jit(solution)/shard_map/reduce_scatter | solution.py:49
  285.1 2.0 fusion.36
  287.1 83.6 %reduce-scatter.11.cloned.1.call-done = f32[512,128]{1,0:T(8,128)} async-done(((f32[512,2048]{1,0:T(8,128)}), f32[512,128]{1,0:T(8,128)}) %reduce-scatter.11.cloned.1.call-update) | async-done | bytes 262160 | tf_op jit(solution)/shard_map/reduce_scatter | solution.py:49
  370.7 61.3 %all-gather.9.cloned.1.call-done = f32[2048,512]{1,0:T(8,128)} async-done(((f32[128,512]{1,0:T(8,128)}), f32[2048,512]{1,0:T(8,128)}) %all-gather.9.cloned.1.call-update) | async-done | bytes 4194320 | tf_op jit(solution)/shard_map/all_gather | solution.py:108
  432.0 1.6 convolution_bitcast_fusion.1
  433.6 82.7 %reduce-scatter.9.cloned.1.call-done = f32[128,512]{1,0:T(8,128)} async-done(((f32[2048,512]{1,0:T(8,128)}), f32[128,512]{1,0:T(8,128)}) %reduce-scatter.9.cloned.1.call-update) | async-done | bytes 262160 | tf_op jit(solution)/shard_map/reduce_scatter | solution.py:26
  516.3 1.5 convolution_subtract_fusion
  517.8 1.4 convolution_bitcast_fusion
  520.0 106.4 %all-reduce.3.cloned.1.call-done = (f32[128,128]{1,0:T(8,128)}, f32[2,1,128,128]{3,2,1,0:T(8,128)}) async-done(((f32[128,128]{1,0:T(8,128)}, f32[2,1,128,128]{3,2,1,0:T(8,128)}), (f32[128,128]{1,0:T(8,128)}, f32[2,1,128,128]{3,2,1,0:T(8,128)})) %all-reduce.3.cloned.1.call-update) | async-done | bytes 196624 | tf_op jit(solution)/shard_map/psum | solution.py:53
  626.4 1.5 dynamic-slice_subtract_fusion
  627.9 47.6 %all-gather.11.cloned.1.call-done = f32[2048,128]{1,0:T(8,128)} async-done(((f32[128,128]{1,0:T(8,128)}), f32[2048,128]{1,0:T(8,128)}) %all-gather.11.cloned.1.call-update) | async-done | bytes 1048592 | tf_op jit(solution)/shard_map/all_gather | solution.py:109
  675.5 1.2 fusion.6
  676.7 1.7 fusion.5
  (35 shorter events, 4.3 us)
Async XLA Ops:
  7.2 55.1 %copy-start = (f32[512,512]{1,0:T(8,128)S(1)}, f32[512,512]{1,0:T(8,128)}, u32[]{:S(2)}) copy-start(f32[512,512]{1,0:T(8,128)} %param.9) | copy-start | bytes 3145732
  7.2 55.1 %all-gather.5.cloned.1.call-start = ((), (), s32[]{:S(2)}) async-start(), calls=%async_computation.4 | async-start | bytes 4456448 | tf_op jit(solution)/shard_map/all_gather | solution.py:22
  10.0 106.0 %all-gather.7.cloned.1.call-start = ((), (), s32[]{:S(2)}) async-start(), calls=%async_computation.7 | async-start | bytes 5570560 | tf_op jit(solution)/shard_map/all_gather | solution.py:22
  13.6 185.5 %reduce-scatter.5.cloned.1.call-start = ((), (), s32[]{:S(2)}) async-start(), calls=%async_computation.5 | async-start | bytes 4456448 | tf_op jit(solution)/shard_map/reduce_scatter | solution.py:26
  72.2 213.0 %reduce-scatter.7.cloned.1.call-start = ((), (), s32[]{:S(2)}) async-start(), calls=%async_computation.6 | async-start | bytes 4456448 | tf_op jit(solution)/shard_map/reduce_scatter | solution.py:49
  74.8 295.8 %reduce-scatter.11.cloned.1.call-start = ((), (), s32[]{:S(2)}) async-start(), calls=%async_computation.10 | async-start | bytes 4456448 | tf_op jit(solution)/shard_map/reduce_scatter | solution.py:49
  120.8 311.2 %all-gather.9.cloned.1.call-start = ((), (), s32[]{:S(2)}) async-start(), calls=%async_computation.9 | async-start | bytes 4456448 | tf_op jit(solution)/shard_map/all_gather | solution.py:108
  199.2 317.1 %reduce-scatter.9.cloned.1.call-start = ((), (), s32[]{:S(2)}) async-start(), calls=%async_computation.8 | async-start | bytes 4456448 | tf_op jit(solution)/shard_map/reduce_scatter | solution.py:26
  209.1 0.7 copy-start.5
  209.1 76.0 %copy-start.1 = (f32[128,512]{1,0:T(8,128)S(1)}, f32[128,512]{1,0:T(8,128)}, u32[]{:S(2)}) copy-start(f32[128,512]{1,0:T(8,128)} %reduce-scatter.5.cloned.1.call-done) | copy-start | bytes 786436
  209.1 467.6 %copy-start.4 = (f32[128,128]{1,0:T(8,128)S(1)}, f32[128,128]{1,0:T(8,128)}, u32[]{:S(2)}) copy-start(f32[128,128]{1,0:T(8,128)} %param.17) | copy-start | bytes 196612
  209.2 417.2 %all-reduce.3.cloned.1.call-start = ((), (), s32[]{:S(2)}) async-start(), calls=%async_computation.12 | async-start | bytes 393216 | tf_op jit(solution)/shard_map/psum | solution.py:53
  517.8 160.7 %copy-start.2 = (f32[128,512]{1,0:T(8,128)}, f32[128,512]{1,0:T(8,128)S(1)}, u32[]{:S(2)}) copy-start(f32[128,512]{1,0:T(8,128)S(1)} %convolution_subtract_fusion) | copy-start | bytes 786436
  519.9 155.6 %all-gather.11.cloned.1.call-start = ((), (), s32[]{:S(2)}) async-start(), calls=%async_computation.11 | async-start | bytes 1114112 | tf_op jit(solution)/shard_map/all_gather | solution.py:109
  676.7 1.7 copy-start.3
Sparse Core Ops, SparseCore 0:
  10.3 51.9 all-gather.4
  64.1 51.8 all-gather.6
  120.2 78.9 reduce-scatter.4
  203.1 82.0 reduce-scatter.6
  288.6 82.0 reduce-scatter.10
  373.8 58.1 all-gather.8
  436.0 80.2 reduce-scatter.8
  520.0 106.3 all-reduce.2
  629.7 45.7 all-gather.10
where the time goes:
time: 687 us; the launch traced here: 685 us
  waiting for transfers between devices  621 us (90%)
  matrix products  31 us (5%)
  between operations  15.9 us (2%)
  other arithmetic  13.9 us (2%)
    reduce_scatter x2, waiting for transfers between devices, reduce_rows(): lax.psum_scatter(-lax.dot_general(left, block, (((0,), (0,)), ((), ())),...  161 us
    reduce_scatter x2, waiting for transfers between devices, deliver(): return lax.psum_scatter(kept, 'prow', scatter_dimension=1, tiled=True)  155 us
    psum x1, waiting for transfers between devices, diag_sum(): return lax.psum(values, 'pcol')  106 us
    all_gather x2, waiting for transfers between devices, gather_cols(): return lax.all_gather(values, 'pcol', axis=1, tiled=True)  89.7 us
    all_gather x1, waiting for transfers between devices, local(): lax.all_gather(anc_one, 'prow', axis=0, tiled=True)  61.3 us
    all_gather x1, waiting for transfers between devices, local(): lax.all_gather(diag_one, 'prow', axis=0, tiled=True)  47.6 us
    dot_general x2, matrix products, reduce_rows(): lax.dot_general(left, block, (((0,), (0,)), ((), ())), precision=precise,...  19.7 us
  transfers between devices with their start and end apart: 9, of which 9 were waited for; matrix products, arithmetic and copies ran while one was open for 5% of the time, Pallas kernels for 0%

commit v1 on v0

v1 whole, which is shorter than its diff:
```python
import functools

import jax
import jax.numpy as jnp
from jax import lax
from jax.experimental import pallas as pl
from jax.experimental.pallas import tpu as pltpu
from jax.sharding import PartitionSpec as P

ROWS = 16
COLS = 16
B = 128
KA = 512
PACK = 288
MASKS = ((1, 3, 4, 12), (3, 1, 12, 4), (4, 12, 1, 3), (12, 4, 3, 1))
precise = lax.Precision.HIGHEST


def slot_mask(variant, slot):
    mask = 0
    for bit in range(4):
        if (slot >> (3 - bit)) & 1:
            mask ^= MASKS[variant][bit]
    return mask


def split(value):
    high = value.astype(jnp.bfloat16)
    low = (value - high.astype(jnp.float32)).astype(jnp.bfloat16)
    return high, low


def dot_split(left, right, dims):
    out = None
    for a, b in ((left[0], right[0]), (left[0], right[1]), (left[1], right[0])):
        term = lax.dot_general(a, b, (dims, ((), ())), preferred_element_type=jnp.float32)
        out = term if out is None else out + term
    return out


def product_kernel(scal_ref, all_ref, ginv_ref, *refs):
    sends = refs[0:4]
    keeps = refs[4:8]
    cross_ref = refs[8]
    two_ref, left_ref = refs[9:]
    row = scal_ref[16]
    target = scal_ref[17]
    ginv = split(ginv_ref[...])

    def correct(m, carry):
        packed = all_ref[m, 256:288, :]
        par = jnp.concatenate([packed[:, 128 * i : 128 * i + 128] for i in range(4)], axis=0)
        one = all_ref[scal_ref[m], 0:128, :]
        fix = dot_split(split(par), split(one), ((1,), (0,)))
        two_ref[m] = all_ref[m, 128:256, :] - fix
        return carry

    lax.fori_loop(0, 16, correct, 0)
    cross_ref[0:128, :] = all_ref[scal_ref[target], 0:128, :]
    cross_ref[128:384, :] = all_ref[target, 0:256, :]
    for variant in range(4):
        lo = 32 * variant
        for half in (1, 0):
            for slot in range(8):
                dest = row ^ slot_mask(variant, slot + 8 * half)
                left_ref[64 * slot : 64 * slot + 32, :] = all_ref[dest, lo : lo + 32, :]
                left_ref[64 * slot + 32 : 64 * slot + 64, :] = two_ref[dest, lo : lo + 32, :]
            value = dot_split(split(left_ref[...]), ginv, ((1,), (0,)))
            out = sends[variant] if half else keeps[variant]
            out[...] = -value.reshape(8, 64, KA)


def products(scalars, gathered, ginv):
    part = jax.ShapeDtypeStruct((8, 64, KA), jnp.float32)
    vmem = pl.BlockSpec(memory_space=pltpu.VMEM)
    return pl.pallas_call(
        product_kernel,
        out_shape=[part] * 8 + [jax.ShapeDtypeStruct((384, KA), jnp.float32)],
        in_specs=[pl.BlockSpec(memory_space=pltpu.SMEM), vmem, vmem],
        out_specs=[vmem] * 9,
        scratch_shapes=[
            pltpu.VMEM((16, 128, KA), jnp.float32),
            pltpu.VMEM((512, KA), jnp.float32),
        ],
        compiler_params=pltpu.CompilerParams(vmem_limit_bytes=48 * 1024 * 1024),
        cost_estimate=pl.CostEstimate(
            flops=8_000_000_000, bytes_accessed=20_000_000, transcendentals=0
        ),
    )(scalars, gathered, ginv)


def block_kernel(a_ref, b_ref, c_ref, d_ref, swap_ref, one_ref, two_ref, sums_ref):
    for variant, ref in enumerate((a_ref, b_ref, c_ref, d_ref)):
        one_ref[32 * variant : 32 * variant + 32, :] = ref[0:32, :]
        two_ref[32 * variant : 32 * variant + 32, :] = ref[32:64, :]
    one = split(one_ref[...])
    two = split(two_ref[...])
    nt = ((1,), (1,))
    sums_ref[0] = dot_split(one, split(swap_ref[128:256, :]), nt)
    sums_ref[1] = dot_split(two, split(swap_ref[0:128, :]), nt)
    sums_ref[2] = dot_split(two, split(swap_ref[256:384, :]), nt)


def blocks(parts, swapped):
    vmem = pl.BlockSpec(memory_space=pltpu.VMEM)
    return pl.pallas_call(
        block_kernel,
        out_shape=[
            jax.ShapeDtypeStruct((128, KA), jnp.float32),
            jax.ShapeDtypeStruct((128, KA), jnp.float32),
            jax.ShapeDtypeStruct((3, 128, 128), jnp.float32),
        ],
        in_specs=[vmem] * 5,
        out_specs=[vmem] * 3,
        compiler_params=pltpu.CompilerParams(vmem_limit_bytes=24 * 1024 * 1024),
    )(*parts, swapped)


def reduce_rows(sends, keeps):
    parts = list(keeps)
    going = list(sends)
    for step in range(4):
        got = [
            lax.ppermute(
                going[v], "prow", [(r, r ^ MASKS[v][step]) for r in range(ROWS)]
            )
            for v in range(4)
        ]
        half = parts[0].shape[0] // 2
        if step < 3:
            going = [parts[v][half:] + got[v][half:] for v in range(4)]
            parts = [parts[v][:half] + got[v][:half] for v in range(4)]
        else:
            parts = [(parts[v] + got[v])[0] for v in range(4)]
    return parts


def sum_cols(values):
    for mask in (1, 2, 6, 8):
        values = values + lax.ppermute(values, "pcol", [(c, c ^ mask) for c in range(COLS)])
    return values


def masked_turn(factor, pattern, row, col):
    blocks_per = KA // B
    picks = lax.dynamic_slice(pattern, (row * blocks_per, col), (blocks_per, 1))
    mask = jnp.repeat(picks[:, 0].astype(jnp.float32), B)
    return factor.T * mask[None, :]


def local(
    ginv_anc,
    factor_one,
    pattern_one,
    dinv_one,
    factor_two,
    factor_parent,
    pattern_two,
    parent,
    dinv_two,
):
    row = lax.axis_index("prow")
    col = lax.axis_index("pcol")
    one = masked_turn(factor_one, pattern_one, row, col)
    two = masked_turn(factor_two, pattern_two, row, col)
    par = factor_parent.T
    packed = jnp.concatenate([par[32 * i : 32 * i + 32] for i in range(4)], axis=1)
    own = jnp.concatenate([one, two, packed], axis=0)
    gathered = lax.all_gather(own, "pcol", axis=0, tiled=False)
    scalars = jnp.concatenate(
        [parent, jnp.stack([row, row ^ col]).astype(jnp.int32)]
    )
    outs = products(scalars, gathered, ginv_anc)
    swapped = lax.ppermute(
        outs[8],
        ("prow", "pcol"),
        [(c * COLS + q, (c ^ q) * COLS + c) for c in range(ROWS) for q in range(COLS)],
    )
    parts = reduce_rows(outs[0:4], outs[4:8])
    anc_one, anc_two, part = blocks(parts, swapped)
    sums = sum_cols(part)
    own_pack = lax.dynamic_index_in_dim(gathered, row, 0, keepdims=False)[256:288]
    own_par = jnp.concatenate([own_pack[:, 128 * i : 128 * i + 128] for i in range(4)], axis=0)
    own_parent = lax.dynamic_index_in_dim(parent, row, 0, keepdims=False)
    one_dinv = lax.dynamic_slice_in_dim(dinv_one, row * B, B, 0)
    par_dinv = lax.dynamic_slice_in_dim(dinv_one, own_parent * B, B, 0)
    diag_one = one_dinv - sums[0]
    cross = -(sums[1] + jnp.dot(own_par, par_dinv, precision=precise))
    diag_two = dinv_two - (
        sums[2]
        + lax.dot_general(cross, own_par, (((1,), (1,)), ((), ())), precision=precise)
    )
    return anc_one, diag_one, anc_two, cross, diag_two


def solution(mesh):
    return jax.shard_map(
        local,
        mesh=mesh,
        in_specs=(
            P("prow", "pcol"),
            P("prow", "pcol"),
            P(),
            P(),
            P("prow", "pcol"),
            P(None, "pcol"),
            P(),
            P(),
            P("prow", None),
        ),
        out_specs=(
            P("prow", "pcol"),
            P("prow", None),
            P("prow", "pcol"),
            P("prow", None),
            P("prow", None),
        ),
        check_vma=False,
    )
```

time: 687 us -> 264 us (0.38)
  the two profiles are of different devices: /device:TPU:7 before, /device:TPU:58 now
where the time goes in v1:
time: 264 us; the launch traced here: 263 us
  starting transfers between devices  114 us (43%)
  waiting for transfers between devices  103 us (39%)
  Pallas kernels  17.5 us (7%)
  between operations  14.9 us (6%)
  other arithmetic  7.75 us (3%)
  local copies, waits for them, and re-layouts  4.7 us (2%)
    ppermute x16, starting transfers between devices, reduce_rows(): lax.ppermute(going[v], 'prow', [(r, r ^ MASKS[v][step]) for r in range(RO...  89.8 us
    all_gather x1, waiting for transfers between devices, local(): gathered = lax.all_gather(own, 'pcol', axis=0, tiled=False)  60.7 us
    ppermute x16, waiting for transfers between devices, reduce_rows(): lax.ppermute(going[v], 'prow', [(r, r ^ MASKS[v][step]) for r in range(RO...  21.9 us
    ppermute x4, waiting for transfers between devices, sum_cols(): lax.ppermute(values, 'pcol', [(c, c ^ mask) for c in range(COLS)])  20.2 us
    ppermute x4, starting transfers between devices, sum_cols(): lax.ppermute(values, 'pcol', [(c, c ^ mask) for c in range(COLS)])  18.2 us
    pallas_call x1, Pallas kernels, products(): pl.pallas_call(product_kernel, out_shape=[part] * 8 + [jax.ShapeDtypeStru...  16.5 us
    ppermute x1, starting transfers between devices, local(): lax.ppermute(outs[8], ('prow', 'pcol'), [(c * COLS + q, (c ^ q) * COLS +...  5.45 us
  transfers between devices with their start and end apart: 22, of which 12 were waited for; matrix products, arithmetic and copies ran while one was open for 2% of the time, Pallas kernels for 0%

profile of v1, /device:TPU:58, one launch (start us, length us, event | category | flops | bytes accessed | tf_op | source)
XLA Modules:
  0.0 263.2 jit_solution(7228048915995443078)
XLA Ops:
  13.0 60.7 %all-gather.3.cloned.1.call-done = f32[4608,512]{1,0:T(8,128)} async-done(((f32[288,512]{1,0:T(8,128)}), f32[4608,512]{1,0:T(8,128)}) %all-gather.3.cloned.1.call-update) | async-done | bytes 9437200 | tf_op jit(solution)/shard_map/all_gather | solution.py:169
  73.7 16.5 %shard_map.128 = (f32[8,64,512]{2,1,0:T(8,128)S(1)}, f32[8,64,512]{2,1,0:T(8,128)S(1)}, f32[8,64,512]{2,1,0:T(8,128)S(1)}, f32[8,64,512]{2,1,0:T(8,128)S(1)}, f3...) custom-call(s32[18]{0:T(128)S(1)} %pad_add_fusion.scal_ref, ...), custom_call_target="tpu_custom_call" | custom-call | flops 8000000000 | bytes 20000000 | tf_op jit(solution)/shard_map/pallas_call | solution.py:76
  90.8 2.1 collective-permute-start.4
  94.8 5.5 %collective-permute-start.16 = (f32[384,512]{1,0:T(8,128)S(1)}, f32[384,512]{1,0:T(8,128)S(1)}, u32[]{:S(2)}, u32[]{:S(2)}) collective-permute-start(f32[384,512]{1,0:T(8,128)S(1)} %get-tuple-element.25), channel_id=1, source_target_pairs={{0,0},{1,16},{2,32},{3,48},{4,64},{5,80},{6,96},{7,112},{8,128},{9... | collective-permute-start | bytes 2359304 | tf_op jit(solution)/shard_map/ppermute | solution.py:174
  100.3 15.2 %collective-permute-done = f32[8,64,512]{2,1,0:T(8,128)S(1)} collective-permute-done((f32[8,64,512]{2,1,0:T(8,128)S(1)}, f32[8,64,512]{2,1,0:T(8,128)S(1)}, u32[]{:S(2)}, u32[]{:S(2)}) %collective-permute-start) | collective-permute-done | bytes 1048608 | tf_op jit(solution)/shard_map/ppermute | solution.py:124
  115.7 1.6 collective-permute-start.1
  117.3 1.4 slice_add_fusion.5
  118.7 1.9 collective-permute-start.5
  122.0 59.6 %collective-permute-start.9 = (f32[4,64,512]{2,1,0:T(8,128)S(1)}, f32[4,64,512]{2,1,0:T(8,128)S(1)}, u32[]{:S(2)}, u32[]{:S(2)}) collective-permute-start(f32[4,64,512]{2,1,0:T(8,128)S(1)} %get-tuple-element.32), channel_id=1, source_target_pairs={{0,192},{16,208},{32,224},{48,240},{64,128},{80,144},{96,160},{112... | collective-permute-start | bytes 1572872 | tf_op jit(solution)/shard_map/ppermute | solution.py:124
  182.0 2.1 collective-permute-start.2
  184.2 11.9 %collective-permute-start.6 = (f32[2,64,512]{2,1,0:T(8,128)S(1)}, f32[2,64,512]{2,1,0:T(8,128)S(1)}, u32[]{:S(2)}, u32[]{:S(2)}) collective-permute-start(f32[2,64,512]{2,1,0:T(8,128)S(1)} %get-tuple-element.42), channel_id=1, source_target_pairs={{0,192},{16,208},{32,224},{48,240},{64,128},{80,144},{96,160},{112... | collective-permute-start | bytes 786440 | tf_op jit(solution)/shard_map/ppermute | solution.py:124
  196.2 2.0 collective-permute-start.10
  198.4 1.5 collective-permute-done.2
  199.9 4.1 %collective-permute-start.3 = (f32[1,64,512]{2,1,0:T(8,128)S(1)}, f32[1,64,512]{2,1,0:T(8,128)S(1)}, u32[]{:S(2)}, u32[]{:S(2)}) collective-permute-start(f32[1,64,512]{2,1,0:T(8,128)S(1)} %slice_add_fusion.22), channel_id=1, source_target_pairs={{0,192},{16,208},{32,224},{48,240},{64,128},{80,144},{96,160},{112... | collective-permute-start | bytes 393224 | tf_op jit(solution)/shard_map/ppermute | solution.py:124
  204.7 1.5 collective-permute-done.14
  206.2 1.6 collective-permute-start.15
  209.7 1.6 collective-permute-done.15
  212.3 1.4 collective-permute-done.17
  213.8 8.6 %collective-permute-start.18 = (f32[3,128,128]{2,1,0:T(8,128)S(1)}, f32[3,128,128]{2,1,0:T(8,128)S(1)}, u32[]{:S(2)}, u32[]{:S(2)}) collective-permute-start(f32[3,128,128]{2,1,0:T(8,128)S(1)} %add.153), channel_id=1, source_target_pairs={{0,2},{1,3},{2,0},{3,1},{4,6},{5,7},{6,4},{7,5},{8,10},{9,11},{10,... | collective-permute-start | bytes 589832 | tf_op jit(solution)/shard_map/ppermute | solution.py:140
  222.3 5.2 %collective-permute-done.18 = f32[3,128,128]{2,1,0:T(8,128)S(1)} collective-permute-done((f32[3,128,128]{2,1,0:T(8,128)S(1)}, f32[3,128,128]{2,1,0:T(8,128)S(1)}, u32[]{:S(2)}, u32[]{:S(2)}) %collective-permute-start.18) | collective-permute-done | bytes 196640 | tf_op jit(solution)/shard_map/ppermute | solution.py:140
  229.8 8.5 %collective-permute-done.19 = f32[3,128,128]{2,1,0:T(8,128)S(1)} collective-permute-done((f32[3,128,128]{2,1,0:T(8,128)S(1)}, f32[3,128,128]{2,1,0:T(8,128)S(1)}, u32[]{:S(2)}, u32[]{:S(2)}) %collective-permute-start.19) | collective-permute-done | bytes 196640 | tf_op jit(solution)/shard_map/ppermute | solution.py:140
  238.3 9.5 %collective-permute-start.20 = (f32[3,128,128]{2,1,0:T(8,128)S(1)}, f32[3,128,128]{2,1,0:T(8,128)S(1)}, u32[]{:S(2)}, u32[]{:S(2)}) collective-permute-start(f32[3,128,128]{2,1,0:T(8,128)S(1)} %add.155), channel_id=1, source_target_pairs={{0,8},{1,9},{2,10},{3,11},{4,12},{5,13},{6,14},{7,15},{8,0},{9,1},... | collective-permute-start | bytes 589832 | tf_op jit(solution)/shard_map/ppermute | solution.py:140
  247.9 5.0 %collective-permute-done.20 = f32[3,128,128]{2,1,0:T(8,128)S(1)} collective-permute-done((f32[3,128,128]{2,1,0:T(8,128)S(1)}, f32[3,128,128]{2,1,0:T(8,128)S(1)}, u32[]{:S(2)}, u32[]{:S(2)}) %collective-permute-start.20) | collective-permute-done | bytes 196640 | tf_op jit(solution)/shard_map/ppermute | solution.py:140
  252.9 1.5 fusion.12
  (68 shorter events, 17.7 us)
Async XLA Ops:
  7.2 66.5 %all-gather.3.cloned.1.call-start = ((), (), s32[]{:S(2)}) async-start(), calls=%async_computation | async-start | bytes 10027008 | tf_op jit(solution)/shard_map/all_gather | solution.py:169
  90.2 25.3 %collective-permute-start = (f32[8,64,512]{2,1,0:T(8,128)S(1)}, f32[8,64,512]{2,1,0:T(8,128)S(1)}, u32[]{:S(2)}, u32[]{:S(2)}) collective-permute-start(f32[8,64,512]{2,1,0:T(8,128)S(1)} %get-tuple-element.18), channel_id=1, source_target_pairs={{0,16},{16,0},{32,48},{48,32},{64,80},{80,64},{96,112},{112,96},{1... | collective-permute-start | bytes 3145736 | tf_op jit(solution)/shard_map/ppermute | solution.py:124
  90.8 26.5 %collective-permute-start.4 = (f32[8,64,512]{2,1,0:T(8,128)S(1)}, f32[8,64,512]{2,1,0:T(8,128)S(1)}, u32[]{:S(2)}, u32[]{:S(2)}) collective-permute-start(f32[8,64,512]{2,1,0:T(8,128)S(1)} %get-tuple-element.20), channel_id=1, source_target_pairs={{0,48},{16,32},{32,16},{48,0},{64,112},{80,96},{96,80},{112,64},{1... | collective-permute-start | bytes 3145736 | tf_op jit(solution)/shard_map/ppermute | solution.py:124
  92.9 27.7 %collective-permute-start.8 = (f32[8,64,512]{2,1,0:T(8,128)S(1)}, f32[8,64,512]{2,1,0:T(8,128)S(1)}, u32[]{:S(2)}, u32[]{:S(2)}) collective-permute-start(f32[8,64,512]{2,1,0:T(8,128)S(1)} %get-tuple-element.22), channel_id=1, source_target_pairs={{0,64},{16,80},{32,96},{48,112},{64,0},{80,16},{96,32},{112,48},{1... | collective-permute-start | bytes 3145736 | tf_op jit(solution)/shard_map/ppermute | solution.py:124
  93.7 87.9 %collective-permute-start.12 = (f32[8,64,512]{2,1,0:T(8,128)S(1)}, f32[8,64,512]{2,1,0:T(8,128)S(1)}, u32[]{:S(2)}, u32[]{:S(2)}) collective-permute-start(f32[8,64,512]{2,1,0:T(8,128)S(1)} %get-tuple-element.24), channel_id=1, source_target_pairs={{0,192},{16,208},{32,224},{48,240},{64,128},{80,144},{96,160},{112... | collective-permute-start | bytes 3145736 | tf_op jit(solution)/shard_map/ppermute | solution.py:124
  94.8 116.4 %collective-permute-start.16 = (f32[384,512]{1,0:T(8,128)S(1)}, f32[384,512]{1,0:T(8,128)S(1)}, u32[]{:S(2)}, u32[]{:S(2)}) collective-permute-start(f32[384,512]{1,0:T(8,128)S(1)} %get-tuple-element.25), channel_id=1, source_target_pairs={{0,0},{1,16},{2,32},{3,48},{4,64},{5,80},{6,96},{7,112},{8,128},{9... | collective-permute-start | bytes 2359304 | tf_op jit(solution)/shard_map/ppermute | solution.py:174
  115.7 66.2 %collective-permute-start.1 = (f32[4,64,512]{2,1,0:T(8,128)S(1)}, f32[4,64,512]{2,1,0:T(8,128)S(1)}, u32[]{:S(2)}, u32[]{:S(2)}) collective-permute-start(f32[4,64,512]{2,1,0:T(8,128)S(1)} %get-tuple-element.36), channel_id=1, source_target_pairs={{0,48},{16,32},{32,16},{48,0},{64,112},{80,96},{96,80},{112,64},{1... | collective-permute-start | bytes 1572872 | tf_op jit(solution)/shard_map/ppermute | solution.py:124
  118.7 109.0 %copy-start.3 = (s32[16]{0:T(128)S(1)}, s32[16]{0:T(128)}, u32[]{:S(2)}) copy-start(s32[16]{0:T(128)} %param.16) | copy-start | bytes 196
  118.7 65.4 %collective-permute-start.5 = (f32[4,64,512]{2,1,0:T(8,128)S(1)}, f32[4,64,512]{2,1,0:T(8,128)S(1)}, u32[]{:S(2)}, u32[]{:S(2)}) collective-permute-start(f32[4,64,512]{2,1,0:T(8,128)S(1)} %get-tuple-element.34), channel_id=1, source_target_pairs={{0,16},{16,0},{32,48},{48,32},{64,80},{80,64},{96,112},{112,96},{1... | collective-permute-start | bytes 1572872 | tf_op jit(solution)/shard_map/ppermute | solution.py:124
  122.0 133.4 %copy-start.2 = (f32[128,128]{1,0:T(8,128)S(1)}, f32[128,128]{1,0:T(8,128)}, u32[]{:S(2)}) copy-start(f32[128,128]{1,0:T(8,128)} %param.17) | copy-start | bytes 196612
  122.0 74.1 %collective-permute-start.9 = (f32[4,64,512]{2,1,0:T(8,128)S(1)}, f32[4,64,512]{2,1,0:T(8,128)S(1)}, u32[]{:S(2)}, u32[]{:S(2)}) collective-permute-start(f32[4,64,512]{2,1,0:T(8,128)S(1)} %get-tuple-element.32), channel_id=1, source_target_pairs={{0,192},{16,208},{32,224},{48,240},{64,128},{80,144},{96,160},{112... | collective-permute-start | bytes 1572872 | tf_op jit(solution)/shard_map/ppermute | solution.py:124
  181.8 16.4 %collective-permute-start.13 = (f32[4,64,512]{2,1,0:T(8,128)S(1)}, f32[4,64,512]{2,1,0:T(8,128)S(1)}, u32[]{:S(2)}, u32[]{:S(2)}) collective-permute-start(f32[4,64,512]{2,1,0:T(8,128)S(1)} %get-tuple-element.30), channel_id=1, source_target_pairs={{0,64},{16,80},{32,96},{48,112},{64,0},{80,16},{96,32},{112,48},{1... | collective-permute-start | bytes 1572872 | tf_op jit(solution)/shard_map/ppermute | solution.py:124
  182.0 17.9 %collective-permute-start.2 = (f32[2,64,512]{2,1,0:T(8,128)S(1)}, f32[2,64,512]{2,1,0:T(8,128)S(1)}, u32[]{:S(2)}, u32[]{:S(2)}) collective-permute-start(f32[2,64,512]{2,1,0:T(8,128)S(1)} %get-tuple-element.44), channel_id=1, source_target_pairs={{0,64},{16,80},{32,96},{48,112},{64,0},{80,16},{96,32},{112,48},{1... | collective-permute-start | bytes 786440 | tf_op jit(solution)/shard_map/ppermute | solution.py:124
  184.2 19.9 %collective-permute-start.6 = (f32[2,64,512]{2,1,0:T(8,128)S(1)}, f32[2,64,512]{2,1,0:T(8,128)S(1)}, u32[]{:S(2)}, u32[]{:S(2)}) collective-permute-start(f32[2,64,512]{2,1,0:T(8,128)S(1)} %get-tuple-element.42), channel_id=1, source_target_pairs={{0,192},{16,208},{32,224},{48,240},{64,128},{80,144},{96,160},{112... | collective-permute-start | bytes 786440 | tf_op jit(solution)/shard_map/ppermute | solution.py:124
  196.2 8.3 %collective-permute-start.10 = (f32[2,64,512]{2,1,0:T(8,128)S(1)}, f32[2,64,512]{2,1,0:T(8,128)S(1)}, u32[]{:S(2)}, u32[]{:S(2)}) collective-permute-start(f32[2,64,512]{2,1,0:T(8,128)S(1)} %get-tuple-element.40), channel_id=1, source_target_pairs={{0,16},{16,0},{32,48},{48,32},{64,80},{80,64},{96,112},{112,96},{1... | collective-permute-start | bytes 786440 | tf_op jit(solution)/shard_map/ppermute | solution.py:124
  198.3 7.9 %collective-permute-start.14 = (f32[2,64,512]{2,1,0:T(8,128)S(1)}, f32[2,64,512]{2,1,0:T(8,128)S(1)}, u32[]{:S(2)}, u32[]{:S(2)}) collective-permute-start(f32[2,64,512]{2,1,0:T(8,128)S(1)} %get-tuple-element.38), channel_id=1, source_target_pairs={{0,48},{16,32},{32,16},{48,0},{64,112},{80,96},{96,80},{112,64},{1... | collective-permute-start | bytes 786440 | tf_op jit(solution)/shard_map/ppermute | solution.py:124
  199.9 7.9 %collective-permute-start.3 = (f32[1,64,512]{2,1,0:T(8,128)S(1)}, f32[1,64,512]{2,1,0:T(8,128)S(1)}, u32[]{:S(2)}, u32[]{:S(2)}) collective-permute-start(f32[1,64,512]{2,1,0:T(8,128)S(1)} %slice_add_fusion.22), channel_id=1, source_target_pairs={{0,192},{16,208},{32,224},{48,240},{64,128},{80,144},{96,160},{112... | collective-permute-start | bytes 393224 | tf_op jit(solution)/shard_map/ppermute | solution.py:124
  204.1 5.1 %collective-permute-start.7 = (f32[1,64,512]{2,1,0:T(8,128)S(1)}, f32[1,64,512]{2,1,0:T(8,128)S(1)}, u32[]{:S(2)}, u32[]{:S(2)}) collective-permute-start(f32[1,64,512]{2,1,0:T(8,128)S(1)} %slice_add_fusion.20), channel_id=1, source_target_pairs={{0,64},{16,80},{32,96},{48,112},{64,0},{80,16},{96,32},{112,48},{1... | collective-permute-start | bytes 393224 | tf_op jit(solution)/shard_map/ppermute | solution.py:124
  204.6 5.1 %collective-permute-start.11 = (f32[1,64,512]{2,1,0:T(8,128)S(1)}, f32[1,64,512]{2,1,0:T(8,128)S(1)}, u32[]{:S(2)}, u32[]{:S(2)}) collective-permute-start(f32[1,64,512]{2,1,0:T(8,128)S(1)} %slice_add_fusion.18), channel_id=1, source_target_pairs={{0,48},{16,32},{32,16},{48,0},{64,112},{80,96},{96,80},{112,64},{1... | collective-permute-start | bytes 393224 | tf_op jit(solution)/shard_map/ppermute | solution.py:124
  206.2 5.1 %collective-permute-start.15 = (f32[1,64,512]{2,1,0:T(8,128)S(1)}, f32[1,64,512]{2,1,0:T(8,128)S(1)}, u32[]{:S(2)}, u32[]{:S(2)}) collective-permute-start(f32[1,64,512]{2,1,0:T(8,128)S(1)} %slice_add_fusion.16), channel_id=1, source_target_pairs={{0,16},{16,0},{32,48},{48,32},{64,80},{80,64},{96,112},{112,96},{1... | collective-permute-start | bytes 393224 | tf_op jit(solution)/shard_map/ppermute | solution.py:124
  212.3 1.4 collective-permute-start.17
  213.8 13.8 %collective-permute-start.18 = (f32[3,128,128]{2,1,0:T(8,128)S(1)}, f32[3,128,128]{2,1,0:T(8,128)S(1)}, u32[]{:S(2)}, u32[]{:S(2)}) collective-permute-start(f32[3,128,128]{2,1,0:T(8,128)S(1)} %add.153), channel_id=1, source_target_pairs={{0,2},{1,3},{2,0},{3,1},{4,6},{5,7},{6,4},{7,5},{8,10},{9,11},{10,... | collective-permute-start | bytes 589832 | tf_op jit(solution)/shard_map/ppermute | solution.py:140
  227.6 10.7 %collective-permute-start.19 = (f32[3,128,128]{2,1,0:T(8,128)S(1)}, f32[3,128,128]{2,1,0:T(8,128)S(1)}, u32[]{:S(2)}, u32[]{:S(2)}) collective-permute-start(f32[3,128,128]{2,1,0:T(8,128)S(1)} %add.154), channel_id=1, source_target_pairs={{0,6},{1,7},{2,4},{3,5},{4,2},{5,3},{6,0},{7,1},{8,14},{9,15},{10,... | collective-permute-start | bytes 589832 | tf_op jit(solution)/shard_map/ppermute | solution.py:140
  238.3 14.6 %collective-permute-start.20 = (f32[3,128,128]{2,1,0:T(8,128)S(1)}, f32[3,128,128]{2,1,0:T(8,128)S(1)}, u32[]{:S(2)}, u32[]{:S(2)}) collective-permute-start(f32[3,128,128]{2,1,0:T(8,128)S(1)} %add.155), channel_id=1, source_target_pairs={{0,8},{1,9},{2,10},{3,11},{4,12},{5,13},{6,14},{7,15},{8,0},{9,1},... | collective-permute-start | bytes 589832 | tf_op jit(solution)/shard_map/ppermute | solution.py:140
  (2 other events, 92.3 us)
Sparse Core Ops, SparseCore 0:
  12.3 61.3 all-gather.2

commit v2 on v0

v2 whole, which is shorter than its diff:
```python
import jax
import jax.numpy as jnp
from jax import lax
from jax.experimental import pallas as pl
from jax.experimental.pallas import tpu as pltpu
from jax.sharding import PartitionSpec as P

N = 16
B = 128
KA = 512
ALL = ("prow", "pcol")
MASKS = (((1, 3, 4, 12), (3, 1, 12, 4)), ((4, 12, 1, 3), (12, 4, 3, 1)))
VMEM = pl.BlockSpec(memory_space=pltpu.VMEM)
SMEM = pl.BlockSpec(memory_space=pltpu.SMEM)
ANY = pl.BlockSpec(memory_space=pl.ANY)
MIB = 1024 * 1024


def f32(*shape):
    return jax.ShapeDtypeStruct(shape, jnp.float32)


def slot_mask(core, variant, slot):
    mask = 0
    for bit in range(4):
        if (slot >> (3 - bit)) & 1:
            mask ^= MASKS[core][variant][bit]
    return mask


def destination(row, core, variant, slot):
    first, second = slot_mask(0, variant, slot), slot_mask(1, variant, slot)
    return row ^ jnp.where(core == 0, first, second)


def split(value):
    high = value.astype(jnp.bfloat16)
    low = (value - high.astype(jnp.float32)).astype(jnp.bfloat16)
    return high, low


def dot_split(left, right, dims):
    out = None
    for a, b in ((left[0], right[0]), (left[0], right[1]), (left[1], right[0])):
        term = lax.dot_general(a, b, (dims, ((), ())), preferred_element_type=jnp.float32)
        out = term if out is None else out + term
    return out


def unpack(packed):
    return jnp.concatenate([packed[:, B * i : B * i + B] for i in range(4)], axis=0)


def permute(value, move):
    pairs = []
    for r in range(N):
        for c in range(N):
            nr, nc = move(r, c)
            pairs.append((r * N + c, nr * N + nc))
    return lax.ppermute(value, ALL, pairs)


def swap(value):
    return permute(value, lambda r, c: (r, c ^ 1))


def ring(value):
    return permute(value, lambda r, c: (r, (c + (2 if c % 2 == 0 else -2)) % N))


def prep_kernel(scal, pat_one, pat_two, fac_one, fac_two, par, one_out, two_out):
    row, col = scal[16], scal[17]
    turned = par[...].T
    for i in range(4):
        cut = pl.ds(B * i, B)
        w_one = pat_one[4 * row + i, col].astype(jnp.float32)
        w_two = pat_two[4 * row + i, col].astype(jnp.float32)
        one_out[:, cut] = fac_one[cut, :].T * w_one
        two_out[0:128, cut] = fac_two[cut, :].T * w_two
        two_out[128:160, cut] = turned[32 * i : 32 * i + 32, :]


def prepare(scal, pat_one, pat_two, fac_one, fac_two, par):
    return pl.pallas_call(
        prep_kernel,
        out_shape=[f32(B, KA), f32(160, KA)],
        in_specs=[SMEM] * 3 + [VMEM] * 3,
        out_specs=[VMEM] * 2,
        compiler_params=pltpu.CompilerParams(vmem_limit_bytes=8 * MIB),
    )(scal, pat_one, pat_two, fac_one, fac_two, par)


def gather(own):
    pair = jnp.stack([own, swap(own)])
    blocks = [pair]
    going = pair
    for step in range(4):
        if step == 3:
            going = going[0:1]
        going = ring(going)
        blocks += [going, swap(going)]
    return blocks


def fetch(scal, refs, target, sems):
    col = scal[17]
    z, core = col // 2, lax.rem(col, 2)
    copies = []
    for at, ref in enumerate(refs):
        step = (at + 1) // 2
        swapped = at > 0 and at % 2 == 0
        side = (1 - core) if swapped else core
        away = jnp.where(side == 0, 8 - step, step)
        plane = lax.rem(z + away, 8)
        for i in range(ref.shape[0]):
            parity = side if i == 0 else 1 - side
            copies.append(
                pltpu.make_async_copy(
                    ref.at[i], target.at[plane * 2 + parity], sems.at[len(copies)]
                )
            )
    return copies


def one_kernel(scal, ginv, *refs):
    blocks, refs = refs[:9], refs[9:]
    sends, keeps, one, turn, left, sems = refs[0:2], refs[2:4], refs[4], refs[5], refs[6], refs[7]
    row, col, target = scal[16], scal[17], scal[18]
    core = lax.rem(col, 2)
    copies = fetch(scal, blocks, one, sems)
    for copy in copies:
        copy.start()
    high, low = split(ginv[...])
    for copy in copies:
        copy.wait()
    turn[0:128, :] = one[scal[target]]
    turn[128:256, :] = one[target]
    for variant in range(2):
        for half in (1, 0):
            for slot in range(8):
                dest = destination(row, core, variant, slot + 8 * half)
                left[64 * slot : 64 * slot + 64, :] = one[dest, 64 * variant : 64 * variant + 64, :]
            value = dot_split(split(left[...]), (high, low), ((1,), (0,)))
            out = sends[variant] if half else keeps[variant]
            out[...] = -value.reshape(8, 64, KA)


def first_level(scal, ginv, blocks):
    return pl.pallas_call(
        one_kernel,
        out_shape=[f32(8, 64, KA)] * 4 + [f32(16, B, KA), f32(256, KA)],
        in_specs=[SMEM, VMEM] + [ANY] * 9,
        out_specs=[VMEM] * 6,
        scratch_shapes=[pltpu.VMEM((512, KA), jnp.float32), pltpu.SemaphoreType.DMA((16,))],
        compiler_params=pltpu.CompilerParams(vmem_limit_bytes=32 * MIB),
        cost_estimate=pl.CostEstimate(
            flops=4_000_000_000, bytes_accessed=14_000_000, transcendentals=0
        ),
    )(scal, ginv, *blocks)


def two_kernel(half, scal, ginv, one, *refs):
    blocks, refs = refs[:9], refs[9:]
    outs, turn, two, left, sems = refs[0:2], refs[2], refs[3], refs[4], refs[5]
    row, col, target = scal[16], scal[17], scal[18]
    core = lax.rem(col, 2)
    copies = fetch(scal, blocks, two, sems)
    for copy in copies:
        copy.start()
    high, low = split(ginv[...])
    for copy in copies:
        copy.wait()
    if half:
        turn[...] = two[target, 0:128, :]
    else:
        turn[...] = unpack(two[row, 128:160, :])
    for variant in range(2):
        lo = 64 * variant

        def correct(slot, carry):
            dest = row ^ scal[32 + 32 * core + 16 * variant + 8 * half + slot]
            par = unpack(two[dest, 128:160, :])[lo : lo + 64, :]
            fix = dot_split(split(par), split(one[scal[dest]]), ((1,), (0,)))
            at = pl.multiple_of(slot * 64, 64)
            left[pl.ds(at, 64), :] = two[dest, lo : lo + 64, :] - fix
            return carry

        lax.fori_loop(0, 8, correct, 0)
        value = dot_split(split(left[...]), (high, low), ((1,), (0,)))
        outs[variant][...] = -value.reshape(8, 64, KA)


def second_level(half, scal, ginv, one, blocks):
    def body(*refs):
        two_kernel(half, *refs)

    return pl.pallas_call(
        body,
        out_shape=[f32(8, 64, KA)] * 2 + [f32(128, KA) if half else f32(128, 128)],
        in_specs=[SMEM, VMEM, VMEM] + [ANY] * 9,
        out_specs=[VMEM] * 3,
        scratch_shapes=[
            pltpu.VMEM((16, 160, KA), jnp.float32),
            pltpu.VMEM((512, KA), jnp.float32),
            pltpu.SemaphoreType.DMA((16,)),
        ],
        compiler_params=pltpu.CompilerParams(vmem_limit_bytes=32 * MIB),
        cost_estimate=pl.CostEstimate(
            flops=3_000_000_000, bytes_accessed=10_000_000, transcendentals=0
        ),
    )(scal, ginv, one, *blocks)


def row_step(value, variant, step):
    return permute(value, lambda r, c: (r ^ MASKS[c % 2][variant][step], c))


def block_kernel(scal, a_ref, b_ref, turn_one, turn_two, one_out, two_out, send_out, keep_out, sums):
    core = lax.rem(scal[17], 2)
    for variant, ref in enumerate((a_ref, b_ref)):
        one_out[64 * variant : 64 * variant + 64, :] = ref[0:64, :]
        two_out[64 * variant : 64 * variant + 64, :] = ref[64:128, :]
    one = split(one_out[...])
    two = split(two_out[...])
    nt = ((1,), (1,))
    for i, (left, right) in enumerate(
        ((one, turn_one[128:256, :]), (two, turn_one[0:128, :]), (two, turn_two[...]))
    ):
        value = dot_split(left, split(right), nt)
        sums[0, 64 * i : 64 * i + 64, :] = value[0:64]
        sums[1, 64 * i : 64 * i + 64, :] = value[64:128]
    keep_out[...] = sums[core]
    send_out[...] = sums[1 - core]


def blocks_of(scal, parts, turn_one, turn_two):
    return pl.pallas_call(
        block_kernel,
        out_shape=[f32(B, KA), f32(B, KA), f32(192, B), f32(192, B)],
        in_specs=[SMEM] + [VMEM] * 4,
        out_specs=[VMEM] * 4,
        scratch_shapes=[pltpu.VMEM((2, 192, B), jnp.float32)],
        compiler_params=pltpu.CompilerParams(vmem_limit_bytes=8 * MIB),
    )(scal, *parts, turn_one, turn_two)


def base_kernel(scal, par, dinv_one, dinv_two, base):
    row, col = scal[16], scal[17]
    top = pl.multiple_of(lax.rem(col, 2) * 64, 64)
    at = pl.multiple_of(row * B, B)
    up = pl.multiple_of(scal[row] * B, B)
    base[0:64, :] = dinv_one[pl.ds(at + top, 64), :]
    base[64:128, :] = -jnp.dot(
        par[pl.ds(top, 64), :],
        dinv_one[pl.ds(up, B), :],
        precision=lax.Precision.HIGHEST,
        preferred_element_type=jnp.float32,
    )
    base[128:192, :] = dinv_two[pl.ds(top, 64), :]


def base_of(scal, par, dinv_one, dinv_two):
    return pl.pallas_call(
        base_kernel,
        out_shape=f32(192, B),
        in_specs=[SMEM] + [VMEM] * 3,
        out_specs=VMEM,
        compiler_params=pltpu.CompilerParams(vmem_limit_bytes=8 * MIB),
    )(scal, par, dinv_one, dinv_two)


def final_kernel(base, par, first, second, out):
    total = first[...] + second[...]
    out[0:64, :] = base[0:64, :] - total[0:64, :]
    cross = base[64:128, :] - total[64:128, :]
    out[64:128, :] = cross
    out[128:192, :] = base[128:192, :] - (
        total[128:192, :]
        + lax.dot_general(
            cross,
            par[...],
            (((1,), (1,)), ((), ())),
            precision=lax.Precision.HIGHEST,
            preferred_element_type=jnp.float32,
        )
    )


def final_of(base, par, first, second):
    return pl.pallas_call(
        final_kernel,
        out_shape=f32(192, B),
        in_specs=[VMEM] * 4,
        out_specs=VMEM,
        compiler_params=pltpu.CompilerParams(vmem_limit_bytes=4 * MIB),
    )(base, par, first, second)


def join_kernel(scal, own, other, a_out, b_out, c_out):
    core = lax.rem(scal[17], 2)
    mine = pl.multiple_of(core * 64, 64)
    rest = pl.multiple_of((1 - core) * 64, 64)
    for i, out in enumerate((a_out, b_out, c_out)):
        out[pl.ds(mine, 64), :] = own[64 * i : 64 * i + 64, :]
        out[pl.ds(rest, 64), :] = other[64 * i : 64 * i + 64, :]


def join(scal, own, other):
    return pl.pallas_call(
        join_kernel,
        out_shape=[f32(B, B)] * 3,
        in_specs=[SMEM] + [VMEM] * 2,
        out_specs=[VMEM] * 3,
        compiler_params=pltpu.CompilerParams(vmem_limit_bytes=4 * MIB),
    )(scal, own, other)


def local(
    ginv_anc,
    factor_one,
    pattern_one,
    dinv_one,
    factor_two,
    factor_parent,
    pattern_two,
    parent,
    dinv_two,
):
    row = lax.axis_index("prow")
    col = lax.axis_index("pcol")
    table = [slot_mask(c, v, s) for c in range(2) for v in range(2) for s in range(16)]
    place = jnp.stack([row, col, lax.rem(row + col, N)]).astype(jnp.int32)
    scal = jnp.concatenate(
        [parent, place, jnp.zeros((13,), jnp.int32), jnp.array(table, jnp.int32)]
    )
    own_one, own_two = prepare(
        scal, pattern_one, pattern_two, factor_one, factor_two, factor_parent
    )
    blocks_one = gather(own_one)
    blocks_two = gather(own_two)
    s1a, s1b, k1a, k1b, one, turn_one = first_level(scal, ginv_anc, blocks_one)
    s2a, s2b, turn_two = second_level(1, scal, ginv_anc, one, blocks_two)
    k2a, k2b, par = second_level(0, scal, ginv_anc, one, blocks_two)
    base = base_of(scal, par, dinv_one, dinv_two)

    def spread(value):
        value = permute(value, lambda r, c: ((r + c) % N, c))
        return permute(value, lambda r, c: (r, (r - c) % N))

    turn_one = spread(turn_one)
    turn_two = spread(turn_two)
    first = [[k1a, row_step(s1a, 0, 0)], [k1b, row_step(s1b, 1, 0)]]
    second = [[k2a, row_step(s2a, 0, 0)], [k2b, row_step(s2b, 1, 0)]]
    going, kept = [], []
    for v in range(2):
        going.append(
            jnp.concatenate([first[v][0][4:] + first[v][1][4:], second[v][0][4:] + second[v][1][4:]], axis=1)
        )
        kept.append(
            jnp.concatenate([first[v][0][:4] + first[v][1][:4], second[v][0][:4] + second[v][1][:4]], axis=1)
        )
    for step in range(1, 4):
        got = [row_step(going[v], v, step) for v in range(2)]
        half = kept[0].shape[0] // 2
        if step < 3:
            going = [kept[v][half:] + got[v][half:] for v in range(2)]
            kept = [kept[v][:half] + got[v][:half] for v in range(2)]
        else:
            kept = [(kept[v] + got[v])[0] for v in range(2)]
    anc_one, anc_two, send, keep = blocks_of(scal, kept, turn_one, turn_two)
    sums = keep + swap(send)
    for mask in (2, 6):
        sums = sums + permute(sums, lambda r, c: (r, c ^ mask))
    done = final_of(base, par, sums, permute(sums, lambda r, c: (r, c ^ 8)))
    diag_one, cross, diag_two = join(scal, done, swap(done))
    return anc_one, diag_one, anc_two, cross, diag_two


def solution(mesh):
    return jax.shard_map(
        local,
        mesh=mesh,
        in_specs=(
            P("prow", "pcol"),
            P("prow", "pcol"),
            P(),
            P(),
            P("prow", "pcol"),
            P(None, "pcol"),
            P(),
            P(),
            P("prow", None),
        ),
        out_specs=(
            P("prow", "pcol"),
            P("prow", None),
            P("prow", "pcol"),
            P("prow", None),
            P("prow", None),
        ),
        check_vma=False,
    )
```

time: 687 us -> 200 us (0.29)
  waiting for transfers between devices: 621 us -> 87.6 us
  starting transfers between devices: 0.37 us -> 75.6 us
  matrix products: 31 us -> 0 us
  Pallas kernels: 0 us -> 26.7 us
  between operations: 15.9 us -> 0.93 us
  other arithmetic: 13.9 us -> 1.69 us
    reduce_scatter x4 -> x0, waiting for transfers between devices: 316 us -> none  [the longest x2 161 us: reduce_rows(): lax.psum_scatter(-lax.dot_general(left, block, (((0,), (0,)), ((), ())),...]
    all_gather x4 -> x0, waiting for transfers between devices: 199 us -> none  [the longest x2 89.7 us: gather_cols(): return lax.all_gather(values, 'pcol', axis=1, tiled=True)]
    psum x1 -> x0, waiting for transfers between devices: 106 us -> none  [diag_sum(): return lax.psum(values, 'pcol')]
    ppermute x0 -> x37, waiting for transfers between devices: none -> 87.6 us  [permute(): return lax.ppermute(value, ALL, pairs)]
    ppermute x0 -> x37, starting transfers between devices: none -> 75.6 us  [permute(): return lax.ppermute(value, ALL, pairs)]
    dot_general x10 -> x0, matrix products: 31 us -> none  [the longest x2 19.7 us: reduce_rows(): lax.dot_general(left, block, (((0,), (0,)), ((), ())), precision=precise,...]
    pallas_call x0 -> x8, Pallas kernels: none -> 26.7 us  [the longest x2 16.4 us: second_level(): pl.pallas_call(body, out_shape=[f32(8, 64, KA)] * 2 + [f32(128, KA) if ha...]
    select_n x3 -> x0, other arithmetic: 7.43 us -> none  [the longest x2 7.42 us: deliver(): jnp.where(lax.axis_index('prow') == root, piece, jnp.zeros_like(piece))]
  transfers between devices with their start and end apart: 9 -> 37, of which waited for: 9 -> 19; matrix products, arithmetic and copies ran while one was open for 5% -> 1% of each run, Pallas kernels for 0% -> 11%
where the time goes in v2:
time: 200 us; the launch traced here: 198 us
  waiting for transfers between devices  87.6 us (44%)
  starting transfers between devices  75.6 us (38%)
  Pallas kernels  26.7 us (13%)
  local copies, waits for them, and re-layouts  5.1 us (3%)
    ppermute x37, waiting for transfers between devices, permute(): return lax.ppermute(value, ALL, pairs)  87.6 us
    ppermute x37, starting transfers between devices, permute(): return lax.ppermute(value, ALL, pairs)  75.6 us
    pallas_call x2, Pallas kernels, second_level(): pl.pallas_call(body, out_shape=[f32(8, 64, KA)] * 2 + [f32(128, KA) if ha...  16.4 us
    pallas_call x1, Pallas kernels, first_level(): pl.pallas_call(one_kernel, out_shape=[f32(8, 64, KA)] * 4 + [f32(16, B, K...  4.77 us
    unnamed x14, local copies, waits for them, and re-layouts  4.31 us
  transfers between devices with their start and end apart: 37, of which 19 were waited for; matrix products, arithmetic and copies ran while one was open for 1% of the time, Pallas kernels for 11%

profile of v2, /device:TPU:7, one launch (start us, length us, event | category | flops | bytes accessed | tf_op | source)
XLA Modules:
  0.0 197.6 jit_solution(3797576090984213267)
XLA Ops:
  9.6 5.7 %collective-permute-start.11 = (f32[2,160,512]{2,1,0:T(8,128)S(1)}, f32[2,160,512]{2,1,0:T(8,128)S(1)}, u32[]{:S(2)}, u32[]{:S(2)}) collective-permute-start(f32[2,160,512]{2,1,0:T(8,128)S(1)} %pad_maximum_fusion.2.refs_3_), channel_id=1, source_target_pairs={{0,2},{1,15},{2,4},{3,1},{4,6},{5,3},{6,8},{7,5},{8,10},{9,7},{10,... | collective-permute-start | bytes 1966088 | tf_op jit(solution)/shard_map/ppermute | solution.py:60
  16.1 6.7 %collective-permute-done.11.refs_4_ = f32[2,160,512]{2,1,0:T(8,128)S(1)} collective-permute-done((f32[2,160,512]{2,1,0:T(8,128)S(1)}, f32[2,160,512]{2,1,0:T(8,128)S(1)}, u32[]{:S(2)}, u32[]{:S(2)}) %collective-permute-start.11) | collective-permute-done | bytes 655392 | tf_op jit(solution)/shard_map/ppermute | solution.py:60
  31.5 9.5 %collective-permute-done.3.refs_3_ = f32[2,128,512]{2,1,0:T(8,128)S(1)} collective-permute-done((f32[2,128,512]{2,1,0:T(8,128)S(1)}, f32[2,128,512]{2,1,0:T(8,128)S(1)}, u32[]{:S(2)}, u32[]{:S(2)}) %collective-permute-start.3) | collective-permute-done | bytes 524320 | tf_op jit(solution)/shard_map/ppermute | solution.py:60
  44.7 5.6 %collective-permute-done.5.refs_5_ = f32[2,128,512]{2,1,0:T(8,128)S(1)} collective-permute-done((f32[2,128,512]{2,1,0:T(8,128)S(1)}, f32[2,128,512]{2,1,0:T(8,128)S(1)}, u32[]{:S(2)}, u32[]{:S(2)}) %collective-permute-start.5) | collective-permute-done | bytes 524320 | tf_op jit(solution)/shard_map/ppermute | solution.py:60
  50.3 3.2 %collective-permute-start.7 = (f32[1,128,512]{2,1,0:T(8,128)S(1)}, f32[1,128,512]{2,1,0:T(8,128)S(1)}, u32[]{:S(2)}, u32[]{:S(2)}) collective-permute-start(f32[1,128,512]{2,1,0:T(8,128)S(1)} %slice.136), channel_id=1, source_target_pairs={{0,2},{1,15},{2,4},{3,1},{4,6},{5,3},{6,8},{7,5},{8,10},{9,7},{10,... | collective-permute-start | bytes 786440 | tf_op jit(solution)/shard_map/ppermute | solution.py:60
  53.5 3.8 %collective-permute-done.15.refs_8_ = f32[2,160,512]{2,1,0:T(8,128)S(1)} collective-permute-done((f32[2,160,512]{2,1,0:T(8,128)S(1)}, f32[2,160,512]{2,1,0:T(8,128)S(1)}, u32[]{:S(2)}, u32[]{:S(2)}) %collective-permute-start.15) | collective-permute-done | bytes 655392 | tf_op jit(solution)/shard_map/ppermute | solution.py:60
  57.3 3.2 %collective-permute-start.17 = (f32[1,160,512]{2,1,0:T(8,128)S(1)}, f32[1,160,512]{2,1,0:T(8,128)S(1)}, u32[]{:S(2)}, u32[]{:S(2)}) collective-permute-start(f32[1,160,512]{2,1,0:T(8,128)S(1)} %slice.138), channel_id=1, source_target_pairs={{0,2},{1,15},{2,4},{3,1},{4,6},{5,3},{6,8},{7,5},{8,10},{9,7},{10,... | collective-permute-start | bytes 983048 | tf_op jit(solution)/shard_map/ppermute | solution.py:60
  64.6 4.0 %collective-permute-start.18 = (f32[1,160,512]{2,1,0:T(8,128)S(1)}, f32[1,160,512]{2,1,0:T(8,128)S(1)}, u32[]{:S(2)}, u32[]{:S(2)}) collective-permute-start(f32[1,160,512]{2,1,0:T(8,128)S(1)} %collective-permute-done.17.refs_10_), channel_id=1, source_target_pairs={{0,1},{1,0},{2,3},{3,2},{4,5},{5,4},{6,7},{7,6},{8,9},{9,8},{10,11... | collective-permute-start | bytes 983048 | tf_op jit(solution)/shard_map/ppermute | solution.py:60
  68.6 4.8 %shard_map.138 = (f32[8,64,512]{2,1,0:T(8,128)S(1)}, f32[8,64,512]{2,1,0:T(8,128)S(1)}, f32[8,64,512]{2,1,0:T(8,128)S(1)}, f32[8,64,512]{2,1,0:T(8,128)S(1)}, f3...) custom-call(s32[96]{0:T(128)S(1)} %concatenate.15.scal.refs_0_, f32[512,512]{1,0:T(8,128)S(1)} %copy-done.5, ...), custom_call_target="tpu_custom_call" | custom-call | flops 4000000000 | bytes 14000000 | tf_op jit(solution)/shard_map/pallas_call | solution.py:149
  76.6 8.2 %shard_map.140 = (f32[8,64,512]{2,1,0:T(8,128)S(1)}, f32[8,64,512]{2,1,0:T(8,128)S(1)}, f32[128,512]{1,0:T(8,128)S(1)}) custom-call(s32[96]{0:T(128)S(1)} %concatenate.15.scal.refs_0_, f32[512,512]{1,0:T(8,128)S(1)} %copy-done.5, f32[16,128,512]{2,1,0:T(8,128)S(1)} %get-tuple-element.29.refs_2_, f32[2,160,512]{2,1,0:T(8,128)S(1)} %pad_maximum_fusion.2.refs_3_, ...), custom_call_target="tpu_custom_call" | custom-call | flops 3000000000 | bytes 10000000 | tf_op jit(solution)/shard_map/pallas_call | solution.py:197
  86.0 8.2 %shard_map.139 = (f32[8,64,512]{2,1,0:T(8,128)S(1)}, f32[8,64,512]{2,1,0:T(8,128)S(1)}, f32[128,128]{1,0:T(8,128)S(1)}) custom-call(s32[96]{0:T(128)S(1)} %concatenate.15.scal.refs_0_, f32[512,512]{1,0:T(8,128)S(1)} %copy-done.5, f32[16,128,512]{2,1,0:T(8,128)S(1)} %get-tuple-element.29.refs_2_, f32[2,160,512]{2,1,0:T(8,128)S(1)} %pad_maximum_fusion.2.refs_3_, ...), custom_call_target="tpu_custom_call" | custom-call | flops 3000000000 | bytes 10000000 | tf_op jit(solution)/shard_map/pallas_call | solution.py:197
  94.6 4.3 %collective-permute-done.19 = f32[8,64,512]{2,1,0:T(8,128)S(1)} collective-permute-done((f32[8,64,512]{2,1,0:T(8,128)S(1)}, f32[8,64,512]{2,1,0:T(8,128)S(1)}, u32[]{:S(2)}, u32[]{:S(2)}) %collective-permute-start.19) | collective-permute-done | bytes 1048608 | tf_op jit(solution)/shard_map/ppermute | solution.py:60
  102.1 3.5 %collective-permute-start.28 = (f32[256,512]{1,0:T(8,128)S(1)}, f32[256,512]{1,0:T(8,128)S(1)}, u32[]{:S(2)}, u32[]{:S(2)}) collective-permute-start(f32[256,512]{1,0:T(8,128)S(1)} %get-tuple-element.37), channel_id=1, source_target_pairs={{0,0},{1,17},{2,34},{3,51},{4,68},{5,85},{6,102},{7,119},{8,136},{... | collective-permute-start | bytes 1572872 | tf_op jit(solution)/shard_map/ppermute | solution.py:60
  105.6 8.8 %collective-permute-done.20 = f32[4,128,512]{2,1,0:T(8,128)S(1)} collective-permute-done((f32[4,128,512]{2,1,0:T(8,128)S(1)}, f32[4,128,512]{2,1,0:T(8,128)S(1)}, u32[]{:S(2)}, u32[]{:S(2)}) %collective-permute-start.20) | collective-permute-done | bytes 1048608 | tf_op jit(solution)/shard_map/ppermute | solution.py:60
  116.3 3.7 %collective-permute-start.26 = (f32[2,128,512]{2,1,0:T(8,128)S(1)}, f32[2,128,512]{2,1,0:T(8,128)S(1)}, u32[]{:S(2)}, u32[]{:S(2)}) collective-permute-start(f32[2,128,512]{2,1,0:T(8,128)S(1)} %get-tuple-element.48), channel_id=1, source_target_pairs={{0,192},{1,49},{2,194},{3,51},{4,196},{5,53},{6,198},{7,55},{8,200... | collective-permute-start | bytes 1572872 | tf_op jit(solution)/shard_map/ppermute | solution.py:60
  119.9 4.0 %collective-permute-start.30 = (f32[128,512]{1,0:T(8,128)S(1)}, f32[128,512]{1,0:T(8,128)S(1)}, u32[]{:S(2)}, u32[]{:S(2)}) collective-permute-start(f32[128,512]{1,0:T(8,128)S(1)} %get-tuple-element.38), channel_id=1, source_target_pairs={{0,0},{1,17},{2,34},{3,51},{4,68},{5,85},{6,102},{7,119},{8,136},{... | collective-permute-start | bytes 786440 | tf_op jit(solution)/shard_map/ppermute | solution.py:60
  123.9 3.6 %collective-permute-done.21 = f32[2,128,512]{2,1,0:T(8,128)S(1)} collective-permute-done((f32[2,128,512]{2,1,0:T(8,128)S(1)}, f32[2,128,512]{2,1,0:T(8,128)S(1)}, u32[]{:S(2)}, u32[]{:S(2)}) %collective-permute-start.21) | collective-permute-done | bytes 524320 | tf_op jit(solution)/shard_map/ppermute | solution.py:60
  127.7 7.3 %collective-permute-start.29 = (f32[256,512]{1,0:T(8,128)S(1)}, f32[256,512]{1,0:T(8,128)S(1)}, u32[]{:S(2)}, u32[]{:S(2)}) collective-permute-start(f32[256,512]{1,0:T(8,128)S(1)} %collective-permute-done.28), channel_id=1, source_target_pairs={{0,0},{1,15},{2,14},{3,13},{4,12},{5,11},{6,10},{7,9},{8,8},{9,7},... | collective-permute-start | bytes 1572872 | tf_op jit(solution)/shard_map/ppermute | solution.py:60
  135.2 5.6 %collective-permute-start.31 = (f32[128,512]{1,0:T(8,128)S(1)}, f32[128,512]{1,0:T(8,128)S(1)}, u32[]{:S(2)}, u32[]{:S(2)}) collective-permute-start(f32[128,512]{1,0:T(8,128)S(1)} %collective-permute-done.30), channel_id=1, source_target_pairs={{0,0},{1,15},{2,14},{3,13},{4,12},{5,11},{6,10},{7,9},{8,8},{9,7},... | collective-permute-start | bytes 786440 | tf_op jit(solution)/shard_map/ppermute | solution.py:60
  141.0 23.5 %collective-permute-done.29.turn_one = f32[256,512]{1,0:T(8,128)S(1)} collective-permute-done((f32[256,512]{1,0:T(8,128)S(1)}, f32[256,512]{1,0:T(8,128)S(1)}, u32[]{:S(2)}, u32[]{:S(2)}) %collective-permute-start.29) | collective-permute-done | bytes 524320 | tf_op jit(solution)/shard_map/ppermute | solution.py:60
  164.5 5.0 %collective-permute-done.31.turn_two = f32[128,512]{1,0:T(8,128)S(1)} collective-permute-done((f32[128,512]{1,0:T(8,128)S(1)}, f32[128,512]{1,0:T(8,128)S(1)}, u32[]{:S(2)}, u32[]{:S(2)}) %collective-permute-start.31) | collective-permute-done | bytes 262176 | tf_op jit(solution)/shard_map/ppermute | solution.py:60
  177.0 5.4 %collective-permute-done.34 = f32[192,128]{1,0:T(8,128)S(1)} collective-permute-done((f32[192,128]{1,0:T(8,128)S(1)}, f32[192,128]{1,0:T(8,128)S(1)}, u32[]{:S(2)}, u32[]{:S(2)}) %collective-permute-start.34) | collective-permute-done | bytes 98336 | tf_op jit(solution)/shard_map/ppermute | solution.py:60
  182.3 7.5 %collective-permute-start.35 = (f32[192,128]{1,0:T(8,128)S(1)}, f32[192,128]{1,0:T(8,128)S(1)}, u32[]{:S(2)}, u32[]{:S(2)}) collective-permute-start(f32[192,128]{1,0:T(8,128)S(1)} %add.87.first), channel_id=1, source_target_pairs={{0,8},{1,9},{2,10},{3,11},{4,12},{5,13},{6,14},{7,15},{8,0},{9,1},... | collective-permute-start | bytes 294920 | tf_op jit(solution)/shard_map/ppermute | solution.py:60
  192.1 3.3 %collective-permute-start.36 = (f32[192,128]{1,0:T(8,128)S(1)}, f32[192,128]{1,0:T(8,128)S(1)}, u32[]{:S(2)}, u32[]{:S(2)}) collective-permute-start(f32[192,128]{1,0:T(8,128)S(1)} %shard_map.143.own), channel_id=1, source_target_pairs={{0,1},{1,0},{2,3},{3,2},{4,5},{5,4},{6,7},{7,6},{8,9},{9,8},{10,11... | collective-permute-start | bytes 294920 | tf_op jit(solution)/shard_map/ppermute | solution.py:60
  (93 shorter events, 48.4 us)
Async XLA Ops:
  9.6 13.2 %collective-permute-start.11 = (f32[2,160,512]{2,1,0:T(8,128)S(1)}, f32[2,160,512]{2,1,0:T(8,128)S(1)}, u32[]{:S(2)}, u32[]{:S(2)}) collective-permute-start(f32[2,160,512]{2,1,0:T(8,128)S(1)} %pad_maximum_fusion.2.refs_3_), channel_id=1, source_target_pairs={{0,2},{1,15},{2,4},{3,1},{4,6},{5,3},{6,8},{7,5},{8,10},{9,7},{10,... | collective-permute-start | bytes 1966088 | tf_op jit(solution)/shard_map/ppermute | solution.py:60
  15.3 13.1 %collective-permute-start.1 = (f32[2,128,512]{2,1,0:T(8,128)S(1)}, f32[2,128,512]{2,1,0:T(8,128)S(1)}, u32[]{:S(2)}, u32[]{:S(2)}) collective-permute-start(f32[2,128,512]{2,1,0:T(8,128)S(1)} %pad_maximum_fusion.5.refs_0_), channel_id=1, source_target_pairs={{0,2},{1,15},{2,4},{3,1},{4,6},{5,3},{6,8},{7,5},{8,10},{9,7},{10,... | collective-permute-start | bytes 1572872 | tf_op jit(solution)/shard_map/ppermute | solution.py:60
  22.8 21.4 %collective-permute-start.13 = (f32[2,160,512]{2,1,0:T(8,128)S(1)}, f32[2,160,512]{2,1,0:T(8,128)S(1)}, u32[]{:S(2)}, u32[]{:S(2)}) collective-permute-start(f32[2,160,512]{2,1,0:T(8,128)S(1)} %collective-permute-done.11.refs_4_), channel_id=1, source_target_pairs={{0,2},{1,15},{2,4},{3,1},{4,6},{5,3},{6,8},{7,5},{8,10},{9,7},{10,... | collective-permute-start | bytes 1966088 | tf_op jit(solution)/shard_map/ppermute | solution.py:60
  28.4 12.6 %collective-permute-start.3 = (f32[2,128,512]{2,1,0:T(8,128)S(1)}, f32[2,128,512]{2,1,0:T(8,128)S(1)}, u32[]{:S(2)}, u32[]{:S(2)}) collective-permute-start(f32[2,128,512]{2,1,0:T(8,128)S(1)} %collective-permute-done.1.refs_1_), channel_id=1, source_target_pairs={{0,2},{1,15},{2,4},{3,1},{4,6},{5,3},{6,8},{7,5},{8,10},{9,7},{10,... | collective-permute-start | bytes 1572872 | tf_op jit(solution)/shard_map/ppermute | solution.py:60
  44.2 13.1 %collective-permute-start.15 = (f32[2,160,512]{2,1,0:T(8,128)S(1)}, f32[2,160,512]{2,1,0:T(8,128)S(1)}, u32[]{:S(2)}, u32[]{:S(2)}) collective-permute-start(f32[2,160,512]{2,1,0:T(8,128)S(1)} %collective-permute-done.13.refs_6_), channel_id=1, source_target_pairs={{0,2},{1,15},{2,4},{3,1},{4,6},{5,3},{6,8},{7,5},{8,10},{9,7},{10,... | collective-permute-start | bytes 1966088 | tf_op jit(solution)/shard_map/ppermute | solution.py:60
  44.2 18.8 %collective-permute-start.2 = (f32[2,128,512]{2,1,0:T(8,128)S(1)}, f32[2,128,512]{2,1,0:T(8,128)S(1)}, u32[]{:S(2)}, u32[]{:S(2)}) collective-permute-start(f32[2,128,512]{2,1,0:T(8,128)S(1)} %collective-permute-done.1.refs_1_), channel_id=1, source_target_pairs={{0,1},{1,0},{2,3},{3,2},{4,5},{5,4},{6,7},{7,6},{8,9},{9,8},{10,11... | collective-permute-start | bytes 1572872 | tf_op jit(solution)/shard_map/ppermute | solution.py:60
  44.2 18.8 %collective-permute-start.4 = (f32[2,128,512]{2,1,0:T(8,128)S(1)}, f32[2,128,512]{2,1,0:T(8,128)S(1)}, u32[]{:S(2)}, u32[]{:S(2)}) collective-permute-start(f32[2,128,512]{2,1,0:T(8,128)S(1)} %collective-permute-done.3.refs_3_), channel_id=1, source_target_pairs={{0,1},{1,0},{2,3},{3,2},{4,5},{5,4},{6,7},{7,6},{8,9},{9,8},{10,11... | collective-permute-start | bytes 1572872 | tf_op jit(solution)/shard_map/ppermute | solution.py:60
  53.5 15.0 %collective-permute-start.6 = (f32[2,128,512]{2,1,0:T(8,128)S(1)}, f32[2,128,512]{2,1,0:T(8,128)S(1)}, u32[]{:S(2)}, u32[]{:S(2)}) collective-permute-start(f32[2,128,512]{2,1,0:T(8,128)S(1)} %collective-permute-done.5.refs_5_), channel_id=1, source_target_pairs={{0,1},{1,0},{2,3},{3,2},{4,5},{5,4},{6,7},{7,6},{8,9},{9,8},{10,11... | collective-permute-start | bytes 1572872 | tf_op jit(solution)/shard_map/ppermute | solution.py:60
  63.0 13.6 %collective-permute-start.14 = (f32[2,160,512]{2,1,0:T(8,128)S(1)}, f32[2,160,512]{2,1,0:T(8,128)S(1)}, u32[]{:S(2)}, u32[]{:S(2)}) collective-permute-start(f32[2,160,512]{2,1,0:T(8,128)S(1)} %collective-permute-done.13.refs_6_), channel_id=1, source_target_pairs={{0,1},{1,0},{2,3},{3,2},{4,5},{5,4},{6,7},{7,6},{8,9},{9,8},{10,11... | collective-permute-start | bytes 1966088 | tf_op jit(solution)/shard_map/ppermute | solution.py:60
  64.1 12.5 %collective-permute-start.16 = (f32[2,160,512]{2,1,0:T(8,128)S(1)}, f32[2,160,512]{2,1,0:T(8,128)S(1)}, u32[]{:S(2)}, u32[]{:S(2)}) collective-permute-start(f32[2,160,512]{2,1,0:T(8,128)S(1)} %collective-permute-done.15.refs_8_), channel_id=1, source_target_pairs={{0,1},{1,0},{2,3},{3,2},{4,5},{5,4},{6,7},{7,6},{8,9},{9,8},{10,11... | collective-permute-start | bytes 1966088 | tf_op jit(solution)/shard_map/ppermute | solution.py:60
  64.6 12.1 %collective-permute-start.18 = (f32[1,160,512]{2,1,0:T(8,128)S(1)}, f32[1,160,512]{2,1,0:T(8,128)S(1)}, u32[]{:S(2)}, u32[]{:S(2)}) collective-permute-start(f32[1,160,512]{2,1,0:T(8,128)S(1)} %collective-permute-done.17.refs_10_), channel_id=1, source_target_pairs={{0,1},{1,0},{2,3},{3,2},{4,5},{5,4},{6,7},{7,6},{8,9},{9,8},{10,11... | collective-permute-start | bytes 983048 | tf_op jit(solution)/shard_map/ppermute | solution.py:60
  73.3 20.8 %collective-permute-start.9 = (f32[8,64,512]{2,1,0:T(8,128)S(1)}, f32[8,64,512]{2,1,0:T(8,128)S(1)}, u32[]{:S(2)}, u32[]{:S(2)}) collective-permute-start(f32[8,64,512]{2,1,0:T(8,128)S(1)} %get-tuple-element.28), channel_id=1, source_target_pairs={{0,16},{1,65},{2,18},{3,67},{4,20},{5,69},{6,22},{7,71},{8,24},{9,... | collective-permute-start | bytes 3145736 | tf_op jit(solution)/shard_map/ppermute | solution.py:60
  74.7 19.7 %collective-permute-start.23 = (f32[8,64,512]{2,1,0:T(8,128)S(1)}, f32[8,64,512]{2,1,0:T(8,128)S(1)}, u32[]{:S(2)}, u32[]{:S(2)}) collective-permute-start(f32[8,64,512]{2,1,0:T(8,128)S(1)} %get-tuple-element.34), channel_id=1, source_target_pairs={{0,48},{1,193},{2,50},{3,195},{4,52},{5,197},{6,54},{7,199},{8,56}... | collective-permute-start | bytes 3145736 | tf_op jit(solution)/shard_map/ppermute | solution.py:60
  84.9 14.0 %collective-permute-start.19 = (f32[8,64,512]{2,1,0:T(8,128)S(1)}, f32[8,64,512]{2,1,0:T(8,128)S(1)}, u32[]{:S(2)}, u32[]{:S(2)}) collective-permute-start(f32[8,64,512]{2,1,0:T(8,128)S(1)} %get-tuple-element.32), channel_id=1, source_target_pairs={{0,16},{1,65},{2,18},{3,67},{4,20},{5,69},{6,22},{7,71},{8,24},{9,... | collective-permute-start | bytes 3145736 | tf_op jit(solution)/shard_map/ppermute | solution.py:60
  85.3 16.4 %collective-permute-start.24 = (f32[8,64,512]{2,1,0:T(8,128)S(1)}, f32[8,64,512]{2,1,0:T(8,128)S(1)}, u32[]{:S(2)}, u32[]{:S(2)}) collective-permute-start(f32[8,64,512]{2,1,0:T(8,128)S(1)} %get-tuple-element.36), channel_id=1, source_target_pairs={{0,48},{1,193},{2,50},{3,195},{4,52},{5,197},{6,54},{7,199},{8,56}... | collective-permute-start | bytes 3145736 | tf_op jit(solution)/shard_map/ppermute | solution.py:60
  99.2 15.2 %collective-permute-start.20 = (f32[4,128,512]{2,1,0:T(8,128)S(1)}, f32[4,128,512]{2,1,0:T(8,128)S(1)}, u32[]{:S(2)}, u32[]{:S(2)}) collective-permute-start(f32[4,128,512]{2,1,0:T(8,128)S(1)} %pad_maximum_fusion), channel_id=1, source_target_pairs={{0,48},{1,193},{2,50},{3,195},{4,52},{5,197},{6,54},{7,199},{8,56}... | collective-permute-start | bytes 3145736 | tf_op jit(solution)/shard_map/ppermute | solution.py:60
  102.0 14.0 %collective-permute-start.25 = (f32[4,128,512]{2,1,0:T(8,128)S(1)}, f32[4,128,512]{2,1,0:T(8,128)S(1)}, u32[]{:S(2)}, u32[]{:S(2)}) collective-permute-start(f32[4,128,512]{2,1,0:T(8,128)S(1)} %pad_maximum_fusion.1), channel_id=1, source_target_pairs={{0,16},{1,65},{2,18},{3,67},{4,20},{5,69},{6,22},{7,71},{8,24},{9,... | collective-permute-start | bytes 3145736 | tf_op jit(solution)/shard_map/ppermute | solution.py:60
  102.1 25.6 %collective-permute-start.28 = (f32[256,512]{1,0:T(8,128)S(1)}, f32[256,512]{1,0:T(8,128)S(1)}, u32[]{:S(2)}, u32[]{:S(2)}) collective-permute-start(f32[256,512]{1,0:T(8,128)S(1)} %get-tuple-element.37), channel_id=1, source_target_pairs={{0,0},{1,17},{2,34},{3,51},{4,68},{5,85},{6,102},{7,119},{8,136},{... | collective-permute-start | bytes 1572872 | tf_op jit(solution)/shard_map/ppermute | solution.py:60
  114.6 12.9 %collective-permute-start.21 = (f32[2,128,512]{2,1,0:T(8,128)S(1)}, f32[2,128,512]{2,1,0:T(8,128)S(1)}, u32[]{:S(2)}, u32[]{:S(2)}) collective-permute-start(f32[2,128,512]{2,1,0:T(8,128)S(1)} %get-tuple-element.54), channel_id=1, source_target_pairs={{0,64},{1,17},{2,66},{3,19},{4,68},{5,21},{6,70},{7,23},{8,72},{9,... | collective-permute-start | bytes 1572872 | tf_op jit(solution)/shard_map/ppermute | solution.py:60
  116.3 18.8 %collective-permute-start.26 = (f32[2,128,512]{2,1,0:T(8,128)S(1)}, f32[2,128,512]{2,1,0:T(8,128)S(1)}, u32[]{:S(2)}, u32[]{:S(2)}) collective-permute-start(f32[2,128,512]{2,1,0:T(8,128)S(1)} %get-tuple-element.48), channel_id=1, source_target_pairs={{0,192},{1,49},{2,194},{3,51},{4,196},{5,53},{6,198},{7,55},{8,200... | collective-permute-start | bytes 1572872 | tf_op jit(solution)/shard_map/ppermute | solution.py:60
  119.9 15.3 %collective-permute-start.30 = (f32[128,512]{1,0:T(8,128)S(1)}, f32[128,512]{1,0:T(8,128)S(1)}, u32[]{:S(2)}, u32[]{:S(2)}) collective-permute-start(f32[128,512]{1,0:T(8,128)S(1)} %get-tuple-element.38), channel_id=1, source_target_pairs={{0,0},{1,17},{2,34},{3,51},{4,68},{5,85},{6,102},{7,119},{8,136},{... | collective-permute-start | bytes 786440 | tf_op jit(solution)/shard_map/ppermute | solution.py:60
  127.6 13.3 %collective-permute-start.22 = (f32[1,128,512]{2,1,0:T(8,128)S(1)}, f32[1,128,512]{2,1,0:T(8,128)S(1)}, u32[]{:S(2)}, u32[]{:S(2)}) collective-permute-start(f32[1,128,512]{2,1,0:T(8,128)S(1)} %slice_add_fusion.12), channel_id=1, source_target_pairs={{0,192},{1,49},{2,194},{3,51},{4,196},{5,53},{6,198},{7,55},{8,200... | collective-permute-start | bytes 786440 | tf_op jit(solution)/shard_map/ppermute | solution.py:60
  127.7 36.7 %collective-permute-start.29 = (f32[256,512]{1,0:T(8,128)S(1)}, f32[256,512]{1,0:T(8,128)S(1)}, u32[]{:S(2)}, u32[]{:S(2)}) collective-permute-start(f32[256,512]{1,0:T(8,128)S(1)} %collective-permute-done.28), channel_id=1, source_target_pairs={{0,0},{1,15},{2,14},{3,13},{4,12},{5,11},{6,10},{7,9},{8,8},{9,7},... | collective-permute-start | bytes 1572872 | tf_op jit(solution)/shard_map/ppermute | solution.py:60
  135.2 34.2 %collective-permute-start.31 = (f32[128,512]{1,0:T(8,128)S(1)}, f32[128,512]{1,0:T(8,128)S(1)}, u32[]{:S(2)}, u32[]{:S(2)}) collective-permute-start(f32[128,512]{1,0:T(8,128)S(1)} %collective-permute-done.30), channel_id=1, source_target_pairs={{0,0},{1,15},{2,14},{3,13},{4,12},{5,11},{6,10},{7,9},{8,8},{9,7},... | collective-permute-start | bytes 786440 | tf_op jit(solution)/shard_map/ppermute | solution.py:60
  (19 other events, 295.2 us)

commit v3 on v2

v3 whole, which is shorter than its diff:
```python
import jax
import jax.numpy as jnp
from jax import lax
from jax.experimental import pallas as pl
from jax.experimental.pallas import tpu as pltpu
from jax.sharding import PartitionSpec as P

N = 16
B = 128
KA = 512
ALL = ("prow", "pcol")
MASKS = (((1, 3, 4, 12), (3, 1, 12, 4)), ((4, 12, 1, 3), (12, 4, 3, 1)))
LAG = 1
SPREAD = (1, 6, 2)
VMEM = pl.BlockSpec(memory_space=pltpu.VMEM)
SMEM = pl.BlockSpec(memory_space=pltpu.SMEM)
ANY = pl.BlockSpec(memory_space=pl.ANY)
HBM = pl.BlockSpec(memory_space=pltpu.HBM)
MIB = 1024 * 1024


def f32(*shape):
    return jax.ShapeDtypeStruct(shape, jnp.float32)


def slot_mask(core, variant, slot):
    mask = 0
    for bit in range(4):
        if (slot >> (3 - bit)) & 1:
            mask ^= MASKS[core][variant][bit]
    return mask


def destination(row, core, variant, slot):
    first, second = slot_mask(0, variant, slot), slot_mask(1, variant, slot)
    return row ^ jnp.where(core == 0, first, second)


def split(value):
    high = value.astype(jnp.bfloat16)
    low = (value - high.astype(jnp.float32)).astype(jnp.bfloat16)
    return high, low


def dot_split(left, right, dims):
    out = None
    for a, b in ((left[0], right[0]), (left[0], right[1]), (left[1], right[0])):
        term = lax.dot_general(a, b, (dims, ((), ())), preferred_element_type=jnp.float32)
        out = term if out is None else out + term
    return out


def unpack(packed):
    return jnp.concatenate([packed[:, B * i : B * i + B] for i in range(4)], axis=0)


def permute(value, move):
    pairs = []
    for r in range(N):
        for c in range(N):
            nr, nc = move(r, c)
            pairs.append((r * N + c, nr * N + nc))
    return lax.ppermute(value, ALL, pairs)


def swap(value):
    return permute(value, lambda r, c: (r, c ^ 1))


def ring(value):
    return permute(value, lambda r, c: (r, (c + (2 if c % 2 == 0 else -2)) % N))


def spread_mask(col):
    mask = 10 if col % 2 else 0
    for bit, part in enumerate(SPREAD):
        if ((col // 2) >> bit) & 1:
            mask ^= part
    return mask


def prep_kernel(pattern, factor, *refs):
    if len(refs) > 4:
        par, out, staged, par_in, sems = refs
        pltpu.make_async_copy(par, par_in, sems.at[4]).start()
    else:
        _, out, staged, sems = refs
    row, col = lax.axis_index("prow"), lax.axis_index("pcol")
    copies = []
    for i in range(4):
        cut = pl.ds(B * i, B)
        copies.append(pltpu.make_async_copy(factor.at[cut], staged.at[cut], sems.at[i]))
        copies[i].start()
    for i in range(4):
        cut = pl.ds(B * i, B)
        weight = pattern[4 * row + i, col].astype(jnp.float32)
        copies[i].wait()
        out[0:128, cut] = staged[cut, :].T * weight
    if len(refs) > 4:
        pltpu.make_async_copy(par, par_in, sems.at[4]).wait()
        turned = par_in[...].T
        for i in range(4):
            out[128:160, B * i : B * i + B] = turned[32 * i : 32 * i + 32, :]


def prepare(pattern, factor, extra, rows):
    scratch = [pltpu.VMEM((KA, B), jnp.float32)]
    if rows > B:
        scratch.append(pltpu.VMEM((B, B), jnp.float32))
    return pl.pallas_call(
        prep_kernel,
        out_shape=f32(rows, KA),
        in_specs=[SMEM, HBM, HBM if rows > B else ANY],
        out_specs=VMEM,
        scratch_shapes=scratch + [pltpu.SemaphoreType.DMA((5,))],
        compiler_params=pltpu.CompilerParams(vmem_limit_bytes=(60 if rows > B else 4) * MIB),
    )(pattern, factor, extra)


def pair_up(own):
    return jnp.stack([own, swap(own)])


def gather(pair):
    blocks = [pair]
    going = pair
    for step in range(4):
        if step == 3:
            going = going[0:1]
        going = ring(going)
        blocks += [going, swap(going)]
    return blocks


def place():
    row, col = lax.axis_index("prow"), lax.axis_index("pcol")
    core = lax.rem(col, 2)
    z = lax.div(col, 2)
    target = row ^ (core * 10)
    for bit, mask in enumerate(SPREAD):
        target = target ^ (lax.rem(lax.shift_right_logical(z, bit), 2) * mask)
    return row, col, core, target


def fetch(refs, target, sems):
    col = lax.axis_index("pcol")
    z, core = lax.div(col, 2), lax.rem(col, 2)
    copies = []
    for at, ref in enumerate(refs):
        step = (at + 1) // 2
        swapped = at > 0 and at % 2 == 0
        side = (1 - core) if swapped else core
        away = jnp.where(side == 0, 8 - step, step)
        plane = lax.rem(z + away, 8)
        for i in range(ref.shape[0]):
            parity = side if i == 0 else 1 - side
            copies.append(
                pltpu.make_async_copy(
                    ref.at[i], target.at[plane * 2 + parity], sems.at[len(copies)]
                )
            )
    return copies


def one_kernel(parent, ginv, *refs):
    blocks, refs = refs[:9], refs[9:]
    sends, keeps, one, turn, left, sems = (
        refs[0:2], refs[2:4], refs[4], refs[5], refs[6], refs[7],
    )
    row, col, core, target = place()
    copies = fetch(blocks, one, sems)
    for copy in copies:
        copy.start()
    high, low = split(ginv[...])
    for copy in copies:
        copy.wait()
    turn[0:128, :] = one[parent[target], 0:128, :]
    turn[128:256, :] = one[target, 0:128, :]
    for variant in range(2):
        for half in (1, 0):
            for slot in range(8):
                dest = destination(row, core, variant, slot + 8 * half)
                left[64 * slot : 64 * slot + 64, :] = one[dest, 64 * variant : 64 * variant + 64, :]
            value = dot_split(split(left[...]), (high, low), ((1,), (0,)))
            out = sends[variant] if half else keeps[variant]
            out[...] = -value.reshape(8, 64, KA)


def first_level(parent, ginv, blocks):
    return pl.pallas_call(
        one_kernel,
        out_shape=[f32(8, 64, KA)] * 4 + [f32(16, 160, KA), f32(256, KA)],
        in_specs=[SMEM, VMEM] + [ANY] * 9,
        out_specs=[VMEM] * 6,
        scratch_shapes=[pltpu.VMEM((512, KA), jnp.float32), pltpu.SemaphoreType.DMA((16,))],
        compiler_params=pltpu.CompilerParams(vmem_limit_bytes=20 * MIB),
        cost_estimate=pl.CostEstimate(
            flops=4_000_000_000, bytes_accessed=1_000_000, transcendentals=0
        ),
    )(parent, ginv, *blocks)


def fix_kernel(parent, one, dinv_one, dinv_two, fix, par_out, base, dinv, sems):
    row, col, core, target = place()
    top = pl.multiple_of(core * 64, 64)
    sources = (
        dinv_one.at[pl.ds(pl.multiple_of(row * B, B), B)],
        dinv_one.at[pl.ds(pl.multiple_of(parent[row] * B, B), B)],
        dinv_two,
    )
    copies = [
        pltpu.make_async_copy(source, dinv.at[i], sems.at[i]) for i, source in enumerate(sources)
    ]
    for copy in copies:
        copy.start()

    def correct(m, carry):
        par = unpack(one[m, 128:160, :])
        fix[m] = dot_split(split(par), split(one[parent[m], 0:128, :]), ((1,), (0,)))
        return carry

    lax.fori_loop(0, 16, correct, 0)
    par_out[...] = unpack(one[row, 128:160, :])
    for copy in copies:
        copy.wait()
    base[0:64, :] = dinv[0, pl.ds(top, 64), :]
    base[64:128, :] = -jnp.dot(
        par_out[pl.ds(top, 64), :],
        dinv[1],
        precision=lax.Precision.HIGHEST,
        preferred_element_type=jnp.float32,
    )
    base[128:192, :] = dinv[2, pl.ds(top, 64), :]


def corrections(parent, one, dinv_one, dinv_two):
    return pl.pallas_call(
        fix_kernel,
        out_shape=[f32(16, B, KA), f32(B, B), f32(192, B)],
        in_specs=[SMEM, VMEM, HBM, HBM],
        out_specs=[VMEM] * 3,
        scratch_shapes=[pltpu.VMEM((3, B, B), jnp.float32), pltpu.SemaphoreType.DMA((3,))],
        compiler_params=pltpu.CompilerParams(vmem_limit_bytes=14 * MIB),
        cost_estimate=pl.CostEstimate(
            flops=4_000_000_000, bytes_accessed=1_000_000, transcendentals=0
        ),
    )(parent, one, dinv_one, dinv_two)


def two_kernel(half, waits, ginv, fix, *refs):
    blocks, refs = refs[:9], refs[9 + waits :]
    outs, refs = refs[0:2], refs[2:]
    two, left, sems = refs[-3:]
    row, col, core, target = place()
    copies = fetch(blocks, two, sems)
    for copy in copies:
        copy.start()
    high, low = split(ginv[...])
    for copy in copies:
        copy.wait()
    if half:
        refs[0][...] = two[target]
    for variant in range(2):
        for slot in range(8):
            dest = destination(row, core, variant, slot + 8 * half)
            rows = pl.ds(64 * variant, 64)
            left[64 * slot : 64 * slot + 64, :] = two[dest, rows, :] - fix[dest, rows, :]
        value = dot_split(split(left[...]), (high, low), ((1,), (0,)))
        outs[variant][...] = -value.reshape(8, 64, KA)


def second_level(half, ginv, fix, blocks, order):
    def body(*refs):
        two_kernel(half, len(order), *refs)

    return pl.pallas_call(
        body,
        out_shape=[f32(8, 64, KA)] * 2 + ([f32(128, KA)] if half else []),
        in_specs=[VMEM, VMEM] + [ANY] * (9 + len(order)),
        out_specs=[VMEM] * (2 + half),
        scratch_shapes=[
            pltpu.VMEM((16, B, KA), jnp.float32),
            pltpu.VMEM((512, KA), jnp.float32),
            pltpu.SemaphoreType.DMA((16,)),
        ],
        compiler_params=pltpu.CompilerParams(vmem_limit_bytes=16 * MIB),
        cost_estimate=pl.CostEstimate(
            flops=1_500_000_000, bytes_accessed=8_000_000, transcendentals=0
        ),
    )(ginv, fix, *blocks, *order)


def merge(part, keep_one, got_one, keep_two, got_two):
    def body(a, b, c, d, out):
        for i in range(4):
            out[i, 0:64, :] = a[4 * part + i] + b[4 * part + i]
            out[i, 64:128, :] = c[4 * part + i] + d[4 * part + i]

    return pl.pallas_call(
        body,
        out_shape=f32(4, B, KA),
        in_specs=[VMEM] * 4,
        out_specs=VMEM,
        compiler_params=pltpu.CompilerParams(vmem_limit_bytes=10 * MIB),
        cost_estimate=pl.CostEstimate(flops=300_000, bytes_accessed=3_000_000, transcendentals=0),
    )(keep_one, got_one, keep_two, got_two)


def row_step(value, variant, step):
    return permute(value, lambda r, c: (r ^ MASKS[c % 2][variant][step], c))


def block_kernel(a_ref, b_ref, turn_one, turn_two, one_out, two_out, send_out, keep_out, sums):
    core = lax.rem(lax.axis_index("pcol"), 2)
    for variant, ref in enumerate((a_ref, b_ref)):
        one_out[64 * variant : 64 * variant + 64, :] = ref[0:64, :]
        two_out[64 * variant : 64 * variant + 64, :] = ref[64:128, :]
    one = split(one_out[...])
    two = split(two_out[...])
    nt = ((1,), (1,))
    for i, (left, right) in enumerate(
        ((one, turn_one[128:256, :]), (two, turn_one[0:128, :]), (two, turn_two[...]))
    ):
        value = dot_split(left, split(right), nt)
        sums[0, 64 * i : 64 * i + 64, :] = value[0:64]
        sums[1, 64 * i : 64 * i + 64, :] = value[64:128]
    keep_out[...] = sums[core]
    send_out[...] = sums[1 - core]


def blocks_of(parts, turn_one, turn_two):
    return pl.pallas_call(
        block_kernel,
        out_shape=[f32(B, KA), f32(B, KA), f32(192, B), f32(192, B)],
        in_specs=[VMEM] * 4,
        out_specs=[VMEM] * 4,
        scratch_shapes=[pltpu.VMEM((2, 192, B), jnp.float32)],
        compiler_params=pltpu.CompilerParams(vmem_limit_bytes=8 * MIB),
    )(*parts, turn_one, turn_two)


def add(kept, got, order):
    half = kept.shape[0] // 2

    def body(a, b, *refs):
        outs = refs[len(order) :]
        if half == 0:
            outs[0][...] = a[0] + b[0]
            return
        outs[1][...] = a[half:] + b[half:]
        outs[0][...] = a[:half] + b[:half]

    shapes = [f32(half, B, KA)] * 2 if half else [f32(B, KA)]
    return pl.pallas_call(
        body,
        out_shape=shapes,
        in_specs=[VMEM] * 2 + [ANY] * len(order),
        out_specs=[VMEM] * len(shapes),
        compiler_params=pltpu.CompilerParams(vmem_limit_bytes=8 * MIB),
        cost_estimate=pl.CostEstimate(flops=300_000, bytes_accessed=1_000_000, transcendentals=0),
    )(kept, got, *order)


def final_kernel(base, par, first, second, out):
    total = first[...] + second[...]
    out[0:64, :] = base[0:64, :] - total[0:64, :]
    cross = base[64:128, :] - total[64:128, :]
    out[64:128, :] = cross
    out[128:192, :] = base[128:192, :] - (
        total[128:192, :]
        + lax.dot_general(
            cross,
            par[...],
            (((1,), (1,)), ((), ())),
            precision=lax.Precision.HIGHEST,
            preferred_element_type=jnp.float32,
        )
    )


def final_of(base, par, first, second):
    return pl.pallas_call(
        final_kernel,
        out_shape=f32(192, B),
        in_specs=[VMEM] * 4,
        out_specs=VMEM,
        compiler_params=pltpu.CompilerParams(vmem_limit_bytes=4 * MIB),
    )(base, par, first, second)


def join_kernel(own, other, a_out, b_out, c_out):
    core = lax.rem(lax.axis_index("pcol"), 2)
    mine = pl.multiple_of(core * 64, 64)
    rest = pl.multiple_of((1 - core) * 64, 64)
    for i, out in enumerate((a_out, b_out, c_out)):
        out[pl.ds(mine, 64), :] = own[64 * i : 64 * i + 64, :]
        out[pl.ds(rest, 64), :] = other[64 * i : 64 * i + 64, :]


def join(own, other):
    return pl.pallas_call(
        join_kernel,
        out_shape=[f32(B, B)] * 3,
        in_specs=[VMEM] * 2,
        out_specs=[VMEM] * 3,
        compiler_params=pltpu.CompilerParams(vmem_limit_bytes=4 * MIB),
    )(own, other)


def local(
    ginv_anc,
    factor_one,
    pattern_one,
    dinv_one,
    factor_two,
    factor_parent,
    pattern_two,
    parent,
    dinv_two,
):
    pair_one = pair_up(prepare(pattern_one, factor_one, factor_parent, 160))
    blocks_one = gather(pair_one)
    pair_two = pair_up(prepare(pattern_two, factor_two, blocks_one[LAG], B))
    blocks_two = gather(pair_two)
    s1a, s1b, k1a, k1b, one, turn_one = first_level(parent, ginv_anc, blocks_one)
    fix, par, base = corrections(parent, one, dinv_one, dinv_two)

    def spread(value):
        return permute(value, lambda r, c: (r ^ spread_mask(c), c))

    def settle(value):
        return permute(value, lambda r, c: (r, r ^ spread_mask(c)))

    turn_one = spread(turn_one)
    r1a, r1b = row_step(s1a, 0, 0), row_step(s1b, 1, 0)
    s2a, s2b, turn_two = second_level(1, ginv_anc, fix, blocks_two, [])
    k2a, k2b = second_level(0, ginv_anc, fix, blocks_two, [r1a, r1b, turn_one])
    turn_one = settle(turn_one)
    turn_two = spread(turn_two)
    r2a, r2b = row_step(s2a, 0, 0), row_step(s2b, 1, 0)
    going = [merge(1, k1a, r1a, k2a, r2a), merge(1, k1b, r1b, k2b, r2b)]
    kept = [merge(0, k1a, r1a, k2a, r2a), merge(0, k1b, r1b, k2b, r2b)]
    got = [row_step(going[v], v, 1) for v in range(2)]
    kept[0], first = add(kept[0], got[0], [turn_two])
    kept[1], second = add(kept[1], got[1], [])
    turn_two = settle(turn_two)
    got = [row_step(first, 0, 2), row_step(second, 1, 2)]
    kept[0], first = add(kept[0], got[0], [])
    kept[1], second = add(kept[1], got[1], [turn_one])
    got = [row_step(first, 0, 3), row_step(second, 1, 3)]
    kept = [add(kept[v], got[v], [])[0] for v in range(2)]
    anc_one, anc_two, send, keep = blocks_of(kept, turn_one, turn_two)
    sums = keep + swap(send)
    for mask in (2, 6):
        sums = sums + permute(sums, lambda r, c: (r, c ^ mask))
    done = final_of(base, par, sums, permute(sums, lambda r, c: (r, c ^ 14)))
    diag_one, cross, diag_two = join(done, swap(done))
    return anc_one, diag_one, anc_two, cross, diag_two


def solution(mesh):
    return jax.shard_map(
        local,
        mesh=mesh,
        in_specs=(
            P("prow", "pcol"),
            P("prow", "pcol"),
            P(),
            P(),
            P("prow", "pcol"),
            P(None, "pcol"),
            P(),
            P(),
            P("prow", None),
        ),
        out_specs=(
            P("prow", "pcol"),
            P("prow", None),
            P("prow", "pcol"),
            P("prow", None),
            P("prow", None),
        ),
        check_vma=False,
    )
```

time: 200 us -> 187 us (0.935)
  waiting for transfers between devices: 87.6 us -> 72.3 us
  starting transfers between devices: 75.6 us -> 81.1 us
  Pallas kernels: 26.7 us -> 24.5 us
    ppermute x37, waiting for transfers between devices: 87.6 us -> 72.3 us  [permute(): return lax.ppermute(value, ALL, pairs)]
    ppermute x37, starting transfers between devices: 75.6 us -> 81.1 us  [permute(): return lax.ppermute(value, ALL, pairs)]
    pallas_call x6 -> x17, Pallas kernels: 25 us -> 23.3 us  [the longest x1 6.23 us: first_level(): pl.pallas_call(one_kernel, out_shape=[f32(8, 64, KA)] * 4 + [f32(16, 160,...]
    unnamed x14 -> x12, local copies, waits for them, and re-layouts: 4.31 us -> 3.23 us
  transfers between devices with their start and end apart: 37 -> 37, of which waited for: 19 -> 19; matrix products, arithmetic and copies ran while one was open for 1% -> 0% of each run, Pallas kernels for 11% -> 11%
where the time goes in v3:
time: 187 us; the launch traced here: 183 us
  starting transfers between devices  81.1 us (43%)
  waiting for transfers between devices  72.3 us (39%)
  Pallas kernels  24.5 us (13%)
  local copies, waits for them, and re-layouts  3.27 us (2%)
    ppermute x37, starting transfers between devices, permute(): return lax.ppermute(value, ALL, pairs)  81.1 us
    ppermute x37, waiting for transfers between devices, permute(): return lax.ppermute(value, ALL, pairs)  72.3 us
    pallas_call x1, Pallas kernels, first_level(): pl.pallas_call(one_kernel, out_shape=[f32(8, 64, KA)] * 4 + [f32(16, 160,...  6.23 us
    pallas_call x1, Pallas kernels, corrections(): pl.pallas_call(fix_kernel, out_shape=[f32(16, B, KA), f32(B, B), f32(192,...  5.28 us
    pallas_call x2, Pallas kernels, prepare(): pl.pallas_call(prep_kernel, out_shape=f32(rows, KA), in_specs=[SMEM, HBM,...  5.2 us
    pallas_call x2, Pallas kernels, second_level(): pl.pallas_call(body, out_shape=[f32(8, 64, KA)] * 2 + ([f32(128, KA)] if...  5.07 us
  transfers between devices with their start and end apart: 37, of which 19 were waited for; matrix products, arithmetic and copies ran while one was open for 0% of the time, Pallas kernels for 11%

profile of v3, /device:TPU:7, one launch (start us, length us, event | category | flops | bytes accessed | tf_op | source)
XLA Modules:
  0.0 183.3 jit_solution(2615124412446974745)
XLA Ops:
  2.1 3.3 %shard_map.128 = f32[160,512]{1,0:T(8,128)} custom-call(s32[64,16]{1,0:T(8,128)} %copy.14.pattern, f32[512,128]{1,0:T(8,128)} %factor.2, f32[128,128]{1,0:T(8,128)} %refs_0_.3), custom_call_target="tpu_custom_call" | custom-call | tf_op jit(solution)/shard_map/pallas_call | solution.py:110
  8.7 5.7 %collective-permute-start.1 = (f32[2,160,512]{2,1,0:T(8,128)S(1)}, f32[2,160,512]{2,1,0:T(8,128)S(1)}, u32[]{:S(2)}, u32[]{:S(2)}) collective-permute-start(f32[2,160,512]{2,1,0:T(8,128)S(1)} %pad_maximum_fusion.refs_0_), channel_id=1, source_target_pairs={{0,2},{1,15},{2,4},{3,1},{4,6},{5,3},{6,8},{7,5},{8,10},{9,7},{10,... | collective-permute-start | bytes 1966088 | tf_op jit(solution)/shard_map/ppermute | solution.py:63
  14.4 7.5 %collective-permute-done.1.refs_1_.refs_0_ = f32[2,160,512]{2,1,0:T(8,128)S(1)} collective-permute-done((f32[2,160,512]{2,1,0:T(8,128)S(1)}, f32[2,160,512]{2,1,0:T(8,128)S(1)}, u32[]{:S(2)}, u32[]{:S(2)}) %collective-permute-start.1) | collective-permute-done | bytes 655392 | tf_op jit(solution)/shard_map/ppermute | solution.py:63
  21.9 3.1 %collective-permute-start.3 = (f32[2,160,512]{2,1,0:T(8,128)S(1)}, f32[2,160,512]{2,1,0:T(8,128)S(1)}, u32[]{:S(2)}, u32[]{:S(2)}) collective-permute-start(f32[2,160,512]{2,1,0:T(8,128)S(1)} %collective-permute-done.1.refs_1_.refs_0_), channel_id=1, source_target_pairs={{0,2},{1,15},{2,4},{3,1},{4,6},{5,3},{6,8},{7,5},{8,10},{9,7},{10,... | collective-permute-start | bytes 1966088 | tf_op jit(solution)/shard_map/ppermute | solution.py:63
  32.6 3.1 %collective-permute-start.5 = (f32[2,160,512]{2,1,0:T(8,128)S(1)}, f32[2,160,512]{2,1,0:T(8,128)S(1)}, u32[]{:S(2)}, u32[]{:S(2)}) collective-permute-start(f32[2,160,512]{2,1,0:T(8,128)S(1)} %collective-permute-done.3.refs_3_), channel_id=1, source_target_pairs={{0,2},{1,15},{2,4},{3,1},{4,6},{5,3},{6,8},{7,5},{8,10},{9,7},{10,... | collective-permute-start | bytes 1966088 | tf_op jit(solution)/shard_map/ppermute | solution.py:63
  35.7 3.0 %collective-permute-done.11.refs_3_ = f32[2,128,512]{2,1,0:T(8,128)S(1)} collective-permute-done((f32[2,128,512]{2,1,0:T(8,128)S(1)}, f32[2,128,512]{2,1,0:T(8,128)S(1)}, u32[]{:S(2)}, u32[]{:S(2)}) %collective-permute-start.11) | collective-permute-done | bytes 524320 | tf_op jit(solution)/shard_map/ppermute | solution.py:63
  41.8 3.9 %collective-permute-done.5.refs_5_ = f32[2,160,512]{2,1,0:T(8,128)S(1)} collective-permute-done((f32[2,160,512]{2,1,0:T(8,128)S(1)}, f32[2,160,512]{2,1,0:T(8,128)S(1)}, u32[]{:S(2)}, u32[]{:S(2)}) %collective-permute-start.5) | collective-permute-done | bytes 655392 | tf_op jit(solution)/shard_map/ppermute | solution.py:63
  48.4 2.9 %collective-permute-done.13.refs_5_ = f32[2,128,512]{2,1,0:T(8,128)S(1)} collective-permute-done((f32[2,128,512]{2,1,0:T(8,128)S(1)}, f32[2,128,512]{2,1,0:T(8,128)S(1)}, u32[]{:S(2)}, u32[]{:S(2)}) %collective-permute-start.13) | collective-permute-done | bytes 524320 | tf_op jit(solution)/shard_map/ppermute | solution.py:63
  57.2 3.3 %collective-permute-done.15.refs_7_ = f32[2,128,512]{2,1,0:T(8,128)S(1)} collective-permute-done((f32[2,128,512]{2,1,0:T(8,128)S(1)}, f32[2,128,512]{2,1,0:T(8,128)S(1)}, u32[]{:S(2)}, u32[]{:S(2)}) %collective-permute-start.15) | collective-permute-done | bytes 524320 | tf_op jit(solution)/shard_map/ppermute | solution.py:63
  60.5 3.6 %collective-permute-start.12 = (f32[2,128,512]{2,1,0:T(8,128)S(1)}, f32[2,128,512]{2,1,0:T(8,128)S(1)}, u32[]{:S(2)}, u32[]{:S(2)}) collective-permute-start(f32[2,128,512]{2,1,0:T(8,128)S(1)} %collective-permute-done.11.refs_3_), channel_id=1, source_target_pairs={{0,1},{1,0},{2,3},{3,2},{4,5},{5,4},{6,7},{7,6},{8,9},{9,8},{10,11... | collective-permute-start | bytes 1572872 | tf_op jit(solution)/shard_map/ppermute | solution.py:63
  65.0 6.2 %shard_map.129 = (f32[8,64,512]{2,1,0:T(8,128)S(1)}, f32[8,64,512]{2,1,0:T(8,128)S(1)}, f32[8,64,512]{2,1,0:T(8,128)S(1)}, f32[8,64,512]{2,1,0:T(8,128)S(1)}, f3...) custom-call(s32[16]{0:T(128)S(1)} %copy-done.4, f32[512,512]{1,0:T(8,128)S(1)} %copy-done, ...), custom_call_target="tpu_custom_call" | custom-call | flops 4000000000 | bytes 1000000 | tf_op jit(solution)/shard_map/pallas_call | solution.py:190
  74.1 5.3 %shard_map.130 = (f32[16,128,512]{2,1,0:T(8,128)S(1)}, f32[128,128]{1,0:T(8,128)S(1)}, f32[192,128]{1,0:T(8,128)S(1)}) custom-call(s32[16]{0:T(128)S(1)} %copy-done.4, f32[16,160,512]{2,1,0:T(8,128)S(1)} %get-tuple-element.36.one, f32[2048,128]{1,0:T(8,128)S(1)} %copy-done.2, f32[128,128]{1,0:T(8,128)S(1)} %copy-done.3), custom_call_target="tpu_custom_call" | custom-call | flops 4000000000 | bytes 1000000 | tf_op jit(solution)/shard_map/pallas_call | solution.py:237
  83.9 4.9 %collective-permute-start.20 = (f32[256,512]{1,0:T(8,128)S(1)}, f32[256,512]{1,0:T(8,128)S(1)}, u32[]{:S(2)}, u32[]{:S(2)}) collective-permute-start(f32[256,512]{1,0:T(8,128)S(1)} %get-tuple-element.39), channel_id=1, source_target_pairs={{0,0},{1,161},{2,18},{3,179},{4,100},{5,197},{6,118},{7,215},{8,40... | collective-permute-start | bytes 1572872 | tf_op jit(solution)/shard_map/ppermute | solution.py:63
  88.9 14.6 %collective-permute-done.20.refs_13_ = f32[256,512]{1,0:T(8,128)S(1)} collective-permute-done((f32[256,512]{1,0:T(8,128)S(1)}, f32[256,512]{1,0:T(8,128)S(1)}, u32[]{:S(2)}, u32[]{:S(2)}) %collective-permute-start.20) | collective-permute-done | bytes 524320 | tf_op jit(solution)/shard_map/ppermute | solution.py:63
  107.2 3.0 %collective-permute-done.21.d = f32[8,64,512]{2,1,0:T(8,128)S(1)} collective-permute-done((f32[8,64,512]{2,1,0:T(8,128)S(1)}, f32[8,64,512]{2,1,0:T(8,128)S(1)}, u32[]{:S(2)}, u32[]{:S(2)}) %collective-permute-start.21) | collective-permute-done | bytes 1048608 | tf_op jit(solution)/shard_map/ppermute | solution.py:63
  111.4 3.7 %collective-permute-start.23 = (f32[128,512]{1,0:T(8,128)S(1)}, f32[128,512]{1,0:T(8,128)S(1)}, u32[]{:S(2)}, u32[]{:S(2)}) collective-permute-start(f32[128,512]{1,0:T(8,128)S(1)} %get-tuple-element.42), channel_id=1, source_target_pairs={{0,0},{1,161},{2,18},{3,179},{4,100},{5,197},{6,118},{7,215},{8,40... | collective-permute-start | bytes 786440 | tf_op jit(solution)/shard_map/ppermute | solution.py:63
  115.1 10.3 %collective-permute-start.29 = (f32[256,512]{1,0:T(8,128)S(1)}, f32[256,512]{1,0:T(8,128)S(1)}, u32[]{:S(2)}, u32[]{:S(2)}) collective-permute-start(f32[256,512]{1,0:T(8,128)S(1)} %collective-permute-done.20.refs_13_), channel_id=1, source_target_pairs={{0,0},{1,10},{2,1},{3,11},{4,6},{5,12},{6,7},{7,13},{8,2},{9,8},{1... | collective-permute-start | bytes 1572872 | tf_op jit(solution)/shard_map/ppermute | solution.py:63
  129.2 8.2 %collective-permute-done.29.refs_0_.turn_one = f32[256,512]{1,0:T(8,128)S(1)} collective-permute-done((f32[256,512]{1,0:T(8,128)S(1)}, f32[256,512]{1,0:T(8,128)S(1)}, u32[]{:S(2)}, u32[]{:S(2)}) %collective-permute-start.29) | collective-permute-done | bytes 524320 | tf_op jit(solution)/shard_map/ppermute | solution.py:63
  137.7 11.1 %collective-permute-start.31 = (f32[128,512]{1,0:T(8,128)S(1)}, f32[128,512]{1,0:T(8,128)S(1)}, u32[]{:S(2)}, u32[]{:S(2)}) collective-permute-start(f32[128,512]{1,0:T(8,128)S(1)} %collective-permute-done.23.refs_0_), channel_id=1, source_target_pairs={{0,0},{1,10},{2,1},{3,11},{4,6},{5,12},{6,7},{7,13},{8,2},{9,8},{1... | collective-permute-start | bytes 786440 | tf_op jit(solution)/shard_map/ppermute | solution.py:63
  148.9 7.7 %collective-permute-done.31.turn_two = f32[128,512]{1,0:T(8,128)S(1)} collective-permute-done((f32[128,512]{1,0:T(8,128)S(1)}, f32[128,512]{1,0:T(8,128)S(1)}, u32[]{:S(2)}, u32[]{:S(2)}) %collective-permute-start.31) | collective-permute-done | bytes 262176 | tf_op jit(solution)/shard_map/ppermute | solution.py:63
  159.0 4.2 %collective-permute-done.33 = f32[192,128]{1,0:T(8,128)S(1)} collective-permute-done((f32[192,128]{1,0:T(8,128)S(1)}, f32[192,128]{1,0:T(8,128)S(1)}, u32[]{:S(2)}, u32[]{:S(2)}) %collective-permute-start.33) | collective-permute-done | bytes 98336 | tf_op jit(solution)/shard_map/ppermute | solution.py:63
  163.2 4.7 %collective-permute-start.34 = (f32[192,128]{1,0:T(8,128)S(1)}, f32[192,128]{1,0:T(8,128)S(1)}, u32[]{:S(2)}, u32[]{:S(2)}) collective-permute-start(f32[192,128]{1,0:T(8,128)S(1)} %add.10), channel_id=1, source_target_pairs={{0,6},{1,7},{2,4},{3,5},{4,2},{5,3},{6,0},{7,1},{8,14},{9,15},{10,... | collective-permute-start | bytes 294920 | tf_op jit(solution)/shard_map/ppermute | solution.py:63
  170.1 5.0 %collective-permute-start.35 = (f32[192,128]{1,0:T(8,128)S(1)}, f32[192,128]{1,0:T(8,128)S(1)}, u32[]{:S(2)}, u32[]{:S(2)}) collective-permute-start(f32[192,128]{1,0:T(8,128)S(1)} %add.11.first), channel_id=1, source_target_pairs={{0,14},{1,15},{2,12},{3,13},{4,10},{5,11},{6,8},{7,9},{8,6},{9,7},... | collective-permute-start | bytes 294920 | tf_op jit(solution)/shard_map/ppermute | solution.py:63
  177.3 4.4 %collective-permute-start.36 = (f32[192,128]{1,0:T(8,128)S(1)}, f32[192,128]{1,0:T(8,128)S(1)}, u32[]{:S(2)}, u32[]{:S(2)}) collective-permute-start(f32[192,128]{1,0:T(8,128)S(1)} %shard_map.145.own), channel_id=1, source_target_pairs={{0,1},{1,0},{2,3},{3,2},{4,5},{5,4},{6,7},{7,6},{8,9},{9,8},{10,11... | collective-permute-start | bytes 294920 | tf_op jit(solution)/shard_map/ppermute | solution.py:63
  (88 shorter events, 49.5 us)
Async XLA Ops:
  8.7 13.2 %collective-permute-start.1 = (f32[2,160,512]{2,1,0:T(8,128)S(1)}, f32[2,160,512]{2,1,0:T(8,128)S(1)}, u32[]{:S(2)}, u32[]{:S(2)}) collective-permute-start(f32[2,160,512]{2,1,0:T(8,128)S(1)} %pad_maximum_fusion.refs_0_), channel_id=1, source_target_pairs={{0,2},{1,15},{2,4},{3,1},{4,6},{5,3},{6,8},{7,5},{8,10},{9,7},{10,... | collective-permute-start | bytes 1966088 | tf_op jit(solution)/shard_map/ppermute | solution.py:63
  21.9 10.6 %collective-permute-start.3 = (f32[2,160,512]{2,1,0:T(8,128)S(1)}, f32[2,160,512]{2,1,0:T(8,128)S(1)}, u32[]{:S(2)}, u32[]{:S(2)}) collective-permute-start(f32[2,160,512]{2,1,0:T(8,128)S(1)} %collective-permute-done.1.refs_1_.refs_0_), channel_id=1, source_target_pairs={{0,2},{1,15},{2,4},{3,1},{4,6},{5,3},{6,8},{7,5},{8,10},{9,7},{10,... | collective-permute-start | bytes 1966088 | tf_op jit(solution)/shard_map/ppermute | solution.py:63
  32.6 13.2 %collective-permute-start.5 = (f32[2,160,512]{2,1,0:T(8,128)S(1)}, f32[2,160,512]{2,1,0:T(8,128)S(1)}, u32[]{:S(2)}, u32[]{:S(2)}) collective-permute-start(f32[2,160,512]{2,1,0:T(8,128)S(1)} %collective-permute-done.3.refs_3_), channel_id=1, source_target_pairs={{0,2},{1,15},{2,4},{3,1},{4,6},{5,3},{6,8},{7,5},{8,10},{9,7},{10,... | collective-permute-start | bytes 1966088 | tf_op jit(solution)/shard_map/ppermute | solution.py:63
  38.7 12.6 %collective-permute-start.13 = (f32[2,128,512]{2,1,0:T(8,128)S(1)}, f32[2,128,512]{2,1,0:T(8,128)S(1)}, u32[]{:S(2)}, u32[]{:S(2)}) collective-permute-start(f32[2,128,512]{2,1,0:T(8,128)S(1)} %collective-permute-done.11.refs_3_), channel_id=1, source_target_pairs={{0,2},{1,15},{2,4},{3,1},{4,6},{5,3},{6,8},{7,5},{8,10},{9,7},{10,... | collective-permute-start | bytes 1572872 | tf_op jit(solution)/shard_map/ppermute | solution.py:63
  41.3 22.8 %collective-permute-start.2 = (f32[2,160,512]{2,1,0:T(8,128)S(1)}, f32[2,160,512]{2,1,0:T(8,128)S(1)}, u32[]{:S(2)}, u32[]{:S(2)}) collective-permute-start(f32[2,160,512]{2,1,0:T(8,128)S(1)} %collective-permute-done.1.refs_1_.refs_0_), channel_id=1, source_target_pairs={{0,1},{1,0},{2,3},{3,2},{4,5},{5,4},{6,7},{7,6},{8,9},{9,8},{10,11... | collective-permute-start | bytes 1966088 | tf_op jit(solution)/shard_map/ppermute | solution.py:63
  41.3 22.9 %collective-permute-start.4 = (f32[2,160,512]{2,1,0:T(8,128)S(1)}, f32[2,160,512]{2,1,0:T(8,128)S(1)}, u32[]{:S(2)}, u32[]{:S(2)}) collective-permute-start(f32[2,160,512]{2,1,0:T(8,128)S(1)} %collective-permute-done.3.refs_3_), channel_id=1, source_target_pairs={{0,1},{1,0},{2,3},{3,2},{4,5},{5,4},{6,7},{7,6},{8,9},{9,8},{10,11... | collective-permute-start | bytes 1966088 | tf_op jit(solution)/shard_map/ppermute | solution.py:63
  48.4 16.6 %collective-permute-start.6 = (f32[2,160,512]{2,1,0:T(8,128)S(1)}, f32[2,160,512]{2,1,0:T(8,128)S(1)}, u32[]{:S(2)}, u32[]{:S(2)}) collective-permute-start(f32[2,160,512]{2,1,0:T(8,128)S(1)} %collective-permute-done.5.refs_5_), channel_id=1, source_target_pairs={{0,1},{1,0},{2,3},{3,2},{4,5},{5,4},{6,7},{7,6},{8,9},{9,8},{10,11... | collective-permute-start | bytes 1966088 | tf_op jit(solution)/shard_map/ppermute | solution.py:63
  60.5 18.9 %collective-permute-start.12 = (f32[2,128,512]{2,1,0:T(8,128)S(1)}, f32[2,128,512]{2,1,0:T(8,128)S(1)}, u32[]{:S(2)}, u32[]{:S(2)}) collective-permute-start(f32[2,128,512]{2,1,0:T(8,128)S(1)} %collective-permute-done.11.refs_3_), channel_id=1, source_target_pairs={{0,1},{1,0},{2,3},{3,2},{4,5},{5,4},{6,7},{7,6},{8,9},{9,8},{10,11... | collective-permute-start | bytes 1572872 | tf_op jit(solution)/shard_map/ppermute | solution.py:63
  64.1 15.4 %collective-permute-start.14 = (f32[2,128,512]{2,1,0:T(8,128)S(1)}, f32[2,128,512]{2,1,0:T(8,128)S(1)}, u32[]{:S(2)}, u32[]{:S(2)}) collective-permute-start(f32[2,128,512]{2,1,0:T(8,128)S(1)} %collective-permute-done.13.refs_5_), channel_id=1, source_target_pairs={{0,1},{1,0},{2,3},{3,2},{4,5},{5,4},{6,7},{7,6},{8,9},{9,8},{10,11... | collective-permute-start | bytes 1572872 | tf_op jit(solution)/shard_map/ppermute | solution.py:63
  64.2 9.8 %collective-permute-start.17 = (f32[1,128,512]{2,1,0:T(8,128)S(1)}, f32[1,128,512]{2,1,0:T(8,128)S(1)}, u32[]{:S(2)}, u32[]{:S(2)}) collective-permute-start(f32[1,128,512]{2,1,0:T(8,128)S(1)} %slice.9), channel_id=1, source_target_pairs={{0,2},{1,15},{2,4},{3,1},{4,6},{5,3},{6,8},{7,5},{8,10},{9,7},{10,... | collective-permute-start | bytes 786440 | tf_op jit(solution)/shard_map/ppermute | solution.py:63
  64.3 15.2 %collective-permute-start.16 = (f32[2,128,512]{2,1,0:T(8,128)S(1)}, f32[2,128,512]{2,1,0:T(8,128)S(1)}, u32[]{:S(2)}, u32[]{:S(2)}) collective-permute-start(f32[2,128,512]{2,1,0:T(8,128)S(1)} %collective-permute-done.15.refs_7_), channel_id=1, source_target_pairs={{0,1},{1,0},{2,3},{3,2},{4,5},{5,4},{6,7},{7,6},{8,9},{9,8},{10,11... | collective-permute-start | bytes 1572872 | tf_op jit(solution)/shard_map/ppermute | solution.py:63
  71.2 32.2 %collective-permute-start.19 = (f32[8,64,512]{2,1,0:T(8,128)S(1)}, f32[8,64,512]{2,1,0:T(8,128)S(1)}, u32[]{:S(2)}, u32[]{:S(2)}) collective-permute-start(f32[8,64,512]{2,1,0:T(8,128)S(1)} %get-tuple-element.38), channel_id=1, source_target_pairs={{0,48},{1,193},{2,50},{3,195},{4,52},{5,197},{6,54},{7,199},{8,56}... | collective-permute-start | bytes 3145736 | tf_op jit(solution)/shard_map/ppermute | solution.py:63
  79.4 24.1 %collective-permute-start.9 = (f32[8,64,512]{2,1,0:T(8,128)S(1)}, f32[8,64,512]{2,1,0:T(8,128)S(1)}, u32[]{:S(2)}, u32[]{:S(2)}) collective-permute-start(f32[8,64,512]{2,1,0:T(8,128)S(1)} %get-tuple-element.35), channel_id=1, source_target_pairs={{0,16},{1,65},{2,18},{3,67},{4,20},{5,69},{6,22},{7,71},{8,24},{9,... | collective-permute-start | bytes 3145736 | tf_op jit(solution)/shard_map/ppermute | solution.py:63
  82.1 23.9 %collective-permute-start.26 = (f32[8,64,512]{2,1,0:T(8,128)S(1)}, f32[8,64,512]{2,1,0:T(8,128)S(1)}, u32[]{:S(2)}, u32[]{:S(2)}) collective-permute-start(f32[8,64,512]{2,1,0:T(8,128)S(1)} %get-tuple-element.49), channel_id=1, source_target_pairs={{0,48},{1,193},{2,50},{3,195},{4,52},{5,197},{6,54},{7,199},{8,56}... | collective-permute-start | bytes 3145736 | tf_op jit(solution)/shard_map/ppermute | solution.py:63
  83.5 26.7 %collective-permute-start.21 = (f32[8,64,512]{2,1,0:T(8,128)S(1)}, f32[8,64,512]{2,1,0:T(8,128)S(1)}, u32[]{:S(2)}, u32[]{:S(2)}) collective-permute-start(f32[8,64,512]{2,1,0:T(8,128)S(1)} %get-tuple-element.41), channel_id=1, source_target_pairs={{0,16},{1,65},{2,18},{3,67},{4,20},{5,69},{6,22},{7,71},{8,24},{9,... | collective-permute-start | bytes 3145736 | tf_op jit(solution)/shard_map/ppermute | solution.py:63
  83.9 19.5 %collective-permute-start.20 = (f32[256,512]{1,0:T(8,128)S(1)}, f32[256,512]{1,0:T(8,128)S(1)}, u32[]{:S(2)}, u32[]{:S(2)}) collective-permute-start(f32[256,512]{1,0:T(8,128)S(1)} %get-tuple-element.39), channel_id=1, source_target_pairs={{0,0},{1,161},{2,18},{3,179},{4,100},{5,197},{6,118},{7,215},{8,40... | collective-permute-start | bytes 1572872 | tf_op jit(solution)/shard_map/ppermute | solution.py:63
  106.1 19.6 %collective-permute-start.27 = (f32[4,128,512]{2,1,0:T(8,128)S(1)}, f32[4,128,512]{2,1,0:T(8,128)S(1)}, u32[]{:S(2)}, u32[]{:S(2)}) collective-permute-start(f32[4,128,512]{2,1,0:T(8,128)S(1)} %shard_map.140), channel_id=1, source_target_pairs={{0,16},{1,65},{2,18},{3,67},{4,20},{5,69},{6,22},{7,71},{8,24},{9,... | collective-permute-start | bytes 3145736 | tf_op jit(solution)/shard_map/ppermute | solution.py:63
  110.4 18.1 %collective-permute-start.22 = (f32[4,128,512]{2,1,0:T(8,128)S(1)}, f32[4,128,512]{2,1,0:T(8,128)S(1)}, u32[]{:S(2)}, u32[]{:S(2)}) collective-permute-start(f32[4,128,512]{2,1,0:T(8,128)S(1)} %shard_map.135), channel_id=1, source_target_pairs={{0,48},{1,193},{2,50},{3,195},{4,52},{5,197},{6,54},{7,199},{8,56}... | collective-permute-start | bytes 3145736 | tf_op jit(solution)/shard_map/ppermute | solution.py:63
  111.4 14.5 %collective-permute-start.23 = (f32[128,512]{1,0:T(8,128)S(1)}, f32[128,512]{1,0:T(8,128)S(1)}, u32[]{:S(2)}, u32[]{:S(2)}) collective-permute-start(f32[128,512]{1,0:T(8,128)S(1)} %get-tuple-element.42), channel_id=1, source_target_pairs={{0,0},{1,161},{2,18},{3,179},{4,100},{5,197},{6,118},{7,215},{8,40... | collective-permute-start | bytes 786440 | tf_op jit(solution)/shard_map/ppermute | solution.py:63
  115.1 22.3 %collective-permute-start.29 = (f32[256,512]{1,0:T(8,128)S(1)}, f32[256,512]{1,0:T(8,128)S(1)}, u32[]{:S(2)}, u32[]{:S(2)}) collective-permute-start(f32[256,512]{1,0:T(8,128)S(1)} %collective-permute-done.20.refs_13_), channel_id=1, source_target_pairs={{0,0},{1,10},{2,1},{3,11},{4,6},{5,12},{6,7},{7,13},{8,2},{9,8},{1... | collective-permute-start | bytes 1572872 | tf_op jit(solution)/shard_map/ppermute | solution.py:63
  125.8 11.6 %collective-permute-start.28 = (f32[2,128,512]{2,1,0:T(8,128)S(1)}, f32[2,128,512]{2,1,0:T(8,128)S(1)}, u32[]{:S(2)}, u32[]{:S(2)}) collective-permute-start(f32[2,128,512]{2,1,0:T(8,128)S(1)} %get-tuple-element.51), channel_id=1, source_target_pairs={{0,192},{1,49},{2,194},{3,51},{4,196},{5,53},{6,198},{7,55},{8,200... | collective-permute-start | bytes 1572872 | tf_op jit(solution)/shard_map/ppermute | solution.py:63
  137.5 11.4 %collective-permute-start.30 = (f32[1,128,512]{2,1,0:T(8,128)S(1)}, f32[1,128,512]{2,1,0:T(8,128)S(1)}, u32[]{:S(2)}, u32[]{:S(2)}) collective-permute-start(f32[1,128,512]{2,1,0:T(8,128)S(1)} %get-tuple-element.53), channel_id=1, source_target_pairs={{0,64},{1,17},{2,66},{3,19},{4,68},{5,21},{6,70},{7,23},{8,72},{9,... | collective-permute-start | bytes 786440 | tf_op jit(solution)/shard_map/ppermute | solution.py:63
  137.6 11.2 %collective-permute-start.25 = (f32[1,128,512]{2,1,0:T(8,128)S(1)}, f32[1,128,512]{2,1,0:T(8,128)S(1)}, u32[]{:S(2)}, u32[]{:S(2)}) collective-permute-start(f32[1,128,512]{2,1,0:T(8,128)S(1)} %get-tuple-element.46), channel_id=1, source_target_pairs={{0,192},{1,49},{2,194},{3,51},{4,196},{5,53},{6,198},{7,55},{8,200... | collective-permute-start | bytes 786440 | tf_op jit(solution)/shard_map/ppermute | solution.py:63
  137.7 18.8 %collective-permute-start.31 = (f32[128,512]{1,0:T(8,128)S(1)}, f32[128,512]{1,0:T(8,128)S(1)}, u32[]{:S(2)}, u32[]{:S(2)}) collective-permute-start(f32[128,512]{1,0:T(8,128)S(1)} %collective-permute-done.23.refs_0_), channel_id=1, source_target_pairs={{0,0},{1,10},{2,1},{3,11},{4,6},{5,12},{6,7},{7,13},{8,2},{9,8},{1... | collective-permute-start | bytes 786440 | tf_op jit(solution)/shard_map/ppermute | solution.py:63
  (18 other events, 228.8 us)

commit v4 on v3

--- a/solution.py
+++ b/solution.py
@@ -10,7 +10,6 @@
 KA = 512
 ALL = ("prow", "pcol")
 MASKS = (((1, 3, 4, 12), (3, 1, 12, 4)), ((4, 12, 1, 3), (12, 4, 3, 1)))
-LAG = 1
 SPREAD = (1, 6, 2)
 VMEM = pl.BlockSpec(memory_space=pltpu.VMEM)
 SMEM = pl.BlockSpec(memory_space=pltpu.SMEM)
@@ -79,42 +78,52 @@
     return mask
 
 
-def prep_kernel(pattern, factor, *refs):
-    if len(refs) > 4:
-        par, out, staged, par_in, sems = refs
-        pltpu.make_async_copy(par, par_in, sems.at[4]).start()
-    else:
-        _, out, staged, sems = refs
+def prep_kernel(pat_one, pat_two, fac_one, fac_two, par, one, two, pat, fac, par_in, sems):
     row, col = lax.axis_index("prow"), lax.axis_index("pcol")
-    copies = []
+    copies = [
+        pltpu.make_async_copy(pat_one, pat.at[0], sems.at[0]),
+        pltpu.make_async_copy(fac_one, fac.at[0], sems.at[1]),
+        pltpu.make_async_copy(par, par_in, sems.at[2]),
+        pltpu.make_async_copy(pat_two, pat.at[1], sems.at[3]),
+        pltpu.make_async_copy(fac_two, fac.at[1], sems.at[4]),
+    ]
+    for copy in copies:
+        copy.start()
+    lanes = lax.broadcasted_iota(jnp.int32, (1, 64), 1)
+
+    def turn(level, out):
+        for i in range(4):
+            cut = pl.ds(B * i, B)
+            flags = jnp.where(lanes == 4 * row + i, pat[level, pl.ds(col, 1), :], 0)
+            weight = jnp.sum(flags.astype(jnp.float32), axis=1, keepdims=True)
+            out[0:128, cut] = fac[level, cut, :].T * weight
+
+    copies[0].wait()
+    copies[1].wait()
+    turn(0, one)
+    copies[2].wait()
+    turned = par_in[...].T
     for i in range(4):
-        cut = pl.ds(B * i, B)
-        copies.append(pltpu.make_async_copy(factor.at[cut], staged.at[cut], sems.at[i]))
-        copies[i].start()
-    for i in range(4):
-        cut = pl.ds(B * i, B)
-        weight = pattern[4 * row + i, col].astype(jnp.float32)
-        copies[i].wait()
-        out[0:128, cut] = staged[cut, :].T * weight
-    if len(refs) > 4:
-        pltpu.make_async_copy(par, par_in, sems.at[4]).wait()
-        turned = par_in[...].T
-        for i in range(4):
-            out[128:160, B * i : B * i + B] = turned[32 * i : 32 * i + 32, :]
-
-
-def prepare(pattern, factor, extra, rows):
-    scratch = [pltpu.VMEM((KA, B), jnp.float32)]
-    if rows > B:
-        scratch.append(pltpu.VMEM((B, B), jnp.float32))
+        one[128:160, B * i : B * i + B] = turned[32 * i : 32 * i + 32, :]
+    copies[3].wait()
+    copies[4].wait()
+    turn(1, two)
+
+
+def prepare(pat_one, pat_two, fac_one, fac_two, par):
     return pl.pallas_call(
         prep_kernel,
-        out_shape=f32(rows, KA),
-        in_specs=[SMEM, HBM, HBM if rows > B else ANY],
-        out_specs=VMEM,
-        scratch_shapes=scratch + [pltpu.SemaphoreType.DMA((5,))],
-        compiler_params=pltpu.CompilerParams(vmem_limit_bytes=(60 if rows > B else 4) * MIB),
-    )(pattern, factor, extra)
+        out_shape=[f32(160, KA), f32(B, KA)],
+        in_specs=[HBM] * 5,
+        out_specs=[VMEM] * 2,
+        scratch_shapes=[
+            pltpu.VMEM((2, N, 64), jnp.int32),
+            pltpu.VMEM((2, KA, B), jnp.float32),
+            pltpu.VMEM((B, B), jnp.float32),
+            pltpu.SemaphoreType.DMA((5,)),
+        ],
+        compiler_params=pltpu.CompilerParams(vmem_limit_bytes=56 * MIB),
+    )(pat_one, pat_two, fac_one, fac_two, par)
 
 
 def pair_up(own):
@@ -193,7 +202,7 @@
         in_specs=[SMEM, VMEM] + [ANY] * 9,
         out_specs=[VMEM] * 6,
         scratch_shapes=[pltpu.VMEM((512, KA), jnp.float32), pltpu.SemaphoreType.DMA((16,))],
-        compiler_params=pltpu.CompilerParams(vmem_limit_bytes=20 * MIB),
+        compiler_params=pltpu.CompilerParams(vmem_limit_bytes=8 * MIB),
         cost_estimate=pl.CostEstimate(
             flops=4_000_000_000, bytes_accessed=1_000_000, transcendentals=0
         ),
@@ -240,54 +249,42 @@
         in_specs=[SMEM, VMEM, HBM, HBM],
         out_specs=[VMEM] * 3,
         scratch_shapes=[pltpu.VMEM((3, B, B), jnp.float32), pltpu.SemaphoreType.DMA((3,))],
-        compiler_params=pltpu.CompilerParams(vmem_limit_bytes=14 * MIB),
+        compiler_params=pltpu.CompilerParams(vmem_limit_bytes=6 * MIB),
         cost_estimate=pl.CostEstimate(
             flops=4_000_000_000, bytes_accessed=1_000_000, transcendentals=0
         ),
     )(parent, one, dinv_one, dinv_two)
 
 
-def two_kernel(half, waits, ginv, fix, *refs):
-    blocks, refs = refs[:9], refs[9 + waits :]
-    outs, refs = refs[0:2], refs[2:]
-    two, left, sems = refs[-3:]
+def two_kernel(half, ginv, fix, two, outs, left):
     row, col, core, target = place()
-    copies = fetch(blocks, two, sems)
-    for copy in copies:
-        copy.start()
-    high, low = split(ginv[...])
-    for copy in copies:
-        copy.wait()
+    ginv = split(ginv[...])
     if half:
-        refs[0][...] = two[target]
+        outs[2][...] = two[target]
     for variant in range(2):
         for slot in range(8):
             dest = destination(row, core, variant, slot + 8 * half)
             rows = pl.ds(64 * variant, 64)
             left[64 * slot : 64 * slot + 64, :] = two[dest, rows, :] - fix[dest, rows, :]
-        value = dot_split(split(left[...]), (high, low), ((1,), (0,)))
+        value = dot_split(split(left[...]), ginv, ((1,), (0,)))
         outs[variant][...] = -value.reshape(8, 64, KA)
 
 
-def second_level(half, ginv, fix, blocks, order):
-    def body(*refs):
-        two_kernel(half, len(order), *refs)
+def second_level(half, ginv, fix, gathered, order):
+    def body(ginv, fix, two, *refs):
+        two_kernel(half, ginv, fix, two, refs[len(order) : -1], refs[-1])
 
     return pl.pallas_call(
         body,
         out_shape=[f32(8, 64, KA)] * 2 + ([f32(128, KA)] if half else []),
-        in_specs=[VMEM, VMEM] + [ANY] * (9 + len(order)),
+        in_specs=[VMEM] * 3 + [ANY] * len(order),
         out_specs=[VMEM] * (2 + half),
-        scratch_shapes=[
-            pltpu.VMEM((16, B, KA), jnp.float32),
-            pltpu.VMEM((512, KA), jnp.float32),
-            pltpu.SemaphoreType.DMA((16,)),
-        ],
-        compiler_params=pltpu.CompilerParams(vmem_limit_bytes=16 * MIB),
+        scratch_shapes=[pltpu.VMEM((512, KA), jnp.float32)],
+        compiler_params=pltpu.CompilerParams(vmem_limit_bytes=8 * MIB),
         cost_estimate=pl.CostEstimate(
             flops=1_500_000_000, bytes_accessed=8_000_000, transcendentals=0
         ),
-    )(ginv, fix, *blocks, *order)
+    )(ginv, fix, gathered, *order)
 
 
 def merge(part, keep_one, got_one, keep_two, got_two):
@@ -301,7 +298,7 @@
         out_shape=f32(4, B, KA),
         in_specs=[VMEM] * 4,
         out_specs=VMEM,
-        compiler_params=pltpu.CompilerParams(vmem_limit_bytes=10 * MIB),
+        compiler_params=pltpu.CompilerParams(vmem_limit_bytes=4 * MIB),
         cost_estimate=pl.CostEstimate(flops=300_000, bytes_accessed=3_000_000, transcendentals=0),
     )(keep_one, got_one, keep_two, got_two)
 
@@ -418,10 +415,9 @@
     parent,
     dinv_two,
 ):
-    pair_one = pair_up(prepare(pattern_one, factor_one, factor_parent, 160))
-    blocks_one = gather(pair_one)
-    pair_two = pair_up(prepare(pattern_two, factor_two, blocks_one[LAG], B))
-    blocks_two = gather(pair_two)
+    own_one, own_two = prepare(pattern_one.T, pattern_two.T, factor_one, factor_two, factor_parent)
+    gathered = lax.all_gather(own_two, "pcol", axis=0, tiled=False)
+    blocks_one = gather(pair_up(own_one))
     s1a, s1b, k1a, k1b, one, turn_one = first_level(parent, ginv_anc, blocks_one)
     fix, par, base = corrections(parent, one, dinv_one, dinv_two)
 
@@ -433,8 +429,8 @@
 
     turn_one = spread(turn_one)
     r1a, r1b = row_step(s1a, 0, 0), row_step(s1b, 1, 0)
-    s2a, s2b, turn_two = second_level(1, ginv_anc, fix, blocks_two, [])
-    k2a, k2b = second_level(0, ginv_anc, fix, blocks_two, [r1a, r1b, turn_one])
+    s2a, s2b, turn_two = second_level(1, ginv_anc, fix, gathered, [r1a, r1b])
+    k2a, k2b = second_level(0, ginv_anc, fix, gathered, [turn_one])
     turn_one = settle(turn_one)
     turn_two = spread(turn_two)
     r2a, r2b = row_step(s2a, 0, 0), row_step(s2b, 1, 0)
@@ -448,7 +444,7 @@
     kept[0], first = add(kept[0], got[0], [])
     kept[1], second = add(kept[1], got[1], [turn_one])
     got = [row_step(first, 0, 3), row_step(second, 1, 3)]
-    kept = [add(kept[v], got[v], [])[0] for v in range(2)]
+    kept = [add(kept[0], got[0], [])[0], add(kept[1], got[1], [])[0]]
     anc_one, anc_two, send, keep = blocks_of(kept, turn_one, turn_two)
     sums = keep + swap(send)
     for mask in (2, 6):

time: 187 us -> 210 us (1.12)
  waiting for transfers between devices: 72.3 us -> 97.6 us
  starting transfers between devices: 81.1 us -> 64.7 us
  between operations: 1.04 us -> 14.3 us
  local copies, waits for them, and re-layouts: 3.27 us -> 10.5 us
  Pallas kernels: 24.5 us -> 20.1 us
    ppermute x37 -> x28, waiting for transfers between devices: 72.3 us -> 97.6 us  [permute(): return lax.ppermute(value, ALL, pairs)]
    ppermute x37 -> x28, starting transfers between devices: 81.1 us -> 64.6 us  [permute(): return lax.ppermute(value, ALL, pairs)]
    unnamed x12 -> x26, local copies, waits for them, and re-layouts: 3.23 us -> 10.5 us
    pallas_call x2 -> x1, Pallas kernels: 5.2 us -> 2.15 us  [prepare(): pl.pallas_call(prep_kernel, out_shape=[f32(160, KA), f32(B, KA)], in_spec...]
  transfers between devices with their start and end apart: 37 -> 29, of which waited for: 19 -> 20; matrix products, arithmetic and copies ran while one was open for 0% -> 1% of each run, Pallas kernels for 11% -> 7%
where the time goes in v4:
time: 210 us; the launch traced here: 208 us
  waiting for transfers between devices  97.6 us (46%)
  starting transfers between devices  64.7 us (31%)
  Pallas kernels  20.1 us (10%)
  between operations  14.3 us (7%)
  local copies, waits for them, and re-layouts  10.5 us (5%)
    ppermute x28, waiting for transfers between devices, permute(): return lax.ppermute(value, ALL, pairs)  97.6 us
    ppermute x28, starting transfers between devices, permute(): return lax.ppermute(value, ALL, pairs)  64.6 us
    unnamed x26, local copies, waits for them, and re-layouts  10.5 us
    pallas_call x1, Pallas kernels, first_level(): pl.pallas_call(one_kernel, out_shape=[f32(8, 64, KA)] * 4 + [f32(16, 160,...  6.25 us
    pallas_call x1, Pallas kernels, corrections(): pl.pallas_call(fix_kernel, out_shape=[f32(16, B, KA), f32(B, B), f32(192,...  5.3 us
  transfers between devices with their start and end apart: 29, of which 20 were waited for; matrix products, arithmetic and copies ran while one was open for 1% of the time, Pallas kernels for 7%

profile of v4, /device:TPU:7, one launch (start us, length us, event | category | flops | bytes accessed | tf_op | source)
XLA Modules:
  0.0 208.2 jit_solution(18314376333341328432)
XLA Ops:
  12.6 5.7 %collective-permute-start.1 = (f32[2,160,512]{2,1,0:T(8,128)S(1)}, f32[2,160,512]{2,1,0:T(8,128)S(1)}, u32[]{:S(2)}, u32[]{:S(2)}) collective-permute-start(f32[2,160,512]{2,1,0:T(8,128)S(1)} %pad_maximum_fusion.refs_0_), channel_id=1, source_target_pairs={{0,2},{1,15},{2,4},{3,1},{4,6},{5,3},{6,8},{7,5},{8,10},{9,7},{10,... | collective-permute-start | bytes 1966088 | tf_op jit(solution)/shard_map/ppermute | solution.py:62
  18.3 9.6 %collective-permute-done.1.refs_1_ = f32[2,160,512]{2,1,0:T(8,128)S(1)} collective-permute-done((f32[2,160,512]{2,1,0:T(8,128)S(1)}, f32[2,160,512]{2,1,0:T(8,128)S(1)}, u32[]{:S(2)}, u32[]{:S(2)}) %collective-permute-start.1) | collective-permute-done | bytes 655392 | tf_op jit(solution)/shard_map/ppermute | solution.py:62
  27.9 3.5 %collective-permute-start.3 = (f32[2,160,512]{2,1,0:T(8,128)S(1)}, f32[2,160,512]{2,1,0:T(8,128)S(1)}, u32[]{:S(2)}, u32[]{:S(2)}) collective-permute-start(f32[2,160,512]{2,1,0:T(8,128)S(1)} %collective-permute-done.1.refs_1_), channel_id=1, source_target_pairs={{0,2},{1,15},{2,4},{3,1},{4,6},{5,3},{6,8},{7,5},{8,10},{9,7},{10,... | collective-permute-start | bytes 1966088 | tf_op jit(solution)/shard_map/ppermute | solution.py:62
  31.4 20.2 %collective-permute-done.3.refs_3_ = f32[2,160,512]{2,1,0:T(8,128)S(1)} collective-permute-done((f32[2,160,512]{2,1,0:T(8,128)S(1)}, f32[2,160,512]{2,1,0:T(8,128)S(1)}, u32[]{:S(2)}, u32[]{:S(2)}) %collective-permute-start.3) | collective-permute-done | bytes 655392 | tf_op jit(solution)/shard_map/ppermute | solution.py:62
  51.6 3.5 %collective-permute-start.5 = (f32[2,160,512]{2,1,0:T(8,128)S(1)}, f32[2,160,512]{2,1,0:T(8,128)S(1)}, u32[]{:S(2)}, u32[]{:S(2)}) collective-permute-start(f32[2,160,512]{2,1,0:T(8,128)S(1)} %collective-permute-done.3.refs_3_), channel_id=1, source_target_pairs={{0,2},{1,15},{2,4},{3,1},{4,6},{5,3},{6,8},{7,5},{8,10},{9,7},{10,... | collective-permute-start | bytes 1966088 | tf_op jit(solution)/shard_map/ppermute | solution.py:62
  55.1 7.7 %collective-permute-done.5.refs_5_ = f32[2,160,512]{2,1,0:T(8,128)S(1)} collective-permute-done((f32[2,160,512]{2,1,0:T(8,128)S(1)}, f32[2,160,512]{2,1,0:T(8,128)S(1)}, u32[]{:S(2)}, u32[]{:S(2)}) %collective-permute-start.5) | collective-permute-done | bytes 655392 | tf_op jit(solution)/shard_map/ppermute | solution.py:62
  62.9 3.0 %collective-permute-start.7 = (f32[1,160,512]{2,1,0:T(8,128)S(1)}, f32[1,160,512]{2,1,0:T(8,128)S(1)}, u32[]{:S(2)}, u32[]{:S(2)}) collective-permute-start(f32[1,160,512]{2,1,0:T(8,128)S(1)} %slice.4), channel_id=1, source_target_pairs={{0,2},{1,15},{2,4},{3,1},{4,6},{5,3},{6,8},{7,5},{8,10},{9,7},{10,... | collective-permute-start | bytes 983048 | tf_op jit(solution)/shard_map/ppermute | solution.py:62
  66.4 3.5 %collective-permute-done.7.refs_7_ = f32[1,160,512]{2,1,0:T(8,128)S(1)} collective-permute-done((f32[1,160,512]{2,1,0:T(8,128)S(1)}, f32[1,160,512]{2,1,0:T(8,128)S(1)}, u32[]{:S(2)}, u32[]{:S(2)}) %collective-permute-start.7) | collective-permute-done | bytes 327712 | tf_op jit(solution)/shard_map/ppermute | solution.py:62
  69.9 3.0 %collective-permute-start.8 = (f32[1,160,512]{2,1,0:T(8,128)S(1)}, f32[1,160,512]{2,1,0:T(8,128)S(1)}, u32[]{:S(2)}, u32[]{:S(2)}) collective-permute-start(f32[1,160,512]{2,1,0:T(8,128)S(1)} %collective-permute-done.7.refs_7_), channel_id=1, source_target_pairs={{0,1},{1,0},{2,3},{3,2},{4,5},{5,4},{6,7},{7,6},{8,9},{9,8},{10,11... | collective-permute-start | bytes 983048 | tf_op jit(solution)/shard_map/ppermute | solution.py:62
  76.0 6.3 %shard_map.129 = (f32[8,64,512]{2,1,0:T(8,128)S(1)}, f32[8,64,512]{2,1,0:T(8,128)S(1)}, f32[8,64,512]{2,1,0:T(8,128)S(1)}, f32[8,64,512]{2,1,0:T(8,128)S(1)}, f3...) custom-call(s32[16]{0:T(128)S(1)} %copy-done.11, f32[512,512]{1,0:T(8,128)S(1)} %copy-done.5, ...), custom_call_target="tpu_custom_call" | custom-call | flops 4000000000 | bytes 1000000 | tf_op jit(solution)/shard_map/pallas_call | solution.py:199
  86.1 5.3 %shard_map.130 = (f32[16,128,512]{2,1,0:T(8,128)S(1)}, f32[128,128]{1,0:T(8,128)S(1)}, f32[192,128]{1,0:T(8,128)S(1)}) custom-call(s32[16]{0:T(128)S(1)} %copy-done.12, f32[16,160,512]{2,1,0:T(8,128)S(1)} %get-tuple-element.39.one, f32[2048,128]{1,0:T(8,128)S(1)} %copy-done.7, f32[128,128]{1,0:T(8,128)S(1)} %copy-done.10), custom_call_target="tpu_custom_call" | custom-call | flops 4000000000 | bytes 1000000 | tf_op jit(solution)/shard_map/pallas_call | solution.py:246
  93.5 5.1 %collective-permute-done.11.refs_1_.b = f32[8,64,512]{2,1,0:T(8,128)S(1)} collective-permute-done((f32[8,64,512]{2,1,0:T(8,128)S(1)}, f32[8,64,512]{2,1,0:T(8,128)S(1)}, u32[]{:S(2)}, u32[]{:S(2)}) %collective-permute-start.11) | collective-permute-done | bytes 1048608 | tf_op jit(solution)/shard_map/ppermute | solution.py:62
  108.8 5.1 %collective-permute-start.10 = (f32[256,512]{1,0:T(8,128)S(1)}, f32[256,512]{1,0:T(8,128)S(1)}, u32[]{:S(2)}, u32[]{:S(2)}) collective-permute-start(f32[256,512]{1,0:T(8,128)S(1)} %copy-done.9), channel_id=1, source_target_pairs={{0,0},{1,161},{2,18},{3,179},{4,100},{5,197},{6,118},{7,215},{8,40... | collective-permute-start | bytes 1572872 | tf_op jit(solution)/shard_map/ppermute | solution.py:62
  114.0 14.5 %collective-permute-done.10.refs_0_ = f32[256,512]{1,0:T(8,128)S(1)} collective-permute-done((f32[256,512]{1,0:T(8,128)S(1)}, f32[256,512]{1,0:T(8,128)S(1)}, u32[]{:S(2)}, u32[]{:S(2)}) %collective-permute-start.10) | collective-permute-done | bytes 524320 | tf_op jit(solution)/shard_map/ppermute | solution.py:62
  133.3 3.0 %collective-permute-start.14 = (f32[128,512]{1,0:T(8,128)S(1)}, f32[128,512]{1,0:T(8,128)S(1)}, u32[]{:S(2)}, u32[]{:S(2)}) collective-permute-start(f32[128,512]{1,0:T(8,128)S(1)} %get-tuple-element.46), channel_id=1, source_target_pairs={{0,0},{1,161},{2,18},{3,179},{4,100},{5,197},{6,118},{7,215},{8,40... | collective-permute-start | bytes 786440 | tf_op jit(solution)/shard_map/ppermute | solution.py:62
  136.4 7.2 %collective-permute-start.20 = (f32[256,512]{1,0:T(8,128)S(1)}, f32[256,512]{1,0:T(8,128)S(1)}, u32[]{:S(2)}, u32[]{:S(2)}) collective-permute-start(f32[256,512]{1,0:T(8,128)S(1)} %collective-permute-done.10.refs_0_), channel_id=1, source_target_pairs={{0,0},{1,10},{2,1},{3,11},{4,6},{5,12},{6,7},{7,13},{8,2},{9,8},{1... | collective-permute-start | bytes 1572872 | tf_op jit(solution)/shard_map/ppermute | solution.py:62
  143.8 3.4 %collective-permute-done.18.b = f32[4,128,512]{2,1,0:T(8,128)S(1)} collective-permute-done((f32[4,128,512]{2,1,0:T(8,128)S(1)}, f32[4,128,512]{2,1,0:T(8,128)S(1)}, u32[]{:S(2)}, u32[]{:S(2)}) %collective-permute-start.18) | collective-permute-done | bytes 1048608 | tf_op jit(solution)/shard_map/ppermute | solution.py:62
  150.5 5.2 %collective-permute-done.20.refs_0_.turn_one = f32[256,512]{1,0:T(8,128)S(1)} collective-permute-done((f32[256,512]{1,0:T(8,128)S(1)}, f32[256,512]{1,0:T(8,128)S(1)}, u32[]{:S(2)}, u32[]{:S(2)}) %collective-permute-start.20) | collective-permute-done | bytes 524320 | tf_op jit(solution)/shard_map/ppermute | solution.py:62
  158.8 7.0 %collective-permute-start.22 = (f32[128,512]{1,0:T(8,128)S(1)}, f32[128,512]{1,0:T(8,128)S(1)}, u32[]{:S(2)}, u32[]{:S(2)}) collective-permute-start(f32[128,512]{1,0:T(8,128)S(1)} %collective-permute-done.14.refs_0_), channel_id=1, source_target_pairs={{0,0},{1,10},{2,1},{3,11},{4,6},{5,12},{6,7},{7,13},{8,2},{9,8},{1... | collective-permute-start | bytes 786440 | tf_op jit(solution)/shard_map/ppermute | solution.py:62
  166.0 9.1 %collective-permute-done.22.turn_two = f32[128,512]{1,0:T(8,128)S(1)} collective-permute-done((f32[128,512]{1,0:T(8,128)S(1)}, f32[128,512]{1,0:T(8,128)S(1)}, u32[]{:S(2)}, u32[]{:S(2)}) %collective-permute-start.22) | collective-permute-done | bytes 262176 | tf_op jit(solution)/shard_map/ppermute | solution.py:62
  177.4 4.2 %collective-permute-done.24 = f32[192,128]{1,0:T(8,128)S(1)} collective-permute-done((f32[192,128]{1,0:T(8,128)S(1)}, f32[192,128]{1,0:T(8,128)S(1)}, u32[]{:S(2)}, u32[]{:S(2)}) %collective-permute-start.24) | collective-permute-done | bytes 98336 | tf_op jit(solution)/shard_map/ppermute | solution.py:62
  181.7 7.1 %collective-permute-start.25 = (f32[192,128]{1,0:T(8,128)S(1)}, f32[192,128]{1,0:T(8,128)S(1)}, u32[]{:S(2)}, u32[]{:S(2)}) collective-permute-start(f32[192,128]{1,0:T(8,128)S(1)} %add.10), channel_id=1, source_target_pairs={{0,6},{1,7},{2,4},{3,5},{4,2},{5,3},{6,0},{7,1},{8,14},{9,15},{10,... | collective-permute-start | bytes 294920 | tf_op jit(solution)/shard_map/ppermute | solution.py:62
  190.9 2.9 %collective-permute-start.26 = (f32[192,128]{1,0:T(8,128)S(1)}, f32[192,128]{1,0:T(8,128)S(1)}, u32[]{:S(2)}, u32[]{:S(2)}) collective-permute-start(f32[192,128]{1,0:T(8,128)S(1)} %add.11.first), channel_id=1, source_target_pairs={{0,14},{1,15},{2,12},{3,13},{4,10},{5,11},{6,8},{7,9},{8,6},{9,7},... | collective-permute-start | bytes 294920 | tf_op jit(solution)/shard_map/ppermute | solution.py:62
  196.0 3.7 %collective-permute-start.27 = (f32[192,128]{1,0:T(8,128)S(1)}, f32[192,128]{1,0:T(8,128)S(1)}, u32[]{:S(2)}, u32[]{:S(2)}) collective-permute-start(f32[192,128]{1,0:T(8,128)S(1)} %shard_map.144.own), channel_id=1, source_target_pairs={{0,1},{1,0},{2,3},{3,2},{4,5},{5,4},{6,7},{7,6},{8,9},{9,8},{10,11... | collective-permute-start | bytes 294920 | tf_op jit(solution)/shard_map/ppermute | solution.py:62
  (84 shorter events, 45.0 us)
Async XLA Ops:
  7.2 92.6 %all-gather.3.cloned.1.call-start = ((), (), s32[]{:S(2)}) async-start(), calls=%async_computation | async-start | bytes 4456448 | tf_op jit(solution)/shard_map/all_gather | solution.py:419
  12.6 15.2 %collective-permute-start.1 = (f32[2,160,512]{2,1,0:T(8,128)S(1)}, f32[2,160,512]{2,1,0:T(8,128)S(1)}, u32[]{:S(2)}, u32[]{:S(2)}) collective-permute-start(f32[2,160,512]{2,1,0:T(8,128)S(1)} %pad_maximum_fusion.refs_0_), channel_id=1, source_target_pairs={{0,2},{1,15},{2,4},{3,1},{4,6},{5,3},{6,8},{7,5},{8,10},{9,7},{10,... | collective-permute-start | bytes 1966088 | tf_op jit(solution)/shard_map/ppermute | solution.py:62
  27.9 23.7 %collective-permute-start.3 = (f32[2,160,512]{2,1,0:T(8,128)S(1)}, f32[2,160,512]{2,1,0:T(8,128)S(1)}, u32[]{:S(2)}, u32[]{:S(2)}) collective-permute-start(f32[2,160,512]{2,1,0:T(8,128)S(1)} %collective-permute-done.1.refs_1_), channel_id=1, source_target_pairs={{0,2},{1,15},{2,4},{3,1},{4,6},{5,3},{6,8},{7,5},{8,10},{9,7},{10,... | collective-permute-start | bytes 1966088 | tf_op jit(solution)/shard_map/ppermute | solution.py:62
  51.6 11.3 %collective-permute-start.5 = (f32[2,160,512]{2,1,0:T(8,128)S(1)}, f32[2,160,512]{2,1,0:T(8,128)S(1)}, u32[]{:S(2)}, u32[]{:S(2)}) collective-permute-start(f32[2,160,512]{2,1,0:T(8,128)S(1)} %collective-permute-done.3.refs_3_), channel_id=1, source_target_pairs={{0,2},{1,15},{2,4},{3,1},{4,6},{5,3},{6,8},{7,5},{8,10},{9,7},{10,... | collective-permute-start | bytes 1966088 | tf_op jit(solution)/shard_map/ppermute | solution.py:62
  55.1 17.7 %collective-permute-start.2 = (f32[2,160,512]{2,1,0:T(8,128)S(1)}, f32[2,160,512]{2,1,0:T(8,128)S(1)}, u32[]{:S(2)}, u32[]{:S(2)}) collective-permute-start(f32[2,160,512]{2,1,0:T(8,128)S(1)} %collective-permute-done.1.refs_1_), channel_id=1, source_target_pairs={{0,1},{1,0},{2,3},{3,2},{4,5},{5,4},{6,7},{7,6},{8,9},{9,8},{10,11... | collective-permute-start | bytes 1966088 | tf_op jit(solution)/shard_map/ppermute | solution.py:62
  62.9 7.0 %collective-permute-start.7 = (f32[1,160,512]{2,1,0:T(8,128)S(1)}, f32[1,160,512]{2,1,0:T(8,128)S(1)}, u32[]{:S(2)}, u32[]{:S(2)}) collective-permute-start(f32[1,160,512]{2,1,0:T(8,128)S(1)} %slice.4), channel_id=1, source_target_pairs={{0,2},{1,15},{2,4},{3,1},{4,6},{5,3},{6,8},{7,5},{8,10},{9,7},{10,... | collective-permute-start | bytes 983048 | tf_op jit(solution)/shard_map/ppermute | solution.py:62
  65.9 7.0 %collective-permute-start.4 = (f32[2,160,512]{2,1,0:T(8,128)S(1)}, f32[2,160,512]{2,1,0:T(8,128)S(1)}, u32[]{:S(2)}, u32[]{:S(2)}) collective-permute-start(f32[2,160,512]{2,1,0:T(8,128)S(1)} %collective-permute-done.3.refs_3_), channel_id=1, source_target_pairs={{0,1},{1,0},{2,3},{3,2},{4,5},{5,4},{6,7},{7,6},{8,9},{9,8},{10,11... | collective-permute-start | bytes 1966088 | tf_op jit(solution)/shard_map/ppermute | solution.py:62
  65.9 8.2 %collective-permute-start.6 = (f32[2,160,512]{2,1,0:T(8,128)S(1)}, f32[2,160,512]{2,1,0:T(8,128)S(1)}, u32[]{:S(2)}, u32[]{:S(2)}) collective-permute-start(f32[2,160,512]{2,1,0:T(8,128)S(1)} %collective-permute-done.5.refs_5_), channel_id=1, source_target_pairs={{0,1},{1,0},{2,3},{3,2},{4,5},{5,4},{6,7},{7,6},{8,9},{9,8},{10,11... | collective-permute-start | bytes 1966088 | tf_op jit(solution)/shard_map/ppermute | solution.py:62
  83.2 15.4 %collective-permute-start.11 = (f32[8,64,512]{2,1,0:T(8,128)S(1)}, f32[8,64,512]{2,1,0:T(8,128)S(1)}, u32[]{:S(2)}, u32[]{:S(2)}) collective-permute-start(f32[8,64,512]{2,1,0:T(8,128)S(1)} %get-tuple-element.44), channel_id=1, source_target_pairs={{0,48},{1,193},{2,50},{3,195},{4,52},{5,197},{6,54},{7,199},{8,56}... | collective-permute-start | bytes 3145736 | tf_op jit(solution)/shard_map/ppermute | solution.py:62
  86.1 13.7 %collective-permute-start.9 = (f32[8,64,512]{2,1,0:T(8,128)S(1)}, f32[8,64,512]{2,1,0:T(8,128)S(1)}, u32[]{:S(2)}, u32[]{:S(2)}) collective-permute-start(f32[8,64,512]{2,1,0:T(8,128)S(1)} %get-tuple-element.38), channel_id=1, source_target_pairs={{0,16},{1,65},{2,18},{3,67},{4,20},{5,69},{6,22},{7,71},{8,24},{9,... | collective-permute-start | bytes 3145736 | tf_op jit(solution)/shard_map/ppermute | solution.py:62
  107.2 23.1 %collective-permute-start.17 = (f32[8,64,512]{2,1,0:T(8,128)S(1)}, f32[8,64,512]{2,1,0:T(8,128)S(1)}, u32[]{:S(2)}, u32[]{:S(2)}) collective-permute-start(f32[8,64,512]{2,1,0:T(8,128)S(1)} %get-tuple-element.53), channel_id=1, source_target_pairs={{0,48},{1,193},{2,50},{3,195},{4,52},{5,197},{6,54},{7,199},{8,56}... | collective-permute-start | bytes 3145736 | tf_op jit(solution)/shard_map/ppermute | solution.py:62
  108.8 23.2 %collective-permute-start.12 = (f32[8,64,512]{2,1,0:T(8,128)S(1)}, f32[8,64,512]{2,1,0:T(8,128)S(1)}, u32[]{:S(2)}, u32[]{:S(2)}) collective-permute-start(f32[8,64,512]{2,1,0:T(8,128)S(1)} %get-tuple-element.45), channel_id=1, source_target_pairs={{0,16},{1,65},{2,18},{3,67},{4,20},{5,69},{6,22},{7,71},{8,24},{9,... | collective-permute-start | bytes 3145736 | tf_op jit(solution)/shard_map/ppermute | solution.py:62
  108.8 19.6 %collective-permute-start.10 = (f32[256,512]{1,0:T(8,128)S(1)}, f32[256,512]{1,0:T(8,128)S(1)}, u32[]{:S(2)}, u32[]{:S(2)}) collective-permute-start(f32[256,512]{1,0:T(8,128)S(1)} %copy-done.9), channel_id=1, source_target_pairs={{0,0},{1,161},{2,18},{3,179},{4,100},{5,197},{6,118},{7,215},{8,40... | collective-permute-start | bytes 1572872 | tf_op jit(solution)/shard_map/ppermute | solution.py:62
  130.4 16.8 %collective-permute-start.18 = (f32[4,128,512]{2,1,0:T(8,128)S(1)}, f32[4,128,512]{2,1,0:T(8,128)S(1)}, u32[]{:S(2)}, u32[]{:S(2)}) collective-permute-start(f32[4,128,512]{2,1,0:T(8,128)S(1)} %shard_map.139), channel_id=1, source_target_pairs={{0,16},{1,65},{2,18},{3,67},{4,20},{5,69},{6,22},{7,71},{8,24},{9,... | collective-permute-start | bytes 3145736 | tf_op jit(solution)/shard_map/ppermute | solution.py:62
  132.1 17.8 %collective-permute-start.13 = (f32[4,128,512]{2,1,0:T(8,128)S(1)}, f32[4,128,512]{2,1,0:T(8,128)S(1)}, u32[]{:S(2)}, u32[]{:S(2)}) collective-permute-start(f32[4,128,512]{2,1,0:T(8,128)S(1)} %shard_map.134), channel_id=1, source_target_pairs={{0,48},{1,193},{2,50},{3,195},{4,52},{5,197},{6,54},{7,199},{8,56}... | collective-permute-start | bytes 3145736 | tf_op jit(solution)/shard_map/ppermute | solution.py:62
  133.3 14.3 %collective-permute-start.14 = (f32[128,512]{1,0:T(8,128)S(1)}, f32[128,512]{1,0:T(8,128)S(1)}, u32[]{:S(2)}, u32[]{:S(2)}) collective-permute-start(f32[128,512]{1,0:T(8,128)S(1)} %get-tuple-element.46), channel_id=1, source_target_pairs={{0,0},{1,161},{2,18},{3,179},{4,100},{5,197},{6,118},{7,215},{8,40... | collective-permute-start | bytes 786440 | tf_op jit(solution)/shard_map/ppermute | solution.py:62
  136.4 19.4 %collective-permute-start.20 = (f32[256,512]{1,0:T(8,128)S(1)}, f32[256,512]{1,0:T(8,128)S(1)}, u32[]{:S(2)}, u32[]{:S(2)}) collective-permute-start(f32[256,512]{1,0:T(8,128)S(1)} %collective-permute-done.10.refs_0_), channel_id=1, source_target_pairs={{0,0},{1,10},{2,1},{3,11},{4,6},{5,12},{6,7},{7,13},{8,2},{9,8},{1... | collective-permute-start | bytes 1572872 | tf_op jit(solution)/shard_map/ppermute | solution.py:62
  147.4 9.4 %collective-permute-start.19 = (f32[2,128,512]{2,1,0:T(8,128)S(1)}, f32[2,128,512]{2,1,0:T(8,128)S(1)}, u32[]{:S(2)}, u32[]{:S(2)}) collective-permute-start(f32[2,128,512]{2,1,0:T(8,128)S(1)} %get-tuple-element.55), channel_id=1, source_target_pairs={{0,192},{1,49},{2,194},{3,51},{4,196},{5,53},{6,198},{7,55},{8,200... | collective-permute-start | bytes 1572872 | tf_op jit(solution)/shard_map/ppermute | solution.py:62
  150.0 8.4 %collective-permute-start.15 = (f32[2,128,512]{2,1,0:T(8,128)S(1)}, f32[2,128,512]{2,1,0:T(8,128)S(1)}, u32[]{:S(2)}, u32[]{:S(2)}) collective-permute-start(f32[2,128,512]{2,1,0:T(8,128)S(1)} %get-tuple-element.48), channel_id=1, source_target_pairs={{0,64},{1,17},{2,66},{3,19},{4,68},{5,21},{6,70},{7,23},{8,72},{9,... | collective-permute-start | bytes 1572872 | tf_op jit(solution)/shard_map/ppermute | solution.py:62
  156.8 9.0 %collective-permute-start.21 = (f32[1,128,512]{2,1,0:T(8,128)S(1)}, f32[1,128,512]{2,1,0:T(8,128)S(1)}, u32[]{:S(2)}, u32[]{:S(2)}) collective-permute-start(f32[1,128,512]{2,1,0:T(8,128)S(1)} %get-tuple-element.57), channel_id=1, source_target_pairs={{0,64},{1,17},{2,66},{3,19},{4,68},{5,21},{6,70},{7,23},{8,72},{9,... | collective-permute-start | bytes 786440 | tf_op jit(solution)/shard_map/ppermute | solution.py:62
  158.4 7.5 %collective-permute-start.16 = (f32[1,128,512]{2,1,0:T(8,128)S(1)}, f32[1,128,512]{2,1,0:T(8,128)S(1)}, u32[]{:S(2)}, u32[]{:S(2)}) collective-permute-start(f32[1,128,512]{2,1,0:T(8,128)S(1)} %get-tuple-element.50), channel_id=1, source_target_pairs={{0,192},{1,49},{2,194},{3,51},{4,196},{5,53},{6,198},{7,55},{8,200... | collective-permute-start | bytes 786440 | tf_op jit(solution)/shard_map/ppermute | solution.py:62
  158.8 16.2 %collective-permute-start.22 = (f32[128,512]{1,0:T(8,128)S(1)}, f32[128,512]{1,0:T(8,128)S(1)}, u32[]{:S(2)}, u32[]{:S(2)}) collective-permute-start(f32[128,512]{1,0:T(8,128)S(1)} %collective-permute-done.14.refs_0_), channel_id=1, source_target_pairs={{0,0},{1,10},{2,1},{3,11},{4,6},{5,12},{6,7},{7,13},{8,2},{9,8},{1... | collective-permute-start | bytes 786440 | tf_op jit(solution)/shard_map/ppermute | solution.py:62
  181.7 9.2 %collective-permute-start.25 = (f32[192,128]{1,0:T(8,128)S(1)}, f32[192,128]{1,0:T(8,128)S(1)}, u32[]{:S(2)}, u32[]{:S(2)}) collective-permute-start(f32[192,128]{1,0:T(8,128)S(1)} %add.10), channel_id=1, source_target_pairs={{0,6},{1,7},{2,4},{3,5},{4,2},{5,3},{6,0},{7,1},{8,14},{9,15},{10,... | collective-permute-start | bytes 294920 | tf_op jit(solution)/shard_map/ppermute | solution.py:62
  190.9 4.9 %collective-permute-start.26 = (f32[192,128]{1,0:T(8,128)S(1)}, f32[192,128]{1,0:T(8,128)S(1)}, u32[]{:S(2)}, u32[]{:S(2)}) collective-permute-start(f32[192,128]{1,0:T(8,128)S(1)} %add.11.first), channel_id=1, source_target_pairs={{0,14},{1,15},{2,12},{3,13},{4,10},{5,11},{6,8},{7,9},{8,6},{9,7},... | collective-permute-start | bytes 294920 | tf_op jit(solution)/shard_map/ppermute | solution.py:62
  (18 other events, 116.9 us)
Sparse Core Ops, SparseCore 0:
  10.4 49.2 all-gather.2

commit v5 on v4

--- a/solution.py
+++ b/solution.py
@@ -78,7 +78,7 @@
     return mask
 
 
-def prep_kernel(pat_one, pat_two, fac_one, fac_two, par, one, two, pat, fac, par_in, sems):
+def prep_kernel(pat_one, pat_two, fac_one, fac_two, par, own, pat, fac, par_in, sems):
     row, col = lax.axis_index("prow"), lax.axis_index("pcol")
     copies = [
         pltpu.make_async_copy(pat_one, pat.at[0], sems.at[0]),
@@ -91,31 +91,31 @@
         copy.start()
     lanes = lax.broadcasted_iota(jnp.int32, (1, 64), 1)
 
-    def turn(level, out):
+    def turn(level, top):
         for i in range(4):
             cut = pl.ds(B * i, B)
             flags = jnp.where(lanes == 4 * row + i, pat[level, pl.ds(col, 1), :], 0)
             weight = jnp.sum(flags.astype(jnp.float32), axis=1, keepdims=True)
-            out[0:128, cut] = fac[level, cut, :].T * weight
+            own[top : top + 128, cut] = fac[level, cut, :].T * weight
 
     copies[0].wait()
     copies[1].wait()
-    turn(0, one)
+    turn(0, 0)
     copies[2].wait()
     turned = par_in[...].T
     for i in range(4):
-        one[128:160, B * i : B * i + B] = turned[32 * i : 32 * i + 32, :]
+        own[128:160, B * i : B * i + B] = turned[32 * i : 32 * i + 32, :]
     copies[3].wait()
     copies[4].wait()
-    turn(1, two)
+    turn(1, 160)
 
 
 def prepare(pat_one, pat_two, fac_one, fac_two, par):
     return pl.pallas_call(
         prep_kernel,
-        out_shape=[f32(160, KA), f32(B, KA)],
+        out_shape=f32(288, KA),
         in_specs=[HBM] * 5,
-        out_specs=[VMEM] * 2,
+        out_specs=VMEM,
         scratch_shapes=[
             pltpu.VMEM((2, N, 64), jnp.int32),
             pltpu.VMEM((2, KA, B), jnp.float32),
@@ -126,8 +126,19 @@
     )(pat_one, pat_two, fac_one, fac_two, par)
 
 
-def pair_up(own):
-    return jnp.stack([own, swap(own)])
+def pair_up(own, other):
+    def body(a, b, one, two):
+        for i, ref in enumerate((a, b)):
+            one[i] = ref[0:160, :]
+            two[i] = ref[160:288, :]
+
+    return pl.pallas_call(
+        body,
+        out_shape=[f32(2, 160, KA), f32(2, B, KA)],
+        in_specs=[VMEM] * 2,
+        out_specs=[VMEM] * 2,
+        compiler_params=pltpu.CompilerParams(vmem_limit_bytes=4 * MIB),
+    )(own, other)
 
 
 def gather(pair):
@@ -171,42 +182,86 @@
     return copies
 
 
-def one_kernel(parent, ginv, *refs):
+def assemble(left, level, row, core, variant, half, fix=None):
+    rows = pl.ds(64 * variant, 64)
+    for slot in range(8):
+        dest = destination(row, core, variant, slot + 8 * half)
+        value = level[dest, rows, :]
+        if fix is not None:
+            value = value - fix[dest, rows, :]
+        left[64 * slot : 64 * slot + 64, :] = value
+
+
+def send_kernel(second, ginv, *refs):
+    refs = list(refs)
+    fix = refs.pop(0) if second else None
+    lower = refs.pop(0) if second else None
+    parent = refs.pop(0) if second else None
     blocks, refs = refs[:9], refs[9:]
-    sends, keeps, one, turn, left, sems = (
-        refs[0:2], refs[2:4], refs[4], refs[5], refs[6], refs[7],
-    )
+    sends, level = refs[0:2], refs[2]
+    left, sems = refs[-2:]
     row, col, core, target = place()
-    copies = fetch(blocks, one, sems)
+    copies = fetch(blocks, level, sems)
     for copy in copies:
         copy.start()
-    high, low = split(ginv[...])
+    ginv = split(ginv[...])
     for copy in copies:
         copy.wait()
-    turn[0:128, :] = one[parent[target], 0:128, :]
-    turn[128:256, :] = one[target, 0:128, :]
     for variant in range(2):
-        for half in (1, 0):
-            for slot in range(8):
-                dest = destination(row, core, variant, slot + 8 * half)
-                left[64 * slot : 64 * slot + 64, :] = one[dest, 64 * variant : 64 * variant + 64, :]
-            value = dot_split(split(left[...]), (high, low), ((1,), (0,)))
-            out = sends[variant] if half else keeps[variant]
-            out[...] = -value.reshape(8, 64, KA)
-
-
-def first_level(parent, ginv, blocks):
-    return pl.pallas_call(
-        one_kernel,
-        out_shape=[f32(8, 64, KA)] * 4 + [f32(16, 160, KA), f32(256, KA)],
-        in_specs=[SMEM, VMEM] + [ANY] * 9,
-        out_specs=[VMEM] * 6,
+        assemble(left, level, row, core, variant, 1, fix)
+        value = dot_split(split(left[...]), ginv, ((1,), (0,)))
+        sends[variant][...] = -value.reshape(8, 64, KA)
+    if second:
+        turn = refs[3]
+        turn[0:128, :] = lower[parent[target], 0:128, :]
+        turn[128:256, :] = lower[target, 0:128, :]
+        turn[256:384, :] = level[target]
+
+
+def send_half(second, ginv, blocks, extra):
+    def body(*refs):
+        send_kernel(second, *refs)
+
+    rows = B if second else 160
+    shapes = [f32(8, 64, KA)] * 2 + [f32(16, rows, KA)] + ([f32(384, KA)] if second else [])
+    return pl.pallas_call(
+        body,
+        out_shape=shapes,
+        in_specs=[VMEM] + ([VMEM, VMEM, SMEM] if second else []) + [ANY] * 9,
+        out_specs=[VMEM] * len(shapes),
         scratch_shapes=[pltpu.VMEM((512, KA), jnp.float32), pltpu.SemaphoreType.DMA((16,))],
+        compiler_params=pltpu.CompilerParams(vmem_limit_bytes=8 * MIB),
+        cost_estimate=pl.CostEstimate(
+            flops=2_000_000_000, bytes_accessed=1_000_000, transcendentals=0
+        ),
+    )(ginv, *extra, *blocks)
+
+
+def keep_kernel(ginv, fix, one, two, outs, left):
+    row, col, core, target = place()
+    ginv = split(ginv[...])
+    for variant in range(2):
+        for at, level in enumerate((one, two)):
+            assemble(left, level, row, core, variant, 0, fix if at else None)
+            value = dot_split(split(left[...]), ginv, ((1,), (0,)))
+            outs[variant][:, 64 * at : 64 * at + 64, :] = -value.reshape(8, 64, KA)
+
+
+def keep_half(ginv, fix, one, two, order):
+    def body(ginv, fix, one, two, *refs):
+        keep_kernel(ginv, fix, one, two, refs[len(order) : -1], refs[-1])
+
+    return pl.pallas_call(
+        body,
+        out_shape=[f32(8, B, KA)] * 2,
+        in_specs=[VMEM] * 4 + [ANY] * len(order),
+        out_specs=[VMEM] * 2,
+        scratch_shapes=[pltpu.VMEM((512, KA), jnp.float32)],
         compiler_params=pltpu.CompilerParams(vmem_limit_bytes=8 * MIB),
         cost_estimate=pl.CostEstimate(
             flops=4_000_000_000, bytes_accessed=1_000_000, transcendentals=0
         ),
-    )(parent, ginv, *blocks)
+    )(ginv, fix, one, two, *order)
 
 
 def fix_kernel(parent, one, dinv_one, dinv_two, fix, par_out, base, dinv, sems):
@@ -223,12 +278,9 @@
     for copy in copies:
         copy.start()
 
-    def correct(m, carry):
+    for m in range(16):
         par = unpack(one[m, 128:160, :])
         fix[m] = dot_split(split(par), split(one[parent[m], 0:128, :]), ((1,), (0,)))
-        return carry
-
-    lax.fori_loop(0, 16, correct, 0)
     par_out[...] = unpack(one[row, 128:160, :])
     for copy in copies:
         copy.wait()
@@ -256,58 +308,28 @@
     )(parent, one, dinv_one, dinv_two)
 
 
-def two_kernel(half, ginv, fix, two, outs, left):
-    row, col, core, target = place()
-    ginv = split(ginv[...])
-    if half:
-        outs[2][...] = two[target]
-    for variant in range(2):
-        for slot in range(8):
-            dest = destination(row, core, variant, slot + 8 * half)
-            rows = pl.ds(64 * variant, 64)
-            left[64 * slot : 64 * slot + 64, :] = two[dest, rows, :] - fix[dest, rows, :]
-        value = dot_split(split(left[...]), ginv, ((1,), (0,)))
-        outs[variant][...] = -value.reshape(8, 64, KA)
-
-
-def second_level(half, ginv, fix, gathered, order):
-    def body(ginv, fix, two, *refs):
-        two_kernel(half, ginv, fix, two, refs[len(order) : -1], refs[-1])
-
-    return pl.pallas_call(
-        body,
-        out_shape=[f32(8, 64, KA)] * 2 + ([f32(128, KA)] if half else []),
-        in_specs=[VMEM] * 3 + [ANY] * len(order),
-        out_specs=[VMEM] * (2 + half),
-        scratch_shapes=[pltpu.VMEM((512, KA), jnp.float32)],
-        compiler_params=pltpu.CompilerParams(vmem_limit_bytes=8 * MIB),
-        cost_estimate=pl.CostEstimate(
-            flops=1_500_000_000, bytes_accessed=8_000_000, transcendentals=0
-        ),
-    )(ginv, fix, gathered, *order)
-
-
-def merge(part, keep_one, got_one, keep_two, got_two):
-    def body(a, b, c, d, out):
+def merge(part, keep, got_one, got_two, order):
+    def body(a, b, c, *refs):
+        out = refs[-1]
         for i in range(4):
-            out[i, 0:64, :] = a[4 * part + i] + b[4 * part + i]
-            out[i, 64:128, :] = c[4 * part + i] + d[4 * part + i]
+            out[i, 0:64, :] = a[4 * part + i, 0:64, :] + b[4 * part + i]
+            out[i, 64:128, :] = a[4 * part + i, 64:128, :] + c[4 * part + i]
 
     return pl.pallas_call(
         body,
         out_shape=f32(4, B, KA),
-        in_specs=[VMEM] * 4,
+        in_specs=[VMEM] * 3 + [ANY] * len(order),
         out_specs=VMEM,
         compiler_params=pltpu.CompilerParams(vmem_limit_bytes=4 * MIB),
-        cost_estimate=pl.CostEstimate(flops=300_000, bytes_accessed=3_000_000, transcendentals=0),
-    )(keep_one, got_one, keep_two, got_two)
+        cost_estimate=pl.CostEstimate(flops=300_000, bytes_accessed=1_000_000, transcendentals=0),
+    )(keep, got_one, got_two, *order)
 
 
 def row_step(value, variant, step):
     return permute(value, lambda r, c: (r ^ MASKS[c % 2][variant][step], c))
 
 
-def block_kernel(a_ref, b_ref, turn_one, turn_two, one_out, two_out, send_out, keep_out, sums):
+def block_kernel(a_ref, b_ref, turn, one_out, two_out, send_out, keep_out, sums):
     core = lax.rem(lax.axis_index("pcol"), 2)
     for variant, ref in enumerate((a_ref, b_ref)):
         one_out[64 * variant : 64 * variant + 64, :] = ref[0:64, :]
@@ -316,7 +338,7 @@
     two = split(two_out[...])
     nt = ((1,), (1,))
     for i, (left, right) in enumerate(
-        ((one, turn_one[128:256, :]), (two, turn_one[0:128, :]), (two, turn_two[...]))
+        ((one, turn[128:256, :]), (two, turn[0:128, :]), (two, turn[256:384, :]))
     ):
         value = dot_split(left, split(right), nt)
         sums[0, 64 * i : 64 * i + 64, :] = value[0:64]
@@ -325,15 +347,15 @@
     send_out[...] = sums[1 - core]
 
 
-def blocks_of(parts, turn_one, turn_two):
+def blocks_of(parts, turn):
     return pl.pallas_call(
         block_kernel,
         out_shape=[f32(B, KA), f32(B, KA), f32(192, B), f32(192, B)],
-        in_specs=[VMEM] * 4,
+        in_specs=[VMEM] * 3,
         out_specs=[VMEM] * 4,
         scratch_shapes=[pltpu.VMEM((2, 192, B), jnp.float32)],
         compiler_params=pltpu.CompilerParams(vmem_limit_bytes=8 * MIB),
-    )(*parts, turn_one, turn_two)
+    )(*parts, turn)
 
 
 def add(kept, got, order):
@@ -415,37 +437,29 @@
     parent,
     dinv_two,
 ):
-    own_one, own_two = prepare(pattern_one.T, pattern_two.T, factor_one, factor_two, factor_parent)
-    gathered = lax.all_gather(own_two, "pcol", axis=0, tiled=False)
-    blocks_one = gather(pair_up(own_one))
-    s1a, s1b, k1a, k1b, one, turn_one = first_level(parent, ginv_anc, blocks_one)
+    own = prepare(pattern_one.T, pattern_two.T, factor_one, factor_two, factor_parent)
+    pair_one, pair_two = pair_up(own, swap(own))
+    blocks_one = gather(pair_one)
+    blocks_two = gather(pair_two)
+    s1a, s1b, one = send_half(0, ginv_anc, blocks_one, [])
     fix, par, base = corrections(parent, one, dinv_one, dinv_two)
-
-    def spread(value):
-        return permute(value, lambda r, c: (r ^ spread_mask(c), c))
-
-    def settle(value):
-        return permute(value, lambda r, c: (r, r ^ spread_mask(c)))
-
-    turn_one = spread(turn_one)
     r1a, r1b = row_step(s1a, 0, 0), row_step(s1b, 1, 0)
-    s2a, s2b, turn_two = second_level(1, ginv_anc, fix, gathered, [r1a, r1b])
-    k2a, k2b = second_level(0, ginv_anc, fix, gathered, [turn_one])
-    turn_one = settle(turn_one)
-    turn_two = spread(turn_two)
+    s2a, s2b, two, turn = send_half(1, ginv_anc, blocks_two, [fix, one, parent])
     r2a, r2b = row_step(s2a, 0, 0), row_step(s2b, 1, 0)
-    going = [merge(1, k1a, r1a, k2a, r2a), merge(1, k1b, r1b, k2b, r2b)]
-    kept = [merge(0, k1a, r1a, k2a, r2a), merge(0, k1b, r1b, k2b, r2b)]
+    turn = permute(turn, lambda r, c: (r ^ spread_mask(c), c))
+    keep_a, keep_b = keep_half(ginv_anc, fix, one, two, [r1a, r1b, turn])
+    going = [merge(1, keep_a, r1a, r2a, []), merge(1, keep_b, r1b, r2b, [])]
+    kept = [merge(0, keep_a, r1a, r2a, []), merge(0, keep_b, r1b, r2b, [])]
+    turn = permute(turn, lambda r, c: (r, r ^ spread_mask(c)))
     got = [row_step(going[v], v, 1) for v in range(2)]
-    kept[0], first = add(kept[0], got[0], [turn_two])
+    kept[0], first = add(kept[0], got[0], [])
     kept[1], second = add(kept[1], got[1], [])
-    turn_two = settle(turn_two)
     got = [row_step(first, 0, 2), row_step(second, 1, 2)]
     kept[0], first = add(kept[0], got[0], [])
-    kept[1], second = add(kept[1], got[1], [turn_one])
+    kept[1], second = add(kept[1], got[1], [turn])
     got = [row_step(first, 0, 3), row_step(second, 1, 3)]
     kept = [add(kept[0], got[0], [])[0], add(kept[1], got[1], [])[0]]
-    anc_one, anc_two, send, keep = blocks_of(kept, turn_one, turn_two)
+    anc_one, anc_two, send, keep = blocks_of(kept, turn)
     sums = keep + swap(send)
     for mask in (2, 6):
         sums = sums + permute(sums, lambda r, c: (r, c ^ mask))

time: 210 us -> 177 us (0.84)
  between operations: 14.3 us -> 0.91 us
  local copies, waits for them, and re-layouts: 10.5 us -> 2.34 us
  starting transfers between devices: 64.7 us -> 58.4 us
    unnamed x26 -> x12, local copies, waits for them, and re-layouts: 10.5 us -> 2.3 us
    ppermute x28 -> x34, starting transfers between devices: 64.6 us -> 58.4 us  [permute(): return lax.ppermute(value, ALL, pairs)]
    pallas_call x1, Pallas kernels: 5.3 us -> 2.9 us  [corrections(): pl.pallas_call(fix_kernel, out_shape=[f32(16, B, KA), f32(B, B), f32(192,...]
    ppermute x28 -> x34, waiting for transfers between devices: 97.6 us -> 96.2 us  [permute(): return lax.ppermute(value, ALL, pairs)]
    pallas_call x8 -> x9, Pallas kernels: 12.5 us -> 13.3 us  [the longest x2 7.11 us: send_half(): pl.pallas_call(body, out_shape=shapes, in_specs=[VMEM] + ([VMEM, VMEM, SM...]
  transfers between devices with their start and end apart: 29 -> 34, of which waited for: 20 -> 18; matrix products, arithmetic and copies ran while one was open for 1% -> 0% of each run, Pallas kernels for 7% -> 8%
where the time goes in v5:
time: 177 us; the launch traced here: 176 us
  waiting for transfers between devices  96.2 us (54%)
  starting transfers between devices  58.4 us (33%)
  Pallas kernels  18.6 us (11%)
  local copies, waits for them, and re-layouts  2.34 us (1%)
    ppermute x34, waiting for transfers between devices, permute(): return lax.ppermute(value, ALL, pairs)  96.2 us
    ppermute x34, starting transfers between devices, permute(): return lax.ppermute(value, ALL, pairs)  58.4 us
    pallas_call x2, Pallas kernels, send_half(): pl.pallas_call(body, out_shape=shapes, in_specs=[VMEM] + ([VMEM, VMEM, SM...  7.11 us
  transfers between devices with their start and end apart: 34, of which 18 were waited for; matrix products, arithmetic and copies ran while one was open for 0% of the time, Pallas kernels for 8%

profile of v5, /device:TPU:7, one launch (start us, length us, event | category | flops | bytes accessed | tf_op | source)
XLA Modules:
  0.0 176.5 jit_solution(14766919321852808175)
XLA Ops:
  6.7 5.7 %collective-permute-start.1 = (f32[2,160,512]{2,1,0:T(8,128)S(1)}, f32[2,160,512]{2,1,0:T(8,128)S(1)}, u32[]{:S(2)}, u32[]{:S(2)}) collective-permute-start(f32[2,160,512]{2,1,0:T(8,128)S(1)} %get-tuple-element.34.refs_1_), channel_id=1, source_target_pairs={{0,2},{1,15},{2,4},{3,1},{4,6},{5,3},{6,8},{7,5},{8,10},{9,7},{10,... | collective-permute-start | bytes 1966088 | tf_op jit(solution)/shard_map/ppermute | solution.py:62
  12.3 7.5 %collective-permute-done.1.refs_2_ = f32[2,160,512]{2,1,0:T(8,128)S(1)} collective-permute-done((f32[2,160,512]{2,1,0:T(8,128)S(1)}, f32[2,160,512]{2,1,0:T(8,128)S(1)}, u32[]{:S(2)}, u32[]{:S(2)}) %collective-permute-start.1) | collective-permute-done | bytes 655392 | tf_op jit(solution)/shard_map/ppermute | solution.py:62
  19.8 3.1 %collective-permute-start.3 = (f32[2,160,512]{2,1,0:T(8,128)S(1)}, f32[2,160,512]{2,1,0:T(8,128)S(1)}, u32[]{:S(2)}, u32[]{:S(2)}) collective-permute-start(f32[2,160,512]{2,1,0:T(8,128)S(1)} %collective-permute-done.1.refs_2_), channel_id=1, source_target_pairs={{0,2},{1,15},{2,4},{3,1},{4,6},{5,3},{6,8},{7,5},{8,10},{9,7},{10,... | collective-permute-start | bytes 1966088 | tf_op jit(solution)/shard_map/ppermute | solution.py:62
  23.1 13.1 %collective-permute-done.9.refs_5_ = f32[2,128,512]{2,1,0:T(8,128)S(1)} collective-permute-done((f32[2,128,512]{2,1,0:T(8,128)S(1)}, f32[2,128,512]{2,1,0:T(8,128)S(1)}, u32[]{:S(2)}, u32[]{:S(2)}) %collective-permute-start.9) | collective-permute-done | bytes 524320 | tf_op jit(solution)/shard_map/ppermute | solution.py:62
  36.1 3.1 %collective-permute-start.11 = (f32[2,128,512]{2,1,0:T(8,128)S(1)}, f32[2,128,512]{2,1,0:T(8,128)S(1)}, u32[]{:S(2)}, u32[]{:S(2)}) collective-permute-start(f32[2,128,512]{2,1,0:T(8,128)S(1)} %collective-permute-done.9.refs_5_), channel_id=1, source_target_pairs={{0,2},{1,15},{2,4},{3,1},{4,6},{5,3},{6,8},{7,5},{8,10},{9,7},{10,... | collective-permute-start | bytes 1572872 | tf_op jit(solution)/shard_map/ppermute | solution.py:62
  39.3 6.1 %collective-permute-done.11.refs_7_ = f32[2,128,512]{2,1,0:T(8,128)S(1)} collective-permute-done((f32[2,128,512]{2,1,0:T(8,128)S(1)}, f32[2,128,512]{2,1,0:T(8,128)S(1)}, u32[]{:S(2)}, u32[]{:S(2)}) %collective-permute-start.11) | collective-permute-done | bytes 524320 | tf_op jit(solution)/shard_map/ppermute | solution.py:62
  52.4 3.2 %collective-permute-start.7 = (f32[1,160,512]{2,1,0:T(8,128)S(1)}, f32[1,160,512]{2,1,0:T(8,128)S(1)}, u32[]{:S(2)}, u32[]{:S(2)}) collective-permute-start(f32[1,160,512]{2,1,0:T(8,128)S(1)} %slice.8), channel_id=1, source_target_pairs={{0,2},{1,15},{2,4},{3,1},{4,6},{5,3},{6,8},{7,5},{8,10},{9,7},{10,... | collective-permute-start | bytes 983048 | tf_op jit(solution)/shard_map/ppermute | solution.py:62
  58.0 4.0 %collective-permute-start.10 = (f32[2,128,512]{2,1,0:T(8,128)S(1)}, f32[2,128,512]{2,1,0:T(8,128)S(1)}, u32[]{:S(2)}, u32[]{:S(2)}) collective-permute-start(f32[2,128,512]{2,1,0:T(8,128)S(1)} %collective-permute-done.9.refs_5_), channel_id=1, source_target_pairs={{0,1},{1,0},{2,3},{3,2},{4,5},{5,4},{6,7},{7,6},{8,9},{9,8},{10,11... | collective-permute-start | bytes 1572872 | tf_op jit(solution)/shard_map/ppermute | solution.py:62
  62.0 3.5 %collective-permute-start.8 = (f32[1,160,512]{2,1,0:T(8,128)S(1)}, f32[1,160,512]{2,1,0:T(8,128)S(1)}, u32[]{:S(2)}, u32[]{:S(2)}) collective-permute-start(f32[1,160,512]{2,1,0:T(8,128)S(1)} %collective-permute-done.7.refs_8_), channel_id=1, source_target_pairs={{0,1},{1,0},{2,3},{3,2},{4,5},{5,4},{6,7},{7,6},{8,9},{9,8},{10,11... | collective-permute-start | bytes 983048 | tf_op jit(solution)/shard_map/ppermute | solution.py:62
  65.6 5.5 %collective-permute-done.15.refs_11_ = f32[1,128,512]{2,1,0:T(8,128)S(1)} collective-permute-done((f32[1,128,512]{2,1,0:T(8,128)S(1)}, f32[1,128,512]{2,1,0:T(8,128)S(1)}, u32[]{:S(2)}, u32[]{:S(2)}) %collective-permute-start.15) | collective-permute-done | bytes 262176 | tf_op jit(solution)/shard_map/ppermute | solution.py:62
  74.9 4.0 %shard_map.130 = (f32[8,64,512]{2,1,0:T(8,128)S(1)}, f32[8,64,512]{2,1,0:T(8,128)S(1)}, f32[16,160,512]{2,1,0:T(8,128)S(1)}) custom-call(f32[512,512]{1,0:T(8,128)S(1)} %copy-done, f32[2,160,512]{2,1,0:T(8,128)S(1)} %get-tuple-element.34.refs_1_, f32[2,160,512]{2,1,0:T(8,128)S(1)} %collective-permute-done.1.refs_2_, ...), custom_call_target="tpu_custom_call" | custom-call | flops 2000000000 | bytes 1000000 | tf_op jit(solution)/shard_map/pallas_call | solution.py:227
  85.2 3.1 %shard_map.132 = (f32[8,64,512]{2,1,0:T(8,128)S(1)}, f32[8,64,512]{2,1,0:T(8,128)S(1)}, f32[16,128,512]{2,1,0:T(8,128)S(1)}, f32[384,512]{1,0:T(8,128)S(1)}) custom-call(f32[512,512]{1,0:T(8,128)S(1)} %copy-done.1, f32[16,128,512]{2,1,0:T(8,128)S(1)} %get-tuple-element.36.refs_1_.fix, f32[16,160,512]{2,1,0:T(8,128)S(1)} %get-tuple-element.35.one.refs_2_, ...), custom_call_target="tpu_custom_call" | custom-call | flops 2000000000 | bytes 1000000 | tf_op jit(solution)/shard_map/pallas_call | solution.py:227
  88.3 3.5 %collective-permute-start.19 = (f32[384,512]{1,0:T(8,128)S(1)}, f32[384,512]{1,0:T(8,128)S(1)}, u32[]{:S(2)}, u32[]{:S(2)}) collective-permute-start(f32[384,512]{1,0:T(8,128)S(1)} %get-tuple-element.41), channel_id=1, source_target_pairs={{0,0},{1,161},{2,18},{3,179},{4,100},{5,197},{6,118},{7,215},{8,40... | collective-permute-start | bytes 2359304 | tf_op jit(solution)/shard_map/ppermute | solution.py:62
  94.4 19.0 %collective-permute-done.19.refs_2_ = f32[384,512]{1,0:T(8,128)S(1)} collective-permute-done((f32[384,512]{1,0:T(8,128)S(1)}, f32[384,512]{1,0:T(8,128)S(1)}, u32[]{:S(2)}, u32[]{:S(2)}) %collective-permute-start.19) | collective-permute-done | bytes 786464 | tf_op jit(solution)/shard_map/ppermute | solution.py:62
  113.5 3.4 %shard_map.133 = (f32[8,128,512]{2,1,0:T(8,128)S(1)}, f32[8,128,512]{2,1,0:T(8,128)S(1)}) custom-call(f32[512,512]{1,0:T(8,128)S(1)} %copy-done.1, f32[16,128,512]{2,1,0:T(8,128)S(1)} %get-tuple-element.36.refs_1_.fix, f32[16,160,512]{2,1,0:T(8,128)S(1)} %get-tuple-element.35.one.refs_2_, f32[16,128,512]{2,1,0:T(8,128)S(1)} %get-tuple-element.38.two, ...), custom_call_target="tpu_custom_call" | custom-call | flops 4000000000 | bytes 1000000 | tf_op jit(solution)/shard_map/pallas_call | solution.py:254
  118.3 3.9 %collective-permute-start.27 = (f32[384,512]{1,0:T(8,128)S(1)}, f32[384,512]{1,0:T(8,128)S(1)}, u32[]{:S(2)}, u32[]{:S(2)}) collective-permute-start(f32[384,512]{1,0:T(8,128)S(1)} %collective-permute-done.19.refs_2_), channel_id=1, source_target_pairs={{0,0},{1,10},{2,1},{3,11},{4,6},{5,12},{6,7},{7,13},{8,2},{9,8},{1... | collective-permute-start | bytes 2359304 | tf_op jit(solution)/shard_map/ppermute | solution.py:62
  122.3 9.9 %collective-permute-done.21.b = f32[4,128,512]{2,1,0:T(8,128)S(1)} collective-permute-done((f32[4,128,512]{2,1,0:T(8,128)S(1)}, f32[4,128,512]{2,1,0:T(8,128)S(1)}, u32[]{:S(2)}, u32[]{:S(2)}) %collective-permute-start.21) | collective-permute-done | bytes 1048608 | tf_op jit(solution)/shard_map/ppermute | solution.py:62
  133.9 6.9 %collective-permute-done.22.b = f32[2,128,512]{2,1,0:T(8,128)S(1)} collective-permute-done((f32[2,128,512]{2,1,0:T(8,128)S(1)}, f32[2,128,512]{2,1,0:T(8,128)S(1)}, u32[]{:S(2)}, u32[]{:S(2)}) %collective-permute-start.22) | collective-permute-done | bytes 524320 | tf_op jit(solution)/shard_map/ppermute | solution.py:62
  143.7 3.7 %collective-permute-done.23.b = f32[1,128,512]{2,1,0:T(8,128)S(1)} collective-permute-done((f32[1,128,512]{2,1,0:T(8,128)S(1)}, f32[1,128,512]{2,1,0:T(8,128)S(1)}, u32[]{:S(2)}, u32[]{:S(2)}) %collective-permute-start.23) | collective-permute-done | bytes 262176 | tf_op jit(solution)/shard_map/ppermute | solution.py:62
  149.0 5.8 %collective-permute-start.29 = (f32[192,128]{1,0:T(8,128)S(1)}, f32[192,128]{1,0:T(8,128)S(1)}, u32[]{:S(2)}, u32[]{:S(2)}) collective-permute-start(f32[192,128]{1,0:T(8,128)S(1)} %get-tuple-element.58), channel_id=1, source_target_pairs={{0,1},{1,0},{2,3},{3,2},{4,5},{5,4},{6,7},{7,6},{8,9},{9,8},{10,11... | collective-permute-start | bytes 294920 | tf_op jit(solution)/shard_map/ppermute | solution.py:62
  155.9 4.0 %collective-permute-done.30 = f32[192,128]{1,0:T(8,128)S(1)} collective-permute-done((f32[192,128]{1,0:T(8,128)S(1)}, f32[192,128]{1,0:T(8,128)S(1)}, u32[]{:S(2)}, u32[]{:S(2)}) %collective-permute-start.30) | collective-permute-done | bytes 98336 | tf_op jit(solution)/shard_map/ppermute | solution.py:62
  160.0 5.4 %collective-permute-done.31 = f32[192,128]{1,0:T(8,128)S(1)} collective-permute-done((f32[192,128]{1,0:T(8,128)S(1)}, f32[192,128]{1,0:T(8,128)S(1)}, u32[]{:S(2)}, u32[]{:S(2)}) %collective-permute-start.31) | collective-permute-done | bytes 98336 | tf_op jit(solution)/shard_map/ppermute | solution.py:62
  165.5 4.8 %collective-permute-done.32.second = f32[192,128]{1,0:T(8,128)S(1)} collective-permute-done((f32[192,128]{1,0:T(8,128)S(1)}, f32[192,128]{1,0:T(8,128)S(1)}, u32[]{:S(2)}, u32[]{:S(2)}) %collective-permute-start.32) | collective-permute-done | bytes 98336 | tf_op jit(solution)/shard_map/ppermute | solution.py:62
  170.5 4.3 %collective-permute-start.33 = (f32[192,128]{1,0:T(8,128)S(1)}, f32[192,128]{1,0:T(8,128)S(1)}, u32[]{:S(2)}, u32[]{:S(2)}) collective-permute-start(f32[192,128]{1,0:T(8,128)S(1)} %shard_map.145.own), channel_id=1, source_target_pairs={{0,1},{1,0},{2,3},{3,2},{4,5},{5,4},{6,7},{7,6},{8,9},{9,8},{10,11... | collective-permute-start | bytes 294920 | tf_op jit(solution)/shard_map/ppermute | solution.py:62
  (80 shorter events, 39.1 us)
Async XLA Ops:
  6.7 13.2 %collective-permute-start.1 = (f32[2,160,512]{2,1,0:T(8,128)S(1)}, f32[2,160,512]{2,1,0:T(8,128)S(1)}, u32[]{:S(2)}, u32[]{:S(2)}) collective-permute-start(f32[2,160,512]{2,1,0:T(8,128)S(1)} %get-tuple-element.34.refs_1_), channel_id=1, source_target_pairs={{0,2},{1,15},{2,4},{3,1},{4,6},{5,3},{6,8},{7,5},{8,10},{9,7},{10,... | collective-permute-start | bytes 1966088 | tf_op jit(solution)/shard_map/ppermute | solution.py:62
  19.8 19.4 %collective-permute-start.3 = (f32[2,160,512]{2,1,0:T(8,128)S(1)}, f32[2,160,512]{2,1,0:T(8,128)S(1)}, u32[]{:S(2)}, u32[]{:S(2)}) collective-permute-start(f32[2,160,512]{2,1,0:T(8,128)S(1)} %collective-permute-done.1.refs_2_), channel_id=1, source_target_pairs={{0,2},{1,15},{2,4},{3,1},{4,6},{5,3},{6,8},{7,5},{8,10},{9,7},{10,... | collective-permute-start | bytes 1966088 | tf_op jit(solution)/shard_map/ppermute | solution.py:62
  23.0 13.1 %collective-permute-start.9 = (f32[2,128,512]{2,1,0:T(8,128)S(1)}, f32[2,128,512]{2,1,0:T(8,128)S(1)}, u32[]{:S(2)}, u32[]{:S(2)}) collective-permute-start(f32[2,128,512]{2,1,0:T(8,128)S(1)} %get-tuple-element.37.refs_4_), channel_id=1, source_target_pairs={{0,2},{1,15},{2,4},{3,1},{4,6},{5,3},{6,8},{7,5},{8,10},{9,7},{10,... | collective-permute-start | bytes 1572872 | tf_op jit(solution)/shard_map/ppermute | solution.py:62
  36.1 9.2 %collective-permute-start.11 = (f32[2,128,512]{2,1,0:T(8,128)S(1)}, f32[2,128,512]{2,1,0:T(8,128)S(1)}, u32[]{:S(2)}, u32[]{:S(2)}) collective-permute-start(f32[2,128,512]{2,1,0:T(8,128)S(1)} %collective-permute-done.9.refs_5_), channel_id=1, source_target_pairs={{0,2},{1,15},{2,4},{3,1},{4,6},{5,3},{6,8},{7,5},{8,10},{9,7},{10,... | collective-permute-start | bytes 1572872 | tf_op jit(solution)/shard_map/ppermute | solution.py:62
  39.2 13.1 %collective-permute-start.5 = (f32[2,160,512]{2,1,0:T(8,128)S(1)}, f32[2,160,512]{2,1,0:T(8,128)S(1)}, u32[]{:S(2)}, u32[]{:S(2)}) collective-permute-start(f32[2,160,512]{2,1,0:T(8,128)S(1)} %collective-permute-done.3.refs_4_), channel_id=1, source_target_pairs={{0,2},{1,15},{2,4},{3,1},{4,6},{5,3},{6,8},{7,5},{8,10},{9,7},{10,... | collective-permute-start | bytes 1966088 | tf_op jit(solution)/shard_map/ppermute | solution.py:62
  39.3 26.3 %collective-permute-start.2 = (f32[2,160,512]{2,1,0:T(8,128)S(1)}, f32[2,160,512]{2,1,0:T(8,128)S(1)}, u32[]{:S(2)}, u32[]{:S(2)}) collective-permute-start(f32[2,160,512]{2,1,0:T(8,128)S(1)} %collective-permute-done.1.refs_2_), channel_id=1, source_target_pairs={{0,1},{1,0},{2,3},{3,2},{4,5},{5,4},{6,7},{7,6},{8,9},{9,8},{10,11... | collective-permute-start | bytes 1966088 | tf_op jit(solution)/shard_map/ppermute | solution.py:62
  45.4 12.6 %collective-permute-start.13 = (f32[2,128,512]{2,1,0:T(8,128)S(1)}, f32[2,128,512]{2,1,0:T(8,128)S(1)}, u32[]{:S(2)}, u32[]{:S(2)}) collective-permute-start(f32[2,128,512]{2,1,0:T(8,128)S(1)} %collective-permute-done.11.refs_7_), channel_id=1, source_target_pairs={{0,2},{1,15},{2,4},{3,1},{4,6},{5,3},{6,8},{7,5},{8,10},{9,7},{10,... | collective-permute-start | bytes 1572872 | tf_op jit(solution)/shard_map/ppermute | solution.py:62
  48.5 24.7 %collective-permute-start.4 = (f32[2,160,512]{2,1,0:T(8,128)S(1)}, f32[2,160,512]{2,1,0:T(8,128)S(1)}, u32[]{:S(2)}, u32[]{:S(2)}) collective-permute-start(f32[2,160,512]{2,1,0:T(8,128)S(1)} %collective-permute-done.3.refs_4_), channel_id=1, source_target_pairs={{0,1},{1,0},{2,3},{3,2},{4,5},{5,4},{6,7},{7,6},{8,9},{9,8},{10,11... | collective-permute-start | bytes 1966088 | tf_op jit(solution)/shard_map/ppermute | solution.py:62
  52.4 9.6 %collective-permute-start.7 = (f32[1,160,512]{2,1,0:T(8,128)S(1)}, f32[1,160,512]{2,1,0:T(8,128)S(1)}, u32[]{:S(2)}, u32[]{:S(2)}) collective-permute-start(f32[1,160,512]{2,1,0:T(8,128)S(1)} %slice.8), channel_id=1, source_target_pairs={{0,2},{1,15},{2,4},{3,1},{4,6},{5,3},{6,8},{7,5},{8,10},{9,7},{10,... | collective-permute-start | bytes 983048 | tf_op jit(solution)/shard_map/ppermute | solution.py:62
  55.6 18.1 %collective-permute-start.6 = (f32[2,160,512]{2,1,0:T(8,128)S(1)}, f32[2,160,512]{2,1,0:T(8,128)S(1)}, u32[]{:S(2)}, u32[]{:S(2)}) collective-permute-start(f32[2,160,512]{2,1,0:T(8,128)S(1)} %collective-permute-done.5.refs_6_), channel_id=1, source_target_pairs={{0,1},{1,0},{2,3},{3,2},{4,5},{5,4},{6,7},{7,6},{8,9},{9,8},{10,11... | collective-permute-start | bytes 1966088 | tf_op jit(solution)/shard_map/ppermute | solution.py:62
  58.0 22.3 %collective-permute-start.10 = (f32[2,128,512]{2,1,0:T(8,128)S(1)}, f32[2,128,512]{2,1,0:T(8,128)S(1)}, u32[]{:S(2)}, u32[]{:S(2)}) collective-permute-start(f32[2,128,512]{2,1,0:T(8,128)S(1)} %collective-permute-done.9.refs_5_), channel_id=1, source_target_pairs={{0,1},{1,0},{2,3},{3,2},{4,5},{5,4},{6,7},{7,6},{8,9},{9,8},{10,11... | collective-permute-start | bytes 1572872 | tf_op jit(solution)/shard_map/ppermute | solution.py:62
  62.0 11.2 %collective-permute-start.8 = (f32[1,160,512]{2,1,0:T(8,128)S(1)}, f32[1,160,512]{2,1,0:T(8,128)S(1)}, u32[]{:S(2)}, u32[]{:S(2)}) collective-permute-start(f32[1,160,512]{2,1,0:T(8,128)S(1)} %collective-permute-done.7.refs_8_), channel_id=1, source_target_pairs={{0,1},{1,0},{2,3},{3,2},{4,5},{5,4},{6,7},{7,6},{8,9},{9,8},{10,11... | collective-permute-start | bytes 983048 | tf_op jit(solution)/shard_map/ppermute | solution.py:62
  71.1 14.0 %collective-permute-start.12 = (f32[2,128,512]{2,1,0:T(8,128)S(1)}, f32[2,128,512]{2,1,0:T(8,128)S(1)}, u32[]{:S(2)}, u32[]{:S(2)}) collective-permute-start(f32[2,128,512]{2,1,0:T(8,128)S(1)} %collective-permute-done.11.refs_7_), channel_id=1, source_target_pairs={{0,1},{1,0},{2,3},{3,2},{4,5},{5,4},{6,7},{7,6},{8,9},{9,8},{10,11... | collective-permute-start | bytes 1572872 | tf_op jit(solution)/shard_map/ppermute | solution.py:62
  73.2 12.0 %collective-permute-start.14 = (f32[2,128,512]{2,1,0:T(8,128)S(1)}, f32[2,128,512]{2,1,0:T(8,128)S(1)}, u32[]{:S(2)}, u32[]{:S(2)}) collective-permute-start(f32[2,128,512]{2,1,0:T(8,128)S(1)} %collective-permute-done.13.refs_9_), channel_id=1, source_target_pairs={{0,1},{1,0},{2,3},{3,2},{4,5},{5,4},{6,7},{7,6},{8,9},{9,8},{10,11... | collective-permute-start | bytes 1572872 | tf_op jit(solution)/shard_map/ppermute | solution.py:62
  73.2 11.9 %collective-permute-start.16 = (f32[1,128,512]{2,1,0:T(8,128)S(1)}, f32[1,128,512]{2,1,0:T(8,128)S(1)}, u32[]{:S(2)}, u32[]{:S(2)}) collective-permute-start(f32[1,128,512]{2,1,0:T(8,128)S(1)} %collective-permute-done.15.refs_11_), channel_id=1, source_target_pairs={{0,1},{1,0},{2,3},{3,2},{4,5},{5,4},{6,7},{7,6},{8,9},{9,8},{10,11... | collective-permute-start | bytes 786440 | tf_op jit(solution)/shard_map/ppermute | solution.py:62
  78.9 34.5 %collective-permute-start.17 = (f32[8,64,512]{2,1,0:T(8,128)S(1)}, f32[8,64,512]{2,1,0:T(8,128)S(1)}, u32[]{:S(2)}, u32[]{:S(2)}) collective-permute-start(f32[8,64,512]{2,1,0:T(8,128)S(1)} %get-tuple-element.39), channel_id=1, source_target_pairs={{0,16},{1,65},{2,18},{3,67},{4,20},{5,69},{6,22},{7,71},{8,24},{9,... | collective-permute-start | bytes 3145736 | tf_op jit(solution)/shard_map/ppermute | solution.py:62
  80.3 33.2 %collective-permute-start.18 = (f32[8,64,512]{2,1,0:T(8,128)S(1)}, f32[8,64,512]{2,1,0:T(8,128)S(1)}, u32[]{:S(2)}, u32[]{:S(2)}) collective-permute-start(f32[8,64,512]{2,1,0:T(8,128)S(1)} %get-tuple-element.40), channel_id=1, source_target_pairs={{0,48},{1,193},{2,50},{3,195},{4,52},{5,197},{6,54},{7,199},{8,56}... | collective-permute-start | bytes 3145736 | tf_op jit(solution)/shard_map/ppermute | solution.py:62
  88.3 25.1 %collective-permute-start.19 = (f32[384,512]{1,0:T(8,128)S(1)}, f32[384,512]{1,0:T(8,128)S(1)}, u32[]{:S(2)}, u32[]{:S(2)}) collective-permute-start(f32[384,512]{1,0:T(8,128)S(1)} %get-tuple-element.41), channel_id=1, source_target_pairs={{0,0},{1,161},{2,18},{3,179},{4,100},{5,197},{6,118},{7,215},{8,40... | collective-permute-start | bytes 2359304 | tf_op jit(solution)/shard_map/ppermute | solution.py:62
  91.8 25.1 %collective-permute-start.20 = (f32[8,64,512]{2,1,0:T(8,128)S(1)}, f32[8,64,512]{2,1,0:T(8,128)S(1)}, u32[]{:S(2)}, u32[]{:S(2)}) collective-permute-start(f32[8,64,512]{2,1,0:T(8,128)S(1)} %get-tuple-element.43), channel_id=1, source_target_pairs={{0,16},{1,65},{2,18},{3,67},{4,20},{5,69},{6,22},{7,71},{8,24},{9,... | collective-permute-start | bytes 3145736 | tf_op jit(solution)/shard_map/ppermute | solution.py:62
  92.5 25.4 %collective-permute-start.24 = (f32[8,64,512]{2,1,0:T(8,128)S(1)}, f32[8,64,512]{2,1,0:T(8,128)S(1)}, u32[]{:S(2)}, u32[]{:S(2)}) collective-permute-start(f32[8,64,512]{2,1,0:T(8,128)S(1)} %get-tuple-element.49), channel_id=1, source_target_pairs={{0,48},{1,193},{2,50},{3,195},{4,52},{5,197},{6,54},{7,199},{8,56}... | collective-permute-start | bytes 3145736 | tf_op jit(solution)/shard_map/ppermute | solution.py:62
  117.0 15.2 %collective-permute-start.21 = (f32[4,128,512]{2,1,0:T(8,128)S(1)}, f32[4,128,512]{2,1,0:T(8,128)S(1)}, u32[]{:S(2)}, u32[]{:S(2)}) collective-permute-start(f32[4,128,512]{2,1,0:T(8,128)S(1)} %shard_map.135), channel_id=1, source_target_pairs={{0,48},{1,193},{2,50},{3,195},{4,52},{5,197},{6,54},{7,199},{8,56}... | collective-permute-start | bytes 3145736 | tf_op jit(solution)/shard_map/ppermute | solution.py:62
  118.0 15.1 %collective-permute-start.25 = (f32[4,128,512]{2,1,0:T(8,128)S(1)}, f32[4,128,512]{2,1,0:T(8,128)S(1)}, u32[]{:S(2)}, u32[]{:S(2)}) collective-permute-start(f32[4,128,512]{2,1,0:T(8,128)S(1)} %shard_map.140), channel_id=1, source_target_pairs={{0,16},{1,65},{2,18},{3,67},{4,20},{5,69},{6,22},{7,71},{8,24},{9,... | collective-permute-start | bytes 3145736 | tf_op jit(solution)/shard_map/ppermute | solution.py:62
  118.3 22.6 %collective-permute-start.27 = (f32[384,512]{1,0:T(8,128)S(1)}, f32[384,512]{1,0:T(8,128)S(1)}, u32[]{:S(2)}, u32[]{:S(2)}) collective-permute-start(f32[384,512]{1,0:T(8,128)S(1)} %collective-permute-done.19.refs_2_), channel_id=1, source_target_pairs={{0,0},{1,10},{2,1},{3,11},{4,6},{5,12},{6,7},{7,13},{8,2},{9,8},{1... | collective-permute-start | bytes 2359304 | tf_op jit(solution)/shard_map/ppermute | solution.py:62
  133.3 9.3 %collective-permute-start.26 = (f32[2,128,512]{2,1,0:T(8,128)S(1)}, f32[2,128,512]{2,1,0:T(8,128)S(1)}, u32[]{:S(2)}, u32[]{:S(2)}) collective-permute-start(f32[2,128,512]{2,1,0:T(8,128)S(1)} %get-tuple-element.51), channel_id=1, source_target_pairs={{0,192},{1,49},{2,194},{3,51},{4,196},{5,53},{6,198},{7,55},{8,200... | collective-permute-start | bytes 1572872 | tf_op jit(solution)/shard_map/ppermute | solution.py:62
  (16 other events, 237.9 us)

commit v6 on v5

--- a/solution.py
+++ b/solution.py
@@ -127,16 +127,26 @@
 
 
 def pair_up(own, other):
-    def body(a, b, one, two):
+    def body(a, b, one, two, sems):
+        copies = []
         for i, ref in enumerate((a, b)):
-            one[i] = ref[0:160, :]
-            two[i] = ref[160:288, :]
+            copies.append(
+                pltpu.make_async_copy(ref.at[pl.ds(0, 160)], one.at[i], sems.at[2 * i])
+            )
+            copies.append(
+                pltpu.make_async_copy(ref.at[pl.ds(160, 128)], two.at[i], sems.at[2 * i + 1])
+            )
+        for copy in copies:
+            copy.start()
+        for copy in copies:
+            copy.wait()
 
     return pl.pallas_call(
         body,
         out_shape=[f32(2, 160, KA), f32(2, B, KA)],
-        in_specs=[VMEM] * 2,
+        in_specs=[HBM, ANY],
         out_specs=[VMEM] * 2,
+        scratch_shapes=[pltpu.SemaphoreType.DMA((4,))],
         compiler_params=pltpu.CompilerParams(vmem_limit_bytes=4 * MIB),
     )(own, other)
 
@@ -162,7 +172,7 @@
     return row, col, core, target
 
 
-def fetch(refs, target, sems):
+def fetch(refs, target, sems, first):
     col = lax.axis_index("pcol")
     z, core = lax.div(col, 2), lax.rem(col, 2)
     copies = []
@@ -176,96 +186,91 @@
             parity = side if i == 0 else 1 - side
             copies.append(
                 pltpu.make_async_copy(
-                    ref.at[i], target.at[plane * 2 + parity], sems.at[len(copies)]
+                    ref.at[i], target.at[plane * 2 + parity], sems.at[first + len(copies)]
                 )
             )
     return copies
 
 
-def assemble(left, level, row, core, variant, half, fix=None):
-    rows = pl.ds(64 * variant, 64)
-    for slot in range(8):
-        dest = destination(row, core, variant, slot + 8 * half)
-        value = level[dest, rows, :]
-        if fix is not None:
-            value = value - fix[dest, rows, :]
-        left[64 * slot : 64 * slot + 64, :] = value
-
-
-def send_kernel(second, ginv, *refs):
-    refs = list(refs)
-    fix = refs.pop(0) if second else None
-    lower = refs.pop(0) if second else None
-    parent = refs.pop(0) if second else None
-    blocks, refs = refs[:9], refs[9:]
-    sends, level = refs[0:2], refs[2]
-    left, sems = refs[-2:]
+def products(ginv, one, two, row, core, half, left, outs):
+    for variant in range(2):
+        rows = pl.ds(64 * variant, 64)
+        for at, level in enumerate((one, two)):
+            for slot in range(8):
+                dest = destination(row, core, variant, slot + 8 * half)
+                left[64 * slot : 64 * slot + 64, :] = level[dest, rows, :]
+            value = dot_split(split(left[...]), ginv, ((1,), (0,)))
+            outs[variant][:, 64 * at : 64 * at + 64, :] = -value.reshape(8, 64, KA)
+
+
+def send_kernel(parent, ginv, *refs):
+    first, second, refs = refs[:9], refs[9:18], refs[18:]
+    sends, one, two, turn, left, block, sems = refs[0:2], *refs[2:]
     row, col, core, target = place()
-    copies = fetch(blocks, level, sems)
-    for copy in copies:
+    load = pltpu.make_async_copy(ginv, block, sems.at[32])
+    low = fetch(first, one, sems, 0)
+    high = fetch(second, two, sems, 16)
+    for copy in low + [load] + high:
         copy.start()
-    ginv = split(ginv[...])
-    for copy in copies:
+    for copy in low:
         copy.wait()
-    for variant in range(2):
-        assemble(left, level, row, core, variant, 1, fix)
-        value = dot_split(split(left[...]), ginv, ((1,), (0,)))
-        sends[variant][...] = -value.reshape(8, 64, KA)
-    if second:
-        turn = refs[3]
-        turn[0:128, :] = lower[parent[target], 0:128, :]
-        turn[128:256, :] = lower[target, 0:128, :]
-        turn[256:384, :] = level[target]
-
-
-def send_half(second, ginv, blocks, extra):
-    def body(*refs):
-        send_kernel(second, *refs)
-
-    rows = B if second else 160
-    shapes = [f32(8, 64, KA)] * 2 + [f32(16, rows, KA)] + ([f32(384, KA)] if second else [])
-    return pl.pallas_call(
-        body,
-        out_shape=shapes,
-        in_specs=[VMEM] + ([VMEM, VMEM, SMEM] if second else []) + [ANY] * 9,
-        out_specs=[VMEM] * len(shapes),
-        scratch_shapes=[pltpu.VMEM((512, KA), jnp.float32), pltpu.SemaphoreType.DMA((16,))],
+    turn[0:128, :] = one[parent[target], 0:128, :]
+    turn[128:256, :] = one[target, 0:128, :]
+    for copy in high:
+        copy.wait()
+    turn[256:384, :] = two[target]
+    for m in range(16):
+        par = split(unpack(one[m, 128:160, :]))
+        two[m] = two[m] - dot_split(par, split(one[parent[m], 0:128, :]), ((1,), (0,)))
+    load.wait()
+    products(split(block[...]), one, two, row, core, 1, left, sends)
+
+
+def send_half(parent, ginv, first, second):
+    return pl.pallas_call(
+        send_kernel,
+        out_shape=[f32(8, B, KA)] * 2
+        + [f32(16, 160, KA), f32(16, B, KA), f32(384, KA)],
+        in_specs=[SMEM, HBM] + [ANY] * 18,
+        out_specs=[VMEM] * 5,
+        scratch_shapes=[
+            pltpu.VMEM((512, KA), jnp.float32),
+            pltpu.VMEM((512, KA), jnp.float32),
+            pltpu.SemaphoreType.DMA((33,)),
+        ],
         compiler_params=pltpu.CompilerParams(vmem_limit_bytes=8 * MIB),
         cost_estimate=pl.CostEstimate(
-            flops=2_000_000_000, bytes_accessed=1_000_000, transcendentals=0
+            flops=8_000_000_000, bytes_accessed=1_000_000, transcendentals=0
         ),
-    )(ginv, *extra, *blocks)
-
-
-def keep_kernel(ginv, fix, one, two, outs, left):
-    row, col, core, target = place()
-    ginv = split(ginv[...])
-    for variant in range(2):
-        for at, level in enumerate((one, two)):
-            assemble(left, level, row, core, variant, 0, fix if at else None)
-            value = dot_split(split(left[...]), ginv, ((1,), (0,)))
-            outs[variant][:, 64 * at : 64 * at + 64, :] = -value.reshape(8, 64, KA)
-
-
-def keep_half(ginv, fix, one, two, order):
-    def body(ginv, fix, one, two, *refs):
-        keep_kernel(ginv, fix, one, two, refs[len(order) : -1], refs[-1])
+    )(parent, ginv, *first, *second)
+
+
+def keep_half(parent, ginv, one, two, dinv_one, dinv_two, order):
+    def body(parent, ginv, one, two, dinv_one, dinv_two, *refs):
+        outs, refs = refs[len(order) : len(order) + 2], refs[len(order) + 2 :]
+        par_out, base, left, dinv, sems = refs
+        row, col, core, target = place()
+        base_parts(parent, one, dinv_one, dinv_two, par_out, base, dinv, sems, row, core)
+        products(split(ginv[...]), one, two, row, core, 0, left, outs)
 
     return pl.pallas_call(
         body,
-        out_shape=[f32(8, B, KA)] * 2,
-        in_specs=[VMEM] * 4 + [ANY] * len(order),
-        out_specs=[VMEM] * 2,
-        scratch_shapes=[pltpu.VMEM((512, KA), jnp.float32)],
+        out_shape=[f32(8, B, KA)] * 2 + [f32(B, B), f32(192, B)],
+        in_specs=[SMEM] + [VMEM] * 3 + [HBM] * 2 + [ANY] * len(order),
+        out_specs=[VMEM] * 4,
+        scratch_shapes=[
+            pltpu.VMEM((512, KA), jnp.float32),
+            pltpu.VMEM((3, B, B), jnp.float32),
+            pltpu.SemaphoreType.DMA((3,)),
+        ],
         compiler_params=pltpu.CompilerParams(vmem_limit_bytes=8 * MIB),
         cost_estimate=pl.CostEstimate(
             flops=4_000_000_000, bytes_accessed=1_000_000, transcendentals=0
         ),
-    )(ginv, fix, one, two, *order)
-
-
-def fix_kernel(parent, one, dinv_one, dinv_two, fix, par_out, base, dinv, sems):
-    row, col, core, target = place()
+    )(parent, ginv, one, two, dinv_one, dinv_two, *order)
+
+
+def base_parts(parent, one, dinv_one, dinv_two, par_out, base, dinv, sems, row, core):
     top = pl.multiple_of(core * 64, 64)
     sources = (
         dinv_one.at[pl.ds(pl.multiple_of(row * B, B), B)],
@@ -277,10 +282,6 @@
     ]
     for copy in copies:
         copy.start()
-
-    for m in range(16):
-        par = unpack(one[m, 128:160, :])
-        fix[m] = dot_split(split(par), split(one[parent[m], 0:128, :]), ((1,), (0,)))
     par_out[...] = unpack(one[row, 128:160, :])
     for copy in copies:
         copy.wait()
@@ -292,37 +293,6 @@
         preferred_element_type=jnp.float32,
     )
     base[128:192, :] = dinv[2, pl.ds(top, 64), :]
-
-
-def corrections(parent, one, dinv_one, dinv_two):
-    return pl.pallas_call(
-        fix_kernel,
-        out_shape=[f32(16, B, KA), f32(B, B), f32(192, B)],
-        in_specs=[SMEM, VMEM, HBM, HBM],
-        out_specs=[VMEM] * 3,
-        scratch_shapes=[pltpu.VMEM((3, B, B), jnp.float32), pltpu.SemaphoreType.DMA((3,))],
-        compiler_params=pltpu.CompilerParams(vmem_limit_bytes=6 * MIB),
-        cost_estimate=pl.CostEstimate(
-            flops=4_000_000_000, bytes_accessed=1_000_000, transcendentals=0
-        ),
-    )(parent, one, dinv_one, dinv_two)
-
-
-def merge(part, keep, got_one, got_two, order):
-    def body(a, b, c, *refs):
-        out = refs[-1]
-        for i in range(4):
-            out[i, 0:64, :] = a[4 * part + i, 0:64, :] + b[4 * part + i]
-            out[i, 64:128, :] = a[4 * part + i, 64:128, :] + c[4 * part + i]
-
-    return pl.pallas_call(
-        body,
-        out_shape=f32(4, B, KA),
-        in_specs=[VMEM] * 3 + [ANY] * len(order),
-        out_specs=VMEM,
-        compiler_params=pltpu.CompilerParams(vmem_limit_bytes=4 * MIB),
-        cost_estimate=pl.CostEstimate(flops=300_000, bytes_accessed=1_000_000, transcendentals=0),
-    )(keep, got_one, got_two, *order)
 
 
 def row_step(value, variant, step):
@@ -358,23 +328,22 @@
     )(*parts, turn)
 
 
-def add(kept, got, order):
+def add(part, kept, got, order=()):
     half = kept.shape[0] // 2
 
     def body(a, b, *refs):
-        outs = refs[len(order) :]
+        out = refs[-1]
         if half == 0:
-            outs[0][...] = a[0] + b[0]
-            return
-        outs[1][...] = a[half:] + b[half:]
-        outs[0][...] = a[:half] + b[:half]
-
-    shapes = [f32(half, B, KA)] * 2 if half else [f32(B, KA)]
+            out[...] = a[0] + b[0]
+        else:
+            at = pl.ds(half * part, half)
+            out[...] = a[at] + b[at]
+
     return pl.pallas_call(
         body,
-        out_shape=shapes,
+        out_shape=f32(half, B, KA) if half else f32(B, KA),
         in_specs=[VMEM] * 2 + [ANY] * len(order),
-        out_specs=[VMEM] * len(shapes),
+        out_specs=VMEM,
         compiler_params=pltpu.CompilerParams(vmem_limit_bytes=8 * MIB),
         cost_estimate=pl.CostEstimate(flops=300_000, bytes_accessed=1_000_000, transcendentals=0),
     )(kept, got, *order)
@@ -441,24 +410,20 @@
     pair_one, pair_two = pair_up(own, swap(own))
     blocks_one = gather(pair_one)
     blocks_two = gather(pair_two)
-    s1a, s1b, one = send_half(0, ginv_anc, blocks_one, [])
-    fix, par, base = corrections(parent, one, dinv_one, dinv_two)
-    r1a, r1b = row_step(s1a, 0, 0), row_step(s1b, 1, 0)
-    s2a, s2b, two, turn = send_half(1, ginv_anc, blocks_two, [fix, one, parent])
-    r2a, r2b = row_step(s2a, 0, 0), row_step(s2b, 1, 0)
+    send_a, send_b, one, two, turn = send_half(parent, ginv_anc, blocks_one, blocks_two)
+    got = [row_step(send_a, 0, 0), row_step(send_b, 1, 0)]
     turn = permute(turn, lambda r, c: (r ^ spread_mask(c), c))
-    keep_a, keep_b = keep_half(ginv_anc, fix, one, two, [r1a, r1b, turn])
-    going = [merge(1, keep_a, r1a, r2a, []), merge(1, keep_b, r1b, r2b, [])]
-    kept = [merge(0, keep_a, r1a, r2a, []), merge(0, keep_b, r1b, r2b, [])]
+    keep_a, keep_b, par, base = keep_half(
+        parent, ginv_anc, one, two, dinv_one, dinv_two, [turn]
+    )
+    kept = [keep_a, keep_b]
     turn = permute(turn, lambda r, c: (r, r ^ spread_mask(c)))
-    got = [row_step(going[v], v, 1) for v in range(2)]
-    kept[0], first = add(kept[0], got[0], [])
-    kept[1], second = add(kept[1], got[1], [])
-    got = [row_step(first, 0, 2), row_step(second, 1, 2)]
-    kept[0], first = add(kept[0], got[0], [])
-    kept[1], second = add(kept[1], got[1], [turn])
-    got = [row_step(first, 0, 3), row_step(second, 1, 3)]
-    kept = [add(kept[0], got[0], [])[0], add(kept[1], got[1], [])[0]]
+    for step in range(1, 4):
+        order = [turn] if step == 3 else []
+        going = [add(1, kept[0], got[0]), add(1, kept[1], got[1], order)]
+        kept = [add(0, kept[v], got[v]) for v in range(2)]
+        got = [row_step(going[v], v, step) for v in range(2)]
+    kept = [add(0, kept[v], got[v]) for v in range(2)]
     anc_one, anc_two, send, keep = blocks_of(kept, turn)
     sums = keep + swap(send)
     for mask in (2, 6):

time: 177 us -> 174 us (0.983); the launches traced: 176 us -> 171 us
  waiting for transfers between devices: 96.2 us -> 81.6 us
  starting transfers between devices: 58.4 us -> 69 us
    ppermute x34 -> x32, waiting for transfers between devices: 96.2 us -> 81.6 us  [permute(): return lax.ppermute(value, ALL, pairs)]
    ppermute x34 -> x32, starting transfers between devices: 58.4 us -> 69 us  [permute(): return lax.ppermute(value, ALL, pairs)]
    pallas_call x14 -> x16, Pallas kernels: 14.3 us -> 13.8 us  [the longest x1 8.64 us: send_half(): pl.pallas_call(send_kernel, out_shape=[f32(8, B, KA)] * 2 + [f32(16, 160,...]
  transfers between devices with their start and end apart: 34 -> 32, of which waited for: 18 -> 20; matrix products, arithmetic and copies ran while one was open for 0% -> 0% of each run, Pallas kernels for 8% -> 3%
where the time goes in v6:
time: 174 us; the launch traced here: 171 us
  waiting for transfers between devices  81.6 us (47%)
  starting transfers between devices  69 us (40%)
  Pallas kernels  18.4 us (11%)
    ppermute x32, waiting for transfers between devices, permute(): return lax.ppermute(value, ALL, pairs)  81.6 us
    ppermute x32, starting transfers between devices, permute(): return lax.ppermute(value, ALL, pairs)  69 us
    pallas_call x1, Pallas kernels, send_half(): pl.pallas_call(send_kernel, out_shape=[f32(8, B, KA)] * 2 + [f32(16, 160,...  8.64 us
    pallas_call x1, Pallas kernels, keep_half(): pl.pallas_call(body, out_shape=[f32(8, B, KA)] * 2 + [f32(B, B), f32(192,...  4.36 us
  transfers between devices with their start and end apart: 32, of which 20 were waited for; matrix products, arithmetic and copies ran while one was open for 0% of the time, Pallas kernels for 3%

profile of v6, /device:TPU:7, one launch (start us, length us, event | category | flops | bytes accessed | tf_op | source)
XLA Modules:
  0.0 171.1 jit_solution(462962709393180419)
XLA Ops:
  0.7 2.3 %shard_map.128.a = f32[288,512]{1,0:T(8,128)} custom-call(s32[16,64]{1,0:T(8,128)} %bitcast.2, s32[16,64]{1,0:T(8,128)} %bitcast.3, f32[512,128]{1,0:T(8,128)} %fac_one.1, f32[512,128]{1,0:T(8,128)} %fac_two.1, f32[128,128]{1,0:T(8,128)} %par.1), custom_call_target="tpu_custom_call" | custom-call | tf_op jit(solution)/shard_map/pallas_call | solution.py:114
  7.0 5.7 %collective-permute-start.1 = (f32[2,160,512]{2,1,0:T(8,128)S(1)}, f32[2,160,512]{2,1,0:T(8,128)S(1)}, u32[]{:S(2)}, u32[]{:S(2)}) collective-permute-start(f32[2,160,512]{2,1,0:T(8,128)S(1)} %get-tuple-element.23.refs_0_), channel_id=1, source_target_pairs={{0,2},{1,15},{2,4},{3,1},{4,6},{5,3},{6,8},{7,5},{8,10},{9,7},{10,... | collective-permute-start | bytes 1966088 | tf_op jit(solution)/shard_map/ppermute | solution.py:62
  13.3 6.8 %collective-permute-done.1.refs_1_ = f32[2,160,512]{2,1,0:T(8,128)S(1)} collective-permute-done((f32[2,160,512]{2,1,0:T(8,128)S(1)}, f32[2,160,512]{2,1,0:T(8,128)S(1)}, u32[]{:S(2)}, u32[]{:S(2)}) %collective-permute-start.1) | collective-permute-done | bytes 655392 | tf_op jit(solution)/shard_map/ppermute | solution.py:62
  20.1 3.1 %collective-permute-start.3 = (f32[2,160,512]{2,1,0:T(8,128)S(1)}, f32[2,160,512]{2,1,0:T(8,128)S(1)}, u32[]{:S(2)}, u32[]{:S(2)}) collective-permute-start(f32[2,160,512]{2,1,0:T(8,128)S(1)} %collective-permute-done.1.refs_1_), channel_id=1, source_target_pairs={{0,2},{1,15},{2,4},{3,1},{4,6},{5,3},{6,8},{7,5},{8,10},{9,7},{10,... | collective-permute-start | bytes 1966088 | tf_op jit(solution)/shard_map/ppermute | solution.py:62
  23.3 2.5 %collective-permute-done.9.refs_10_ = f32[2,128,512]{2,1,0:T(8,128)S(1)} collective-permute-done((f32[2,128,512]{2,1,0:T(8,128)S(1)}, f32[2,128,512]{2,1,0:T(8,128)S(1)}, u32[]{:S(2)}, u32[]{:S(2)}) %collective-permute-start.9) | collective-permute-done | bytes 524320 | tf_op jit(solution)/shard_map/ppermute | solution.py:62
  25.8 3.1 %collective-permute-start.11 = (f32[2,128,512]{2,1,0:T(8,128)S(1)}, f32[2,128,512]{2,1,0:T(8,128)S(1)}, u32[]{:S(2)}, u32[]{:S(2)}) collective-permute-start(f32[2,128,512]{2,1,0:T(8,128)S(1)} %collective-permute-done.9.refs_10_), channel_id=1, source_target_pairs={{0,2},{1,15},{2,4},{3,1},{4,6},{5,3},{6,8},{7,5},{8,10},{9,7},{10,... | collective-permute-start | bytes 1572872 | tf_op jit(solution)/shard_map/ppermute | solution.py:62
  28.9 3.9 %collective-permute-done.3.refs_3_ = f32[2,160,512]{2,1,0:T(8,128)S(1)} collective-permute-done((f32[2,160,512]{2,1,0:T(8,128)S(1)}, f32[2,160,512]{2,1,0:T(8,128)S(1)}, u32[]{:S(2)}, u32[]{:S(2)}) %collective-permute-start.3) | collective-permute-done | bytes 655392 | tf_op jit(solution)/shard_map/ppermute | solution.py:62
  32.8 3.1 %collective-permute-start.5 = (f32[2,160,512]{2,1,0:T(8,128)S(1)}, f32[2,160,512]{2,1,0:T(8,128)S(1)}, u32[]{:S(2)}, u32[]{:S(2)}) collective-permute-start(f32[2,160,512]{2,1,0:T(8,128)S(1)} %collective-permute-done.3.refs_3_), channel_id=1, source_target_pairs={{0,2},{1,15},{2,4},{3,1},{4,6},{5,3},{6,8},{7,5},{8,10},{9,7},{10,... | collective-permute-start | bytes 1966088 | tf_op jit(solution)/shard_map/ppermute | solution.py:62
  38.4 3.1 %collective-permute-start.13 = (f32[2,128,512]{2,1,0:T(8,128)S(1)}, f32[2,128,512]{2,1,0:T(8,128)S(1)}, u32[]{:S(2)}, u32[]{:S(2)}) collective-permute-start(f32[2,128,512]{2,1,0:T(8,128)S(1)} %collective-permute-done.11.refs_12_), channel_id=1, source_target_pairs={{0,2},{1,15},{2,4},{3,1},{4,6},{5,3},{6,8},{7,5},{8,10},{9,7},{10,... | collective-permute-start | bytes 1572872 | tf_op jit(solution)/shard_map/ppermute | solution.py:62
  41.5 3.9 %collective-permute-done.5.refs_5_ = f32[2,160,512]{2,1,0:T(8,128)S(1)} collective-permute-done((f32[2,160,512]{2,1,0:T(8,128)S(1)}, f32[2,160,512]{2,1,0:T(8,128)S(1)}, u32[]{:S(2)}, u32[]{:S(2)}) %collective-permute-start.5) | collective-permute-done | bytes 655392 | tf_op jit(solution)/shard_map/ppermute | solution.py:62
  61.6 8.6 %shard_map.130 = (f32[8,128,512]{2,1,0:T(8,128)S(1)}, f32[8,128,512]{2,1,0:T(8,128)S(1)}, f32[16,160,512]{2,1,0:T(8,128)S(1)}, f32[16,128,512]{2,1,0:T(8,128)S(1)}, f32[384,512]{1,0:T(8,128)S(1)}) custom-call(s32[16]{0:T(128)S(1)} %copy-done.4, f32[512,512]{1,0:T(8,128)S(1)} %copy-done.1, f32[2,160,512]{2,1,0:T(8,128)S(1)} %get-tuple-element.23.refs_0_, ...), custom_call_target="tpu_custom_call" | custom-call | flops 8000000000 | bytes 1000000 | tf_op jit(solution)/shard_map/pallas_call | solution.py:230
  73.6 3.5 %collective-permute-start.17 = (f32[384,512]{1,0:T(8,128)S(1)}, f32[384,512]{1,0:T(8,128)S(1)}, u32[]{:S(2)}, u32[]{:S(2)}) collective-permute-start(f32[384,512]{1,0:T(8,128)S(1)} %get-tuple-element.27), channel_id=1, source_target_pairs={{0,0},{1,161},{2,18},{3,179},{4,100},{5,197},{6,118},{7,215},{8,40... | collective-permute-start | bytes 2359304 | tf_op jit(solution)/shard_map/ppermute | solution.py:62
  77.1 21.7 %collective-permute-done.17.refs_0_ = f32[384,512]{1,0:T(8,128)S(1)} collective-permute-done((f32[384,512]{1,0:T(8,128)S(1)}, f32[384,512]{1,0:T(8,128)S(1)}, u32[]{:S(2)}, u32[]{:S(2)}) %collective-permute-start.17) | collective-permute-done | bytes 786464 | tf_op jit(solution)/shard_map/ppermute | solution.py:62
  98.7 4.4 %shard_map.131 = (f32[8,128,512]{2,1,0:T(8,128)S(1)}, f32[8,128,512]{2,1,0:T(8,128)S(1)}, f32[128,128]{1,0:T(8,128)S(1)}, f32[192,128]{1,0:T(8,128)S(1)}) custom-call(s32[16]{0:T(128)S(1)} %copy-done.4, f32[512,512]{1,0:T(8,128)S(1)} %copy-done.1, f32[16,160,512]{2,1,0:T(8,128)S(1)} %get-tuple-element.25.one, f32[16,128,512]{2,1,0:T(8,128)S(1)} %get-tuple-element.26.two, ...), custom_call_target="tpu_custom_call" | custom-call | flops 4000000000 | bytes 1000000 | tf_op jit(solution)/shard_map/pallas_call | solution.py:256
  104.1 2.8 %collective-permute-start.19 = (f32[4,128,512]{2,1,0:T(8,128)S(1)}, f32[4,128,512]{2,1,0:T(8,128)S(1)}, u32[]{:S(2)}, u32[]{:S(2)}) collective-permute-start(f32[4,128,512]{2,1,0:T(8,128)S(1)} %shard_map.133), channel_id=1, source_target_pairs={{0,48},{1,193},{2,50},{3,195},{4,52},{5,197},{6,54},{7,199},{8,56}... | collective-permute-start | bytes 3145736 | tf_op jit(solution)/shard_map/ppermute | solution.py:62
  107.1 10.4 %collective-permute-start.25 = (f32[384,512]{1,0:T(8,128)S(1)}, f32[384,512]{1,0:T(8,128)S(1)}, u32[]{:S(2)}, u32[]{:S(2)}) collective-permute-start(f32[384,512]{1,0:T(8,128)S(1)} %collective-permute-done.17.refs_0_), channel_id=1, source_target_pairs={{0,0},{1,10},{2,1},{3,11},{4,6},{5,12},{6,7},{7,13},{8,2},{9,8},{1... | collective-permute-start | bytes 2359304 | tf_op jit(solution)/shard_map/ppermute | solution.py:62
  121.5 6.6 %collective-permute-done.20.b = f32[2,128,512]{2,1,0:T(8,128)S(1)} collective-permute-done((f32[2,128,512]{2,1,0:T(8,128)S(1)}, f32[2,128,512]{2,1,0:T(8,128)S(1)}, u32[]{:S(2)}, u32[]{:S(2)}) %collective-permute-start.20) | collective-permute-done | bytes 524320 | tf_op jit(solution)/shard_map/ppermute | solution.py:62
  128.7 6.6 %collective-permute-done.25.refs_0_.turn = f32[384,512]{1,0:T(8,128)S(1)} collective-permute-done((f32[384,512]{1,0:T(8,128)S(1)}, f32[384,512]{1,0:T(8,128)S(1)}, u32[]{:S(2)}, u32[]{:S(2)}) %collective-permute-start.25) | collective-permute-done | bytes 786464 | tf_op jit(solution)/shard_map/ppermute | solution.py:62
  135.5 5.1 %collective-permute-done.26.b = f32[1,128,512]{2,1,0:T(8,128)S(1)} collective-permute-done((f32[1,128,512]{2,1,0:T(8,128)S(1)}, f32[1,128,512]{2,1,0:T(8,128)S(1)}, u32[]{:S(2)}, u32[]{:S(2)}) %collective-permute-start.26) | collective-permute-done | bytes 262176 | tf_op jit(solution)/shard_map/ppermute | solution.py:62
  141.7 6.3 %collective-permute-start.27 = (f32[192,128]{1,0:T(8,128)S(1)}, f32[192,128]{1,0:T(8,128)S(1)}, u32[]{:S(2)}, u32[]{:S(2)}) collective-permute-start(f32[192,128]{1,0:T(8,128)S(1)} %get-tuple-element.36), channel_id=1, source_target_pairs={{0,1},{1,0},{2,3},{3,2},{4,5},{5,4},{6,7},{7,6},{8,9},{9,8},{10,11... | collective-permute-start | bytes 294920 | tf_op jit(solution)/shard_map/ppermute | solution.py:62
  149.0 4.0 %collective-permute-done.28 = f32[192,128]{1,0:T(8,128)S(1)} collective-permute-done((f32[192,128]{1,0:T(8,128)S(1)}, f32[192,128]{1,0:T(8,128)S(1)}, u32[]{:S(2)}, u32[]{:S(2)}) %collective-permute-start.28) | collective-permute-done | bytes 98336 | tf_op jit(solution)/shard_map/ppermute | solution.py:62
  153.1 6.0 %collective-permute-start.29 = (f32[192,128]{1,0:T(8,128)S(1)}, f32[192,128]{1,0:T(8,128)S(1)}, u32[]{:S(2)}, u32[]{:S(2)}) collective-permute-start(f32[192,128]{1,0:T(8,128)S(1)} %add.10), channel_id=1, source_target_pairs={{0,6},{1,7},{2,4},{3,5},{4,2},{5,3},{6,0},{7,1},{8,14},{9,15},{10,... | collective-permute-start | bytes 294920 | tf_op jit(solution)/shard_map/ppermute | solution.py:62
  161.3 4.7 %collective-permute-done.30.second = f32[192,128]{1,0:T(8,128)S(1)} collective-permute-done((f32[192,128]{1,0:T(8,128)S(1)}, f32[192,128]{1,0:T(8,128)S(1)}, u32[]{:S(2)}, u32[]{:S(2)}) %collective-permute-start.30) | collective-permute-done | bytes 98336 | tf_op jit(solution)/shard_map/ppermute | solution.py:62
  166.2 3.2 %collective-permute-start.31 = (f32[192,128]{1,0:T(8,128)S(1)}, f32[192,128]{1,0:T(8,128)S(1)}, u32[]{:S(2)}, u32[]{:S(2)}) collective-permute-start(f32[192,128]{1,0:T(8,128)S(1)} %shard_map.147.own), channel_id=1, source_target_pairs={{0,1},{1,0},{2,3},{3,2},{4,5},{5,4},{6,7},{7,6},{8,9},{9,8},{10,11... | collective-permute-start | bytes 294920 | tf_op jit(solution)/shard_map/ppermute | solution.py:62
  (76 shorter events, 38.9 us)
Async XLA Ops:
  7.0 13.2 %collective-permute-start.1 = (f32[2,160,512]{2,1,0:T(8,128)S(1)}, f32[2,160,512]{2,1,0:T(8,128)S(1)}, u32[]{:S(2)}, u32[]{:S(2)}) collective-permute-start(f32[2,160,512]{2,1,0:T(8,128)S(1)} %get-tuple-element.23.refs_0_), channel_id=1, source_target_pairs={{0,2},{1,15},{2,4},{3,1},{4,6},{5,3},{6,8},{7,5},{8,10},{9,7},{10,... | collective-permute-start | bytes 1966088 | tf_op jit(solution)/shard_map/ppermute | solution.py:62
  12.6 13.1 %collective-permute-start.9 = (f32[2,128,512]{2,1,0:T(8,128)S(1)}, f32[2,128,512]{2,1,0:T(8,128)S(1)}, u32[]{:S(2)}, u32[]{:S(2)}) collective-permute-start(f32[2,128,512]{2,1,0:T(8,128)S(1)} %get-tuple-element.24.refs_9_), channel_id=1, source_target_pairs={{0,2},{1,15},{2,4},{3,1},{4,6},{5,3},{6,8},{7,5},{8,10},{9,7},{10,... | collective-permute-start | bytes 1572872 | tf_op jit(solution)/shard_map/ppermute | solution.py:62
  20.1 12.6 %collective-permute-start.3 = (f32[2,160,512]{2,1,0:T(8,128)S(1)}, f32[2,160,512]{2,1,0:T(8,128)S(1)}, u32[]{:S(2)}, u32[]{:S(2)}) collective-permute-start(f32[2,160,512]{2,1,0:T(8,128)S(1)} %collective-permute-done.1.refs_1_), channel_id=1, source_target_pairs={{0,2},{1,15},{2,4},{3,1},{4,6},{5,3},{6,8},{7,5},{8,10},{9,7},{10,... | collective-permute-start | bytes 1966088 | tf_op jit(solution)/shard_map/ppermute | solution.py:62
  25.8 12.6 %collective-permute-start.11 = (f32[2,128,512]{2,1,0:T(8,128)S(1)}, f32[2,128,512]{2,1,0:T(8,128)S(1)}, u32[]{:S(2)}, u32[]{:S(2)}) collective-permute-start(f32[2,128,512]{2,1,0:T(8,128)S(1)} %collective-permute-done.9.refs_10_), channel_id=1, source_target_pairs={{0,2},{1,15},{2,4},{3,1},{4,6},{5,3},{6,8},{7,5},{8,10},{9,7},{10,... | collective-permute-start | bytes 1572872 | tf_op jit(solution)/shard_map/ppermute | solution.py:62
  32.8 12.6 %collective-permute-start.5 = (f32[2,160,512]{2,1,0:T(8,128)S(1)}, f32[2,160,512]{2,1,0:T(8,128)S(1)}, u32[]{:S(2)}, u32[]{:S(2)}) collective-permute-start(f32[2,160,512]{2,1,0:T(8,128)S(1)} %collective-permute-done.3.refs_3_), channel_id=1, source_target_pairs={{0,2},{1,15},{2,4},{3,1},{4,6},{5,3},{6,8},{7,5},{8,10},{9,7},{10,... | collective-permute-start | bytes 1966088 | tf_op jit(solution)/shard_map/ppermute | solution.py:62
  35.9 16.9 %collective-permute-start.2 = (f32[2,160,512]{2,1,0:T(8,128)S(1)}, f32[2,160,512]{2,1,0:T(8,128)S(1)}, u32[]{:S(2)}, u32[]{:S(2)}) collective-permute-start(f32[2,160,512]{2,1,0:T(8,128)S(1)} %collective-permute-done.1.refs_1_), channel_id=1, source_target_pairs={{0,1},{1,0},{2,3},{3,2},{4,5},{5,4},{6,7},{7,6},{8,9},{9,8},{10,11... | collective-permute-start | bytes 1966088 | tf_op jit(solution)/shard_map/ppermute | solution.py:62
  35.9 11.2 %collective-permute-start.10 = (f32[2,128,512]{2,1,0:T(8,128)S(1)}, f32[2,128,512]{2,1,0:T(8,128)S(1)}, u32[]{:S(2)}, u32[]{:S(2)}) collective-permute-start(f32[2,128,512]{2,1,0:T(8,128)S(1)} %collective-permute-done.9.refs_10_), channel_id=1, source_target_pairs={{0,1},{1,0},{2,3},{3,2},{4,5},{5,4},{6,7},{7,6},{8,9},{9,8},{10,11... | collective-permute-start | bytes 1572872 | tf_op jit(solution)/shard_map/ppermute | solution.py:62
  38.4 12.6 %collective-permute-start.13 = (f32[2,128,512]{2,1,0:T(8,128)S(1)}, f32[2,128,512]{2,1,0:T(8,128)S(1)}, u32[]{:S(2)}, u32[]{:S(2)}) collective-permute-start(f32[2,128,512]{2,1,0:T(8,128)S(1)} %collective-permute-done.11.refs_12_), channel_id=1, source_target_pairs={{0,2},{1,15},{2,4},{3,1},{4,6},{5,3},{6,8},{7,5},{8,10},{9,7},{10,... | collective-permute-start | bytes 1572872 | tf_op jit(solution)/shard_map/ppermute | solution.py:62
  41.5 13.1 %collective-permute-start.12 = (f32[2,128,512]{2,1,0:T(8,128)S(1)}, f32[2,128,512]{2,1,0:T(8,128)S(1)}, u32[]{:S(2)}, u32[]{:S(2)}) collective-permute-start(f32[2,128,512]{2,1,0:T(8,128)S(1)} %collective-permute-done.11.refs_12_), channel_id=1, source_target_pairs={{0,1},{1,0},{2,3},{3,2},{4,5},{5,4},{6,7},{7,6},{8,9},{9,8},{10,11... | collective-permute-start | bytes 1572872 | tf_op jit(solution)/shard_map/ppermute | solution.py:62
  45.4 15.0 %collective-permute-start.4 = (f32[2,160,512]{2,1,0:T(8,128)S(1)}, f32[2,160,512]{2,1,0:T(8,128)S(1)}, u32[]{:S(2)}, u32[]{:S(2)}) collective-permute-start(f32[2,160,512]{2,1,0:T(8,128)S(1)} %collective-permute-done.3.refs_3_), channel_id=1, source_target_pairs={{0,1},{1,0},{2,3},{3,2},{4,5},{5,4},{6,7},{7,6},{8,9},{9,8},{10,11... | collective-permute-start | bytes 1966088 | tf_op jit(solution)/shard_map/ppermute | solution.py:62
  47.2 7.5 %collective-permute-start.7 = (f32[1,160,512]{2,1,0:T(8,128)S(1)}, f32[1,160,512]{2,1,0:T(8,128)S(1)}, u32[]{:S(2)}, u32[]{:S(2)}) collective-permute-start(f32[1,160,512]{2,1,0:T(8,128)S(1)} %slice.8), channel_id=1, source_target_pairs={{0,2},{1,15},{2,4},{3,1},{4,6},{5,3},{6,8},{7,5},{8,10},{9,7},{10,... | collective-permute-start | bytes 983048 | tf_op jit(solution)/shard_map/ppermute | solution.py:62
  51.0 10.6 %collective-permute-start.6 = (f32[2,160,512]{2,1,0:T(8,128)S(1)}, f32[2,160,512]{2,1,0:T(8,128)S(1)}, u32[]{:S(2)}, u32[]{:S(2)}) collective-permute-start(f32[2,160,512]{2,1,0:T(8,128)S(1)} %collective-permute-done.5.refs_5_), channel_id=1, source_target_pairs={{0,1},{1,0},{2,3},{3,2},{4,5},{5,4},{6,7},{7,6},{8,9},{9,8},{10,11... | collective-permute-start | bytes 1966088 | tf_op jit(solution)/shard_map/ppermute | solution.py:62
  54.6 7.0 %collective-permute-start.14 = (f32[2,128,512]{2,1,0:T(8,128)S(1)}, f32[2,128,512]{2,1,0:T(8,128)S(1)}, u32[]{:S(2)}, u32[]{:S(2)}) collective-permute-start(f32[2,128,512]{2,1,0:T(8,128)S(1)} %collective-permute-done.13.refs_14_), channel_id=1, source_target_pairs={{0,1},{1,0},{2,3},{3,2},{4,5},{5,4},{6,7},{7,6},{8,9},{9,8},{10,11... | collective-permute-start | bytes 1572872 | tf_op jit(solution)/shard_map/ppermute | solution.py:62
  70.3 33.7 %collective-permute-start.18 = (f32[8,128,512]{2,1,0:T(8,128)S(1)}, f32[8,128,512]{2,1,0:T(8,128)S(1)}, u32[]{:S(2)}, u32[]{:S(2)}) collective-permute-start(f32[8,128,512]{2,1,0:T(8,128)S(1)} %get-tuple-element.29), channel_id=1, source_target_pairs={{0,16},{1,65},{2,18},{3,67},{4,20},{5,69},{6,22},{7,71},{8,24},{9,... | collective-permute-start | bytes 6291464 | tf_op jit(solution)/shard_map/ppermute | solution.py:62
  71.7 35.2 %collective-permute-start.22 = (f32[8,128,512]{2,1,0:T(8,128)S(1)}, f32[8,128,512]{2,1,0:T(8,128)S(1)}, u32[]{:S(2)}, u32[]{:S(2)}) collective-permute-start(f32[8,128,512]{2,1,0:T(8,128)S(1)} %get-tuple-element.31), channel_id=1, source_target_pairs={{0,48},{1,193},{2,50},{3,195},{4,52},{5,197},{6,54},{7,199},{8,56}... | collective-permute-start | bytes 6291464 | tf_op jit(solution)/shard_map/ppermute | solution.py:62
  73.6 25.1 %collective-permute-start.17 = (f32[384,512]{1,0:T(8,128)S(1)}, f32[384,512]{1,0:T(8,128)S(1)}, u32[]{:S(2)}, u32[]{:S(2)}) collective-permute-start(f32[384,512]{1,0:T(8,128)S(1)} %get-tuple-element.27), channel_id=1, source_target_pairs={{0,0},{1,161},{2,18},{3,179},{4,100},{5,197},{6,118},{7,215},{8,40... | collective-permute-start | bytes 2359304 | tf_op jit(solution)/shard_map/ppermute | solution.py:62
  104.1 15.3 %collective-permute-start.19 = (f32[4,128,512]{2,1,0:T(8,128)S(1)}, f32[4,128,512]{2,1,0:T(8,128)S(1)}, u32[]{:S(2)}, u32[]{:S(2)}) collective-permute-start(f32[4,128,512]{2,1,0:T(8,128)S(1)} %shard_map.133), channel_id=1, source_target_pairs={{0,48},{1,193},{2,50},{3,195},{4,52},{5,197},{6,54},{7,199},{8,56}... | collective-permute-start | bytes 3145736 | tf_op jit(solution)/shard_map/ppermute | solution.py:62
  107.0 14.2 %collective-permute-start.23 = (f32[4,128,512]{2,1,0:T(8,128)S(1)}, f32[4,128,512]{2,1,0:T(8,128)S(1)}, u32[]{:S(2)}, u32[]{:S(2)}) collective-permute-start(f32[4,128,512]{2,1,0:T(8,128)S(1)} %shard_map.140), channel_id=1, source_target_pairs={{0,16},{1,65},{2,18},{3,67},{4,20},{5,69},{6,22},{7,71},{8,24},{9,... | collective-permute-start | bytes 3145736 | tf_op jit(solution)/shard_map/ppermute | solution.py:62
  107.1 28.1 %collective-permute-start.25 = (f32[384,512]{1,0:T(8,128)S(1)}, f32[384,512]{1,0:T(8,128)S(1)}, u32[]{:S(2)}, u32[]{:S(2)}) collective-permute-start(f32[384,512]{1,0:T(8,128)S(1)} %collective-permute-done.17.refs_0_), channel_id=1, source_target_pairs={{0,0},{1,10},{2,1},{3,11},{4,6},{5,12},{6,7},{7,13},{8,2},{9,8},{1... | collective-permute-start | bytes 2359304 | tf_op jit(solution)/shard_map/ppermute | solution.py:62
  119.5 8.6 %collective-permute-start.20 = (f32[2,128,512]{2,1,0:T(8,128)S(1)}, f32[2,128,512]{2,1,0:T(8,128)S(1)}, u32[]{:S(2)}, u32[]{:S(2)}) collective-permute-start(f32[2,128,512]{2,1,0:T(8,128)S(1)} %shard_map.135), channel_id=1, source_target_pairs={{0,64},{1,17},{2,66},{3,19},{4,68},{5,21},{6,70},{7,23},{8,72},{9,... | collective-permute-start | bytes 1572872 | tf_op jit(solution)/shard_map/ppermute | solution.py:62
  121.3 14.0 %collective-permute-start.24 = (f32[2,128,512]{2,1,0:T(8,128)S(1)}, f32[2,128,512]{2,1,0:T(8,128)S(1)}, u32[]{:S(2)}, u32[]{:S(2)}) collective-permute-start(f32[2,128,512]{2,1,0:T(8,128)S(1)} %shard_map.142), channel_id=1, source_target_pairs={{0,192},{1,49},{2,194},{3,51},{4,196},{5,53},{6,198},{7,55},{8,200... | collective-permute-start | bytes 1572872 | tf_op jit(solution)/shard_map/ppermute | solution.py:62
  128.1 7.4 %collective-permute-start.21 = (f32[1,128,512]{2,1,0:T(8,128)S(1)}, f32[1,128,512]{2,1,0:T(8,128)S(1)}, u32[]{:S(2)}, u32[]{:S(2)}) collective-permute-start(f32[1,128,512]{2,1,0:T(8,128)S(1)} %shard_map.137), channel_id=1, source_target_pairs={{0,192},{1,49},{2,194},{3,51},{4,196},{5,53},{6,198},{7,55},{8,200... | collective-permute-start | bytes 786440 | tf_op jit(solution)/shard_map/ppermute | solution.py:62
  141.7 7.2 %collective-permute-start.27 = (f32[192,128]{1,0:T(8,128)S(1)}, f32[192,128]{1,0:T(8,128)S(1)}, u32[]{:S(2)}, u32[]{:S(2)}) collective-permute-start(f32[192,128]{1,0:T(8,128)S(1)} %get-tuple-element.36), channel_id=1, source_target_pairs={{0,1},{1,0},{2,3},{3,2},{4,5},{5,4},{6,7},{7,6},{8,9},{9,8},{10,11... | collective-permute-start | bytes 294920 | tf_op jit(solution)/shard_map/ppermute | solution.py:62
  153.1 8.1 %collective-permute-start.29 = (f32[192,128]{1,0:T(8,128)S(1)}, f32[192,128]{1,0:T(8,128)S(1)}, u32[]{:S(2)}, u32[]{:S(2)}) collective-permute-start(f32[192,128]{1,0:T(8,128)S(1)} %add.10), channel_id=1, source_target_pairs={{0,6},{1,7},{2,4},{3,5},{4,2},{5,3},{6,0},{7,1},{8,14},{9,15},{10,... | collective-permute-start | bytes 294920 | tf_op jit(solution)/shard_map/ppermute | solution.py:62
  (13 other events, 251.8 us)

commit v7 on v6

--- a/solution.py
+++ b/solution.py
@@ -172,10 +172,10 @@
     return row, col, core, target
 
 
-def fetch(refs, target, sems, first):
+def sources(refs):
     col = lax.axis_index("pcol")
     z, core = lax.div(col, 2), lax.rem(col, 2)
-    copies = []
+    found = []
     for at, ref in enumerate(refs):
         step = (at + 1) // 2
         swapped = at > 0 and at % 2 == 0
@@ -184,55 +184,85 @@
         plane = lax.rem(z + away, 8)
         for i in range(ref.shape[0]):
             parity = side if i == 0 else 1 - side
-            copies.append(
+            found.append((ref.at[i], plane * 2 + parity))
+    return found
+
+
+def fetch(refs, target, sems, first):
+    return [
+        pltpu.make_async_copy(source, target.at[m], sems.at[first + k])
+        for k, (source, m) in enumerate(sources(refs))
+    ]
+
+
+def turn_kernel(parent, *refs):
+    first, second, turn, sems = refs[:9], refs[9:18], refs[18], refs[19]
+    row, col, core, target = place()
+    wanted = ((first, parent[target]), (first, target), (second, target))
+    for k, (blocks, which) in enumerate(wanted):
+        for source, m in sources(blocks):
+
+            @pl.when(m == which)
+            def start():
                 pltpu.make_async_copy(
-                    ref.at[i], target.at[plane * 2 + parity], sems.at[first + len(copies)]
-                )
-            )
-    return copies
-
-
-def products(ginv, one, two, row, core, half, left, outs):
+                    source.at[pl.ds(0, 128)], turn.at[pl.ds(128 * k, 128)], sems.at[k]
+                ).start()
+
+    for k in range(3):
+        part = turn.at[pl.ds(128 * k, 128)]
+        pltpu.make_async_copy(part, part, sems.at[k]).wait()
+
+
+def pick_turn(parent, first, second):
+    return pl.pallas_call(
+        turn_kernel,
+        out_shape=f32(384, KA),
+        in_specs=[SMEM] + [ANY] * 18,
+        out_specs=VMEM,
+        scratch_shapes=[pltpu.SemaphoreType.DMA((3,))],
+        compiler_params=pltpu.CompilerParams(vmem_limit_bytes=4 * MIB),
+        cost_estimate=pl.CostEstimate(flops=1000, bytes_accessed=1000, transcendentals=0),
+    )(parent, *first, *second)
+
+
+def products(ginv, level, at, row, core, half, left, outs):
     for variant in range(2):
         rows = pl.ds(64 * variant, 64)
-        for at, level in enumerate((one, two)):
-            for slot in range(8):
-                dest = destination(row, core, variant, slot + 8 * half)
-                left[64 * slot : 64 * slot + 64, :] = level[dest, rows, :]
-            value = dot_split(split(left[...]), ginv, ((1,), (0,)))
-            outs[variant][:, 64 * at : 64 * at + 64, :] = -value.reshape(8, 64, KA)
-
-
-def send_kernel(parent, ginv, *refs):
+        for slot in range(8):
+            dest = destination(row, core, variant, slot + 8 * half)
+            left[64 * slot : 64 * slot + 64, :] = level[dest, rows, :]
+        value = dot_split(split(left[...]), ginv, ((1,), (0,)))
+        outs[variant][:, 64 * at : 64 * at + 64, :] = -value.reshape(8, 64, KA)
+
+
+def send_kernel(parent, ginv, turn, *refs):
     first, second, refs = refs[:9], refs[9:18], refs[18:]
-    sends, one, two, turn, left, block, sems = refs[0:2], *refs[2:]
+    sends, one, two, left, block, sems = refs[0:2], *refs[2:]
     row, col, core, target = place()
     load = pltpu.make_async_copy(ginv, block, sems.at[32])
     low = fetch(first, one, sems, 0)
     high = fetch(second, two, sems, 16)
-    for copy in low + [load] + high:
+    for copy in [load] + low + high:
         copy.start()
+    load.wait()
+    ginv = split(block[...])
     for copy in low:
         copy.wait()
-    turn[0:128, :] = one[parent[target], 0:128, :]
-    turn[128:256, :] = one[target, 0:128, :]
+    products(ginv, one, 0, row, core, 1, left, sends)
     for copy in high:
         copy.wait()
-    turn[256:384, :] = two[target]
     for m in range(16):
         par = split(unpack(one[m, 128:160, :]))
         two[m] = two[m] - dot_split(par, split(one[parent[m], 0:128, :]), ((1,), (0,)))
-    load.wait()
-    products(split(block[...]), one, two, row, core, 1, left, sends)
-
-
-def send_half(parent, ginv, first, second):
+    products(ginv, two, 1, row, core, 1, left, sends)
+
+
+def send_half(parent, ginv, turn, first, second):
     return pl.pallas_call(
         send_kernel,
-        out_shape=[f32(8, B, KA)] * 2
-        + [f32(16, 160, KA), f32(16, B, KA), f32(384, KA)],
-        in_specs=[SMEM, HBM] + [ANY] * 18,
-        out_specs=[VMEM] * 5,
+        out_shape=[f32(8, B, KA)] * 2 + [f32(16, 160, KA), f32(16, B, KA)],
+        in_specs=[SMEM, HBM] + [ANY] * 19,
+        out_specs=[VMEM] * 4,
         scratch_shapes=[
             pltpu.VMEM((512, KA), jnp.float32),
             pltpu.VMEM((512, KA), jnp.float32),
@@ -240,9 +270,9 @@
         ],
         compiler_params=pltpu.CompilerParams(vmem_limit_bytes=8 * MIB),
         cost_estimate=pl.CostEstimate(
-            flops=8_000_000_000, bytes_accessed=1_000_000, transcendentals=0
+            flops=20_000_000_000, bytes_accessed=1_000_000, transcendentals=0
         ),
-    )(parent, ginv, *first, *second)
+    )(parent, ginv, turn, *first, *second)
 
 
 def keep_half(parent, ginv, one, two, dinv_one, dinv_two, order):
@@ -251,7 +281,9 @@
         par_out, base, left, dinv, sems = refs
         row, col, core, target = place()
         base_parts(parent, one, dinv_one, dinv_two, par_out, base, dinv, sems, row, core)
-        products(split(ginv[...]), one, two, row, core, 0, left, outs)
+        ginv = split(ginv[...])
+        products(ginv, one, 0, row, core, 0, left, outs)
+        products(ginv, two, 1, row, core, 0, left, outs)
 
     return pl.pallas_call(
         body,
@@ -265,7 +297,7 @@
         ],
         compiler_params=pltpu.CompilerParams(vmem_limit_bytes=8 * MIB),
         cost_estimate=pl.CostEstimate(
-            flops=4_000_000_000, bytes_accessed=1_000_000, transcendentals=0
+            flops=60_000_000_000, bytes_accessed=1_000_000, transcendentals=0
         ),
     )(parent, ginv, one, two, dinv_one, dinv_two, *order)
 
@@ -410,9 +442,10 @@
     pair_one, pair_two = pair_up(own, swap(own))
     blocks_one = gather(pair_one)
     blocks_two = gather(pair_two)
-    send_a, send_b, one, two, turn = send_half(parent, ginv_anc, blocks_one, blocks_two)
+    turn = pick_turn(parent, blocks_one, blocks_two)
+    send_a, send_b, one, two = send_half(parent, ginv_anc, turn, blocks_one, blocks_two)
+    turn = permute(turn, lambda r, c: (r ^ spread_mask(c), c))
     got = [row_step(send_a, 0, 0), row_step(send_b, 1, 0)]
-    turn = permute(turn, lambda r, c: (r ^ spread_mask(c), c))
     keep_a, keep_b, par, base = keep_half(
         parent, ginv_anc, one, two, dinv_one, dinv_two, [turn]
     )

time: 174 us -> 169 us (0.971); the launches traced: 171 us -> 169 us
  starting transfers between devices: 69 us -> 62.1 us
  waiting for transfers between devices: 81.6 us -> 84.7 us
    ppermute x32, starting transfers between devices: 69 us -> 62.1 us  [permute(): return lax.ppermute(value, ALL, pairs)]
    ppermute x32, waiting for transfers between devices: 81.6 us -> 84.7 us  [permute(): return lax.ppermute(value, ALL, pairs)]
  transfers between devices with their start and end apart: 32 -> 32, of which waited for: 20 -> 20; matrix products, arithmetic and copies ran while one was open for 0% -> 0% of each run, Pallas kernels for 3% -> 8%
where the time goes in v7:
time: 169 us
  waiting for transfers between devices  84.7 us (50%)
  starting transfers between devices  62.1 us (37%)
  Pallas kernels  19.8 us (12%)
    ppermute x32, waiting for transfers between devices, permute(): return lax.ppermute(value, ALL, pairs)  84.7 us
    ppermute x32, starting transfers between devices, permute(): return lax.ppermute(value, ALL, pairs)  62.1 us
    pallas_call x1, Pallas kernels, send_half(): pl.pallas_call(send_kernel, out_shape=[f32(8, B, KA)] * 2 + [f32(16, 160,...  8.91 us
    pallas_call x1, Pallas kernels, keep_half(): pl.pallas_call(body, out_shape=[f32(8, B, KA)] * 2 + [f32(B, B), f32(192,...  4.39 us
  transfers between devices with their start and end apart: 32, of which 20 were waited for; matrix products, arithmetic and copies ran while one was open for 0% of the time, Pallas kernels for 8%

profile of v7, /device:TPU:7, one launch (start us, length us, event | category | flops | bytes accessed | tf_op | source)
XLA Modules:
  0.0 168.8 jit_solution(11172671727190459085)
XLA Ops:
  0.6 2.3 %shard_map.128.a = f32[288,512]{1,0:T(8,128)} custom-call(s32[16,64]{1,0:T(8,128)} %bitcast.2, s32[16,64]{1,0:T(8,128)} %bitcast.3, f32[512,128]{1,0:T(8,128)} %fac_one.1, f32[512,128]{1,0:T(8,128)} %fac_two.1, f32[128,128]{1,0:T(8,128)} %par.1), custom_call_target="tpu_custom_call" | custom-call | tf_op jit(solution)/shard_map/pallas_call | solution.py:114
  6.9 5.7 %collective-permute-start.1 = (f32[2,160,512]{2,1,0:T(8,128)S(1)}, f32[2,160,512]{2,1,0:T(8,128)S(1)}, u32[]{:S(2)}, u32[]{:S(2)}) collective-permute-start(f32[2,160,512]{2,1,0:T(8,128)S(1)} %get-tuple-element.22.refs_0_), channel_id=1, source_target_pairs={{0,2},{1,15},{2,4},{3,1},{4,6},{5,3},{6,8},{7,5},{8,10},{9,7},{10,... | collective-permute-start | bytes 1966088 | tf_op jit(solution)/shard_map/ppermute | solution.py:62
  13.3 6.8 %collective-permute-done.1.refs_1_ = f32[2,160,512]{2,1,0:T(8,128)S(1)} collective-permute-done((f32[2,160,512]{2,1,0:T(8,128)S(1)}, f32[2,160,512]{2,1,0:T(8,128)S(1)}, u32[]{:S(2)}, u32[]{:S(2)}) %collective-permute-start.1) | collective-permute-done | bytes 655392 | tf_op jit(solution)/shard_map/ppermute | solution.py:62
  20.1 3.1 %collective-permute-start.3 = (f32[2,160,512]{2,1,0:T(8,128)S(1)}, f32[2,160,512]{2,1,0:T(8,128)S(1)}, u32[]{:S(2)}, u32[]{:S(2)}) collective-permute-start(f32[2,160,512]{2,1,0:T(8,128)S(1)} %collective-permute-done.1.refs_1_), channel_id=1, source_target_pairs={{0,2},{1,15},{2,4},{3,1},{4,6},{5,3},{6,8},{7,5},{8,10},{9,7},{10,... | collective-permute-start | bytes 1966088 | tf_op jit(solution)/shard_map/ppermute | solution.py:62
  23.2 2.5 %collective-permute-done.9.refs_10_ = f32[2,128,512]{2,1,0:T(8,128)S(1)} collective-permute-done((f32[2,128,512]{2,1,0:T(8,128)S(1)}, f32[2,128,512]{2,1,0:T(8,128)S(1)}, u32[]{:S(2)}, u32[]{:S(2)}) %collective-permute-start.9) | collective-permute-done | bytes 524320 | tf_op jit(solution)/shard_map/ppermute | solution.py:62
  25.7 3.1 %collective-permute-start.11 = (f32[2,128,512]{2,1,0:T(8,128)S(1)}, f32[2,128,512]{2,1,0:T(8,128)S(1)}, u32[]{:S(2)}, u32[]{:S(2)}) collective-permute-start(f32[2,128,512]{2,1,0:T(8,128)S(1)} %collective-permute-done.9.refs_10_), channel_id=1, source_target_pairs={{0,2},{1,15},{2,4},{3,1},{4,6},{5,3},{6,8},{7,5},{8,10},{9,7},{10,... | collective-permute-start | bytes 1572872 | tf_op jit(solution)/shard_map/ppermute | solution.py:62
  28.8 3.9 %collective-permute-done.3.refs_3_ = f32[2,160,512]{2,1,0:T(8,128)S(1)} collective-permute-done((f32[2,160,512]{2,1,0:T(8,128)S(1)}, f32[2,160,512]{2,1,0:T(8,128)S(1)}, u32[]{:S(2)}, u32[]{:S(2)}) %collective-permute-start.3) | collective-permute-done | bytes 655392 | tf_op jit(solution)/shard_map/ppermute | solution.py:62
  32.7 3.1 %collective-permute-start.5 = (f32[2,160,512]{2,1,0:T(8,128)S(1)}, f32[2,160,512]{2,1,0:T(8,128)S(1)}, u32[]{:S(2)}, u32[]{:S(2)}) collective-permute-start(f32[2,160,512]{2,1,0:T(8,128)S(1)} %collective-permute-done.3.refs_3_), channel_id=1, source_target_pairs={{0,2},{1,15},{2,4},{3,1},{4,6},{5,3},{6,8},{7,5},{8,10},{9,7},{10,... | collective-permute-start | bytes 1966088 | tf_op jit(solution)/shard_map/ppermute | solution.py:62
  38.3 3.1 %collective-permute-start.13 = (f32[2,128,512]{2,1,0:T(8,128)S(1)}, f32[2,128,512]{2,1,0:T(8,128)S(1)}, u32[]{:S(2)}, u32[]{:S(2)}) collective-permute-start(f32[2,128,512]{2,1,0:T(8,128)S(1)} %collective-permute-done.11.refs_12_), channel_id=1, source_target_pairs={{0,2},{1,15},{2,4},{3,1},{4,6},{5,3},{6,8},{7,5},{8,10},{9,7},{10,... | collective-permute-start | bytes 1572872 | tf_op jit(solution)/shard_map/ppermute | solution.py:62
  41.4 3.9 %collective-permute-done.5.refs_5_ = f32[2,160,512]{2,1,0:T(8,128)S(1)} collective-permute-done((f32[2,160,512]{2,1,0:T(8,128)S(1)}, f32[2,160,512]{2,1,0:T(8,128)S(1)}, u32[]{:S(2)}, u32[]{:S(2)}) %collective-permute-start.5) | collective-permute-done | bytes 655392 | tf_op jit(solution)/shard_map/ppermute | solution.py:62
  62.7 5.8 %collective-permute-start.17 = (f32[384,512]{1,0:T(8,128)S(1)}, f32[384,512]{1,0:T(8,128)S(1)}, u32[]{:S(2)}, u32[]{:S(2)}) collective-permute-start(f32[384,512]{1,0:T(8,128)S(1)} %shard_map.130.turn), channel_id=1, source_target_pairs={{0,0},{1,161},{2,18},{3,179},{4,100},{5,197},{6,118},{7,215},{8,40... | collective-permute-start | bytes 2359304 | tf_op jit(solution)/shard_map/ppermute | solution.py:62
  68.5 8.9 %shard_map.131 = (f32[8,128,512]{2,1,0:T(8,128)S(1)}, f32[8,128,512]{2,1,0:T(8,128)S(1)}, f32[16,160,512]{2,1,0:T(8,128)S(1)}, f32[16,128,512]{2,1,0:T(8,128)S(1)}) custom-call(s32[16]{0:T(128)S(1)} %copy-done.1, f32[512,512]{1,0:T(8,128)S(1)} %copy-done.2, f32[384,512]{1,0:T(8,128)S(1)} %shard_map.130.turn, f32[2,160,512]{2,1,0:T(8,128)S(1)} %get-tuple-element.22.refs_0_, ...), custom_call_target="tpu_custom_call" | custom-call | flops 20000000000 | bytes 1000000 | tf_op jit(solution)/shard_map/pallas_call | solution.py:261
  79.8 4.4 %shard_map.132 = (f32[8,128,512]{2,1,0:T(8,128)S(1)}, f32[8,128,512]{2,1,0:T(8,128)S(1)}, f32[128,128]{1,0:T(8,128)S(1)}, f32[192,128]{1,0:T(8,128)S(1)}) custom-call(s32[16]{0:T(128)S(1)} %copy-done.1, f32[512,512]{1,0:T(8,128)S(1)} %copy-done.2, f32[16,160,512]{2,1,0:T(8,128)S(1)} %get-tuple-element.24.one, f32[16,128,512]{2,1,0:T(8,128)S(1)} %get-tuple-element.25.two, ...), custom_call_target="tpu_custom_call" | custom-call | flops 60000002048 | bytes 1000000 | tf_op jit(solution)/shard_map/pallas_call | solution.py:288
  84.2 19.4 %collective-permute-done.22.b = f32[8,128,512]{2,1,0:T(8,128)S(1)} collective-permute-done((f32[8,128,512]{2,1,0:T(8,128)S(1)}, f32[8,128,512]{2,1,0:T(8,128)S(1)}, u32[]{:S(2)}, u32[]{:S(2)}) %collective-permute-start.22) | collective-permute-done | bytes 2097184 | tf_op jit(solution)/shard_map/ppermute | solution.py:62
  105.7 5.3 %collective-permute-start.25 = (f32[384,512]{1,0:T(8,128)S(1)}, f32[384,512]{1,0:T(8,128)S(1)}, u32[]{:S(2)}, u32[]{:S(2)}) collective-permute-start(f32[384,512]{1,0:T(8,128)S(1)} %collective-permute-done.17.refs_0_), channel_id=1, source_target_pairs={{0,0},{1,10},{2,1},{3,11},{4,6},{5,12},{6,7},{7,13},{8,2},{9,8},{1... | collective-permute-start | bytes 2359304 | tf_op jit(solution)/shard_map/ppermute | solution.py:62
  111.2 6.6 %collective-permute-done.23.b = f32[4,128,512]{2,1,0:T(8,128)S(1)} collective-permute-done((f32[4,128,512]{2,1,0:T(8,128)S(1)}, f32[4,128,512]{2,1,0:T(8,128)S(1)}, u32[]{:S(2)}, u32[]{:S(2)}) %collective-permute-start.23) | collective-permute-done | bytes 1048608 | tf_op jit(solution)/shard_map/ppermute | solution.py:62
  120.3 8.6 %collective-permute-done.25.refs_0_.turn = f32[384,512]{1,0:T(8,128)S(1)} collective-permute-done((f32[384,512]{1,0:T(8,128)S(1)}, f32[384,512]{1,0:T(8,128)S(1)}, u32[]{:S(2)}, u32[]{:S(2)}) %collective-permute-start.25) | collective-permute-done | bytes 786464 | tf_op jit(solution)/shard_map/ppermute | solution.py:62
  131.1 3.5 %collective-permute-done.26.b = f32[1,128,512]{2,1,0:T(8,128)S(1)} collective-permute-done((f32[1,128,512]{2,1,0:T(8,128)S(1)}, f32[1,128,512]{2,1,0:T(8,128)S(1)}, u32[]{:S(2)}, u32[]{:S(2)}) %collective-permute-start.26) | collective-permute-done | bytes 262176 | tf_op jit(solution)/shard_map/ppermute | solution.py:62
  134.7 2.8 %collective-permute-done.21.b = f32[1,128,512]{2,1,0:T(8,128)S(1)} collective-permute-done((f32[1,128,512]{2,1,0:T(8,128)S(1)}, f32[1,128,512]{2,1,0:T(8,128)S(1)}, u32[]{:S(2)}, u32[]{:S(2)}) %collective-permute-start.21) | collective-permute-done | bytes 262176 | tf_op jit(solution)/shard_map/ppermute | solution.py:62
  138.5 8.6 %collective-permute-start.27 = (f32[192,128]{1,0:T(8,128)S(1)}, f32[192,128]{1,0:T(8,128)S(1)}, u32[]{:S(2)}, u32[]{:S(2)}) collective-permute-start(f32[192,128]{1,0:T(8,128)S(1)} %get-tuple-element.34), channel_id=1, source_target_pairs={{0,1},{1,0},{2,3},{3,2},{4,5},{5,4},{6,7},{7,6},{8,9},{9,8},{10,11... | collective-permute-start | bytes 294920 | tf_op jit(solution)/shard_map/ppermute | solution.py:62
  148.2 4.0 %collective-permute-done.28 = f32[192,128]{1,0:T(8,128)S(1)} collective-permute-done((f32[192,128]{1,0:T(8,128)S(1)}, f32[192,128]{1,0:T(8,128)S(1)}, u32[]{:S(2)}, u32[]{:S(2)}) %collective-permute-start.28) | collective-permute-done | bytes 98336 | tf_op jit(solution)/shard_map/ppermute | solution.py:62
  152.3 5.4 %collective-permute-done.29 = f32[192,128]{1,0:T(8,128)S(1)} collective-permute-done((f32[192,128]{1,0:T(8,128)S(1)}, f32[192,128]{1,0:T(8,128)S(1)}, u32[]{:S(2)}, u32[]{:S(2)}) %collective-permute-start.29) | collective-permute-done | bytes 98336 | tf_op jit(solution)/shard_map/ppermute | solution.py:62
  157.8 4.8 %collective-permute-done.30.second = f32[192,128]{1,0:T(8,128)S(1)} collective-permute-done((f32[192,128]{1,0:T(8,128)S(1)}, f32[192,128]{1,0:T(8,128)S(1)}, u32[]{:S(2)}, u32[]{:S(2)}) %collective-permute-start.30) | collective-permute-done | bytes 98336 | tf_op jit(solution)/shard_map/ppermute | solution.py:62
  162.8 4.3 %collective-permute-start.31 = (f32[192,128]{1,0:T(8,128)S(1)}, f32[192,128]{1,0:T(8,128)S(1)}, u32[]{:S(2)}, u32[]{:S(2)}) collective-permute-start(f32[192,128]{1,0:T(8,128)S(1)} %shard_map.148.own), channel_id=1, source_target_pairs={{0,1},{1,0},{2,3},{3,2},{4,5},{5,4},{6,7},{7,6},{8,9},{9,8},{10,11... | collective-permute-start | bytes 294920 | tf_op jit(solution)/shard_map/ppermute | solution.py:62
  (77 shorter events, 37.9 us)
Async XLA Ops:
  6.9 13.2 %collective-permute-start.1 = (f32[2,160,512]{2,1,0:T(8,128)S(1)}, f32[2,160,512]{2,1,0:T(8,128)S(1)}, u32[]{:S(2)}, u32[]{:S(2)}) collective-permute-start(f32[2,160,512]{2,1,0:T(8,128)S(1)} %get-tuple-element.22.refs_0_), channel_id=1, source_target_pairs={{0,2},{1,15},{2,4},{3,1},{4,6},{5,3},{6,8},{7,5},{8,10},{9,7},{10,... | collective-permute-start | bytes 1966088 | tf_op jit(solution)/shard_map/ppermute | solution.py:62
  12.5 13.1 %collective-permute-start.9 = (f32[2,128,512]{2,1,0:T(8,128)S(1)}, f32[2,128,512]{2,1,0:T(8,128)S(1)}, u32[]{:S(2)}, u32[]{:S(2)}) collective-permute-start(f32[2,128,512]{2,1,0:T(8,128)S(1)} %get-tuple-element.23.refs_9_), channel_id=1, source_target_pairs={{0,2},{1,15},{2,4},{3,1},{4,6},{5,3},{6,8},{7,5},{8,10},{9,7},{10,... | collective-permute-start | bytes 1572872 | tf_op jit(solution)/shard_map/ppermute | solution.py:62
  20.1 12.6 %collective-permute-start.3 = (f32[2,160,512]{2,1,0:T(8,128)S(1)}, f32[2,160,512]{2,1,0:T(8,128)S(1)}, u32[]{:S(2)}, u32[]{:S(2)}) collective-permute-start(f32[2,160,512]{2,1,0:T(8,128)S(1)} %collective-permute-done.1.refs_1_), channel_id=1, source_target_pairs={{0,2},{1,15},{2,4},{3,1},{4,6},{5,3},{6,8},{7,5},{8,10},{9,7},{10,... | collective-permute-start | bytes 1966088 | tf_op jit(solution)/shard_map/ppermute | solution.py:62
  25.7 12.6 %collective-permute-start.11 = (f32[2,128,512]{2,1,0:T(8,128)S(1)}, f32[2,128,512]{2,1,0:T(8,128)S(1)}, u32[]{:S(2)}, u32[]{:S(2)}) collective-permute-start(f32[2,128,512]{2,1,0:T(8,128)S(1)} %collective-permute-done.9.refs_10_), channel_id=1, source_target_pairs={{0,2},{1,15},{2,4},{3,1},{4,6},{5,3},{6,8},{7,5},{8,10},{9,7},{10,... | collective-permute-start | bytes 1572872 | tf_op jit(solution)/shard_map/ppermute | solution.py:62
  32.7 12.6 %collective-permute-start.5 = (f32[2,160,512]{2,1,0:T(8,128)S(1)}, f32[2,160,512]{2,1,0:T(8,128)S(1)}, u32[]{:S(2)}, u32[]{:S(2)}) collective-permute-start(f32[2,160,512]{2,1,0:T(8,128)S(1)} %collective-permute-done.3.refs_3_), channel_id=1, source_target_pairs={{0,2},{1,15},{2,4},{3,1},{4,6},{5,3},{6,8},{7,5},{8,10},{9,7},{10,... | collective-permute-start | bytes 1966088 | tf_op jit(solution)/shard_map/ppermute | solution.py:62
  35.8 16.9 %collective-permute-start.2 = (f32[2,160,512]{2,1,0:T(8,128)S(1)}, f32[2,160,512]{2,1,0:T(8,128)S(1)}, u32[]{:S(2)}, u32[]{:S(2)}) collective-permute-start(f32[2,160,512]{2,1,0:T(8,128)S(1)} %collective-permute-done.1.refs_1_), channel_id=1, source_target_pairs={{0,1},{1,0},{2,3},{3,2},{4,5},{5,4},{6,7},{7,6},{8,9},{9,8},{10,11... | collective-permute-start | bytes 1966088 | tf_op jit(solution)/shard_map/ppermute | solution.py:62
  35.8 11.2 %collective-permute-start.10 = (f32[2,128,512]{2,1,0:T(8,128)S(1)}, f32[2,128,512]{2,1,0:T(8,128)S(1)}, u32[]{:S(2)}, u32[]{:S(2)}) collective-permute-start(f32[2,128,512]{2,1,0:T(8,128)S(1)} %collective-permute-done.9.refs_10_), channel_id=1, source_target_pairs={{0,1},{1,0},{2,3},{3,2},{4,5},{5,4},{6,7},{7,6},{8,9},{9,8},{10,11... | collective-permute-start | bytes 1572872 | tf_op jit(solution)/shard_map/ppermute | solution.py:62
  38.3 12.6 %collective-permute-start.13 = (f32[2,128,512]{2,1,0:T(8,128)S(1)}, f32[2,128,512]{2,1,0:T(8,128)S(1)}, u32[]{:S(2)}, u32[]{:S(2)}) collective-permute-start(f32[2,128,512]{2,1,0:T(8,128)S(1)} %collective-permute-done.11.refs_12_), channel_id=1, source_target_pairs={{0,2},{1,15},{2,4},{3,1},{4,6},{5,3},{6,8},{7,5},{8,10},{9,7},{10,... | collective-permute-start | bytes 1572872 | tf_op jit(solution)/shard_map/ppermute | solution.py:62
  41.4 13.1 %collective-permute-start.12 = (f32[2,128,512]{2,1,0:T(8,128)S(1)}, f32[2,128,512]{2,1,0:T(8,128)S(1)}, u32[]{:S(2)}, u32[]{:S(2)}) collective-permute-start(f32[2,128,512]{2,1,0:T(8,128)S(1)} %collective-permute-done.11.refs_12_), channel_id=1, source_target_pairs={{0,1},{1,0},{2,3},{3,2},{4,5},{5,4},{6,7},{7,6},{8,9},{9,8},{10,11... | collective-permute-start | bytes 1572872 | tf_op jit(solution)/shard_map/ppermute | solution.py:62
  45.3 15.0 %collective-permute-start.4 = (f32[2,160,512]{2,1,0:T(8,128)S(1)}, f32[2,160,512]{2,1,0:T(8,128)S(1)}, u32[]{:S(2)}, u32[]{:S(2)}) collective-permute-start(f32[2,160,512]{2,1,0:T(8,128)S(1)} %collective-permute-done.3.refs_3_), channel_id=1, source_target_pairs={{0,1},{1,0},{2,3},{3,2},{4,5},{5,4},{6,7},{7,6},{8,9},{9,8},{10,11... | collective-permute-start | bytes 1966088 | tf_op jit(solution)/shard_map/ppermute | solution.py:62
  47.1 7.5 %collective-permute-start.7 = (f32[1,160,512]{2,1,0:T(8,128)S(1)}, f32[1,160,512]{2,1,0:T(8,128)S(1)}, u32[]{:S(2)}, u32[]{:S(2)}) collective-permute-start(f32[1,160,512]{2,1,0:T(8,128)S(1)} %slice.8), channel_id=1, source_target_pairs={{0,2},{1,15},{2,4},{3,1},{4,6},{5,3},{6,8},{7,5},{8,10},{9,7},{10,... | collective-permute-start | bytes 983048 | tf_op jit(solution)/shard_map/ppermute | solution.py:62
  51.0 10.6 %collective-permute-start.6 = (f32[2,160,512]{2,1,0:T(8,128)S(1)}, f32[2,160,512]{2,1,0:T(8,128)S(1)}, u32[]{:S(2)}, u32[]{:S(2)}) collective-permute-start(f32[2,160,512]{2,1,0:T(8,128)S(1)} %collective-permute-done.5.refs_5_), channel_id=1, source_target_pairs={{0,1},{1,0},{2,3},{3,2},{4,5},{5,4},{6,7},{7,6},{8,9},{9,8},{10,11... | collective-permute-start | bytes 1966088 | tf_op jit(solution)/shard_map/ppermute | solution.py:62
  54.5 7.0 %collective-permute-start.14 = (f32[2,128,512]{2,1,0:T(8,128)S(1)}, f32[2,128,512]{2,1,0:T(8,128)S(1)}, u32[]{:S(2)}, u32[]{:S(2)}) collective-permute-start(f32[2,128,512]{2,1,0:T(8,128)S(1)} %collective-permute-done.13.refs_14_), channel_id=1, source_target_pairs={{0,1},{1,0},{2,3},{3,2},{4,5},{5,4},{6,7},{7,6},{8,9},{9,8},{10,11... | collective-permute-start | bytes 1572872 | tf_op jit(solution)/shard_map/ppermute | solution.py:62
  54.5 7.0 %collective-permute-start.8 = (f32[1,160,512]{2,1,0:T(8,128)S(1)}, f32[1,160,512]{2,1,0:T(8,128)S(1)}, u32[]{:S(2)}, u32[]{:S(2)}) collective-permute-start(f32[1,160,512]{2,1,0:T(8,128)S(1)} %collective-permute-done.7.refs_7_), channel_id=1, source_target_pairs={{0,1},{1,0},{2,3},{3,2},{4,5},{5,4},{6,7},{7,6},{8,9},{9,8},{10,11... | collective-permute-start | bytes 983048 | tf_op jit(solution)/shard_map/ppermute | solution.py:62
  62.7 17.1 %collective-permute-start.17 = (f32[384,512]{1,0:T(8,128)S(1)}, f32[384,512]{1,0:T(8,128)S(1)}, u32[]{:S(2)}, u32[]{:S(2)}) collective-permute-start(f32[384,512]{1,0:T(8,128)S(1)} %shard_map.130.turn), channel_id=1, source_target_pairs={{0,0},{1,161},{2,18},{3,179},{4,100},{5,197},{6,118},{7,215},{8,40... | collective-permute-start | bytes 2359304 | tf_op jit(solution)/shard_map/ppermute | solution.py:62
  77.5 26.2 %collective-permute-start.22 = (f32[8,128,512]{2,1,0:T(8,128)S(1)}, f32[8,128,512]{2,1,0:T(8,128)S(1)}, u32[]{:S(2)}, u32[]{:S(2)}) collective-permute-start(f32[8,128,512]{2,1,0:T(8,128)S(1)} %get-tuple-element.29), channel_id=1, source_target_pairs={{0,48},{1,193},{2,50},{3,195},{4,52},{5,197},{6,54},{7,199},{8,56}... | collective-permute-start | bytes 6291464 | tf_op jit(solution)/shard_map/ppermute | solution.py:62
  78.3 25.5 %collective-permute-start.18 = (f32[8,128,512]{2,1,0:T(8,128)S(1)}, f32[8,128,512]{2,1,0:T(8,128)S(1)}, u32[]{:S(2)}, u32[]{:S(2)}) collective-permute-start(f32[8,128,512]{2,1,0:T(8,128)S(1)} %get-tuple-element.27), channel_id=1, source_target_pairs={{0,16},{1,65},{2,18},{3,67},{4,20},{5,69},{6,22},{7,71},{8,24},{9,... | collective-permute-start | bytes 6291464 | tf_op jit(solution)/shard_map/ppermute | solution.py:62
  103.8 14.0 %collective-permute-start.23 = (f32[4,128,512]{2,1,0:T(8,128)S(1)}, f32[4,128,512]{2,1,0:T(8,128)S(1)}, u32[]{:S(2)}, u32[]{:S(2)}) collective-permute-start(f32[4,128,512]{2,1,0:T(8,128)S(1)} %shard_map.141), channel_id=1, source_target_pairs={{0,16},{1,65},{2,18},{3,67},{4,20},{5,69},{6,22},{7,71},{8,24},{9,... | collective-permute-start | bytes 3145736 | tf_op jit(solution)/shard_map/ppermute | solution.py:62
  104.0 16.0 %collective-permute-start.19 = (f32[4,128,512]{2,1,0:T(8,128)S(1)}, f32[4,128,512]{2,1,0:T(8,128)S(1)}, u32[]{:S(2)}, u32[]{:S(2)}) collective-permute-start(f32[4,128,512]{2,1,0:T(8,128)S(1)} %shard_map.134), channel_id=1, source_target_pairs={{0,48},{1,193},{2,50},{3,195},{4,52},{5,197},{6,54},{7,199},{8,56}... | collective-permute-start | bytes 3145736 | tf_op jit(solution)/shard_map/ppermute | solution.py:62
  105.7 23.2 %collective-permute-start.25 = (f32[384,512]{1,0:T(8,128)S(1)}, f32[384,512]{1,0:T(8,128)S(1)}, u32[]{:S(2)}, u32[]{:S(2)}) collective-permute-start(f32[384,512]{1,0:T(8,128)S(1)} %collective-permute-done.17.refs_0_), channel_id=1, source_target_pairs={{0,0},{1,10},{2,1},{3,11},{4,6},{5,12},{6,7},{7,13},{8,2},{9,8},{1... | collective-permute-start | bytes 2359304 | tf_op jit(solution)/shard_map/ppermute | solution.py:62
  117.8 11.0 %collective-permute-start.24 = (f32[2,128,512]{2,1,0:T(8,128)S(1)}, f32[2,128,512]{2,1,0:T(8,128)S(1)}, u32[]{:S(2)}, u32[]{:S(2)}) collective-permute-start(f32[2,128,512]{2,1,0:T(8,128)S(1)} %shard_map.143), channel_id=1, source_target_pairs={{0,192},{1,49},{2,194},{3,51},{4,196},{5,53},{6,198},{7,55},{8,200... | collective-permute-start | bytes 1572872 | tf_op jit(solution)/shard_map/ppermute | solution.py:62
  120.0 10.9 %collective-permute-start.20 = (f32[2,128,512]{2,1,0:T(8,128)S(1)}, f32[2,128,512]{2,1,0:T(8,128)S(1)}, u32[]{:S(2)}, u32[]{:S(2)}) collective-permute-start(f32[2,128,512]{2,1,0:T(8,128)S(1)} %shard_map.136), channel_id=1, source_target_pairs={{0,64},{1,17},{2,66},{3,19},{4,68},{5,21},{6,70},{7,23},{8,72},{9,... | collective-permute-start | bytes 1572872 | tf_op jit(solution)/shard_map/ppermute | solution.py:62
  131.0 6.5 %collective-permute-start.21 = (f32[1,128,512]{2,1,0:T(8,128)S(1)}, f32[1,128,512]{2,1,0:T(8,128)S(1)}, u32[]{:S(2)}, u32[]{:S(2)}) collective-permute-start(f32[1,128,512]{2,1,0:T(8,128)S(1)} %shard_map.138), channel_id=1, source_target_pairs={{0,192},{1,49},{2,194},{3,51},{4,196},{5,53},{6,198},{7,55},{8,200... | collective-permute-start | bytes 786440 | tf_op jit(solution)/shard_map/ppermute | solution.py:62
  138.5 9.6 %collective-permute-start.27 = (f32[192,128]{1,0:T(8,128)S(1)}, f32[192,128]{1,0:T(8,128)S(1)}, u32[]{:S(2)}, u32[]{:S(2)}) collective-permute-start(f32[192,128]{1,0:T(8,128)S(1)} %get-tuple-element.34), channel_id=1, source_target_pairs={{0,1},{1,0},{2,3},{3,2},{4,5},{5,4},{6,7},{7,6},{8,9},{9,8},{10,11... | collective-permute-start | bytes 294920 | tf_op jit(solution)/shard_map/ppermute | solution.py:62
  (13 other events, 148.9 us)

commit v8 on v7

--- a/solution.py
+++ b/solution.py
@@ -452,8 +452,8 @@
     kept = [keep_a, keep_b]
     turn = permute(turn, lambda r, c: (r, r ^ spread_mask(c)))
     for step in range(1, 4):
-        order = [turn] if step == 3 else []
-        going = [add(1, kept[0], got[0]), add(1, kept[1], got[1], order)]
+        order = [turn] if step == 1 else []
+        going = [add(1, kept[0], got[0], order), add(1, kept[1], got[1], [])]
         kept = [add(0, kept[v], got[v]) for v in range(2)]
         got = [row_step(going[v], v, step) for v in range(2)]
     kept = [add(0, kept[v], got[v]) for v in range(2)]

time: 169 us -> 172 us (1.018); the launches traced: 169 us -> 169 us
  starting transfers between devices: 62.1 us -> 66.2 us
  waiting for transfers between devices: 84.7 us -> 81.3 us
    ppermute x32, starting transfers between devices: 62.1 us -> 66.2 us  [permute(): return lax.ppermute(value, ALL, pairs)]
    ppermute x32, waiting for transfers between devices: 84.7 us -> 81.3 us  [permute(): return lax.ppermute(value, ALL, pairs)]
where the time goes in v8:
time: 172 us; the launch traced here: 169 us
  waiting for transfers between devices  81.3 us (47%)
  starting transfers between devices  66.2 us (38%)
  Pallas kernels  19.7 us (11%)
    ppermute x32, waiting for transfers between devices, permute(): return lax.ppermute(value, ALL, pairs)  81.3 us
    ppermute x32, starting transfers between devices, permute(): return lax.ppermute(value, ALL, pairs)  66.2 us
    pallas_call x1, Pallas kernels, send_half(): pl.pallas_call(send_kernel, out_shape=[f32(8, B, KA)] * 2 + [f32(16, 160,...  8.86 us
    pallas_call x1, Pallas kernels, keep_half(): pl.pallas_call(body, out_shape=[f32(8, B, KA)] * 2 + [f32(B, B), f32(192,...  4.36 us
  transfers between devices with their start and end apart: 32, of which 20 were waited for; matrix products, arithmetic and copies ran while one was open for 0% of the time, Pallas kernels for 8%

profile of v8, /device:TPU:7, one launch (start us, length us, event | category | flops | bytes accessed | tf_op | source)
XLA Modules:
  0.0 169.4 jit_solution(6828436274424156138)
XLA Ops:
  0.6 2.3 %shard_map.128.a = f32[288,512]{1,0:T(8,128)} custom-call(s32[16,64]{1,0:T(8,128)} %bitcast.2, s32[16,64]{1,0:T(8,128)} %bitcast.3, f32[512,128]{1,0:T(8,128)} %fac_one.1, f32[512,128]{1,0:T(8,128)} %fac_two.1, f32[128,128]{1,0:T(8,128)} %par.1), custom_call_target="tpu_custom_call" | custom-call | tf_op jit(solution)/shard_map/pallas_call | solution.py:114
  6.9 5.7 %collective-permute-start.1 = (f32[2,160,512]{2,1,0:T(8,128)S(1)}, f32[2,160,512]{2,1,0:T(8,128)S(1)}, u32[]{:S(2)}, u32[]{:S(2)}) collective-permute-start(f32[2,160,512]{2,1,0:T(8,128)S(1)} %get-tuple-element.22.refs_0_), channel_id=1, source_target_pairs={{0,2},{1,15},{2,4},{3,1},{4,6},{5,3},{6,8},{7,5},{8,10},{9,7},{10,... | collective-permute-start | bytes 1966088 | tf_op jit(solution)/shard_map/ppermute | solution.py:62
  13.3 6.8 %collective-permute-done.1.refs_1_ = f32[2,160,512]{2,1,0:T(8,128)S(1)} collective-permute-done((f32[2,160,512]{2,1,0:T(8,128)S(1)}, f32[2,160,512]{2,1,0:T(8,128)S(1)}, u32[]{:S(2)}, u32[]{:S(2)}) %collective-permute-start.1) | collective-permute-done | bytes 655392 | tf_op jit(solution)/shard_map/ppermute | solution.py:62
  20.1 3.1 %collective-permute-start.3 = (f32[2,160,512]{2,1,0:T(8,128)S(1)}, f32[2,160,512]{2,1,0:T(8,128)S(1)}, u32[]{:S(2)}, u32[]{:S(2)}) collective-permute-start(f32[2,160,512]{2,1,0:T(8,128)S(1)} %collective-permute-done.1.refs_1_), channel_id=1, source_target_pairs={{0,2},{1,15},{2,4},{3,1},{4,6},{5,3},{6,8},{7,5},{8,10},{9,7},{10,... | collective-permute-start | bytes 1966088 | tf_op jit(solution)/shard_map/ppermute | solution.py:62
  23.2 2.5 %collective-permute-done.9.refs_10_ = f32[2,128,512]{2,1,0:T(8,128)S(1)} collective-permute-done((f32[2,128,512]{2,1,0:T(8,128)S(1)}, f32[2,128,512]{2,1,0:T(8,128)S(1)}, u32[]{:S(2)}, u32[]{:S(2)}) %collective-permute-start.9) | collective-permute-done | bytes 524320 | tf_op jit(solution)/shard_map/ppermute | solution.py:62
  25.7 3.1 %collective-permute-start.11 = (f32[2,128,512]{2,1,0:T(8,128)S(1)}, f32[2,128,512]{2,1,0:T(8,128)S(1)}, u32[]{:S(2)}, u32[]{:S(2)}) collective-permute-start(f32[2,128,512]{2,1,0:T(8,128)S(1)} %collective-permute-done.9.refs_10_), channel_id=1, source_target_pairs={{0,2},{1,15},{2,4},{3,1},{4,6},{5,3},{6,8},{7,5},{8,10},{9,7},{10,... | collective-permute-start | bytes 1572872 | tf_op jit(solution)/shard_map/ppermute | solution.py:62
  28.8 3.9 %collective-permute-done.3.refs_3_ = f32[2,160,512]{2,1,0:T(8,128)S(1)} collective-permute-done((f32[2,160,512]{2,1,0:T(8,128)S(1)}, f32[2,160,512]{2,1,0:T(8,128)S(1)}, u32[]{:S(2)}, u32[]{:S(2)}) %collective-permute-start.3) | collective-permute-done | bytes 655392 | tf_op jit(solution)/shard_map/ppermute | solution.py:62
  32.7 3.1 %collective-permute-start.5 = (f32[2,160,512]{2,1,0:T(8,128)S(1)}, f32[2,160,512]{2,1,0:T(8,128)S(1)}, u32[]{:S(2)}, u32[]{:S(2)}) collective-permute-start(f32[2,160,512]{2,1,0:T(8,128)S(1)} %collective-permute-done.3.refs_3_), channel_id=1, source_target_pairs={{0,2},{1,15},{2,4},{3,1},{4,6},{5,3},{6,8},{7,5},{8,10},{9,7},{10,... | collective-permute-start | bytes 1966088 | tf_op jit(solution)/shard_map/ppermute | solution.py:62
  38.3 3.1 %collective-permute-start.13 = (f32[2,128,512]{2,1,0:T(8,128)S(1)}, f32[2,128,512]{2,1,0:T(8,128)S(1)}, u32[]{:S(2)}, u32[]{:S(2)}) collective-permute-start(f32[2,128,512]{2,1,0:T(8,128)S(1)} %collective-permute-done.11.refs_12_), channel_id=1, source_target_pairs={{0,2},{1,15},{2,4},{3,1},{4,6},{5,3},{6,8},{7,5},{8,10},{9,7},{10,... | collective-permute-start | bytes 1572872 | tf_op jit(solution)/shard_map/ppermute | solution.py:62
  41.4 3.9 %collective-permute-done.5.refs_5_ = f32[2,160,512]{2,1,0:T(8,128)S(1)} collective-permute-done((f32[2,160,512]{2,1,0:T(8,128)S(1)}, f32[2,160,512]{2,1,0:T(8,128)S(1)}, u32[]{:S(2)}, u32[]{:S(2)}) %collective-permute-start.5) | collective-permute-done | bytes 655392 | tf_op jit(solution)/shard_map/ppermute | solution.py:62
  62.7 5.8 %collective-permute-start.17 = (f32[384,512]{1,0:T(8,128)S(1)}, f32[384,512]{1,0:T(8,128)S(1)}, u32[]{:S(2)}, u32[]{:S(2)}) collective-permute-start(f32[384,512]{1,0:T(8,128)S(1)} %shard_map.130.turn), channel_id=1, source_target_pairs={{0,0},{1,161},{2,18},{3,179},{4,100},{5,197},{6,118},{7,215},{8,40... | collective-permute-start | bytes 2359304 | tf_op jit(solution)/shard_map/ppermute | solution.py:62
  68.5 8.9 %shard_map.131 = (f32[8,128,512]{2,1,0:T(8,128)S(1)}, f32[8,128,512]{2,1,0:T(8,128)S(1)}, f32[16,160,512]{2,1,0:T(8,128)S(1)}, f32[16,128,512]{2,1,0:T(8,128)S(1)}) custom-call(s32[16]{0:T(128)S(1)} %copy-done.1, f32[512,512]{1,0:T(8,128)S(1)} %copy-done.2, f32[384,512]{1,0:T(8,128)S(1)} %shard_map.130.turn, f32[2,160,512]{2,1,0:T(8,128)S(1)} %get-tuple-element.22.refs_0_, ...), custom_call_target="tpu_custom_call" | custom-call | flops 20000000000 | bytes 1000000 | tf_op jit(solution)/shard_map/pallas_call | solution.py:261
  79.8 3.8 %collective-permute-start.19 = (f32[384,512]{1,0:T(8,128)S(1)}, f32[384,512]{1,0:T(8,128)S(1)}, u32[]{:S(2)}, u32[]{:S(2)}) collective-permute-start(f32[384,512]{1,0:T(8,128)S(1)} %collective-permute-done.17.refs_0_), channel_id=1, source_target_pairs={{0,0},{1,10},{2,1},{3,11},{4,6},{5,12},{6,7},{7,13},{8,2},{9,8},{1... | collective-permute-start | bytes 2359304 | tf_op jit(solution)/shard_map/ppermute | solution.py:62
  83.7 4.4 %shard_map.132 = (f32[8,128,512]{2,1,0:T(8,128)S(1)}, f32[8,128,512]{2,1,0:T(8,128)S(1)}, f32[128,128]{1,0:T(8,128)S(1)}, f32[192,128]{1,0:T(8,128)S(1)}) custom-call(s32[16]{0:T(128)S(1)} %copy-done.1, f32[512,512]{1,0:T(8,128)S(1)} %copy-done.2, f32[16,160,512]{2,1,0:T(8,128)S(1)} %get-tuple-element.24.one, f32[16,128,512]{2,1,0:T(8,128)S(1)} %get-tuple-element.25.two, ...), custom_call_target="tpu_custom_call" | custom-call | flops 60000002048 | bytes 1000000 | tf_op jit(solution)/shard_map/pallas_call | solution.py:288
  88.0 15.6 %collective-permute-done.23.b = f32[8,128,512]{2,1,0:T(8,128)S(1)} collective-permute-done((f32[8,128,512]{2,1,0:T(8,128)S(1)}, f32[8,128,512]{2,1,0:T(8,128)S(1)}, u32[]{:S(2)}, u32[]{:S(2)}) %collective-permute-start.23) | collective-permute-done | bytes 2097184 | tf_op jit(solution)/shard_map/ppermute | solution.py:62
  105.9 11.8 %collective-permute-done.24.b = f32[4,128,512]{2,1,0:T(8,128)S(1)} collective-permute-done((f32[4,128,512]{2,1,0:T(8,128)S(1)}, f32[4,128,512]{2,1,0:T(8,128)S(1)}, u32[]{:S(2)}, u32[]{:S(2)}) %collective-permute-start.24) | collective-permute-done | bytes 1048608 | tf_op jit(solution)/shard_map/ppermute | solution.py:62
  120.2 7.4 %collective-permute-done.25.b = f32[2,128,512]{2,1,0:T(8,128)S(1)} collective-permute-done((f32[2,128,512]{2,1,0:T(8,128)S(1)}, f32[2,128,512]{2,1,0:T(8,128)S(1)}, u32[]{:S(2)}, u32[]{:S(2)}) %collective-permute-start.25) | collective-permute-done | bytes 524320 | tf_op jit(solution)/shard_map/ppermute | solution.py:62
  128.3 7.1 %collective-permute-start.22 = (f32[1,128,512]{2,1,0:T(8,128)S(1)}, f32[1,128,512]{2,1,0:T(8,128)S(1)}, u32[]{:S(2)}, u32[]{:S(2)}) collective-permute-start(f32[1,128,512]{2,1,0:T(8,128)S(1)} %shard_map.138), channel_id=1, source_target_pairs={{0,192},{1,49},{2,194},{3,51},{4,196},{5,53},{6,198},{7,55},{8,200... | collective-permute-start | bytes 786440 | tf_op jit(solution)/shard_map/ppermute | solution.py:62
  135.5 3.6 %collective-permute-done.22.b = f32[1,128,512]{2,1,0:T(8,128)S(1)} collective-permute-done((f32[1,128,512]{2,1,0:T(8,128)S(1)}, f32[1,128,512]{2,1,0:T(8,128)S(1)}, u32[]{:S(2)}, u32[]{:S(2)}) %collective-permute-start.22) | collective-permute-done | bytes 262176 | tf_op jit(solution)/shard_map/ppermute | solution.py:62
  140.2 7.6 %collective-permute-start.27 = (f32[192,128]{1,0:T(8,128)S(1)}, f32[192,128]{1,0:T(8,128)S(1)}, u32[]{:S(2)}, u32[]{:S(2)}) collective-permute-start(f32[192,128]{1,0:T(8,128)S(1)} %get-tuple-element.34), channel_id=1, source_target_pairs={{0,1},{1,0},{2,3},{3,2},{4,5},{5,4},{6,7},{7,6},{8,9},{9,8},{10,11... | collective-permute-start | bytes 294920 | tf_op jit(solution)/shard_map/ppermute | solution.py:62
  148.8 4.0 %collective-permute-done.28 = f32[192,128]{1,0:T(8,128)S(1)} collective-permute-done((f32[192,128]{1,0:T(8,128)S(1)}, f32[192,128]{1,0:T(8,128)S(1)}, u32[]{:S(2)}, u32[]{:S(2)}) %collective-permute-start.28) | collective-permute-done | bytes 98336 | tf_op jit(solution)/shard_map/ppermute | solution.py:62
  153.5 4.7 %collective-permute-done.29 = f32[192,128]{1,0:T(8,128)S(1)} collective-permute-done((f32[192,128]{1,0:T(8,128)S(1)}, f32[192,128]{1,0:T(8,128)S(1)}, u32[]{:S(2)}, u32[]{:S(2)}) %collective-permute-start.29) | collective-permute-done | bytes 98336 | tf_op jit(solution)/shard_map/ppermute | solution.py:62
  159.3 3.8 %collective-permute-done.30.second = f32[192,128]{1,0:T(8,128)S(1)} collective-permute-done((f32[192,128]{1,0:T(8,128)S(1)}, f32[192,128]{1,0:T(8,128)S(1)}, u32[]{:S(2)}, u32[]{:S(2)}) %collective-permute-start.30) | collective-permute-done | bytes 98336 | tf_op jit(solution)/shard_map/ppermute | solution.py:62
  163.4 4.3 %collective-permute-start.31 = (f32[192,128]{1,0:T(8,128)S(1)}, f32[192,128]{1,0:T(8,128)S(1)}, u32[]{:S(2)}, u32[]{:S(2)}) collective-permute-start(f32[192,128]{1,0:T(8,128)S(1)} %shard_map.148.own), channel_id=1, source_target_pairs={{0,1},{1,0},{2,3},{3,2},{4,5},{5,4},{6,7},{7,6},{8,9},{9,8},{10,11... | collective-permute-start | bytes 294920 | tf_op jit(solution)/shard_map/ppermute | solution.py:62
  (77 shorter events, 38.0 us)
Async XLA Ops:
  6.9 13.2 %collective-permute-start.1 = (f32[2,160,512]{2,1,0:T(8,128)S(1)}, f32[2,160,512]{2,1,0:T(8,128)S(1)}, u32[]{:S(2)}, u32[]{:S(2)}) collective-permute-start(f32[2,160,512]{2,1,0:T(8,128)S(1)} %get-tuple-element.22.refs_0_), channel_id=1, source_target_pairs={{0,2},{1,15},{2,4},{3,1},{4,6},{5,3},{6,8},{7,5},{8,10},{9,7},{10,... | collective-permute-start | bytes 1966088 | tf_op jit(solution)/shard_map/ppermute | solution.py:62
  12.5 13.1 %collective-permute-start.9 = (f32[2,128,512]{2,1,0:T(8,128)S(1)}, f32[2,128,512]{2,1,0:T(8,128)S(1)}, u32[]{:S(2)}, u32[]{:S(2)}) collective-permute-start(f32[2,128,512]{2,1,0:T(8,128)S(1)} %get-tuple-element.23.refs_9_), channel_id=1, source_target_pairs={{0,2},{1,15},{2,4},{3,1},{4,6},{5,3},{6,8},{7,5},{8,10},{9,7},{10,... | collective-permute-start | bytes 1572872 | tf_op jit(solution)/shard_map/ppermute | solution.py:62
  20.1 12.6 %collective-permute-start.3 = (f32[2,160,512]{2,1,0:T(8,128)S(1)}, f32[2,160,512]{2,1,0:T(8,128)S(1)}, u32[]{:S(2)}, u32[]{:S(2)}) collective-permute-start(f32[2,160,512]{2,1,0:T(8,128)S(1)} %collective-permute-done.1.refs_1_), channel_id=1, source_target_pairs={{0,2},{1,15},{2,4},{3,1},{4,6},{5,3},{6,8},{7,5},{8,10},{9,7},{10,... | collective-permute-start | bytes 1966088 | tf_op jit(solution)/shard_map/ppermute | solution.py:62
  25.7 12.6 %collective-permute-start.11 = (f32[2,128,512]{2,1,0:T(8,128)S(1)}, f32[2,128,512]{2,1,0:T(8,128)S(1)}, u32[]{:S(2)}, u32[]{:S(2)}) collective-permute-start(f32[2,128,512]{2,1,0:T(8,128)S(1)} %collective-permute-done.9.refs_10_), channel_id=1, source_target_pairs={{0,2},{1,15},{2,4},{3,1},{4,6},{5,3},{6,8},{7,5},{8,10},{9,7},{10,... | collective-permute-start | bytes 1572872 | tf_op jit(solution)/shard_map/ppermute | solution.py:62
  32.7 12.6 %collective-permute-start.5 = (f32[2,160,512]{2,1,0:T(8,128)S(1)}, f32[2,160,512]{2,1,0:T(8,128)S(1)}, u32[]{:S(2)}, u32[]{:S(2)}) collective-permute-start(f32[2,160,512]{2,1,0:T(8,128)S(1)} %collective-permute-done.3.refs_3_), channel_id=1, source_target_pairs={{0,2},{1,15},{2,4},{3,1},{4,6},{5,3},{6,8},{7,5},{8,10},{9,7},{10,... | collective-permute-start | bytes 1966088 | tf_op jit(solution)/shard_map/ppermute | solution.py:62
  35.8 16.9 %collective-permute-start.2 = (f32[2,160,512]{2,1,0:T(8,128)S(1)}, f32[2,160,512]{2,1,0:T(8,128)S(1)}, u32[]{:S(2)}, u32[]{:S(2)}) collective-permute-start(f32[2,160,512]{2,1,0:T(8,128)S(1)} %collective-permute-done.1.refs_1_), channel_id=1, source_target_pairs={{0,1},{1,0},{2,3},{3,2},{4,5},{5,4},{6,7},{7,6},{8,9},{9,8},{10,11... | collective-permute-start | bytes 1966088 | tf_op jit(solution)/shard_map/ppermute | solution.py:62
  35.8 11.2 %collective-permute-start.10 = (f32[2,128,512]{2,1,0:T(8,128)S(1)}, f32[2,128,512]{2,1,0:T(8,128)S(1)}, u32[]{:S(2)}, u32[]{:S(2)}) collective-permute-start(f32[2,128,512]{2,1,0:T(8,128)S(1)} %collective-permute-done.9.refs_10_), channel_id=1, source_target_pairs={{0,1},{1,0},{2,3},{3,2},{4,5},{5,4},{6,7},{7,6},{8,9},{9,8},{10,11... | collective-permute-start | bytes 1572872 | tf_op jit(solution)/shard_map/ppermute | solution.py:62
  38.3 12.6 %collective-permute-start.13 = (f32[2,128,512]{2,1,0:T(8,128)S(1)}, f32[2,128,512]{2,1,0:T(8,128)S(1)}, u32[]{:S(2)}, u32[]{:S(2)}) collective-permute-start(f32[2,128,512]{2,1,0:T(8,128)S(1)} %collective-permute-done.11.refs_12_), channel_id=1, source_target_pairs={{0,2},{1,15},{2,4},{3,1},{4,6},{5,3},{6,8},{7,5},{8,10},{9,7},{10,... | collective-permute-start | bytes 1572872 | tf_op jit(solution)/shard_map/ppermute | solution.py:62
  41.4 13.1 %collective-permute-start.12 = (f32[2,128,512]{2,1,0:T(8,128)S(1)}, f32[2,128,512]{2,1,0:T(8,128)S(1)}, u32[]{:S(2)}, u32[]{:S(2)}) collective-permute-start(f32[2,128,512]{2,1,0:T(8,128)S(1)} %collective-permute-done.11.refs_12_), channel_id=1, source_target_pairs={{0,1},{1,0},{2,3},{3,2},{4,5},{5,4},{6,7},{7,6},{8,9},{9,8},{10,11... | collective-permute-start | bytes 1572872 | tf_op jit(solution)/shard_map/ppermute | solution.py:62
  45.3 15.0 %collective-permute-start.4 = (f32[2,160,512]{2,1,0:T(8,128)S(1)}, f32[2,160,512]{2,1,0:T(8,128)S(1)}, u32[]{:S(2)}, u32[]{:S(2)}) collective-permute-start(f32[2,160,512]{2,1,0:T(8,128)S(1)} %collective-permute-done.3.refs_3_), channel_id=1, source_target_pairs={{0,1},{1,0},{2,3},{3,2},{4,5},{5,4},{6,7},{7,6},{8,9},{9,8},{10,11... | collective-permute-start | bytes 1966088 | tf_op jit(solution)/shard_map/ppermute | solution.py:62
  47.1 7.5 %collective-permute-start.7 = (f32[1,160,512]{2,1,0:T(8,128)S(1)}, f32[1,160,512]{2,1,0:T(8,128)S(1)}, u32[]{:S(2)}, u32[]{:S(2)}) collective-permute-start(f32[1,160,512]{2,1,0:T(8,128)S(1)} %slice.8), channel_id=1, source_target_pairs={{0,2},{1,15},{2,4},{3,1},{4,6},{5,3},{6,8},{7,5},{8,10},{9,7},{10,... | collective-permute-start | bytes 983048 | tf_op jit(solution)/shard_map/ppermute | solution.py:62
  51.0 10.6 %collective-permute-start.6 = (f32[2,160,512]{2,1,0:T(8,128)S(1)}, f32[2,160,512]{2,1,0:T(8,128)S(1)}, u32[]{:S(2)}, u32[]{:S(2)}) collective-permute-start(f32[2,160,512]{2,1,0:T(8,128)S(1)} %collective-permute-done.5.refs_5_), channel_id=1, source_target_pairs={{0,1},{1,0},{2,3},{3,2},{4,5},{5,4},{6,7},{7,6},{8,9},{9,8},{10,11... | collective-permute-start | bytes 1966088 | tf_op jit(solution)/shard_map/ppermute | solution.py:62
  54.5 7.0 %collective-permute-start.14 = (f32[2,128,512]{2,1,0:T(8,128)S(1)}, f32[2,128,512]{2,1,0:T(8,128)S(1)}, u32[]{:S(2)}, u32[]{:S(2)}) collective-permute-start(f32[2,128,512]{2,1,0:T(8,128)S(1)} %collective-permute-done.13.refs_14_), channel_id=1, source_target_pairs={{0,1},{1,0},{2,3},{3,2},{4,5},{5,4},{6,7},{7,6},{8,9},{9,8},{10,11... | collective-permute-start | bytes 1572872 | tf_op jit(solution)/shard_map/ppermute | solution.py:62
  62.7 17.1 %collective-permute-start.17 = (f32[384,512]{1,0:T(8,128)S(1)}, f32[384,512]{1,0:T(8,128)S(1)}, u32[]{:S(2)}, u32[]{:S(2)}) collective-permute-start(f32[384,512]{1,0:T(8,128)S(1)} %shard_map.130.turn), channel_id=1, source_target_pairs={{0,0},{1,161},{2,18},{3,179},{4,100},{5,197},{6,118},{7,215},{8,40... | collective-permute-start | bytes 2359304 | tf_op jit(solution)/shard_map/ppermute | solution.py:62
  77.4 26.2 %collective-permute-start.23 = (f32[8,128,512]{2,1,0:T(8,128)S(1)}, f32[8,128,512]{2,1,0:T(8,128)S(1)}, u32[]{:S(2)}, u32[]{:S(2)}) collective-permute-start(f32[8,128,512]{2,1,0:T(8,128)S(1)} %get-tuple-element.29), channel_id=1, source_target_pairs={{0,48},{1,193},{2,50},{3,195},{4,52},{5,197},{6,54},{7,199},{8,56}... | collective-permute-start | bytes 6291464 | tf_op jit(solution)/shard_map/ppermute | solution.py:62
  78.3 25.5 %collective-permute-start.18 = (f32[8,128,512]{2,1,0:T(8,128)S(1)}, f32[8,128,512]{2,1,0:T(8,128)S(1)}, u32[]{:S(2)}, u32[]{:S(2)}) collective-permute-start(f32[8,128,512]{2,1,0:T(8,128)S(1)} %get-tuple-element.27), channel_id=1, source_target_pairs={{0,16},{1,65},{2,18},{3,67},{4,20},{5,69},{6,22},{7,71},{8,24},{9,... | collective-permute-start | bytes 6291464 | tf_op jit(solution)/shard_map/ppermute | solution.py:62
  79.8 24.0 %collective-permute-start.19 = (f32[384,512]{1,0:T(8,128)S(1)}, f32[384,512]{1,0:T(8,128)S(1)}, u32[]{:S(2)}, u32[]{:S(2)}) collective-permute-start(f32[384,512]{1,0:T(8,128)S(1)} %collective-permute-done.17.refs_0_), channel_id=1, source_target_pairs={{0,0},{1,10},{2,1},{3,11},{4,6},{5,12},{6,7},{7,13},{8,2},{9,8},{1... | collective-permute-start | bytes 2359304 | tf_op jit(solution)/shard_map/ppermute | solution.py:62
  103.7 14.0 %collective-permute-start.24 = (f32[4,128,512]{2,1,0:T(8,128)S(1)}, f32[4,128,512]{2,1,0:T(8,128)S(1)}, u32[]{:S(2)}, u32[]{:S(2)}) collective-permute-start(f32[4,128,512]{2,1,0:T(8,128)S(1)} %shard_map.141), channel_id=1, source_target_pairs={{0,16},{1,65},{2,18},{3,67},{4,20},{5,69},{6,22},{7,71},{8,24},{9,... | collective-permute-start | bytes 3145736 | tf_op jit(solution)/shard_map/ppermute | solution.py:62
  103.9 16.0 %collective-permute-start.20 = (f32[4,128,512]{2,1,0:T(8,128)S(1)}, f32[4,128,512]{2,1,0:T(8,128)S(1)}, u32[]{:S(2)}, u32[]{:S(2)}) collective-permute-start(f32[4,128,512]{2,1,0:T(8,128)S(1)} %shard_map.134), channel_id=1, source_target_pairs={{0,48},{1,193},{2,50},{3,195},{4,52},{5,197},{6,54},{7,199},{8,56}... | collective-permute-start | bytes 3145736 | tf_op jit(solution)/shard_map/ppermute | solution.py:62
  117.8 9.8 %collective-permute-start.25 = (f32[2,128,512]{2,1,0:T(8,128)S(1)}, f32[2,128,512]{2,1,0:T(8,128)S(1)}, u32[]{:S(2)}, u32[]{:S(2)}) collective-permute-start(f32[2,128,512]{2,1,0:T(8,128)S(1)} %shard_map.143), channel_id=1, source_target_pairs={{0,192},{1,49},{2,194},{3,51},{4,196},{5,53},{6,198},{7,55},{8,200... | collective-permute-start | bytes 1572872 | tf_op jit(solution)/shard_map/ppermute | solution.py:62
  120.0 8.3 %collective-permute-start.21 = (f32[2,128,512]{2,1,0:T(8,128)S(1)}, f32[2,128,512]{2,1,0:T(8,128)S(1)}, u32[]{:S(2)}, u32[]{:S(2)}) collective-permute-start(f32[2,128,512]{2,1,0:T(8,128)S(1)} %shard_map.136), channel_id=1, source_target_pairs={{0,64},{1,17},{2,66},{3,19},{4,68},{5,21},{6,70},{7,23},{8,72},{9,... | collective-permute-start | bytes 1572872 | tf_op jit(solution)/shard_map/ppermute | solution.py:62
  127.7 7.8 %collective-permute-start.26 = (f32[1,128,512]{2,1,0:T(8,128)S(1)}, f32[1,128,512]{2,1,0:T(8,128)S(1)}, u32[]{:S(2)}, u32[]{:S(2)}) collective-permute-start(f32[1,128,512]{2,1,0:T(8,128)S(1)} %shard_map.145), channel_id=1, source_target_pairs={{0,64},{1,17},{2,66},{3,19},{4,68},{5,21},{6,70},{7,23},{8,72},{9,... | collective-permute-start | bytes 786440 | tf_op jit(solution)/shard_map/ppermute | solution.py:62
  128.3 10.9 %collective-permute-start.22 = (f32[1,128,512]{2,1,0:T(8,128)S(1)}, f32[1,128,512]{2,1,0:T(8,128)S(1)}, u32[]{:S(2)}, u32[]{:S(2)}) collective-permute-start(f32[1,128,512]{2,1,0:T(8,128)S(1)} %shard_map.138), channel_id=1, source_target_pairs={{0,192},{1,49},{2,194},{3,51},{4,196},{5,53},{6,198},{7,55},{8,200... | collective-permute-start | bytes 786440 | tf_op jit(solution)/shard_map/ppermute | solution.py:62
  140.2 8.5 %collective-permute-start.27 = (f32[192,128]{1,0:T(8,128)S(1)}, f32[192,128]{1,0:T(8,128)S(1)}, u32[]{:S(2)}, u32[]{:S(2)}) collective-permute-start(f32[192,128]{1,0:T(8,128)S(1)} %get-tuple-element.34), channel_id=1, source_target_pairs={{0,1},{1,0},{2,3},{3,2},{4,5},{5,4},{6,7},{7,6},{8,9},{9,8},{10,11... | collective-permute-start | bytes 294920 | tf_op jit(solution)/shard_map/ppermute | solution.py:62
  (13 other events, 157.8 us)

commit v9 on v7

--- a/solution.py
+++ b/solution.py
@@ -126,40 +126,29 @@
     )(pat_one, pat_two, fac_one, fac_two, par)
 
 
-def pair_up(own, other):
-    def body(a, b, one, two, sems):
-        copies = []
-        for i, ref in enumerate((a, b)):
-            copies.append(
-                pltpu.make_async_copy(ref.at[pl.ds(0, 160)], one.at[i], sems.at[2 * i])
-            )
-            copies.append(
-                pltpu.make_async_copy(ref.at[pl.ds(160, 128)], two.at[i], sems.at[2 * i + 1])
-            )
-        for copy in copies:
-            copy.start()
-        for copy in copies:
-            copy.wait()
+def gather(block, steps):
+    blocks = [block]
+    for _ in range(steps):
+        block = ring(block)
+        blocks += [block, swap(block)]
+    return blocks
+
+
+def stage(own):
+    def body(source, out, sem):
+        copy = pltpu.make_async_copy(source, out, sem)
+        copy.start()
+        copy.wait()
 
     return pl.pallas_call(
         body,
-        out_shape=[f32(2, 160, KA), f32(2, B, KA)],
-        in_specs=[HBM, ANY],
-        out_specs=[VMEM] * 2,
-        scratch_shapes=[pltpu.SemaphoreType.DMA((4,))],
+        out_shape=f32(288, KA),
+        in_specs=[ANY],
+        out_specs=VMEM,
+        scratch_shapes=[pltpu.SemaphoreType.DMA],
         compiler_params=pltpu.CompilerParams(vmem_limit_bytes=4 * MIB),
-    )(own, other)
-
-
-def gather(pair):
-    blocks = [pair]
-    going = pair
-    for step in range(4):
-        if step == 3:
-            going = going[0:1]
-        going = ring(going)
-        blocks += [going, swap(going)]
-    return blocks
+        cost_estimate=pl.CostEstimate(flops=1000, bytes_accessed=1000, transcendentals=0),
+    )(own)
 
 
 def place():
@@ -172,57 +161,54 @@
     return row, col, core, target
 
 
-def sources(refs):
+def sources(own, other, start, rows):
     col = lax.axis_index("pcol")
     z, core = lax.div(col, 2), lax.rem(col, 2)
     found = []
-    for at, ref in enumerate(refs):
-        step = (at + 1) // 2
-        swapped = at > 0 and at % 2 == 0
-        side = (1 - core) if swapped else core
-        away = jnp.where(side == 0, 8 - step, step)
-        plane = lax.rem(z + away, 8)
-        for i in range(ref.shape[0]):
-            parity = side if i == 0 else 1 - side
-            found.append((ref.at[i], plane * 2 + parity))
+    for sibling, refs in enumerate((own, other)):
+        for at, ref in enumerate(refs):
+            step = (at + 1) // 2
+            swapped = at > 0 and at % 2 == 0
+            side = (1 - core) if swapped else core
+            away = jnp.where(side == 0, 8 - step, step)
+            plane = lax.rem(z + away, 8)
+            parity = (1 - side) if sibling else side
+            found.append((ref.at[pl.ds(start, rows)], plane * 2 + parity))
     return found
 
 
-def fetch(refs, target, sems, first):
+def fetch(own, other, start, rows, target, sems, first):
     return [
         pltpu.make_async_copy(source, target.at[m], sems.at[first + k])
-        for k, (source, m) in enumerate(sources(refs))
+        for k, (source, m) in enumerate(sources(own, other, start, rows))
     ]
 
 
 def turn_kernel(parent, *refs):
-    first, second, turn, sems = refs[:9], refs[9:18], refs[18], refs[19]
+    own, other, turn, sems = refs[:7], refs[7:16], refs[16], refs[17]
     row, col, core, target = place()
-    wanted = ((first, parent[target]), (first, target), (second, target))
-    for k, (blocks, which) in enumerate(wanted):
-        for source, m in sources(blocks):
+    for k, (start_row, which) in enumerate(((0, parent[target]), (0, target), (160, target))):
+        for source, m in sources(own, other, start_row, B):
 
             @pl.when(m == which)
             def start():
-                pltpu.make_async_copy(
-                    source.at[pl.ds(0, 128)], turn.at[pl.ds(128 * k, 128)], sems.at[k]
-                ).start()
+                pltpu.make_async_copy(source, turn.at[pl.ds(B * k, B)], sems.at[k]).start()
 
     for k in range(3):
-        part = turn.at[pl.ds(128 * k, 128)]
+        part = turn.at[pl.ds(B * k, B)]
         pltpu.make_async_copy(part, part, sems.at[k]).wait()
 
 
-def pick_turn(parent, first, second):
+def pick_turn(parent, own, other):
     return pl.pallas_call(
         turn_kernel,
         out_shape=f32(384, KA),
-        in_specs=[SMEM] + [ANY] * 18,
+        in_specs=[SMEM] + [ANY] * 16,
         out_specs=VMEM,
         scratch_shapes=[pltpu.SemaphoreType.DMA((3,))],
         compiler_params=pltpu.CompilerParams(vmem_limit_bytes=4 * MIB),
         cost_estimate=pl.CostEstimate(flops=1000, bytes_accessed=1000, transcendentals=0),
-    )(parent, *first, *second)
+    )(parent, *own, *other)
 
 
 def products(ginv, level, at, row, core, half, left, outs):
@@ -236,12 +222,12 @@
 
 
 def send_kernel(parent, ginv, turn, *refs):
-    first, second, refs = refs[:9], refs[9:18], refs[18:]
+    own, other, refs = refs[:7], refs[7:16], refs[16:]
     sends, one, two, left, block, sems = refs[0:2], *refs[2:]
     row, col, core, target = place()
     load = pltpu.make_async_copy(ginv, block, sems.at[32])
-    low = fetch(first, one, sems, 0)
-    high = fetch(second, two, sems, 16)
+    low = fetch(own, other, 0, 160, one, sems, 0)
+    high = fetch(own, other, 160, B, two, sems, 16)
     for copy in [load] + low + high:
         copy.start()
     load.wait()
@@ -261,7 +247,7 @@
     return pl.pallas_call(
         send_kernel,
         out_shape=[f32(8, B, KA)] * 2 + [f32(16, 160, KA), f32(16, B, KA)],
-        in_specs=[SMEM, HBM] + [ANY] * 19,
+        in_specs=[SMEM, HBM] + [ANY] * 17,
         out_specs=[VMEM] * 4,
         scratch_shapes=[
             pltpu.VMEM((512, KA), jnp.float32),
@@ -439,11 +425,10 @@
     dinv_two,
 ):
     own = prepare(pattern_one.T, pattern_two.T, factor_one, factor_two, factor_parent)
-    pair_one, pair_two = pair_up(own, swap(own))
-    blocks_one = gather(pair_one)
-    blocks_two = gather(pair_two)
-    turn = pick_turn(parent, blocks_one, blocks_two)
-    send_a, send_b, one, two = send_half(parent, ginv_anc, turn, blocks_one, blocks_two)
+    blocks_own = gather(stage(own), 3)
+    blocks_other = gather(swap(own), 4)
+    turn = pick_turn(parent, blocks_own, blocks_other)
+    send_a, send_b, one, two = send_half(parent, ginv_anc, turn, blocks_own, blocks_other)
     turn = permute(turn, lambda r, c: (r ^ spread_mask(c), c))
     got = [row_step(send_a, 0, 0), row_step(send_b, 1, 0)]
     keep_a, keep_b, par, base = keep_half(

time: 169 us -> 167 us (0.988)
  starting transfers between devices: 62.1 us -> 59.2 us
    ppermute x32 -> x30, starting transfers between devices: 62.1 us -> 59.2 us  [permute(): return lax.ppermute(value, ALL, pairs)]
    ppermute x32 -> x30, waiting for transfers between devices: 84.7 us -> 85.8 us  [permute(): return lax.ppermute(value, ALL, pairs)]
  transfers between devices with their start and end apart: 32 -> 30, of which waited for: 20 -> 20; matrix products, arithmetic and copies ran while one was open for 0% -> 0% of each run, Pallas kernels for 8% -> 9%
where the time goes in v9:
time: 167 us; the launch traced here: 166 us
  waiting for transfers between devices  85.8 us (51%)
  starting transfers between devices  59.2 us (35%)
  Pallas kernels  19.4 us (12%)
    ppermute x30, waiting for transfers between devices, permute(): return lax.ppermute(value, ALL, pairs)  85.8 us
    ppermute x30, starting transfers between devices, permute(): return lax.ppermute(value, ALL, pairs)  59.2 us
    pallas_call x1, Pallas kernels, send_half(): pl.pallas_call(send_kernel, out_shape=[f32(8, B, KA)] * 2 + [f32(16, 160,...  8.85 us
    pallas_call x1, Pallas kernels, keep_half(): pl.pallas_call(body, out_shape=[f32(8, B, KA)] * 2 + [f32(B, B), f32(192,...  4.39 us
  transfers between devices with their start and end apart: 30, of which 20 were waited for; matrix products, arithmetic and copies ran while one was open for 0% of the time, Pallas kernels for 9%

profile of v9, /device:TPU:7, one launch (start us, length us, event | category | flops | bytes accessed | tf_op | source)
XLA Modules:
  0.0 166.4 jit_solution(14063408312975962332)
XLA Ops:
  5.5 5.6 %collective-permute-start.7 = (f32[288,512]{1,0:T(8,128)S(1)}, f32[288,512]{1,0:T(8,128)S(1)}, u32[]{:S(2)}, u32[]{:S(2)}) collective-permute-start(f32[288,512]{1,0:T(8,128)S(1)} %collective-permute-done.6.refs_7_), channel_id=1, source_target_pairs={{0,2},{1,15},{2,4},{3,1},{4,6},{5,3},{6,8},{7,5},{8,10},{9,7},{10,... | collective-permute-start | bytes 1769480 | tf_op jit(solution)/shard_map/ppermute | solution.py:62
  13.1 4.8 %collective-permute-done.7.refs_8_ = f32[288,512]{1,0:T(8,128)S(1)} collective-permute-done((f32[288,512]{1,0:T(8,128)S(1)}, f32[288,512]{1,0:T(8,128)S(1)}, u32[]{:S(2)}, u32[]{:S(2)}) %collective-permute-start.7) | collective-permute-done | bytes 589856 | tf_op jit(solution)/shard_map/ppermute | solution.py:62
  17.9 3.1 %collective-permute-start.9 = (f32[288,512]{1,0:T(8,128)S(1)}, f32[288,512]{1,0:T(8,128)S(1)}, u32[]{:S(2)}, u32[]{:S(2)}) collective-permute-start(f32[288,512]{1,0:T(8,128)S(1)} %collective-permute-done.7.refs_8_), channel_id=1, source_target_pairs={{0,2},{1,15},{2,4},{3,1},{4,6},{5,3},{6,8},{7,5},{8,10},{9,7},{10,... | collective-permute-start | bytes 1769480 | tf_op jit(solution)/shard_map/ppermute | solution.py:62
  21.0 3.2 %collective-permute-done.refs_1_ = f32[288,512]{1,0:T(8,128)S(1)} collective-permute-done((f32[288,512]{1,0:T(8,128)S(1)}, f32[288,512]{1,0:T(8,128)S(1)}, u32[]{:S(2)}, u32[]{:S(2)}) %collective-permute-start) | collective-permute-done | bytes 589856 | tf_op jit(solution)/shard_map/ppermute | solution.py:62
  24.2 3.1 %collective-permute-start.2 = (f32[288,512]{1,0:T(8,128)S(1)}, f32[288,512]{1,0:T(8,128)S(1)}, u32[]{:S(2)}, u32[]{:S(2)}) collective-permute-start(f32[288,512]{1,0:T(8,128)S(1)} %collective-permute-done.refs_1_), channel_id=1, source_target_pairs={{0,2},{1,15},{2,4},{3,1},{4,6},{5,3},{6,8},{7,5},{8,10},{9,7},{10,... | collective-permute-start | bytes 1769480 | tf_op jit(solution)/shard_map/ppermute | solution.py:62
  27.4 3.2 %collective-permute-done.9.refs_10_ = f32[288,512]{1,0:T(8,128)S(1)} collective-permute-done((f32[288,512]{1,0:T(8,128)S(1)}, f32[288,512]{1,0:T(8,128)S(1)}, u32[]{:S(2)}, u32[]{:S(2)}) %collective-permute-start.9) | collective-permute-done | bytes 589856 | tf_op jit(solution)/shard_map/ppermute | solution.py:62
  30.6 3.1 %collective-permute-start.11 = (f32[288,512]{1,0:T(8,128)S(1)}, f32[288,512]{1,0:T(8,128)S(1)}, u32[]{:S(2)}, u32[]{:S(2)}) collective-permute-start(f32[288,512]{1,0:T(8,128)S(1)} %collective-permute-done.9.refs_10_), channel_id=1, source_target_pairs={{0,2},{1,15},{2,4},{3,1},{4,6},{5,3},{6,8},{7,5},{8,10},{9,7},{10,... | collective-permute-start | bytes 1769480 | tf_op jit(solution)/shard_map/ppermute | solution.py:62
  33.7 3.2 %collective-permute-done.2.refs_3_ = f32[288,512]{1,0:T(8,128)S(1)} collective-permute-done((f32[288,512]{1,0:T(8,128)S(1)}, f32[288,512]{1,0:T(8,128)S(1)}, u32[]{:S(2)}, u32[]{:S(2)}) %collective-permute-start.2) | collective-permute-done | bytes 589856 | tf_op jit(solution)/shard_map/ppermute | solution.py:62
  36.9 3.1 %collective-permute-start.4 = (f32[288,512]{1,0:T(8,128)S(1)}, f32[288,512]{1,0:T(8,128)S(1)}, u32[]{:S(2)}, u32[]{:S(2)}) collective-permute-start(f32[288,512]{1,0:T(8,128)S(1)} %collective-permute-done.2.refs_3_), channel_id=1, source_target_pairs={{0,2},{1,15},{2,4},{3,1},{4,6},{5,3},{6,8},{7,5},{8,10},{9,7},{10,... | collective-permute-start | bytes 1769480 | tf_op jit(solution)/shard_map/ppermute | solution.py:62
  40.0 3.2 %collective-permute-done.11.refs_12_ = f32[288,512]{1,0:T(8,128)S(1)} collective-permute-done((f32[288,512]{1,0:T(8,128)S(1)}, f32[288,512]{1,0:T(8,128)S(1)}, u32[]{:S(2)}, u32[]{:S(2)}) %collective-permute-start.11) | collective-permute-done | bytes 589856 | tf_op jit(solution)/shard_map/ppermute | solution.py:62
  51.2 4.6 %collective-permute-done.13.refs_14_ = f32[288,512]{1,0:T(8,128)S(1)} collective-permute-done((f32[288,512]{1,0:T(8,128)S(1)}, f32[288,512]{1,0:T(8,128)S(1)}, u32[]{:S(2)}, u32[]{:S(2)}) %collective-permute-start.13) | collective-permute-done | bytes 589856 | tf_op jit(solution)/shard_map/ppermute | solution.py:62
  60.2 6.0 %collective-permute-start.15 = (f32[384,512]{1,0:T(8,128)S(1)}, f32[384,512]{1,0:T(8,128)S(1)}, u32[]{:S(2)}, u32[]{:S(2)}) collective-permute-start(f32[384,512]{1,0:T(8,128)S(1)} %shard_map.130.turn), channel_id=1, source_target_pairs={{0,0},{1,161},{2,18},{3,179},{4,100},{5,197},{6,118},{7,215},{8,40... | collective-permute-start | bytes 2359304 | tf_op jit(solution)/shard_map/ppermute | solution.py:62
  66.2 8.8 %shard_map.131 = (f32[8,128,512]{2,1,0:T(8,128)S(1)}, f32[8,128,512]{2,1,0:T(8,128)S(1)}, f32[16,160,512]{2,1,0:T(8,128)S(1)}, f32[16,128,512]{2,1,0:T(8,128)S(1)}) custom-call(s32[16]{0:T(128)S(1)} %copy-done.1, f32[512,512]{1,0:T(8,128)S(1)} %copy-done.2, f32[384,512]{1,0:T(8,128)S(1)} %shard_map.130.turn, f32[288,512]{1,0:T(8,128)S(1)} %shard_map.129.refs_0_, ...), custom_call_target="tpu_custom_call" | custom-call | flops 20000000000 | bytes 1000000 | tf_op jit(solution)/shard_map/pallas_call | solution.py:247
  77.1 4.4 %shard_map.132 = (f32[8,128,512]{2,1,0:T(8,128)S(1)}, f32[8,128,512]{2,1,0:T(8,128)S(1)}, f32[128,128]{1,0:T(8,128)S(1)}, f32[192,128]{1,0:T(8,128)S(1)}) custom-call(s32[16]{0:T(128)S(1)} %copy-done.1, f32[512,512]{1,0:T(8,128)S(1)} %copy-done.2, f32[16,160,512]{2,1,0:T(8,128)S(1)} %get-tuple-element.20.one, f32[16,128,512]{2,1,0:T(8,128)S(1)} %get-tuple-element.21.two, ...), custom_call_target="tpu_custom_call" | custom-call | flops 60000002048 | bytes 1000000 | tf_op jit(solution)/shard_map/pallas_call | solution.py:274
  81.5 19.7 %collective-permute-done.20.b = f32[8,128,512]{2,1,0:T(8,128)S(1)} collective-permute-done((f32[8,128,512]{2,1,0:T(8,128)S(1)}, f32[8,128,512]{2,1,0:T(8,128)S(1)}, u32[]{:S(2)}, u32[]{:S(2)}) %collective-permute-start.20) | collective-permute-done | bytes 2097184 | tf_op jit(solution)/shard_map/ppermute | solution.py:62
  103.1 5.4 %collective-permute-start.23 = (f32[384,512]{1,0:T(8,128)S(1)}, f32[384,512]{1,0:T(8,128)S(1)}, u32[]{:S(2)}, u32[]{:S(2)}) collective-permute-start(f32[384,512]{1,0:T(8,128)S(1)} %collective-permute-done.15.refs_0_), channel_id=1, source_target_pairs={{0,0},{1,10},{2,1},{3,11},{4,6},{5,12},{6,7},{7,13},{8,2},{9,8},{1... | collective-permute-start | bytes 2359304 | tf_op jit(solution)/shard_map/ppermute | solution.py:62
  108.7 6.6 %collective-permute-done.21.b = f32[4,128,512]{2,1,0:T(8,128)S(1)} collective-permute-done((f32[4,128,512]{2,1,0:T(8,128)S(1)}, f32[4,128,512]{2,1,0:T(8,128)S(1)}, u32[]{:S(2)}, u32[]{:S(2)}) %collective-permute-start.21) | collective-permute-done | bytes 1048608 | tf_op jit(solution)/shard_map/ppermute | solution.py:62
  117.8 8.6 %collective-permute-done.23.refs_0_.turn = f32[384,512]{1,0:T(8,128)S(1)} collective-permute-done((f32[384,512]{1,0:T(8,128)S(1)}, f32[384,512]{1,0:T(8,128)S(1)}, u32[]{:S(2)}, u32[]{:S(2)}) %collective-permute-start.23) | collective-permute-done | bytes 786464 | tf_op jit(solution)/shard_map/ppermute | solution.py:62
  128.6 3.5 %collective-permute-done.24.b = f32[1,128,512]{2,1,0:T(8,128)S(1)} collective-permute-done((f32[1,128,512]{2,1,0:T(8,128)S(1)}, f32[1,128,512]{2,1,0:T(8,128)S(1)}, u32[]{:S(2)}, u32[]{:S(2)}) %collective-permute-start.24) | collective-permute-done | bytes 262176 | tf_op jit(solution)/shard_map/ppermute | solution.py:62
  136.0 8.8 %collective-permute-start.25 = (f32[192,128]{1,0:T(8,128)S(1)}, f32[192,128]{1,0:T(8,128)S(1)}, u32[]{:S(2)}, u32[]{:S(2)}) collective-permute-start(f32[192,128]{1,0:T(8,128)S(1)} %get-tuple-element.30), channel_id=1, source_target_pairs={{0,1},{1,0},{2,3},{3,2},{4,5},{5,4},{6,7},{7,6},{8,9},{9,8},{10,11... | collective-permute-start | bytes 294920 | tf_op jit(solution)/shard_map/ppermute | solution.py:62
  145.9 4.0 %collective-permute-done.26 = f32[192,128]{1,0:T(8,128)S(1)} collective-permute-done((f32[192,128]{1,0:T(8,128)S(1)}, f32[192,128]{1,0:T(8,128)S(1)}, u32[]{:S(2)}, u32[]{:S(2)}) %collective-permute-start.26) | collective-permute-done | bytes 98336 | tf_op jit(solution)/shard_map/ppermute | solution.py:62
  150.0 5.4 %collective-permute-done.27 = f32[192,128]{1,0:T(8,128)S(1)} collective-permute-done((f32[192,128]{1,0:T(8,128)S(1)}, f32[192,128]{1,0:T(8,128)S(1)}, u32[]{:S(2)}, u32[]{:S(2)}) %collective-permute-start.27) | collective-permute-done | bytes 98336 | tf_op jit(solution)/shard_map/ppermute | solution.py:62
  156.5 3.7 %collective-permute-done.28.second = f32[192,128]{1,0:T(8,128)S(1)} collective-permute-done((f32[192,128]{1,0:T(8,128)S(1)}, f32[192,128]{1,0:T(8,128)S(1)}, u32[]{:S(2)}, u32[]{:S(2)}) %collective-permute-start.28) | collective-permute-done | bytes 98336 | tf_op jit(solution)/shard_map/ppermute | solution.py:62
  160.5 4.3 %collective-permute-start.29 = (f32[192,128]{1,0:T(8,128)S(1)}, f32[192,128]{1,0:T(8,128)S(1)}, u32[]{:S(2)}, u32[]{:S(2)}) collective-permute-start(f32[192,128]{1,0:T(8,128)S(1)} %shard_map.148.own), channel_id=1, source_target_pairs={{0,1},{1,0},{2,3},{3,2},{4,5},{5,4},{6,7},{7,6},{8,9},{9,8},{10,11... | collective-permute-start | bytes 294920 | tf_op jit(solution)/shard_map/ppermute | solution.py:62
  (71 shorter events, 36.0 us)
Async XLA Ops:
  5.5 12.4 %collective-permute-start.7 = (f32[288,512]{1,0:T(8,128)S(1)}, f32[288,512]{1,0:T(8,128)S(1)}, u32[]{:S(2)}, u32[]{:S(2)}) collective-permute-start(f32[288,512]{1,0:T(8,128)S(1)} %collective-permute-done.6.refs_7_), channel_id=1, source_target_pairs={{0,2},{1,15},{2,4},{3,1},{4,6},{5,3},{6,8},{7,5},{8,10},{9,7},{10,... | collective-permute-start | bytes 1769480 | tf_op jit(solution)/shard_map/ppermute | solution.py:62
  12.3 11.9 %collective-permute-start = (f32[288,512]{1,0:T(8,128)S(1)}, f32[288,512]{1,0:T(8,128)S(1)}, u32[]{:S(2)}, u32[]{:S(2)}) collective-permute-start(f32[288,512]{1,0:T(8,128)S(1)} %shard_map.129.refs_0_), channel_id=1, source_target_pairs={{0,2},{1,15},{2,4},{3,1},{4,6},{5,3},{6,8},{7,5},{8,10},{9,7},{10,... | collective-permute-start | bytes 1769480 | tf_op jit(solution)/shard_map/ppermute | solution.py:62
  17.9 12.6 %collective-permute-start.9 = (f32[288,512]{1,0:T(8,128)S(1)}, f32[288,512]{1,0:T(8,128)S(1)}, u32[]{:S(2)}, u32[]{:S(2)}) collective-permute-start(f32[288,512]{1,0:T(8,128)S(1)} %collective-permute-done.7.refs_8_), channel_id=1, source_target_pairs={{0,2},{1,15},{2,4},{3,1},{4,6},{5,3},{6,8},{7,5},{8,10},{9,7},{10,... | collective-permute-start | bytes 1769480 | tf_op jit(solution)/shard_map/ppermute | solution.py:62
  24.2 12.6 %collective-permute-start.2 = (f32[288,512]{1,0:T(8,128)S(1)}, f32[288,512]{1,0:T(8,128)S(1)}, u32[]{:S(2)}, u32[]{:S(2)}) collective-permute-start(f32[288,512]{1,0:T(8,128)S(1)} %collective-permute-done.refs_1_), channel_id=1, source_target_pairs={{0,2},{1,15},{2,4},{3,1},{4,6},{5,3},{6,8},{7,5},{8,10},{9,7},{10,... | collective-permute-start | bytes 1769480 | tf_op jit(solution)/shard_map/ppermute | solution.py:62
  30.6 12.6 %collective-permute-start.11 = (f32[288,512]{1,0:T(8,128)S(1)}, f32[288,512]{1,0:T(8,128)S(1)}, u32[]{:S(2)}, u32[]{:S(2)}) collective-permute-start(f32[288,512]{1,0:T(8,128)S(1)} %collective-permute-done.9.refs_10_), channel_id=1, source_target_pairs={{0,2},{1,15},{2,4},{3,1},{4,6},{5,3},{6,8},{7,5},{8,10},{9,7},{10,... | collective-permute-start | bytes 1769480 | tf_op jit(solution)/shard_map/ppermute | solution.py:62
  33.7 12.6 %collective-permute-start.1 = (f32[288,512]{1,0:T(8,128)S(1)}, f32[288,512]{1,0:T(8,128)S(1)}, u32[]{:S(2)}, u32[]{:S(2)}) collective-permute-start(f32[288,512]{1,0:T(8,128)S(1)} %collective-permute-done.refs_1_), channel_id=1, source_target_pairs={{0,1},{1,0},{2,3},{3,2},{4,5},{5,4},{6,7},{7,6},{8,9},{9,8},{10,11... | collective-permute-start | bytes 1769480 | tf_op jit(solution)/shard_map/ppermute | solution.py:62
  36.9 12.6 %collective-permute-start.4 = (f32[288,512]{1,0:T(8,128)S(1)}, f32[288,512]{1,0:T(8,128)S(1)}, u32[]{:S(2)}, u32[]{:S(2)}) collective-permute-start(f32[288,512]{1,0:T(8,128)S(1)} %collective-permute-done.2.refs_3_), channel_id=1, source_target_pairs={{0,2},{1,15},{2,4},{3,1},{4,6},{5,3},{6,8},{7,5},{8,10},{9,7},{10,... | collective-permute-start | bytes 1769480 | tf_op jit(solution)/shard_map/ppermute | solution.py:62
  40.0 11.2 %collective-permute-start.3 = (f32[288,512]{1,0:T(8,128)S(1)}, f32[288,512]{1,0:T(8,128)S(1)}, u32[]{:S(2)}, u32[]{:S(2)}) collective-permute-start(f32[288,512]{1,0:T(8,128)S(1)} %collective-permute-done.2.refs_3_), channel_id=1, source_target_pairs={{0,1},{1,0},{2,3},{3,2},{4,5},{5,4},{6,7},{7,6},{8,9},{9,8},{10,11... | collective-permute-start | bytes 1769480 | tf_op jit(solution)/shard_map/ppermute | solution.py:62
  43.2 12.6 %collective-permute-start.13 = (f32[288,512]{1,0:T(8,128)S(1)}, f32[288,512]{1,0:T(8,128)S(1)}, u32[]{:S(2)}, u32[]{:S(2)}) collective-permute-start(f32[288,512]{1,0:T(8,128)S(1)} %collective-permute-done.11.refs_12_), channel_id=1, source_target_pairs={{0,2},{1,15},{2,4},{3,1},{4,6},{5,3},{6,8},{7,5},{8,10},{9,7},{10,... | collective-permute-start | bytes 1769480 | tf_op jit(solution)/shard_map/ppermute | solution.py:62
  46.3 11.2 %collective-permute-start.8 = (f32[288,512]{1,0:T(8,128)S(1)}, f32[288,512]{1,0:T(8,128)S(1)}, u32[]{:S(2)}, u32[]{:S(2)}) collective-permute-start(f32[288,512]{1,0:T(8,128)S(1)} %collective-permute-done.7.refs_8_), channel_id=1, source_target_pairs={{0,1},{1,0},{2,3},{3,2},{4,5},{5,4},{6,7},{7,6},{8,9},{9,8},{10,11... | collective-permute-start | bytes 1769480 | tf_op jit(solution)/shard_map/ppermute | solution.py:62
  46.3 11.2 %collective-permute-start.10 = (f32[288,512]{1,0:T(8,128)S(1)}, f32[288,512]{1,0:T(8,128)S(1)}, u32[]{:S(2)}, u32[]{:S(2)}) collective-permute-start(f32[288,512]{1,0:T(8,128)S(1)} %collective-permute-done.9.refs_10_), channel_id=1, source_target_pairs={{0,1},{1,0},{2,3},{3,2},{4,5},{5,4},{6,7},{7,6},{8,9},{9,8},{10,11... | collective-permute-start | bytes 1769480 | tf_op jit(solution)/shard_map/ppermute | solution.py:62
  49.5 8.0 %collective-permute-start.5 = (f32[288,512]{1,0:T(8,128)S(1)}, f32[288,512]{1,0:T(8,128)S(1)}, u32[]{:S(2)}, u32[]{:S(2)}) collective-permute-start(f32[288,512]{1,0:T(8,128)S(1)} %collective-permute-done.4.refs_5_), channel_id=1, source_target_pairs={{0,1},{1,0},{2,3},{3,2},{4,5},{5,4},{6,7},{7,6},{8,9},{9,8},{10,11... | collective-permute-start | bytes 1769480 | tf_op jit(solution)/shard_map/ppermute | solution.py:62
  51.2 6.3 %collective-permute-start.12 = (f32[288,512]{1,0:T(8,128)S(1)}, f32[288,512]{1,0:T(8,128)S(1)}, u32[]{:S(2)}, u32[]{:S(2)}) collective-permute-start(f32[288,512]{1,0:T(8,128)S(1)} %collective-permute-done.11.refs_12_), channel_id=1, source_target_pairs={{0,1},{1,0},{2,3},{3,2},{4,5},{5,4},{6,7},{7,6},{8,9},{9,8},{10,11... | collective-permute-start | bytes 1769480 | tf_op jit(solution)/shard_map/ppermute | solution.py:62
  60.2 17.0 %collective-permute-start.15 = (f32[384,512]{1,0:T(8,128)S(1)}, f32[384,512]{1,0:T(8,128)S(1)}, u32[]{:S(2)}, u32[]{:S(2)}) collective-permute-start(f32[384,512]{1,0:T(8,128)S(1)} %shard_map.130.turn), channel_id=1, source_target_pairs={{0,0},{1,161},{2,18},{3,179},{4,100},{5,197},{6,118},{7,215},{8,40... | collective-permute-start | bytes 2359304 | tf_op jit(solution)/shard_map/ppermute | solution.py:62
  75.0 26.2 %collective-permute-start.20 = (f32[8,128,512]{2,1,0:T(8,128)S(1)}, f32[8,128,512]{2,1,0:T(8,128)S(1)}, u32[]{:S(2)}, u32[]{:S(2)}) collective-permute-start(f32[8,128,512]{2,1,0:T(8,128)S(1)} %get-tuple-element.25), channel_id=1, source_target_pairs={{0,48},{1,193},{2,50},{3,195},{4,52},{5,197},{6,54},{7,199},{8,56}... | collective-permute-start | bytes 6291464 | tf_op jit(solution)/shard_map/ppermute | solution.py:62
  75.9 25.5 %collective-permute-start.16 = (f32[8,128,512]{2,1,0:T(8,128)S(1)}, f32[8,128,512]{2,1,0:T(8,128)S(1)}, u32[]{:S(2)}, u32[]{:S(2)}) collective-permute-start(f32[8,128,512]{2,1,0:T(8,128)S(1)} %get-tuple-element.23), channel_id=1, source_target_pairs={{0,16},{1,65},{2,18},{3,67},{4,20},{5,69},{6,22},{7,71},{8,24},{9,... | collective-permute-start | bytes 6291464 | tf_op jit(solution)/shard_map/ppermute | solution.py:62
  101.3 14.0 %collective-permute-start.21 = (f32[4,128,512]{2,1,0:T(8,128)S(1)}, f32[4,128,512]{2,1,0:T(8,128)S(1)}, u32[]{:S(2)}, u32[]{:S(2)}) collective-permute-start(f32[4,128,512]{2,1,0:T(8,128)S(1)} %shard_map.141), channel_id=1, source_target_pairs={{0,16},{1,65},{2,18},{3,67},{4,20},{5,69},{6,22},{7,71},{8,24},{9,... | collective-permute-start | bytes 3145736 | tf_op jit(solution)/shard_map/ppermute | solution.py:62
  101.5 15.8 %collective-permute-start.17 = (f32[4,128,512]{2,1,0:T(8,128)S(1)}, f32[4,128,512]{2,1,0:T(8,128)S(1)}, u32[]{:S(2)}, u32[]{:S(2)}) collective-permute-start(f32[4,128,512]{2,1,0:T(8,128)S(1)} %shard_map.134), channel_id=1, source_target_pairs={{0,48},{1,193},{2,50},{3,195},{4,52},{5,197},{6,54},{7,199},{8,56}... | collective-permute-start | bytes 3145736 | tf_op jit(solution)/shard_map/ppermute | solution.py:62
  103.1 23.3 %collective-permute-start.23 = (f32[384,512]{1,0:T(8,128)S(1)}, f32[384,512]{1,0:T(8,128)S(1)}, u32[]{:S(2)}, u32[]{:S(2)}) collective-permute-start(f32[384,512]{1,0:T(8,128)S(1)} %collective-permute-done.15.refs_0_), channel_id=1, source_target_pairs={{0,0},{1,10},{2,1},{3,11},{4,6},{5,12},{6,7},{7,13},{8,2},{9,8},{1... | collective-permute-start | bytes 2359304 | tf_op jit(solution)/shard_map/ppermute | solution.py:62
  115.4 11.0 %collective-permute-start.22 = (f32[2,128,512]{2,1,0:T(8,128)S(1)}, f32[2,128,512]{2,1,0:T(8,128)S(1)}, u32[]{:S(2)}, u32[]{:S(2)}) collective-permute-start(f32[2,128,512]{2,1,0:T(8,128)S(1)} %shard_map.143), channel_id=1, source_target_pairs={{0,192},{1,49},{2,194},{3,51},{4,196},{5,53},{6,198},{7,55},{8,200... | collective-permute-start | bytes 1572872 | tf_op jit(solution)/shard_map/ppermute | solution.py:62
  117.4 11.0 %collective-permute-start.18 = (f32[2,128,512]{2,1,0:T(8,128)S(1)}, f32[2,128,512]{2,1,0:T(8,128)S(1)}, u32[]{:S(2)}, u32[]{:S(2)}) collective-permute-start(f32[2,128,512]{2,1,0:T(8,128)S(1)} %shard_map.136), channel_id=1, source_target_pairs={{0,64},{1,17},{2,66},{3,19},{4,68},{5,21},{6,70},{7,23},{8,72},{9,... | collective-permute-start | bytes 1572872 | tf_op jit(solution)/shard_map/ppermute | solution.py:62
  126.4 5.7 %collective-permute-start.24 = (f32[1,128,512]{2,1,0:T(8,128)S(1)}, f32[1,128,512]{2,1,0:T(8,128)S(1)}, u32[]{:S(2)}, u32[]{:S(2)}) collective-permute-start(f32[1,128,512]{2,1,0:T(8,128)S(1)} %shard_map.145), channel_id=1, source_target_pairs={{0,64},{1,17},{2,66},{3,19},{4,68},{5,21},{6,70},{7,23},{8,72},{9,... | collective-permute-start | bytes 786440 | tf_op jit(solution)/shard_map/ppermute | solution.py:62
  128.4 6.5 %collective-permute-start.19 = (f32[1,128,512]{2,1,0:T(8,128)S(1)}, f32[1,128,512]{2,1,0:T(8,128)S(1)}, u32[]{:S(2)}, u32[]{:S(2)}) collective-permute-start(f32[1,128,512]{2,1,0:T(8,128)S(1)} %shard_map.138), channel_id=1, source_target_pairs={{0,192},{1,49},{2,194},{3,51},{4,196},{5,53},{6,198},{7,55},{8,200... | collective-permute-start | bytes 786440 | tf_op jit(solution)/shard_map/ppermute | solution.py:62
  136.0 9.8 %collective-permute-start.25 = (f32[192,128]{1,0:T(8,128)S(1)}, f32[192,128]{1,0:T(8,128)S(1)}, u32[]{:S(2)}, u32[]{:S(2)}) collective-permute-start(f32[192,128]{1,0:T(8,128)S(1)} %get-tuple-element.30), channel_id=1, source_target_pairs={{0,1},{1,0},{2,3},{3,2},{4,5},{5,4},{6,7},{7,6},{8,9},{9,8},{10,11... | collective-permute-start | bytes 294920 | tf_op jit(solution)/shard_map/ppermute | solution.py:62
  (11 other events, 173.0 us)

commit v10 on v9

--- a/solution.py
+++ b/solution.py
@@ -273,7 +273,7 @@
 
     return pl.pallas_call(
         body,
-        out_shape=[f32(8, B, KA)] * 2 + [f32(B, B), f32(192, B)],
+        out_shape=[f32(8, B, KA)] * 2 + [f32(B, B), f32(384, B)],
         in_specs=[SMEM] + [VMEM] * 3 + [HBM] * 2 + [ANY] * len(order),
         out_specs=[VMEM] * 4,
         scratch_shapes=[
@@ -289,7 +289,6 @@
 
 
 def base_parts(parent, one, dinv_one, dinv_two, par_out, base, dinv, sems, row, core):
-    top = pl.multiple_of(core * 64, 64)
     sources = (
         dinv_one.at[pl.ds(pl.multiple_of(row * B, B), B)],
         dinv_one.at[pl.ds(pl.multiple_of(parent[row] * B, B), B)],
@@ -303,21 +302,28 @@
     par_out[...] = unpack(one[row, 128:160, :])
     for copy in copies:
         copy.wait()
-    base[0:64, :] = dinv[0, pl.ds(top, 64), :]
-    base[64:128, :] = -jnp.dot(
-        par_out[pl.ds(top, 64), :],
+    base[0:128, :] = dinv[0]
+    side = -jnp.dot(
+        par_out[...],
         dinv[1],
         precision=lax.Precision.HIGHEST,
         preferred_element_type=jnp.float32,
     )
-    base[128:192, :] = dinv[2, pl.ds(top, 64), :]
+    base[128:256, :] = side
+    base[256:384, :] = dinv[2] - lax.dot_general(
+        side,
+        par_out[...],
+        (((1,), (1,)), ((), ())),
+        precision=lax.Precision.HIGHEST,
+        preferred_element_type=jnp.float32,
+    )
 
 
 def row_step(value, variant, step):
     return permute(value, lambda r, c: (r ^ MASKS[c % 2][variant][step], c))
 
 
-def block_kernel(a_ref, b_ref, turn, one_out, two_out, send_out, keep_out, sums):
+def block_kernel(a_ref, b_ref, turn, par, one_out, two_out, send_out, keep_out, sums):
     core = lax.rem(lax.axis_index("pcol"), 2)
     for variant, ref in enumerate((a_ref, b_ref)):
         one_out[64 * variant : 64 * variant + 64, :] = ref[0:64, :]
@@ -325,25 +331,31 @@
     one = split(one_out[...])
     two = split(two_out[...])
     nt = ((1,), (1,))
-    for i, (left, right) in enumerate(
-        ((one, turn[128:256, :]), (two, turn[0:128, :]), (two, turn[256:384, :]))
-    ):
-        value = dot_split(left, split(right), nt)
-        sums[0, 64 * i : 64 * i + 64, :] = value[0:64]
-        sums[1, 64 * i : 64 * i + 64, :] = value[64:128]
+    upper = dot_split(one, split(turn[128:256, :]), nt)
+    side = dot_split(two, split(turn[0:128, :]), nt)
+    lower = dot_split(two, split(turn[256:384, :]), nt)
+    lower = lower - dot_split(split(side), split(par[...]), nt)
+    i = lax.broadcasted_iota(jnp.int32, (B, B), 0)
+    j = lax.broadcasted_iota(jnp.int32, (B, B), 1)
+    both = jnp.where(i >= j, upper, lower)
+    middle = jnp.sum(jnp.where(i == j, lower, 0.0), axis=0, keepdims=True)
+    for half in range(2):
+        sums[half, 0:64, :] = both[64 * half : 64 * half + 64]
+        sums[half, 64:128, :] = side[64 * half : 64 * half + 64]
+        sums[half, 128:136, :] = jnp.broadcast_to(middle, (8, B))
     keep_out[...] = sums[core]
     send_out[...] = sums[1 - core]
 
 
-def blocks_of(parts, turn):
+def blocks_of(parts, turn, par):
     return pl.pallas_call(
         block_kernel,
-        out_shape=[f32(B, KA), f32(B, KA), f32(192, B), f32(192, B)],
-        in_specs=[VMEM] * 3,
+        out_shape=[f32(B, KA), f32(B, KA), f32(136, B), f32(136, B)],
+        in_specs=[VMEM] * 4,
         out_specs=[VMEM] * 4,
-        scratch_shapes=[pltpu.VMEM((2, 192, B), jnp.float32)],
+        scratch_shapes=[pltpu.VMEM((2, 136, B), jnp.float32)],
         compiler_params=pltpu.CompilerParams(vmem_limit_bytes=8 * MIB),
-    )(*parts, turn)
+    )(*parts, turn, par)
 
 
 def add(part, kept, got, order=()):
@@ -367,50 +379,31 @@
     )(kept, got, *order)
 
 
-def final_kernel(base, par, first, second, out):
-    total = first[...] + second[...]
-    out[0:64, :] = base[0:64, :] - total[0:64, :]
-    cross = base[64:128, :] - total[64:128, :]
-    out[64:128, :] = cross
-    out[128:192, :] = base[128:192, :] - (
-        total[128:192, :]
-        + lax.dot_general(
-            cross,
-            par[...],
-            (((1,), (1,)), ((), ())),
-            precision=lax.Precision.HIGHEST,
-            preferred_element_type=jnp.float32,
-        )
-    )
-
-
-def final_of(base, par, first, second):
-    return pl.pallas_call(
-        final_kernel,
-        out_shape=f32(192, B),
-        in_specs=[VMEM] * 4,
-        out_specs=VMEM,
-        compiler_params=pltpu.CompilerParams(vmem_limit_bytes=4 * MIB),
-    )(base, par, first, second)
-
-
-def join_kernel(own, other, a_out, b_out, c_out):
+def join_kernel(base, own, other, a_out, b_out, c_out, full):
     core = lax.rem(lax.axis_index("pcol"), 2)
-    mine = pl.multiple_of(core * 64, 64)
-    rest = pl.multiple_of((1 - core) * 64, 64)
-    for i, out in enumerate((a_out, b_out, c_out)):
-        out[pl.ds(mine, 64), :] = own[64 * i : 64 * i + 64, :]
-        out[pl.ds(rest, 64), :] = other[64 * i : 64 * i + 64, :]
-
-
-def join(own, other):
+    for at, ref in ((core, own), (1 - core, other)):
+        rows = pl.ds(pl.multiple_of(at * 64, 64), 64)
+        full[rows, :] = ref[0:64, :]
+        b_out[rows, :] = base[pl.ds(pl.multiple_of(B + at * 64, 64), 64), :] - ref[64:128, :]
+    i = lax.broadcasted_iota(jnp.int32, (B, B), 0)
+    j = lax.broadcasted_iota(jnp.int32, (B, B), 1)
+    both = full[...]
+    turned = both.T
+    middle = jnp.broadcast_to(own[128:129, :], (B, B))
+    a_out[...] = base[0:128, :] - jnp.where(i >= j, both, turned)
+    lower = jnp.where(i == j, middle, jnp.where(i < j, both, turned))
+    c_out[...] = base[256:384, :] - lower
+
+
+def join(base, own, other):
     return pl.pallas_call(
         join_kernel,
         out_shape=[f32(B, B)] * 3,
-        in_specs=[VMEM] * 2,
+        in_specs=[VMEM] * 3,
         out_specs=[VMEM] * 3,
+        scratch_shapes=[pltpu.VMEM((B, B), jnp.float32)],
         compiler_params=pltpu.CompilerParams(vmem_limit_bytes=4 * MIB),
-    )(own, other)
+    )(base, own, other)
 
 
 def local(
@@ -442,12 +435,11 @@
         kept = [add(0, kept[v], got[v]) for v in range(2)]
         got = [row_step(going[v], v, step) for v in range(2)]
     kept = [add(0, kept[v], got[v]) for v in range(2)]
-    anc_one, anc_two, send, keep = blocks_of(kept, turn)
+    anc_one, anc_two, send, keep = blocks_of(kept, turn, par)
     sums = keep + swap(send)
-    for mask in (2, 6):
+    for mask in (2, 6, 14):
         sums = sums + permute(sums, lambda r, c: (r, c ^ mask))
-    done = final_of(base, par, sums, permute(sums, lambda r, c: (r, c ^ 14)))
-    diag_one, cross, diag_two = join(done, swap(done))
+    diag_one, cross, diag_two = join(base, sums, swap(sums))
     return anc_one, diag_one, anc_two, cross, diag_two
 
 

time: 167 us -> 165 us (0.988)
  waiting for transfers between devices: 85.8 us -> 83.9 us
    ppermute x30, waiting for transfers between devices: 85.8 us -> 83.9 us  [permute(): return lax.ppermute(value, ALL, pairs)]
    pallas_call x3 -> x2, Pallas kernels: 5.64 us -> 5.83 us  [the longest x1 4.69 us: keep_half(): pl.pallas_call(body, out_shape=[f32(8, B, KA)] * 2 + [f32(B, B), f32(384,...]
where the time goes in v10:
time: 165 us; the launch traced here: 164 us
  waiting for transfers between devices  83.9 us (51%)
  starting transfers between devices  58.9 us (36%)
  Pallas kernels  19.6 us (12%)
    ppermute x30, waiting for transfers between devices, permute(): return lax.ppermute(value, ALL, pairs)  83.9 us
    ppermute x30, starting transfers between devices, permute(): return lax.ppermute(value, ALL, pairs)  58.9 us
    pallas_call x1, Pallas kernels, send_half(): pl.pallas_call(send_kernel, out_shape=[f32(8, B, KA)] * 2 + [f32(16, 160,...  8.85 us
    pallas_call x1, Pallas kernels, keep_half(): pl.pallas_call(body, out_shape=[f32(8, B, KA)] * 2 + [f32(B, B), f32(384,...  4.69 us
  transfers between devices with their start and end apart: 30, of which 20 were waited for; matrix products, arithmetic and copies ran while one was open for 0% of the time, Pallas kernels for 9%

profile of v10, /device:TPU:7, one launch (start us, length us, event | category | flops | bytes accessed | tf_op | source)
XLA Modules:
  0.0 164.5 jit_solution(471436452160459600)
XLA Ops:
  5.5 5.6 %collective-permute-start.7 = (f32[288,512]{1,0:T(8,128)S(1)}, f32[288,512]{1,0:T(8,128)S(1)}, u32[]{:S(2)}, u32[]{:S(2)}) collective-permute-start(f32[288,512]{1,0:T(8,128)S(1)} %collective-permute-done.6.refs_7_), channel_id=1, source_target_pairs={{0,2},{1,15},{2,4},{3,1},{4,6},{5,3},{6,8},{7,5},{8,10},{9,7},{10,... | collective-permute-start | bytes 1769480 | tf_op jit(solution)/shard_map/ppermute | solution.py:62
  13.1 4.8 %collective-permute-done.7.refs_8_ = f32[288,512]{1,0:T(8,128)S(1)} collective-permute-done((f32[288,512]{1,0:T(8,128)S(1)}, f32[288,512]{1,0:T(8,128)S(1)}, u32[]{:S(2)}, u32[]{:S(2)}) %collective-permute-start.7) | collective-permute-done | bytes 589856 | tf_op jit(solution)/shard_map/ppermute | solution.py:62
  17.9 3.1 %collective-permute-start.9 = (f32[288,512]{1,0:T(8,128)S(1)}, f32[288,512]{1,0:T(8,128)S(1)}, u32[]{:S(2)}, u32[]{:S(2)}) collective-permute-start(f32[288,512]{1,0:T(8,128)S(1)} %collective-permute-done.7.refs_8_), channel_id=1, source_target_pairs={{0,2},{1,15},{2,4},{3,1},{4,6},{5,3},{6,8},{7,5},{8,10},{9,7},{10,... | collective-permute-start | bytes 1769480 | tf_op jit(solution)/shard_map/ppermute | solution.py:62
  21.0 3.2 %collective-permute-done.refs_1_ = f32[288,512]{1,0:T(8,128)S(1)} collective-permute-done((f32[288,512]{1,0:T(8,128)S(1)}, f32[288,512]{1,0:T(8,128)S(1)}, u32[]{:S(2)}, u32[]{:S(2)}) %collective-permute-start) | collective-permute-done | bytes 589856 | tf_op jit(solution)/shard_map/ppermute | solution.py:62
  24.2 3.1 %collective-permute-start.2 = (f32[288,512]{1,0:T(8,128)S(1)}, f32[288,512]{1,0:T(8,128)S(1)}, u32[]{:S(2)}, u32[]{:S(2)}) collective-permute-start(f32[288,512]{1,0:T(8,128)S(1)} %collective-permute-done.refs_1_), channel_id=1, source_target_pairs={{0,2},{1,15},{2,4},{3,1},{4,6},{5,3},{6,8},{7,5},{8,10},{9,7},{10,... | collective-permute-start | bytes 1769480 | tf_op jit(solution)/shard_map/ppermute | solution.py:62
  27.4 3.2 %collective-permute-done.9.refs_10_ = f32[288,512]{1,0:T(8,128)S(1)} collective-permute-done((f32[288,512]{1,0:T(8,128)S(1)}, f32[288,512]{1,0:T(8,128)S(1)}, u32[]{:S(2)}, u32[]{:S(2)}) %collective-permute-start.9) | collective-permute-done | bytes 589856 | tf_op jit(solution)/shard_map/ppermute | solution.py:62
  30.6 3.1 %collective-permute-start.11 = (f32[288,512]{1,0:T(8,128)S(1)}, f32[288,512]{1,0:T(8,128)S(1)}, u32[]{:S(2)}, u32[]{:S(2)}) collective-permute-start(f32[288,512]{1,0:T(8,128)S(1)} %collective-permute-done.9.refs_10_), channel_id=1, source_target_pairs={{0,2},{1,15},{2,4},{3,1},{4,6},{5,3},{6,8},{7,5},{8,10},{9,7},{10,... | collective-permute-start | bytes 1769480 | tf_op jit(solution)/shard_map/ppermute | solution.py:62
  33.7 3.2 %collective-permute-done.2.refs_3_ = f32[288,512]{1,0:T(8,128)S(1)} collective-permute-done((f32[288,512]{1,0:T(8,128)S(1)}, f32[288,512]{1,0:T(8,128)S(1)}, u32[]{:S(2)}, u32[]{:S(2)}) %collective-permute-start.2) | collective-permute-done | bytes 589856 | tf_op jit(solution)/shard_map/ppermute | solution.py:62
  36.9 3.1 %collective-permute-start.4 = (f32[288,512]{1,0:T(8,128)S(1)}, f32[288,512]{1,0:T(8,128)S(1)}, u32[]{:S(2)}, u32[]{:S(2)}) collective-permute-start(f32[288,512]{1,0:T(8,128)S(1)} %collective-permute-done.2.refs_3_), channel_id=1, source_target_pairs={{0,2},{1,15},{2,4},{3,1},{4,6},{5,3},{6,8},{7,5},{8,10},{9,7},{10,... | collective-permute-start | bytes 1769480 | tf_op jit(solution)/shard_map/ppermute | solution.py:62
  40.0 3.2 %collective-permute-done.11.refs_12_ = f32[288,512]{1,0:T(8,128)S(1)} collective-permute-done((f32[288,512]{1,0:T(8,128)S(1)}, f32[288,512]{1,0:T(8,128)S(1)}, u32[]{:S(2)}, u32[]{:S(2)}) %collective-permute-start.11) | collective-permute-done | bytes 589856 | tf_op jit(solution)/shard_map/ppermute | solution.py:62
  51.2 4.6 %collective-permute-done.13.refs_14_ = f32[288,512]{1,0:T(8,128)S(1)} collective-permute-done((f32[288,512]{1,0:T(8,128)S(1)}, f32[288,512]{1,0:T(8,128)S(1)}, u32[]{:S(2)}, u32[]{:S(2)}) %collective-permute-start.13) | collective-permute-done | bytes 589856 | tf_op jit(solution)/shard_map/ppermute | solution.py:62
  60.2 6.0 %collective-permute-start.15 = (f32[384,512]{1,0:T(8,128)S(1)}, f32[384,512]{1,0:T(8,128)S(1)}, u32[]{:S(2)}, u32[]{:S(2)}) collective-permute-start(f32[384,512]{1,0:T(8,128)S(1)} %shard_map.130.turn), channel_id=1, source_target_pairs={{0,0},{1,161},{2,18},{3,179},{4,100},{5,197},{6,118},{7,215},{8,40... | collective-permute-start | bytes 2359304 | tf_op jit(solution)/shard_map/ppermute | solution.py:62
  66.2 8.8 %shard_map.131 = (f32[8,128,512]{2,1,0:T(8,128)S(1)}, f32[8,128,512]{2,1,0:T(8,128)S(1)}, f32[16,160,512]{2,1,0:T(8,128)S(1)}, f32[16,128,512]{2,1,0:T(8,128)S(1)}) custom-call(s32[16]{0:T(128)S(1)} %copy-done.1, f32[512,512]{1,0:T(8,128)S(1)} %copy-done.2, f32[384,512]{1,0:T(8,128)S(1)} %shard_map.130.turn, f32[288,512]{1,0:T(8,128)S(1)} %shard_map.129.refs_0_, ...), custom_call_target="tpu_custom_call" | custom-call | flops 20000000000 | bytes 1000000 | tf_op jit(solution)/shard_map/pallas_call | solution.py:247
  77.1 4.7 %shard_map.132 = (f32[8,128,512]{2,1,0:T(8,128)S(1)}, f32[8,128,512]{2,1,0:T(8,128)S(1)}, f32[128,128]{1,0:T(8,128)S(1)}, f32[384,128]{1,0:T(8,128)S(1)}) custom-call(s32[16]{0:T(128)S(1)} %copy-done.1, f32[512,512]{1,0:T(8,128)S(1)} %copy-done.2, f32[16,160,512]{2,1,0:T(8,128)S(1)} %get-tuple-element.20.one, f32[16,128,512]{2,1,0:T(8,128)S(1)} %get-tuple-element.21.two, ...), custom_call_target="tpu_custom_call" | custom-call | flops 60000002048 | bytes 1000000 | tf_op jit(solution)/shard_map/pallas_call | solution.py:274
  81.8 19.4 %collective-permute-done.20.b = f32[8,128,512]{2,1,0:T(8,128)S(1)} collective-permute-done((f32[8,128,512]{2,1,0:T(8,128)S(1)}, f32[8,128,512]{2,1,0:T(8,128)S(1)}, u32[]{:S(2)}, u32[]{:S(2)}) %collective-permute-start.20) | collective-permute-done | bytes 2097184 | tf_op jit(solution)/shard_map/ppermute | solution.py:62
  103.1 5.4 %collective-permute-start.23 = (f32[384,512]{1,0:T(8,128)S(1)}, f32[384,512]{1,0:T(8,128)S(1)}, u32[]{:S(2)}, u32[]{:S(2)}) collective-permute-start(f32[384,512]{1,0:T(8,128)S(1)} %collective-permute-done.15.refs_0_), channel_id=1, source_target_pairs={{0,0},{1,10},{2,1},{3,11},{4,6},{5,12},{6,7},{7,13},{8,2},{9,8},{1... | collective-permute-start | bytes 2359304 | tf_op jit(solution)/shard_map/ppermute | solution.py:62
  108.7 6.6 %collective-permute-done.21.b = f32[4,128,512]{2,1,0:T(8,128)S(1)} collective-permute-done((f32[4,128,512]{2,1,0:T(8,128)S(1)}, f32[4,128,512]{2,1,0:T(8,128)S(1)}, u32[]{:S(2)}, u32[]{:S(2)}) %collective-permute-start.21) | collective-permute-done | bytes 1048608 | tf_op jit(solution)/shard_map/ppermute | solution.py:62
  117.8 8.6 %collective-permute-done.23.refs_0_.turn = f32[384,512]{1,0:T(8,128)S(1)} collective-permute-done((f32[384,512]{1,0:T(8,128)S(1)}, f32[384,512]{1,0:T(8,128)S(1)}, u32[]{:S(2)}, u32[]{:S(2)}) %collective-permute-start.23) | collective-permute-done | bytes 786464 | tf_op jit(solution)/shard_map/ppermute | solution.py:62
  128.6 3.5 %collective-permute-done.24.b = f32[1,128,512]{2,1,0:T(8,128)S(1)} collective-permute-done((f32[1,128,512]{2,1,0:T(8,128)S(1)}, f32[1,128,512]{2,1,0:T(8,128)S(1)}, u32[]{:S(2)}, u32[]{:S(2)}) %collective-permute-start.24) | collective-permute-done | bytes 262176 | tf_op jit(solution)/shard_map/ppermute | solution.py:62
  136.1 8.8 %collective-permute-start.25 = (f32[136,128]{1,0:T(8,128)S(1)}, f32[136,128]{1,0:T(8,128)S(1)}, u32[]{:S(2)}, u32[]{:S(2)}) collective-permute-start(f32[136,128]{1,0:T(8,128)S(1)} %get-tuple-element.30), channel_id=1, source_target_pairs={{0,1},{1,0},{2,3},{3,2},{4,5},{5,4},{6,7},{7,6},{8,9},{9,8},{10,11... | collective-permute-start | bytes 208904 | tf_op jit(solution)/shard_map/ppermute | solution.py:62
  146.0 3.1 %collective-permute-done.26 = f32[136,128]{1,0:T(8,128)S(1)} collective-permute-done((f32[136,128]{1,0:T(8,128)S(1)}, f32[136,128]{1,0:T(8,128)S(1)}, u32[]{:S(2)}, u32[]{:S(2)}) %collective-permute-start.26) | collective-permute-done | bytes 69664 | tf_op jit(solution)/shard_map/ppermute | solution.py:62
  149.2 5.0 %collective-permute-done.27 = f32[136,128]{1,0:T(8,128)S(1)} collective-permute-done((f32[136,128]{1,0:T(8,128)S(1)}, f32[136,128]{1,0:T(8,128)S(1)}, u32[]{:S(2)}, u32[]{:S(2)}) %collective-permute-start.27) | collective-permute-done | bytes 69664 | tf_op jit(solution)/shard_map/ppermute | solution.py:62
  155.4 3.4 %collective-permute-done.28 = f32[136,128]{1,0:T(8,128)S(1)} collective-permute-done((f32[136,128]{1,0:T(8,128)S(1)}, f32[136,128]{1,0:T(8,128)S(1)}, u32[]{:S(2)}, u32[]{:S(2)}) %collective-permute-start.28) | collective-permute-done | bytes 69664 | tf_op jit(solution)/shard_map/ppermute | solution.py:62
  158.8 4.0 %collective-permute-start.29 = (f32[136,128]{1,0:T(8,128)S(1)}, f32[136,128]{1,0:T(8,128)S(1)}, u32[]{:S(2)}, u32[]{:S(2)}) collective-permute-start(f32[136,128]{1,0:T(8,128)S(1)} %add.15.own), channel_id=1, source_target_pairs={{0,1},{1,0},{2,3},{3,2},{4,5},{5,4},{6,7},{7,6},{8,9},{9,8},{10,11... | collective-permute-start | bytes 208904 | tf_op jit(solution)/shard_map/ppermute | solution.py:62
  (71 shorter events, 35.9 us)
Async XLA Ops:
  5.5 12.4 %collective-permute-start.7 = (f32[288,512]{1,0:T(8,128)S(1)}, f32[288,512]{1,0:T(8,128)S(1)}, u32[]{:S(2)}, u32[]{:S(2)}) collective-permute-start(f32[288,512]{1,0:T(8,128)S(1)} %collective-permute-done.6.refs_7_), channel_id=1, source_target_pairs={{0,2},{1,15},{2,4},{3,1},{4,6},{5,3},{6,8},{7,5},{8,10},{9,7},{10,... | collective-permute-start | bytes 1769480 | tf_op jit(solution)/shard_map/ppermute | solution.py:62
  12.3 11.9 %collective-permute-start = (f32[288,512]{1,0:T(8,128)S(1)}, f32[288,512]{1,0:T(8,128)S(1)}, u32[]{:S(2)}, u32[]{:S(2)}) collective-permute-start(f32[288,512]{1,0:T(8,128)S(1)} %shard_map.129.refs_0_), channel_id=1, source_target_pairs={{0,2},{1,15},{2,4},{3,1},{4,6},{5,3},{6,8},{7,5},{8,10},{9,7},{10,... | collective-permute-start | bytes 1769480 | tf_op jit(solution)/shard_map/ppermute | solution.py:62
  17.9 12.6 %collective-permute-start.9 = (f32[288,512]{1,0:T(8,128)S(1)}, f32[288,512]{1,0:T(8,128)S(1)}, u32[]{:S(2)}, u32[]{:S(2)}) collective-permute-start(f32[288,512]{1,0:T(8,128)S(1)} %collective-permute-done.7.refs_8_), channel_id=1, source_target_pairs={{0,2},{1,15},{2,4},{3,1},{4,6},{5,3},{6,8},{7,5},{8,10},{9,7},{10,... | collective-permute-start | bytes 1769480 | tf_op jit(solution)/shard_map/ppermute | solution.py:62
  24.2 12.6 %collective-permute-start.2 = (f32[288,512]{1,0:T(8,128)S(1)}, f32[288,512]{1,0:T(8,128)S(1)}, u32[]{:S(2)}, u32[]{:S(2)}) collective-permute-start(f32[288,512]{1,0:T(8,128)S(1)} %collective-permute-done.refs_1_), channel_id=1, source_target_pairs={{0,2},{1,15},{2,4},{3,1},{4,6},{5,3},{6,8},{7,5},{8,10},{9,7},{10,... | collective-permute-start | bytes 1769480 | tf_op jit(solution)/shard_map/ppermute | solution.py:62
  30.6 12.6 %collective-permute-start.11 = (f32[288,512]{1,0:T(8,128)S(1)}, f32[288,512]{1,0:T(8,128)S(1)}, u32[]{:S(2)}, u32[]{:S(2)}) collective-permute-start(f32[288,512]{1,0:T(8,128)S(1)} %collective-permute-done.9.refs_10_), channel_id=1, source_target_pairs={{0,2},{1,15},{2,4},{3,1},{4,6},{5,3},{6,8},{7,5},{8,10},{9,7},{10,... | collective-permute-start | bytes 1769480 | tf_op jit(solution)/shard_map/ppermute | solution.py:62
  33.7 12.6 %collective-permute-start.1 = (f32[288,512]{1,0:T(8,128)S(1)}, f32[288,512]{1,0:T(8,128)S(1)}, u32[]{:S(2)}, u32[]{:S(2)}) collective-permute-start(f32[288,512]{1,0:T(8,128)S(1)} %collective-permute-done.refs_1_), channel_id=1, source_target_pairs={{0,1},{1,0},{2,3},{3,2},{4,5},{5,4},{6,7},{7,6},{8,9},{9,8},{10,11... | collective-permute-start | bytes 1769480 | tf_op jit(solution)/shard_map/ppermute | solution.py:62
  36.9 12.6 %collective-permute-start.4 = (f32[288,512]{1,0:T(8,128)S(1)}, f32[288,512]{1,0:T(8,128)S(1)}, u32[]{:S(2)}, u32[]{:S(2)}) collective-permute-start(f32[288,512]{1,0:T(8,128)S(1)} %collective-permute-done.2.refs_3_), channel_id=1, source_target_pairs={{0,2},{1,15},{2,4},{3,1},{4,6},{5,3},{6,8},{7,5},{8,10},{9,7},{10,... | collective-permute-start | bytes 1769480 | tf_op jit(solution)/shard_map/ppermute | solution.py:62
  40.0 11.2 %collective-permute-start.3 = (f32[288,512]{1,0:T(8,128)S(1)}, f32[288,512]{1,0:T(8,128)S(1)}, u32[]{:S(2)}, u32[]{:S(2)}) collective-permute-start(f32[288,512]{1,0:T(8,128)S(1)} %collective-permute-done.2.refs_3_), channel_id=1, source_target_pairs={{0,1},{1,0},{2,3},{3,2},{4,5},{5,4},{6,7},{7,6},{8,9},{9,8},{10,11... | collective-permute-start | bytes 1769480 | tf_op jit(solution)/shard_map/ppermute | solution.py:62
  43.2 12.6 %collective-permute-start.13 = (f32[288,512]{1,0:T(8,128)S(1)}, f32[288,512]{1,0:T(8,128)S(1)}, u32[]{:S(2)}, u32[]{:S(2)}) collective-permute-start(f32[288,512]{1,0:T(8,128)S(1)} %collective-permute-done.11.refs_12_), channel_id=1, source_target_pairs={{0,2},{1,15},{2,4},{3,1},{4,6},{5,3},{6,8},{7,5},{8,10},{9,7},{10,... | collective-permute-start | bytes 1769480 | tf_op jit(solution)/shard_map/ppermute | solution.py:62
  46.3 11.2 %collective-permute-start.8 = (f32[288,512]{1,0:T(8,128)S(1)}, f32[288,512]{1,0:T(8,128)S(1)}, u32[]{:S(2)}, u32[]{:S(2)}) collective-permute-start(f32[288,512]{1,0:T(8,128)S(1)} %collective-permute-done.7.refs_8_), channel_id=1, source_target_pairs={{0,1},{1,0},{2,3},{3,2},{4,5},{5,4},{6,7},{7,6},{8,9},{9,8},{10,11... | collective-permute-start | bytes 1769480 | tf_op jit(solution)/shard_map/ppermute | solution.py:62
  46.3 11.2 %collective-permute-start.10 = (f32[288,512]{1,0:T(8,128)S(1)}, f32[288,512]{1,0:T(8,128)S(1)}, u32[]{:S(2)}, u32[]{:S(2)}) collective-permute-start(f32[288,512]{1,0:T(8,128)S(1)} %collective-permute-done.9.refs_10_), channel_id=1, source_target_pairs={{0,1},{1,0},{2,3},{3,2},{4,5},{5,4},{6,7},{7,6},{8,9},{9,8},{10,11... | collective-permute-start | bytes 1769480 | tf_op jit(solution)/shard_map/ppermute | solution.py:62
  49.5 8.0 %collective-permute-start.5 = (f32[288,512]{1,0:T(8,128)S(1)}, f32[288,512]{1,0:T(8,128)S(1)}, u32[]{:S(2)}, u32[]{:S(2)}) collective-permute-start(f32[288,512]{1,0:T(8,128)S(1)} %collective-permute-done.4.refs_5_), channel_id=1, source_target_pairs={{0,1},{1,0},{2,3},{3,2},{4,5},{5,4},{6,7},{7,6},{8,9},{9,8},{10,11... | collective-permute-start | bytes 1769480 | tf_op jit(solution)/shard_map/ppermute | solution.py:62
  51.2 6.3 %collective-permute-start.12 = (f32[288,512]{1,0:T(8,128)S(1)}, f32[288,512]{1,0:T(8,128)S(1)}, u32[]{:S(2)}, u32[]{:S(2)}) collective-permute-start(f32[288,512]{1,0:T(8,128)S(1)} %collective-permute-done.11.refs_12_), channel_id=1, source_target_pairs={{0,1},{1,0},{2,3},{3,2},{4,5},{5,4},{6,7},{7,6},{8,9},{9,8},{10,11... | collective-permute-start | bytes 1769480 | tf_op jit(solution)/shard_map/ppermute | solution.py:62
  60.2 17.0 %collective-permute-start.15 = (f32[384,512]{1,0:T(8,128)S(1)}, f32[384,512]{1,0:T(8,128)S(1)}, u32[]{:S(2)}, u32[]{:S(2)}) collective-permute-start(f32[384,512]{1,0:T(8,128)S(1)} %shard_map.130.turn), channel_id=1, source_target_pairs={{0,0},{1,161},{2,18},{3,179},{4,100},{5,197},{6,118},{7,215},{8,40... | collective-permute-start | bytes 2359304 | tf_op jit(solution)/shard_map/ppermute | solution.py:62
  75.0 26.2 %collective-permute-start.20 = (f32[8,128,512]{2,1,0:T(8,128)S(1)}, f32[8,128,512]{2,1,0:T(8,128)S(1)}, u32[]{:S(2)}, u32[]{:S(2)}) collective-permute-start(f32[8,128,512]{2,1,0:T(8,128)S(1)} %get-tuple-element.25), channel_id=1, source_target_pairs={{0,48},{1,193},{2,50},{3,195},{4,52},{5,197},{6,54},{7,199},{8,56}... | collective-permute-start | bytes 6291464 | tf_op jit(solution)/shard_map/ppermute | solution.py:62
  75.9 25.5 %collective-permute-start.16 = (f32[8,128,512]{2,1,0:T(8,128)S(1)}, f32[8,128,512]{2,1,0:T(8,128)S(1)}, u32[]{:S(2)}, u32[]{:S(2)}) collective-permute-start(f32[8,128,512]{2,1,0:T(8,128)S(1)} %get-tuple-element.23), channel_id=1, source_target_pairs={{0,16},{1,65},{2,18},{3,67},{4,20},{5,69},{6,22},{7,71},{8,24},{9,... | collective-permute-start | bytes 6291464 | tf_op jit(solution)/shard_map/ppermute | solution.py:62
  101.3 14.0 %collective-permute-start.21 = (f32[4,128,512]{2,1,0:T(8,128)S(1)}, f32[4,128,512]{2,1,0:T(8,128)S(1)}, u32[]{:S(2)}, u32[]{:S(2)}) collective-permute-start(f32[4,128,512]{2,1,0:T(8,128)S(1)} %shard_map.141), channel_id=1, source_target_pairs={{0,16},{1,65},{2,18},{3,67},{4,20},{5,69},{6,22},{7,71},{8,24},{9,... | collective-permute-start | bytes 3145736 | tf_op jit(solution)/shard_map/ppermute | solution.py:62
  101.5 15.8 %collective-permute-start.17 = (f32[4,128,512]{2,1,0:T(8,128)S(1)}, f32[4,128,512]{2,1,0:T(8,128)S(1)}, u32[]{:S(2)}, u32[]{:S(2)}) collective-permute-start(f32[4,128,512]{2,1,0:T(8,128)S(1)} %shard_map.134), channel_id=1, source_target_pairs={{0,48},{1,193},{2,50},{3,195},{4,52},{5,197},{6,54},{7,199},{8,56}... | collective-permute-start | bytes 3145736 | tf_op jit(solution)/shard_map/ppermute | solution.py:62
  103.1 23.3 %collective-permute-start.23 = (f32[384,512]{1,0:T(8,128)S(1)}, f32[384,512]{1,0:T(8,128)S(1)}, u32[]{:S(2)}, u32[]{:S(2)}) collective-permute-start(f32[384,512]{1,0:T(8,128)S(1)} %collective-permute-done.15.refs_0_), channel_id=1, source_target_pairs={{0,0},{1,10},{2,1},{3,11},{4,6},{5,12},{6,7},{7,13},{8,2},{9,8},{1... | collective-permute-start | bytes 2359304 | tf_op jit(solution)/shard_map/ppermute | solution.py:62
  115.4 11.0 %collective-permute-start.22 = (f32[2,128,512]{2,1,0:T(8,128)S(1)}, f32[2,128,512]{2,1,0:T(8,128)S(1)}, u32[]{:S(2)}, u32[]{:S(2)}) collective-permute-start(f32[2,128,512]{2,1,0:T(8,128)S(1)} %shard_map.143), channel_id=1, source_target_pairs={{0,192},{1,49},{2,194},{3,51},{4,196},{5,53},{6,198},{7,55},{8,200... | collective-permute-start | bytes 1572872 | tf_op jit(solution)/shard_map/ppermute | solution.py:62
  117.4 11.0 %collective-permute-start.18 = (f32[2,128,512]{2,1,0:T(8,128)S(1)}, f32[2,128,512]{2,1,0:T(8,128)S(1)}, u32[]{:S(2)}, u32[]{:S(2)}) collective-permute-start(f32[2,128,512]{2,1,0:T(8,128)S(1)} %shard_map.136), channel_id=1, source_target_pairs={{0,64},{1,17},{2,66},{3,19},{4,68},{5,21},{6,70},{7,23},{8,72},{9,... | collective-permute-start | bytes 1572872 | tf_op jit(solution)/shard_map/ppermute | solution.py:62
  126.4 5.7 %collective-permute-start.24 = (f32[1,128,512]{2,1,0:T(8,128)S(1)}, f32[1,128,512]{2,1,0:T(8,128)S(1)}, u32[]{:S(2)}, u32[]{:S(2)}) collective-permute-start(f32[1,128,512]{2,1,0:T(8,128)S(1)} %shard_map.145), channel_id=1, source_target_pairs={{0,64},{1,17},{2,66},{3,19},{4,68},{5,21},{6,70},{7,23},{8,72},{9,... | collective-permute-start | bytes 786440 | tf_op jit(solution)/shard_map/ppermute | solution.py:62
  128.4 6.5 %collective-permute-start.19 = (f32[1,128,512]{2,1,0:T(8,128)S(1)}, f32[1,128,512]{2,1,0:T(8,128)S(1)}, u32[]{:S(2)}, u32[]{:S(2)}) collective-permute-start(f32[1,128,512]{2,1,0:T(8,128)S(1)} %shard_map.138), channel_id=1, source_target_pairs={{0,192},{1,49},{2,194},{3,51},{4,196},{5,53},{6,198},{7,55},{8,200... | collective-permute-start | bytes 786440 | tf_op jit(solution)/shard_map/ppermute | solution.py:62
  136.1 9.7 %collective-permute-start.25 = (f32[136,128]{1,0:T(8,128)S(1)}, f32[136,128]{1,0:T(8,128)S(1)}, u32[]{:S(2)}, u32[]{:S(2)}) collective-permute-start(f32[136,128]{1,0:T(8,128)S(1)} %get-tuple-element.30), channel_id=1, source_target_pairs={{0,1},{1,0},{2,3},{3,2},{4,5},{5,4},{6,7},{7,6},{8,9},{9,8},{10,11... | collective-permute-start | bytes 208904 | tf_op jit(solution)/shard_map/ppermute | solution.py:62
  (11 other events, 171.1 us)

commit v11 on v10

--- a/solution.py
+++ b/solution.py
@@ -185,7 +185,7 @@
 
 
 def turn_kernel(parent, *refs):
-    own, other, turn, sems = refs[:7], refs[7:16], refs[16], refs[17]
+    own, other, turn, sems = refs[:9], refs[9:16], refs[16], refs[17]
     row, col, core, target = place()
     for k, (start_row, which) in enumerate(((0, parent[target]), (0, target), (160, target))):
         for source, m in sources(own, other, start_row, B):
@@ -222,7 +222,7 @@
 
 
 def send_kernel(parent, ginv, turn, *refs):
-    own, other, refs = refs[:7], refs[7:16], refs[16:]
+    own, other, refs = refs[:9], refs[9:16], refs[16:]
     sends, one, two, left, block, sems = refs[0:2], *refs[2:]
     row, col, core, target = place()
     load = pltpu.make_async_copy(ginv, block, sems.at[32])
@@ -418,8 +418,9 @@
     dinv_two,
 ):
     own = prepare(pattern_one.T, pattern_two.T, factor_one, factor_two, factor_parent)
-    blocks_own = gather(stage(own), 3)
-    blocks_other = gather(swap(own), 4)
+    near = stage(own)
+    blocks_own = [near] + gather(own, 4)[1:]
+    blocks_other = gather(swap(near), 3)
     turn = pick_turn(parent, blocks_own, blocks_other)
     send_a, send_b, one, two = send_half(parent, ginv_anc, turn, blocks_own, blocks_other)
     turn = permute(turn, lambda r, c: (r ^ spread_mask(c), c))

time: 165 us -> 164 us (level)
  waiting for transfers between devices: 83.9 us -> 82.1 us
    ppermute x30, waiting for transfers between devices: 83.9 us -> 82.1 us  [permute(): return lax.ppermute(value, ALL, pairs)]
  transfers between devices with their start and end apart: 30 -> 30, of which waited for: 20 -> 19; matrix products, arithmetic and copies ran while one was open for 0% -> 0% of each run, Pallas kernels for 9% -> 9%
where the time goes in v11:
time: 164 us
  waiting for transfers between devices  82.1 us (50%)
  starting transfers between devices  59.8 us (36%)
  Pallas kernels  19.6 us (12%)
    ppermute x30, waiting for transfers between devices, permute(): return lax.ppermute(value, ALL, pairs)  82.1 us
    ppermute x30, starting transfers between devices, permute(): return lax.ppermute(value, ALL, pairs)  59.8 us
    pallas_call x1, Pallas kernels, send_half(): pl.pallas_call(send_kernel, out_shape=[f32(8, B, KA)] * 2 + [f32(16, 160,...  8.84 us
    pallas_call x1, Pallas kernels, keep_half(): pl.pallas_call(body, out_shape=[f32(8, B, KA)] * 2 + [f32(B, B), f32(384,...  4.68 us
  transfers between devices with their start and end apart: 30, of which 19 were waited for; matrix products, arithmetic and copies ran while one was open for 0% of the time, Pallas kernels for 9%

profile of v11, /device:TPU:7, one launch (start us, length us, event | category | flops | bytes accessed | tf_op | source)
XLA Modules:
  0.0 163.5 jit_solution(5739249886838013079)
XLA Ops:
  4.9 5.6 %collective-permute-start = (f32[288,512]{1,0:T(8,128)S(1)}, f32[288,512]{1,0:T(8,128)S(1)}, u32[]{:S(2)}, u32[]{:S(2)}) collective-permute-start(f32[288,512]{1,0:T(8,128)S(1)} %copy-done), channel_id=1, source_target_pairs={{0,2},{1,15},{2,4},{3,1},{4,6},{5,3},{6,8},{7,5},{8,10},{9,7},{10,... | collective-permute-start | bytes 1769480 | tf_op jit(solution)/shard_map/ppermute | solution.py:62
  12.1 5.2 %collective-permute-done.refs_1_ = f32[288,512]{1,0:T(8,128)S(1)} collective-permute-done((f32[288,512]{1,0:T(8,128)S(1)}, f32[288,512]{1,0:T(8,128)S(1)}, u32[]{:S(2)}, u32[]{:S(2)}) %collective-permute-start) | collective-permute-done | bytes 589856 | tf_op jit(solution)/shard_map/ppermute | solution.py:62
  17.3 3.1 %collective-permute-start.2 = (f32[288,512]{1,0:T(8,128)S(1)}, f32[288,512]{1,0:T(8,128)S(1)}, u32[]{:S(2)}, u32[]{:S(2)}) collective-permute-start(f32[288,512]{1,0:T(8,128)S(1)} %collective-permute-done.refs_1_), channel_id=1, source_target_pairs={{0,2},{1,15},{2,4},{3,1},{4,6},{5,3},{6,8},{7,5},{8,10},{9,7},{10,... | collective-permute-start | bytes 1769480 | tf_op jit(solution)/shard_map/ppermute | solution.py:62
  20.4 3.2 %collective-permute-done.9.refs_10_ = f32[288,512]{1,0:T(8,128)S(1)} collective-permute-done((f32[288,512]{1,0:T(8,128)S(1)}, f32[288,512]{1,0:T(8,128)S(1)}, u32[]{:S(2)}, u32[]{:S(2)}) %collective-permute-start.9) | collective-permute-done | bytes 589856 | tf_op jit(solution)/shard_map/ppermute | solution.py:62
  23.6 3.1 %collective-permute-start.11 = (f32[288,512]{1,0:T(8,128)S(1)}, f32[288,512]{1,0:T(8,128)S(1)}, u32[]{:S(2)}, u32[]{:S(2)}) collective-permute-start(f32[288,512]{1,0:T(8,128)S(1)} %collective-permute-done.9.refs_10_), channel_id=1, source_target_pairs={{0,2},{1,15},{2,4},{3,1},{4,6},{5,3},{6,8},{7,5},{8,10},{9,7},{10,... | collective-permute-start | bytes 1769480 | tf_op jit(solution)/shard_map/ppermute | solution.py:62
  26.7 3.2 %collective-permute-done.2.refs_3_ = f32[288,512]{1,0:T(8,128)S(1)} collective-permute-done((f32[288,512]{1,0:T(8,128)S(1)}, f32[288,512]{1,0:T(8,128)S(1)}, u32[]{:S(2)}, u32[]{:S(2)}) %collective-permute-start.2) | collective-permute-done | bytes 589856 | tf_op jit(solution)/shard_map/ppermute | solution.py:62
  29.9 3.1 %collective-permute-start.4 = (f32[288,512]{1,0:T(8,128)S(1)}, f32[288,512]{1,0:T(8,128)S(1)}, u32[]{:S(2)}, u32[]{:S(2)}) collective-permute-start(f32[288,512]{1,0:T(8,128)S(1)} %collective-permute-done.2.refs_3_), channel_id=1, source_target_pairs={{0,2},{1,15},{2,4},{3,1},{4,6},{5,3},{6,8},{7,5},{8,10},{9,7},{10,... | collective-permute-start | bytes 1769480 | tf_op jit(solution)/shard_map/ppermute | solution.py:62
  36.2 3.1 %collective-permute-start.13 = (f32[288,512]{1,0:T(8,128)S(1)}, f32[288,512]{1,0:T(8,128)S(1)}, u32[]{:S(2)}, u32[]{:S(2)}) collective-permute-start(f32[288,512]{1,0:T(8,128)S(1)} %collective-permute-done.11.refs_12_), channel_id=1, source_target_pairs={{0,2},{1,15},{2,4},{3,1},{4,6},{5,3},{6,8},{7,5},{8,10},{9,7},{10,... | collective-permute-start | bytes 1769480 | tf_op jit(solution)/shard_map/ppermute | solution.py:62
  39.4 3.2 %collective-permute-done.4.refs_5_ = f32[288,512]{1,0:T(8,128)S(1)} collective-permute-done((f32[288,512]{1,0:T(8,128)S(1)}, f32[288,512]{1,0:T(8,128)S(1)}, u32[]{:S(2)}, u32[]{:S(2)}) %collective-permute-start.4) | collective-permute-done | bytes 589856 | tf_op jit(solution)/shard_map/ppermute | solution.py:62
  42.6 3.1 %collective-permute-start.6 = (f32[288,512]{1,0:T(8,128)S(1)}, f32[288,512]{1,0:T(8,128)S(1)}, u32[]{:S(2)}, u32[]{:S(2)}) collective-permute-start(f32[288,512]{1,0:T(8,128)S(1)} %collective-permute-done.4.refs_5_), channel_id=1, source_target_pairs={{0,2},{1,15},{2,4},{3,1},{4,6},{5,3},{6,8},{7,5},{8,10},{9,7},{10,... | collective-permute-start | bytes 1769480 | tf_op jit(solution)/shard_map/ppermute | solution.py:62
  50.3 4.9 %collective-permute-done.6.refs_7_ = f32[288,512]{1,0:T(8,128)S(1)} collective-permute-done((f32[288,512]{1,0:T(8,128)S(1)}, f32[288,512]{1,0:T(8,128)S(1)}, u32[]{:S(2)}, u32[]{:S(2)}) %collective-permute-start.6) | collective-permute-done | bytes 589856 | tf_op jit(solution)/shard_map/ppermute | solution.py:62
  59.2 6.0 %collective-permute-start.15 = (f32[384,512]{1,0:T(8,128)S(1)}, f32[384,512]{1,0:T(8,128)S(1)}, u32[]{:S(2)}, u32[]{:S(2)}) collective-permute-start(f32[384,512]{1,0:T(8,128)S(1)} %shard_map.130.turn), channel_id=1, source_target_pairs={{0,0},{1,161},{2,18},{3,179},{4,100},{5,197},{6,118},{7,215},{8,40... | collective-permute-start | bytes 2359304 | tf_op jit(solution)/shard_map/ppermute | solution.py:62
  65.2 8.8 %shard_map.131 = (f32[8,128,512]{2,1,0:T(8,128)S(1)}, f32[8,128,512]{2,1,0:T(8,128)S(1)}, f32[16,160,512]{2,1,0:T(8,128)S(1)}, f32[16,128,512]{2,1,0:T(8,128)S(1)}) custom-call(s32[16]{0:T(128)S(1)} %copy-done.1, f32[512,512]{1,0:T(8,128)S(1)} %copy-done.2, f32[384,512]{1,0:T(8,128)S(1)} %shard_map.130.turn, f32[288,512]{1,0:T(8,128)S(1)} %shard_map.129.refs_0_, ...), custom_call_target="tpu_custom_call" | custom-call | flops 20000000000 | bytes 1000000 | tf_op jit(solution)/shard_map/pallas_call | solution.py:247
  76.2 4.7 %shard_map.132 = (f32[8,128,512]{2,1,0:T(8,128)S(1)}, f32[8,128,512]{2,1,0:T(8,128)S(1)}, f32[128,128]{1,0:T(8,128)S(1)}, f32[384,128]{1,0:T(8,128)S(1)}) custom-call(s32[16]{0:T(128)S(1)} %copy-done.1, f32[512,512]{1,0:T(8,128)S(1)} %copy-done.2, f32[16,160,512]{2,1,0:T(8,128)S(1)} %get-tuple-element.20.one, f32[16,128,512]{2,1,0:T(8,128)S(1)} %get-tuple-element.21.two, ...), custom_call_target="tpu_custom_call" | custom-call | flops 60000002048 | bytes 1000000 | tf_op jit(solution)/shard_map/pallas_call | solution.py:274
  80.9 19.4 %collective-permute-done.20.b = f32[8,128,512]{2,1,0:T(8,128)S(1)} collective-permute-done((f32[8,128,512]{2,1,0:T(8,128)S(1)}, f32[8,128,512]{2,1,0:T(8,128)S(1)}, u32[]{:S(2)}, u32[]{:S(2)}) %collective-permute-start.20) | collective-permute-done | bytes 2097184 | tf_op jit(solution)/shard_map/ppermute | solution.py:62
  102.2 5.4 %collective-permute-start.23 = (f32[384,512]{1,0:T(8,128)S(1)}, f32[384,512]{1,0:T(8,128)S(1)}, u32[]{:S(2)}, u32[]{:S(2)}) collective-permute-start(f32[384,512]{1,0:T(8,128)S(1)} %collective-permute-done.15.refs_0_), channel_id=1, source_target_pairs={{0,0},{1,10},{2,1},{3,11},{4,6},{5,12},{6,7},{7,13},{8,2},{9,8},{1... | collective-permute-start | bytes 2359304 | tf_op jit(solution)/shard_map/ppermute | solution.py:62
  107.8 6.6 %collective-permute-done.21.b = f32[4,128,512]{2,1,0:T(8,128)S(1)} collective-permute-done((f32[4,128,512]{2,1,0:T(8,128)S(1)}, f32[4,128,512]{2,1,0:T(8,128)S(1)}, u32[]{:S(2)}, u32[]{:S(2)}) %collective-permute-start.21) | collective-permute-done | bytes 1048608 | tf_op jit(solution)/shard_map/ppermute | solution.py:62
  116.9 8.6 %collective-permute-done.23.refs_0_.turn = f32[384,512]{1,0:T(8,128)S(1)} collective-permute-done((f32[384,512]{1,0:T(8,128)S(1)}, f32[384,512]{1,0:T(8,128)S(1)}, u32[]{:S(2)}, u32[]{:S(2)}) %collective-permute-start.23) | collective-permute-done | bytes 786464 | tf_op jit(solution)/shard_map/ppermute | solution.py:62
  127.7 3.5 %collective-permute-done.24.b = f32[1,128,512]{2,1,0:T(8,128)S(1)} collective-permute-done((f32[1,128,512]{2,1,0:T(8,128)S(1)}, f32[1,128,512]{2,1,0:T(8,128)S(1)}, u32[]{:S(2)}, u32[]{:S(2)}) %collective-permute-start.24) | collective-permute-done | bytes 262176 | tf_op jit(solution)/shard_map/ppermute | solution.py:62
  135.2 8.8 %collective-permute-start.25 = (f32[136,128]{1,0:T(8,128)S(1)}, f32[136,128]{1,0:T(8,128)S(1)}, u32[]{:S(2)}, u32[]{:S(2)}) collective-permute-start(f32[136,128]{1,0:T(8,128)S(1)} %get-tuple-element.30), channel_id=1, source_target_pairs={{0,1},{1,0},{2,3},{3,2},{4,5},{5,4},{6,7},{7,6},{8,9},{9,8},{10,11... | collective-permute-start | bytes 208904 | tf_op jit(solution)/shard_map/ppermute | solution.py:62
  145.0 3.1 %collective-permute-done.26 = f32[136,128]{1,0:T(8,128)S(1)} collective-permute-done((f32[136,128]{1,0:T(8,128)S(1)}, f32[136,128]{1,0:T(8,128)S(1)}, u32[]{:S(2)}, u32[]{:S(2)}) %collective-permute-start.26) | collective-permute-done | bytes 69664 | tf_op jit(solution)/shard_map/ppermute | solution.py:62
  148.3 5.0 %collective-permute-done.27 = f32[136,128]{1,0:T(8,128)S(1)} collective-permute-done((f32[136,128]{1,0:T(8,128)S(1)}, f32[136,128]{1,0:T(8,128)S(1)}, u32[]{:S(2)}, u32[]{:S(2)}) %collective-permute-start.27) | collective-permute-done | bytes 69664 | tf_op jit(solution)/shard_map/ppermute | solution.py:62
  154.5 3.4 %collective-permute-done.28 = f32[136,128]{1,0:T(8,128)S(1)} collective-permute-done((f32[136,128]{1,0:T(8,128)S(1)}, f32[136,128]{1,0:T(8,128)S(1)}, u32[]{:S(2)}, u32[]{:S(2)}) %collective-permute-start.28) | collective-permute-done | bytes 69664 | tf_op jit(solution)/shard_map/ppermute | solution.py:62
  157.9 4.0 %collective-permute-start.29 = (f32[136,128]{1,0:T(8,128)S(1)}, f32[136,128]{1,0:T(8,128)S(1)}, u32[]{:S(2)}, u32[]{:S(2)}) collective-permute-start(f32[136,128]{1,0:T(8,128)S(1)} %add.15.own), channel_id=1, source_target_pairs={{0,1},{1,0},{2,3},{3,2},{4,5},{5,4},{6,7},{7,6},{8,9},{9,8},{10,11... | collective-permute-start | bytes 208904 | tf_op jit(solution)/shard_map/ppermute | solution.py:62
  (71 shorter events, 34.4 us)
Async XLA Ops:
  4.1 6.3 %collective-permute-start.8 = (f32[288,512]{1,0:T(8,128)S(1)}, f32[288,512]{1,0:T(8,128)S(1)}, u32[]{:S(2)}, u32[]{:S(2)}) collective-permute-start(f32[288,512]{1,0:T(8,128)S(1)} %shard_map.129.refs_0_), channel_id=1, source_target_pairs={{0,1},{1,0},{2,3},{3,2},{4,5},{5,4},{6,7},{7,6},{8,9},{9,8},{10,11... | collective-permute-start | bytes 1769480 | tf_op jit(solution)/shard_map/ppermute | solution.py:62
  4.9 12.4 %collective-permute-start = (f32[288,512]{1,0:T(8,128)S(1)}, f32[288,512]{1,0:T(8,128)S(1)}, u32[]{:S(2)}, u32[]{:S(2)}) collective-permute-start(f32[288,512]{1,0:T(8,128)S(1)} %copy-done), channel_id=1, source_target_pairs={{0,2},{1,15},{2,4},{3,1},{4,6},{5,3},{6,8},{7,5},{8,10},{9,7},{10,... | collective-permute-start | bytes 1769480 | tf_op jit(solution)/shard_map/ppermute | solution.py:62
  10.5 13.1 %collective-permute-start.9 = (f32[288,512]{1,0:T(8,128)S(1)}, f32[288,512]{1,0:T(8,128)S(1)}, u32[]{:S(2)}, u32[]{:S(2)}) collective-permute-start(f32[288,512]{1,0:T(8,128)S(1)} %collective-permute-done.8.refs_9_), channel_id=1, source_target_pairs={{0,2},{1,15},{2,4},{3,1},{4,6},{5,3},{6,8},{7,5},{8,10},{9,7},{10,... | collective-permute-start | bytes 1769480 | tf_op jit(solution)/shard_map/ppermute | solution.py:62
  17.3 12.6 %collective-permute-start.2 = (f32[288,512]{1,0:T(8,128)S(1)}, f32[288,512]{1,0:T(8,128)S(1)}, u32[]{:S(2)}, u32[]{:S(2)}) collective-permute-start(f32[288,512]{1,0:T(8,128)S(1)} %collective-permute-done.refs_1_), channel_id=1, source_target_pairs={{0,2},{1,15},{2,4},{3,1},{4,6},{5,3},{6,8},{7,5},{8,10},{9,7},{10,... | collective-permute-start | bytes 1769480 | tf_op jit(solution)/shard_map/ppermute | solution.py:62
  23.6 12.6 %collective-permute-start.11 = (f32[288,512]{1,0:T(8,128)S(1)}, f32[288,512]{1,0:T(8,128)S(1)}, u32[]{:S(2)}, u32[]{:S(2)}) collective-permute-start(f32[288,512]{1,0:T(8,128)S(1)} %collective-permute-done.9.refs_10_), channel_id=1, source_target_pairs={{0,2},{1,15},{2,4},{3,1},{4,6},{5,3},{6,8},{7,5},{8,10},{9,7},{10,... | collective-permute-start | bytes 1769480 | tf_op jit(solution)/shard_map/ppermute | solution.py:62
  29.9 12.6 %collective-permute-start.4 = (f32[288,512]{1,0:T(8,128)S(1)}, f32[288,512]{1,0:T(8,128)S(1)}, u32[]{:S(2)}, u32[]{:S(2)}) collective-permute-start(f32[288,512]{1,0:T(8,128)S(1)} %collective-permute-done.2.refs_3_), channel_id=1, source_target_pairs={{0,2},{1,15},{2,4},{3,1},{4,6},{5,3},{6,8},{7,5},{8,10},{9,7},{10,... | collective-permute-start | bytes 1769480 | tf_op jit(solution)/shard_map/ppermute | solution.py:62
  33.0 12.6 %collective-permute-start.1 = (f32[288,512]{1,0:T(8,128)S(1)}, f32[288,512]{1,0:T(8,128)S(1)}, u32[]{:S(2)}, u32[]{:S(2)}) collective-permute-start(f32[288,512]{1,0:T(8,128)S(1)} %collective-permute-done.refs_1_), channel_id=1, source_target_pairs={{0,1},{1,0},{2,3},{3,2},{4,5},{5,4},{6,7},{7,6},{8,9},{9,8},{10,11... | collective-permute-start | bytes 1769480 | tf_op jit(solution)/shard_map/ppermute | solution.py:62
  33.0 13.2 %collective-permute-start.10 = (f32[288,512]{1,0:T(8,128)S(1)}, f32[288,512]{1,0:T(8,128)S(1)}, u32[]{:S(2)}, u32[]{:S(2)}) collective-permute-start(f32[288,512]{1,0:T(8,128)S(1)} %collective-permute-done.9.refs_10_), channel_id=1, source_target_pairs={{0,1},{1,0},{2,3},{3,2},{4,5},{5,4},{6,7},{7,6},{8,9},{9,8},{10,11... | collective-permute-start | bytes 1769480 | tf_op jit(solution)/shard_map/ppermute | solution.py:62
  36.2 12.6 %collective-permute-start.13 = (f32[288,512]{1,0:T(8,128)S(1)}, f32[288,512]{1,0:T(8,128)S(1)}, u32[]{:S(2)}, u32[]{:S(2)}) collective-permute-start(f32[288,512]{1,0:T(8,128)S(1)} %collective-permute-done.11.refs_12_), channel_id=1, source_target_pairs={{0,2},{1,15},{2,4},{3,1},{4,6},{5,3},{6,8},{7,5},{8,10},{9,7},{10,... | collective-permute-start | bytes 1769480 | tf_op jit(solution)/shard_map/ppermute | solution.py:62
  42.6 12.6 %collective-permute-start.6 = (f32[288,512]{1,0:T(8,128)S(1)}, f32[288,512]{1,0:T(8,128)S(1)}, u32[]{:S(2)}, u32[]{:S(2)}) collective-permute-start(f32[288,512]{1,0:T(8,128)S(1)} %collective-permute-done.4.refs_5_), channel_id=1, source_target_pairs={{0,2},{1,15},{2,4},{3,1},{4,6},{5,3},{6,8},{7,5},{8,10},{9,7},{10,... | collective-permute-start | bytes 1769480 | tf_op jit(solution)/shard_map/ppermute | solution.py:62
  45.7 10.9 %collective-permute-start.3 = (f32[288,512]{1,0:T(8,128)S(1)}, f32[288,512]{1,0:T(8,128)S(1)}, u32[]{:S(2)}, u32[]{:S(2)}) collective-permute-start(f32[288,512]{1,0:T(8,128)S(1)} %collective-permute-done.2.refs_3_), channel_id=1, source_target_pairs={{0,1},{1,0},{2,3},{3,2},{4,5},{5,4},{6,7},{7,6},{8,9},{9,8},{10,11... | collective-permute-start | bytes 1769480 | tf_op jit(solution)/shard_map/ppermute | solution.py:62
  45.7 10.9 %collective-permute-start.12 = (f32[288,512]{1,0:T(8,128)S(1)}, f32[288,512]{1,0:T(8,128)S(1)}, u32[]{:S(2)}, u32[]{:S(2)}) collective-permute-start(f32[288,512]{1,0:T(8,128)S(1)} %collective-permute-done.11.refs_12_), channel_id=1, source_target_pairs={{0,1},{1,0},{2,3},{3,2},{4,5},{5,4},{6,7},{7,6},{8,9},{9,8},{10,11... | collective-permute-start | bytes 1769480 | tf_op jit(solution)/shard_map/ppermute | solution.py:62
  46.2 10.4 %collective-permute-start.5 = (f32[288,512]{1,0:T(8,128)S(1)}, f32[288,512]{1,0:T(8,128)S(1)}, u32[]{:S(2)}, u32[]{:S(2)}) collective-permute-start(f32[288,512]{1,0:T(8,128)S(1)} %collective-permute-done.4.refs_5_), channel_id=1, source_target_pairs={{0,1},{1,0},{2,3},{3,2},{4,5},{5,4},{6,7},{7,6},{8,9},{9,8},{10,11... | collective-permute-start | bytes 1769480 | tf_op jit(solution)/shard_map/ppermute | solution.py:62
  48.9 7.7 %collective-permute-start.14 = (f32[288,512]{1,0:T(8,128)S(1)}, f32[288,512]{1,0:T(8,128)S(1)}, u32[]{:S(2)}, u32[]{:S(2)}) collective-permute-start(f32[288,512]{1,0:T(8,128)S(1)} %collective-permute-done.13.refs_14_), channel_id=1, source_target_pairs={{0,1},{1,0},{2,3},{3,2},{4,5},{5,4},{6,7},{7,6},{8,9},{9,8},{10,11... | collective-permute-start | bytes 1769480 | tf_op jit(solution)/shard_map/ppermute | solution.py:62
  59.2 17.0 %collective-permute-start.15 = (f32[384,512]{1,0:T(8,128)S(1)}, f32[384,512]{1,0:T(8,128)S(1)}, u32[]{:S(2)}, u32[]{:S(2)}) collective-permute-start(f32[384,512]{1,0:T(8,128)S(1)} %shard_map.130.turn), channel_id=1, source_target_pairs={{0,0},{1,161},{2,18},{3,179},{4,100},{5,197},{6,118},{7,215},{8,40... | collective-permute-start | bytes 2359304 | tf_op jit(solution)/shard_map/ppermute | solution.py:62
  74.1 26.2 %collective-permute-start.20 = (f32[8,128,512]{2,1,0:T(8,128)S(1)}, f32[8,128,512]{2,1,0:T(8,128)S(1)}, u32[]{:S(2)}, u32[]{:S(2)}) collective-permute-start(f32[8,128,512]{2,1,0:T(8,128)S(1)} %get-tuple-element.25), channel_id=1, source_target_pairs={{0,48},{1,193},{2,50},{3,195},{4,52},{5,197},{6,54},{7,199},{8,56}... | collective-permute-start | bytes 6291464 | tf_op jit(solution)/shard_map/ppermute | solution.py:62
  74.9 25.5 %collective-permute-start.16 = (f32[8,128,512]{2,1,0:T(8,128)S(1)}, f32[8,128,512]{2,1,0:T(8,128)S(1)}, u32[]{:S(2)}, u32[]{:S(2)}) collective-permute-start(f32[8,128,512]{2,1,0:T(8,128)S(1)} %get-tuple-element.23), channel_id=1, source_target_pairs={{0,16},{1,65},{2,18},{3,67},{4,20},{5,69},{6,22},{7,71},{8,24},{9,... | collective-permute-start | bytes 6291464 | tf_op jit(solution)/shard_map/ppermute | solution.py:62
  100.4 14.0 %collective-permute-start.21 = (f32[4,128,512]{2,1,0:T(8,128)S(1)}, f32[4,128,512]{2,1,0:T(8,128)S(1)}, u32[]{:S(2)}, u32[]{:S(2)}) collective-permute-start(f32[4,128,512]{2,1,0:T(8,128)S(1)} %shard_map.141), channel_id=1, source_target_pairs={{0,16},{1,65},{2,18},{3,67},{4,20},{5,69},{6,22},{7,71},{8,24},{9,... | collective-permute-start | bytes 3145736 | tf_op jit(solution)/shard_map/ppermute | solution.py:62
  100.6 15.8 %collective-permute-start.17 = (f32[4,128,512]{2,1,0:T(8,128)S(1)}, f32[4,128,512]{2,1,0:T(8,128)S(1)}, u32[]{:S(2)}, u32[]{:S(2)}) collective-permute-start(f32[4,128,512]{2,1,0:T(8,128)S(1)} %shard_map.134), channel_id=1, source_target_pairs={{0,48},{1,193},{2,50},{3,195},{4,52},{5,197},{6,54},{7,199},{8,56}... | collective-permute-start | bytes 3145736 | tf_op jit(solution)/shard_map/ppermute | solution.py:62
  102.2 23.3 %collective-permute-start.23 = (f32[384,512]{1,0:T(8,128)S(1)}, f32[384,512]{1,0:T(8,128)S(1)}, u32[]{:S(2)}, u32[]{:S(2)}) collective-permute-start(f32[384,512]{1,0:T(8,128)S(1)} %collective-permute-done.15.refs_0_), channel_id=1, source_target_pairs={{0,0},{1,10},{2,1},{3,11},{4,6},{5,12},{6,7},{7,13},{8,2},{9,8},{1... | collective-permute-start | bytes 2359304 | tf_op jit(solution)/shard_map/ppermute | solution.py:62
  114.5 11.0 %collective-permute-start.22 = (f32[2,128,512]{2,1,0:T(8,128)S(1)}, f32[2,128,512]{2,1,0:T(8,128)S(1)}, u32[]{:S(2)}, u32[]{:S(2)}) collective-permute-start(f32[2,128,512]{2,1,0:T(8,128)S(1)} %shard_map.143), channel_id=1, source_target_pairs={{0,192},{1,49},{2,194},{3,51},{4,196},{5,53},{6,198},{7,55},{8,200... | collective-permute-start | bytes 1572872 | tf_op jit(solution)/shard_map/ppermute | solution.py:62
  116.4 11.0 %collective-permute-start.18 = (f32[2,128,512]{2,1,0:T(8,128)S(1)}, f32[2,128,512]{2,1,0:T(8,128)S(1)}, u32[]{:S(2)}, u32[]{:S(2)}) collective-permute-start(f32[2,128,512]{2,1,0:T(8,128)S(1)} %shard_map.136), channel_id=1, source_target_pairs={{0,64},{1,17},{2,66},{3,19},{4,68},{5,21},{6,70},{7,23},{8,72},{9,... | collective-permute-start | bytes 1572872 | tf_op jit(solution)/shard_map/ppermute | solution.py:62
  127.5 6.5 %collective-permute-start.19 = (f32[1,128,512]{2,1,0:T(8,128)S(1)}, f32[1,128,512]{2,1,0:T(8,128)S(1)}, u32[]{:S(2)}, u32[]{:S(2)}) collective-permute-start(f32[1,128,512]{2,1,0:T(8,128)S(1)} %shard_map.138), channel_id=1, source_target_pairs={{0,192},{1,49},{2,194},{3,51},{4,196},{5,53},{6,198},{7,55},{8,200... | collective-permute-start | bytes 786440 | tf_op jit(solution)/shard_map/ppermute | solution.py:62
  135.2 9.7 %collective-permute-start.25 = (f32[136,128]{1,0:T(8,128)S(1)}, f32[136,128]{1,0:T(8,128)S(1)}, u32[]{:S(2)}, u32[]{:S(2)}) collective-permute-start(f32[136,128]{1,0:T(8,128)S(1)} %get-tuple-element.30), channel_id=1, source_target_pairs={{0,1},{1,0},{2,3},{3,2},{4,5},{5,4},{6,7},{7,6},{8,9},{9,8},{10,11... | collective-permute-start | bytes 208904 | tf_op jit(solution)/shard_map/ppermute | solution.py:62
  (11 other events, 180.3 us)

commit v12 on v11

--- a/solution.py
+++ b/solution.py
@@ -238,8 +238,13 @@
     for copy in high:
         copy.wait()
     for m in range(16):
-        par = split(unpack(one[m, 128:160, :]))
-        two[m] = two[m] - dot_split(par, split(one[parent[m], 0:128, :]), ((1,), (0,)))
+        high_par, low_par = split(unpack(one[m, 128:160, :]))
+        high_one, low_one = split(one[parent[m], 0:128, :])
+        two[m] = two[m] - jnp.dot(
+            jnp.concatenate([high_par, low_par, high_par], axis=1),
+            jnp.concatenate([high_one, high_one, low_one], axis=0),
+            preferred_element_type=jnp.float32,
+        )
     products(ginv, two, 1, row, core, 1, left, sends)
 
 

time: 164 us -> 164 us (level)
  transfers between devices with their start and end apart: 30 -> 30, of which waited for: 19 -> 19; matrix products, arithmetic and copies ran while one was open for 0% -> 0% of each run, Pallas kernels for 9% -> 8%
where the time goes in v12:
time: 164 us
  waiting for transfers between devices  82.2 us (50%)
  starting transfers between devices  60.2 us (37%)
  Pallas kernels  19.1 us (12%)
    ppermute x30, waiting for transfers between devices, permute(): return lax.ppermute(value, ALL, pairs)  82.2 us
    ppermute x30, starting transfers between devices, permute(): return lax.ppermute(value, ALL, pairs)  60.2 us
    pallas_call x1, Pallas kernels, send_half(): pl.pallas_call(send_kernel, out_shape=[f32(8, B, KA)] * 2 + [f32(16, 160,...  8.3 us
    pallas_call x1, Pallas kernels, keep_half(): pl.pallas_call(body, out_shape=[f32(8, B, KA)] * 2 + [f32(B, B), f32(384,...  4.69 us
  transfers between devices with their start and end apart: 30, of which 19 were waited for; matrix products, arithmetic and copies ran while one was open for 0% of the time, Pallas kernels for 8%

profile of v12, /device:TPU:7, one launch (start us, length us, event | category | flops | bytes accessed | tf_op | source)
XLA Modules:
  0.0 163.5 jit_solution(7173572869057997956)
XLA Ops:
  4.9 5.6 %collective-permute-start = (f32[288,512]{1,0:T(8,128)S(1)}, f32[288,512]{1,0:T(8,128)S(1)}, u32[]{:S(2)}, u32[]{:S(2)}) collective-permute-start(f32[288,512]{1,0:T(8,128)S(1)} %copy-done), channel_id=1, source_target_pairs={{0,2},{1,15},{2,4},{3,1},{4,6},{5,3},{6,8},{7,5},{8,10},{9,7},{10,... | collective-permute-start | bytes 1769480 | tf_op jit(solution)/shard_map/ppermute | solution.py:62
  12.1 5.2 %collective-permute-done.refs_1_ = f32[288,512]{1,0:T(8,128)S(1)} collective-permute-done((f32[288,512]{1,0:T(8,128)S(1)}, f32[288,512]{1,0:T(8,128)S(1)}, u32[]{:S(2)}, u32[]{:S(2)}) %collective-permute-start) | collective-permute-done | bytes 589856 | tf_op jit(solution)/shard_map/ppermute | solution.py:62
  17.3 3.1 %collective-permute-start.2 = (f32[288,512]{1,0:T(8,128)S(1)}, f32[288,512]{1,0:T(8,128)S(1)}, u32[]{:S(2)}, u32[]{:S(2)}) collective-permute-start(f32[288,512]{1,0:T(8,128)S(1)} %collective-permute-done.refs_1_), channel_id=1, source_target_pairs={{0,2},{1,15},{2,4},{3,1},{4,6},{5,3},{6,8},{7,5},{8,10},{9,7},{10,... | collective-permute-start | bytes 1769480 | tf_op jit(solution)/shard_map/ppermute | solution.py:62
  20.4 3.2 %collective-permute-done.9.refs_10_ = f32[288,512]{1,0:T(8,128)S(1)} collective-permute-done((f32[288,512]{1,0:T(8,128)S(1)}, f32[288,512]{1,0:T(8,128)S(1)}, u32[]{:S(2)}, u32[]{:S(2)}) %collective-permute-start.9) | collective-permute-done | bytes 589856 | tf_op jit(solution)/shard_map/ppermute | solution.py:62
  23.6 3.1 %collective-permute-start.11 = (f32[288,512]{1,0:T(8,128)S(1)}, f32[288,512]{1,0:T(8,128)S(1)}, u32[]{:S(2)}, u32[]{:S(2)}) collective-permute-start(f32[288,512]{1,0:T(8,128)S(1)} %collective-permute-done.9.refs_10_), channel_id=1, source_target_pairs={{0,2},{1,15},{2,4},{3,1},{4,6},{5,3},{6,8},{7,5},{8,10},{9,7},{10,... | collective-permute-start | bytes 1769480 | tf_op jit(solution)/shard_map/ppermute | solution.py:62
  26.7 3.2 %collective-permute-done.2.refs_3_ = f32[288,512]{1,0:T(8,128)S(1)} collective-permute-done((f32[288,512]{1,0:T(8,128)S(1)}, f32[288,512]{1,0:T(8,128)S(1)}, u32[]{:S(2)}, u32[]{:S(2)}) %collective-permute-start.2) | collective-permute-done | bytes 589856 | tf_op jit(solution)/shard_map/ppermute | solution.py:62
  29.9 3.1 %collective-permute-start.4 = (f32[288,512]{1,0:T(8,128)S(1)}, f32[288,512]{1,0:T(8,128)S(1)}, u32[]{:S(2)}, u32[]{:S(2)}) collective-permute-start(f32[288,512]{1,0:T(8,128)S(1)} %collective-permute-done.2.refs_3_), channel_id=1, source_target_pairs={{0,2},{1,15},{2,4},{3,1},{4,6},{5,3},{6,8},{7,5},{8,10},{9,7},{10,... | collective-permute-start | bytes 1769480 | tf_op jit(solution)/shard_map/ppermute | solution.py:62
  36.2 3.1 %collective-permute-start.13 = (f32[288,512]{1,0:T(8,128)S(1)}, f32[288,512]{1,0:T(8,128)S(1)}, u32[]{:S(2)}, u32[]{:S(2)}) collective-permute-start(f32[288,512]{1,0:T(8,128)S(1)} %collective-permute-done.11.refs_12_), channel_id=1, source_target_pairs={{0,2},{1,15},{2,4},{3,1},{4,6},{5,3},{6,8},{7,5},{8,10},{9,7},{10,... | collective-permute-start | bytes 1769480 | tf_op jit(solution)/shard_map/ppermute | solution.py:62
  39.4 3.2 %collective-permute-done.4.refs_5_ = f32[288,512]{1,0:T(8,128)S(1)} collective-permute-done((f32[288,512]{1,0:T(8,128)S(1)}, f32[288,512]{1,0:T(8,128)S(1)}, u32[]{:S(2)}, u32[]{:S(2)}) %collective-permute-start.4) | collective-permute-done | bytes 589856 | tf_op jit(solution)/shard_map/ppermute | solution.py:62
  42.6 3.1 %collective-permute-start.6 = (f32[288,512]{1,0:T(8,128)S(1)}, f32[288,512]{1,0:T(8,128)S(1)}, u32[]{:S(2)}, u32[]{:S(2)}) collective-permute-start(f32[288,512]{1,0:T(8,128)S(1)} %collective-permute-done.4.refs_5_), channel_id=1, source_target_pairs={{0,2},{1,15},{2,4},{3,1},{4,6},{5,3},{6,8},{7,5},{8,10},{9,7},{10,... | collective-permute-start | bytes 1769480 | tf_op jit(solution)/shard_map/ppermute | solution.py:62
  50.3 4.9 %collective-permute-done.6.refs_7_ = f32[288,512]{1,0:T(8,128)S(1)} collective-permute-done((f32[288,512]{1,0:T(8,128)S(1)}, f32[288,512]{1,0:T(8,128)S(1)}, u32[]{:S(2)}, u32[]{:S(2)}) %collective-permute-start.6) | collective-permute-done | bytes 589856 | tf_op jit(solution)/shard_map/ppermute | solution.py:62
  59.2 6.0 %collective-permute-start.15 = (f32[384,512]{1,0:T(8,128)S(1)}, f32[384,512]{1,0:T(8,128)S(1)}, u32[]{:S(2)}, u32[]{:S(2)}) collective-permute-start(f32[384,512]{1,0:T(8,128)S(1)} %shard_map.130.turn), channel_id=1, source_target_pairs={{0,0},{1,161},{2,18},{3,179},{4,100},{5,197},{6,118},{7,215},{8,40... | collective-permute-start | bytes 2359304 | tf_op jit(solution)/shard_map/ppermute | solution.py:62
  65.2 8.3 %shard_map.131 = (f32[8,128,512]{2,1,0:T(8,128)S(1)}, f32[8,128,512]{2,1,0:T(8,128)S(1)}, f32[16,160,512]{2,1,0:T(8,128)S(1)}, f32[16,128,512]{2,1,0:T(8,128)S(1)}) custom-call(s32[16]{0:T(128)S(1)} %copy-done.1, f32[512,512]{1,0:T(8,128)S(1)} %copy-done.2, f32[384,512]{1,0:T(8,128)S(1)} %shard_map.130.turn, f32[288,512]{1,0:T(8,128)S(1)} %shard_map.129.refs_0_, ...), custom_call_target="tpu_custom_call" | custom-call | flops 20000000000 | bytes 1000000 | tf_op jit(solution)/shard_map/pallas_call | solution.py:252
  76.8 4.7 %shard_map.132 = (f32[8,128,512]{2,1,0:T(8,128)S(1)}, f32[8,128,512]{2,1,0:T(8,128)S(1)}, f32[128,128]{1,0:T(8,128)S(1)}, f32[384,128]{1,0:T(8,128)S(1)}) custom-call(s32[16]{0:T(128)S(1)} %copy-done.1, f32[512,512]{1,0:T(8,128)S(1)} %copy-done.2, f32[16,160,512]{2,1,0:T(8,128)S(1)} %get-tuple-element.20.one, f32[16,128,512]{2,1,0:T(8,128)S(1)} %get-tuple-element.21.two, ...), custom_call_target="tpu_custom_call" | custom-call | flops 60000002048 | bytes 1000000 | tf_op jit(solution)/shard_map/pallas_call | solution.py:279
  81.4 18.3 %collective-permute-done.20.b = f32[8,128,512]{2,1,0:T(8,128)S(1)} collective-permute-done((f32[8,128,512]{2,1,0:T(8,128)S(1)}, f32[8,128,512]{2,1,0:T(8,128)S(1)}, u32[]{:S(2)}, u32[]{:S(2)}) %collective-permute-start.20) | collective-permute-done | bytes 2097184 | tf_op jit(solution)/shard_map/ppermute | solution.py:62
  102.2 4.9 %collective-permute-start.23 = (f32[384,512]{1,0:T(8,128)S(1)}, f32[384,512]{1,0:T(8,128)S(1)}, u32[]{:S(2)}, u32[]{:S(2)}) collective-permute-start(f32[384,512]{1,0:T(8,128)S(1)} %collective-permute-done.15.refs_0_), channel_id=1, source_target_pairs={{0,0},{1,10},{2,1},{3,11},{4,6},{5,12},{6,7},{7,13},{8,2},{9,8},{1... | collective-permute-start | bytes 2359304 | tf_op jit(solution)/shard_map/ppermute | solution.py:62
  107.3 6.6 %collective-permute-done.21.b = f32[4,128,512]{2,1,0:T(8,128)S(1)} collective-permute-done((f32[4,128,512]{2,1,0:T(8,128)S(1)}, f32[4,128,512]{2,1,0:T(8,128)S(1)}, u32[]{:S(2)}, u32[]{:S(2)}) %collective-permute-start.21) | collective-permute-done | bytes 1048608 | tf_op jit(solution)/shard_map/ppermute | solution.py:62
  116.4 8.5 %collective-permute-done.23.refs_0_.turn = f32[384,512]{1,0:T(8,128)S(1)} collective-permute-done((f32[384,512]{1,0:T(8,128)S(1)}, f32[384,512]{1,0:T(8,128)S(1)}, u32[]{:S(2)}, u32[]{:S(2)}) %collective-permute-start.23) | collective-permute-done | bytes 786464 | tf_op jit(solution)/shard_map/ppermute | solution.py:62
  127.6 3.5 %collective-permute-done.24.b = f32[1,128,512]{2,1,0:T(8,128)S(1)} collective-permute-done((f32[1,128,512]{2,1,0:T(8,128)S(1)}, f32[1,128,512]{2,1,0:T(8,128)S(1)}, u32[]{:S(2)}, u32[]{:S(2)}) %collective-permute-start.24) | collective-permute-done | bytes 262176 | tf_op jit(solution)/shard_map/ppermute | solution.py:62
  135.2 8.8 %collective-permute-start.25 = (f32[136,128]{1,0:T(8,128)S(1)}, f32[136,128]{1,0:T(8,128)S(1)}, u32[]{:S(2)}, u32[]{:S(2)}) collective-permute-start(f32[136,128]{1,0:T(8,128)S(1)} %get-tuple-element.30), channel_id=1, source_target_pairs={{0,1},{1,0},{2,3},{3,2},{4,5},{5,4},{6,7},{7,6},{8,9},{9,8},{10,11... | collective-permute-start | bytes 208904 | tf_op jit(solution)/shard_map/ppermute | solution.py:62
  145.0 3.1 %collective-permute-done.26 = f32[136,128]{1,0:T(8,128)S(1)} collective-permute-done((f32[136,128]{1,0:T(8,128)S(1)}, f32[136,128]{1,0:T(8,128)S(1)}, u32[]{:S(2)}, u32[]{:S(2)}) %collective-permute-start.26) | collective-permute-done | bytes 69664 | tf_op jit(solution)/shard_map/ppermute | solution.py:62
  148.3 5.0 %collective-permute-done.27 = f32[136,128]{1,0:T(8,128)S(1)} collective-permute-done((f32[136,128]{1,0:T(8,128)S(1)}, f32[136,128]{1,0:T(8,128)S(1)}, u32[]{:S(2)}, u32[]{:S(2)}) %collective-permute-start.27) | collective-permute-done | bytes 69664 | tf_op jit(solution)/shard_map/ppermute | solution.py:62
  154.3 3.5 %collective-permute-done.28 = f32[136,128]{1,0:T(8,128)S(1)} collective-permute-done((f32[136,128]{1,0:T(8,128)S(1)}, f32[136,128]{1,0:T(8,128)S(1)}, u32[]{:S(2)}, u32[]{:S(2)}) %collective-permute-start.28) | collective-permute-done | bytes 69664 | tf_op jit(solution)/shard_map/ppermute | solution.py:62
  157.8 4.0 %collective-permute-start.29 = (f32[136,128]{1,0:T(8,128)S(1)}, f32[136,128]{1,0:T(8,128)S(1)}, u32[]{:S(2)}, u32[]{:S(2)}) collective-permute-start(f32[136,128]{1,0:T(8,128)S(1)} %add.15.own), channel_id=1, source_target_pairs={{0,1},{1,0},{2,3},{3,2},{4,5},{5,4},{6,7},{7,6},{8,9},{9,8},{10,11... | collective-permute-start | bytes 208904 | tf_op jit(solution)/shard_map/ppermute | solution.py:62
  (71 shorter events, 36.5 us)
Async XLA Ops:
  4.1 6.3 %collective-permute-start.8 = (f32[288,512]{1,0:T(8,128)S(1)}, f32[288,512]{1,0:T(8,128)S(1)}, u32[]{:S(2)}, u32[]{:S(2)}) collective-permute-start(f32[288,512]{1,0:T(8,128)S(1)} %shard_map.129.refs_0_), channel_id=1, source_target_pairs={{0,1},{1,0},{2,3},{3,2},{4,5},{5,4},{6,7},{7,6},{8,9},{9,8},{10,11... | collective-permute-start | bytes 1769480 | tf_op jit(solution)/shard_map/ppermute | solution.py:62
  4.9 12.4 %collective-permute-start = (f32[288,512]{1,0:T(8,128)S(1)}, f32[288,512]{1,0:T(8,128)S(1)}, u32[]{:S(2)}, u32[]{:S(2)}) collective-permute-start(f32[288,512]{1,0:T(8,128)S(1)} %copy-done), channel_id=1, source_target_pairs={{0,2},{1,15},{2,4},{3,1},{4,6},{5,3},{6,8},{7,5},{8,10},{9,7},{10,... | collective-permute-start | bytes 1769480 | tf_op jit(solution)/shard_map/ppermute | solution.py:62
  10.5 13.1 %collective-permute-start.9 = (f32[288,512]{1,0:T(8,128)S(1)}, f32[288,512]{1,0:T(8,128)S(1)}, u32[]{:S(2)}, u32[]{:S(2)}) collective-permute-start(f32[288,512]{1,0:T(8,128)S(1)} %collective-permute-done.8.refs_9_), channel_id=1, source_target_pairs={{0,2},{1,15},{2,4},{3,1},{4,6},{5,3},{6,8},{7,5},{8,10},{9,7},{10,... | collective-permute-start | bytes 1769480 | tf_op jit(solution)/shard_map/ppermute | solution.py:62
  17.3 12.6 %collective-permute-start.2 = (f32[288,512]{1,0:T(8,128)S(1)}, f32[288,512]{1,0:T(8,128)S(1)}, u32[]{:S(2)}, u32[]{:S(2)}) collective-permute-start(f32[288,512]{1,0:T(8,128)S(1)} %collective-permute-done.refs_1_), channel_id=1, source_target_pairs={{0,2},{1,15},{2,4},{3,1},{4,6},{5,3},{6,8},{7,5},{8,10},{9,7},{10,... | collective-permute-start | bytes 1769480 | tf_op jit(solution)/shard_map/ppermute | solution.py:62
  23.6 12.6 %collective-permute-start.11 = (f32[288,512]{1,0:T(8,128)S(1)}, f32[288,512]{1,0:T(8,128)S(1)}, u32[]{:S(2)}, u32[]{:S(2)}) collective-permute-start(f32[288,512]{1,0:T(8,128)S(1)} %collective-permute-done.9.refs_10_), channel_id=1, source_target_pairs={{0,2},{1,15},{2,4},{3,1},{4,6},{5,3},{6,8},{7,5},{8,10},{9,7},{10,... | collective-permute-start | bytes 1769480 | tf_op jit(solution)/shard_map/ppermute | solution.py:62
  29.9 12.6 %collective-permute-start.4 = (f32[288,512]{1,0:T(8,128)S(1)}, f32[288,512]{1,0:T(8,128)S(1)}, u32[]{:S(2)}, u32[]{:S(2)}) collective-permute-start(f32[288,512]{1,0:T(8,128)S(1)} %collective-permute-done.2.refs_3_), channel_id=1, source_target_pairs={{0,2},{1,15},{2,4},{3,1},{4,6},{5,3},{6,8},{7,5},{8,10},{9,7},{10,... | collective-permute-start | bytes 1769480 | tf_op jit(solution)/shard_map/ppermute | solution.py:62
  33.0 12.6 %collective-permute-start.1 = (f32[288,512]{1,0:T(8,128)S(1)}, f32[288,512]{1,0:T(8,128)S(1)}, u32[]{:S(2)}, u32[]{:S(2)}) collective-permute-start(f32[288,512]{1,0:T(8,128)S(1)} %collective-permute-done.refs_1_), channel_id=1, source_target_pairs={{0,1},{1,0},{2,3},{3,2},{4,5},{5,4},{6,7},{7,6},{8,9},{9,8},{10,11... | collective-permute-start | bytes 1769480 | tf_op jit(solution)/shard_map/ppermute | solution.py:62
  33.0 13.2 %collective-permute-start.10 = (f32[288,512]{1,0:T(8,128)S(1)}, f32[288,512]{1,0:T(8,128)S(1)}, u32[]{:S(2)}, u32[]{:S(2)}) collective-permute-start(f32[288,512]{1,0:T(8,128)S(1)} %collective-permute-done.9.refs_10_), channel_id=1, source_target_pairs={{0,1},{1,0},{2,3},{3,2},{4,5},{5,4},{6,7},{7,6},{8,9},{9,8},{10,11... | collective-permute-start | bytes 1769480 | tf_op jit(solution)/shard_map/ppermute | solution.py:62
  36.2 12.6 %collective-permute-start.13 = (f32[288,512]{1,0:T(8,128)S(1)}, f32[288,512]{1,0:T(8,128)S(1)}, u32[]{:S(2)}, u32[]{:S(2)}) collective-permute-start(f32[288,512]{1,0:T(8,128)S(1)} %collective-permute-done.11.refs_12_), channel_id=1, source_target_pairs={{0,2},{1,15},{2,4},{3,1},{4,6},{5,3},{6,8},{7,5},{8,10},{9,7},{10,... | collective-permute-start | bytes 1769480 | tf_op jit(solution)/shard_map/ppermute | solution.py:62
  42.6 12.6 %collective-permute-start.6 = (f32[288,512]{1,0:T(8,128)S(1)}, f32[288,512]{1,0:T(8,128)S(1)}, u32[]{:S(2)}, u32[]{:S(2)}) collective-permute-start(f32[288,512]{1,0:T(8,128)S(1)} %collective-permute-done.4.refs_5_), channel_id=1, source_target_pairs={{0,2},{1,15},{2,4},{3,1},{4,6},{5,3},{6,8},{7,5},{8,10},{9,7},{10,... | collective-permute-start | bytes 1769480 | tf_op jit(solution)/shard_map/ppermute | solution.py:62
  45.7 10.9 %collective-permute-start.3 = (f32[288,512]{1,0:T(8,128)S(1)}, f32[288,512]{1,0:T(8,128)S(1)}, u32[]{:S(2)}, u32[]{:S(2)}) collective-permute-start(f32[288,512]{1,0:T(8,128)S(1)} %collective-permute-done.2.refs_3_), channel_id=1, source_target_pairs={{0,1},{1,0},{2,3},{3,2},{4,5},{5,4},{6,7},{7,6},{8,9},{9,8},{10,11... | collective-permute-start | bytes 1769480 | tf_op jit(solution)/shard_map/ppermute | solution.py:62
  45.7 10.9 %collective-permute-start.12 = (f32[288,512]{1,0:T(8,128)S(1)}, f32[288,512]{1,0:T(8,128)S(1)}, u32[]{:S(2)}, u32[]{:S(2)}) collective-permute-start(f32[288,512]{1,0:T(8,128)S(1)} %collective-permute-done.11.refs_12_), channel_id=1, source_target_pairs={{0,1},{1,0},{2,3},{3,2},{4,5},{5,4},{6,7},{7,6},{8,9},{9,8},{10,11... | collective-permute-start | bytes 1769480 | tf_op jit(solution)/shard_map/ppermute | solution.py:62
  46.2 10.4 %collective-permute-start.5 = (f32[288,512]{1,0:T(8,128)S(1)}, f32[288,512]{1,0:T(8,128)S(1)}, u32[]{:S(2)}, u32[]{:S(2)}) collective-permute-start(f32[288,512]{1,0:T(8,128)S(1)} %collective-permute-done.4.refs_5_), channel_id=1, source_target_pairs={{0,1},{1,0},{2,3},{3,2},{4,5},{5,4},{6,7},{7,6},{8,9},{9,8},{10,11... | collective-permute-start | bytes 1769480 | tf_op jit(solution)/shard_map/ppermute | solution.py:62
  48.9 7.7 %collective-permute-start.14 = (f32[288,512]{1,0:T(8,128)S(1)}, f32[288,512]{1,0:T(8,128)S(1)}, u32[]{:S(2)}, u32[]{:S(2)}) collective-permute-start(f32[288,512]{1,0:T(8,128)S(1)} %collective-permute-done.13.refs_14_), channel_id=1, source_target_pairs={{0,1},{1,0},{2,3},{3,2},{4,5},{5,4},{6,7},{7,6},{8,9},{9,8},{10,11... | collective-permute-start | bytes 1769480 | tf_op jit(solution)/shard_map/ppermute | solution.py:62
  59.2 17.5 %collective-permute-start.15 = (f32[384,512]{1,0:T(8,128)S(1)}, f32[384,512]{1,0:T(8,128)S(1)}, u32[]{:S(2)}, u32[]{:S(2)}) collective-permute-start(f32[384,512]{1,0:T(8,128)S(1)} %shard_map.130.turn), channel_id=1, source_target_pairs={{0,0},{1,161},{2,18},{3,179},{4,100},{5,197},{6,118},{7,215},{8,40... | collective-permute-start | bytes 2359304 | tf_op jit(solution)/shard_map/ppermute | solution.py:62
  73.5 26.2 %collective-permute-start.20 = (f32[8,128,512]{2,1,0:T(8,128)S(1)}, f32[8,128,512]{2,1,0:T(8,128)S(1)}, u32[]{:S(2)}, u32[]{:S(2)}) collective-permute-start(f32[8,128,512]{2,1,0:T(8,128)S(1)} %get-tuple-element.25), channel_id=1, source_target_pairs={{0,48},{1,193},{2,50},{3,195},{4,52},{5,197},{6,54},{7,199},{8,56}... | collective-permute-start | bytes 6291464 | tf_op jit(solution)/shard_map/ppermute | solution.py:62
  74.4 25.6 %collective-permute-start.16 = (f32[8,128,512]{2,1,0:T(8,128)S(1)}, f32[8,128,512]{2,1,0:T(8,128)S(1)}, u32[]{:S(2)}, u32[]{:S(2)}) collective-permute-start(f32[8,128,512]{2,1,0:T(8,128)S(1)} %get-tuple-element.23), channel_id=1, source_target_pairs={{0,16},{1,65},{2,18},{3,67},{4,20},{5,69},{6,22},{7,71},{8,24},{9,... | collective-permute-start | bytes 6291464 | tf_op jit(solution)/shard_map/ppermute | solution.py:62
  99.8 14.0 %collective-permute-start.21 = (f32[4,128,512]{2,1,0:T(8,128)S(1)}, f32[4,128,512]{2,1,0:T(8,128)S(1)}, u32[]{:S(2)}, u32[]{:S(2)}) collective-permute-start(f32[4,128,512]{2,1,0:T(8,128)S(1)} %shard_map.141), channel_id=1, source_target_pairs={{0,16},{1,65},{2,18},{3,67},{4,20},{5,69},{6,22},{7,71},{8,24},{9,... | collective-permute-start | bytes 3145736 | tf_op jit(solution)/shard_map/ppermute | solution.py:62
  100.1 15.7 %collective-permute-start.17 = (f32[4,128,512]{2,1,0:T(8,128)S(1)}, f32[4,128,512]{2,1,0:T(8,128)S(1)}, u32[]{:S(2)}, u32[]{:S(2)}) collective-permute-start(f32[4,128,512]{2,1,0:T(8,128)S(1)} %shard_map.134), channel_id=1, source_target_pairs={{0,48},{1,193},{2,50},{3,195},{4,52},{5,197},{6,54},{7,199},{8,56}... | collective-permute-start | bytes 3145736 | tf_op jit(solution)/shard_map/ppermute | solution.py:62
  102.2 22.8 %collective-permute-start.23 = (f32[384,512]{1,0:T(8,128)S(1)}, f32[384,512]{1,0:T(8,128)S(1)}, u32[]{:S(2)}, u32[]{:S(2)}) collective-permute-start(f32[384,512]{1,0:T(8,128)S(1)} %collective-permute-done.15.refs_0_), channel_id=1, source_target_pairs={{0,0},{1,10},{2,1},{3,11},{4,6},{5,12},{6,7},{7,13},{8,2},{9,8},{1... | collective-permute-start | bytes 2359304 | tf_op jit(solution)/shard_map/ppermute | solution.py:62
  113.9 11.0 %collective-permute-start.22 = (f32[2,128,512]{2,1,0:T(8,128)S(1)}, f32[2,128,512]{2,1,0:T(8,128)S(1)}, u32[]{:S(2)}, u32[]{:S(2)}) collective-permute-start(f32[2,128,512]{2,1,0:T(8,128)S(1)} %shard_map.143), channel_id=1, source_target_pairs={{0,192},{1,49},{2,194},{3,51},{4,196},{5,53},{6,198},{7,55},{8,200... | collective-permute-start | bytes 1572872 | tf_op jit(solution)/shard_map/ppermute | solution.py:62
  115.9 11.5 %collective-permute-start.18 = (f32[2,128,512]{2,1,0:T(8,128)S(1)}, f32[2,128,512]{2,1,0:T(8,128)S(1)}, u32[]{:S(2)}, u32[]{:S(2)}) collective-permute-start(f32[2,128,512]{2,1,0:T(8,128)S(1)} %shard_map.136), channel_id=1, source_target_pairs={{0,64},{1,17},{2,66},{3,19},{4,68},{5,21},{6,70},{7,23},{8,72},{9,... | collective-permute-start | bytes 1572872 | tf_op jit(solution)/shard_map/ppermute | solution.py:62
  127.5 6.5 %collective-permute-start.19 = (f32[1,128,512]{2,1,0:T(8,128)S(1)}, f32[1,128,512]{2,1,0:T(8,128)S(1)}, u32[]{:S(2)}, u32[]{:S(2)}) collective-permute-start(f32[1,128,512]{2,1,0:T(8,128)S(1)} %shard_map.138), channel_id=1, source_target_pairs={{0,192},{1,49},{2,194},{3,51},{4,196},{5,53},{6,198},{7,55},{8,200... | collective-permute-start | bytes 786440 | tf_op jit(solution)/shard_map/ppermute | solution.py:62
  135.2 9.7 %collective-permute-start.25 = (f32[136,128]{1,0:T(8,128)S(1)}, f32[136,128]{1,0:T(8,128)S(1)}, u32[]{:S(2)}, u32[]{:S(2)}) collective-permute-start(f32[136,128]{1,0:T(8,128)S(1)} %get-tuple-element.30), channel_id=1, source_target_pairs={{0,1},{1,0},{2,3},{3,2},{4,5},{5,4},{6,7},{7,6},{8,9},{9,8},{10,11... | collective-permute-start | bytes 208904 | tf_op jit(solution)/shard_map/ppermute | solution.py:62
  (11 other events, 181.9 us)
